TPU v7x, 32 devices: a whole 2x2x4 slice. The times are simulated.
32 devices in a mesh: slab: 8 (over z, y), col: 4 (over x, core).
Axes of the slice: x: 2, y: 2, z: 4, core: 2. Of those that a mesh axis runs over, the one named last changes fastest.
Arguments:
- wave_amplitudes: float32 [8, 512, 128], P('slab', 'col'), may hold values from -6 to 6
- energy_block_per_segment: float32 [8, 512, 512], P('slab', 'col'), as said below
- tunnel_coupling_block: float32 [8, 512, 512], P('slab', 'col'), may hold values from -0.25 to 0.25
- reduced_block_reciprocal: float32 [8, 2, 512, 512], P('slab', None, 'col'), may hold values from -0.1875 to 0.1875
- beneath_reduce_multiplier: float32 [8, 2, 512, 512], P('slab', None, 'col'), may hold values from -0.09375 to 0.09375
- above_reduce_multiplier: float32 [8, 2, 512, 512], P('slab', None, 'col'), may hold values from -0.09375 to 0.09375
- beneath_solve_multiplier: float32 [8, 2, 512, 512], P('slab', None, 'col'), may hold values from -0.09375 to 0.09375
- above_solve_multiplier: float32 [8, 2, 512, 512], P('slab', None, 'col'), may hold values from -0.09375 to 0.09375
Outputs:
- psi_next: float32 [8, 512, 128], P('slab', 'col')
Inputs may be any that keep to these rules, and one draw needn't show every extreme that they name: energy_block_per_segment[s] is a symmetric matrix for every slab s.
All inputs are finite; a program needn't handle non-finite values.
Results may differ from a plain program's by a relative error of at most 0.00011.
Values sent between devices are 32-bit elements; how exact they have to be, the bound alone decides.
No kernel may reach another device: no remote copies, remote signals or barrier semaphores. Data moves between devices by JAX's collectives and lax.ppermute only.
A program may use at most 64 MiB of HBM per device.

v0:
```python
import jax
import jax.numpy as jnp
from jax import lax
from jax.sharding import PartitionSpec as P

half_step = 0.5
highest = lax.Precision.HIGHEST


def from_behind(block, axis, distance):
    devices = range(lax.axis_size(axis))
    route = [(i - distance, i) for i in devices if i - distance in devices]
    return lax.ppermute(block, axis, route)


def rotate(values):
    column = lax.broadcasted_iota(jnp.int32, values.shape, values.ndim - 1)
    return jnp.where(column % 2 == 0, -jnp.roll(values, -1, axis=-1), jnp.roll(values, 1, axis=-1))


def plain_dot(left, right):
    return jnp.dot(left, right, precision=highest, preferred_element_type=jnp.float32)


def transposed_dot(left, right):
    return lax.dot_general(
        left, right, (((0,), (0,)), ((), ())), precision=highest, preferred_element_type=jnp.float32
    )


def complex_matmul(block, vectors):
    return plain_dot(block[0], vectors) + rotate(plain_dot(block[1], vectors))


def slab_step(values, tier_spacing):
    return from_behind(values, "slab", tier_spacing)


def gather_rows(values):
    return lax.all_gather(values, "col", axis=0, tiled=True)


def per_device(
    wave_amplitudes,
    energy_block_per_segment,
    tunnel_coupling_block,
    reduced_block_reciprocal,
    beneath_reduce_multiplier,
    above_reduce_multiplier,
    beneath_solve_multiplier,
    above_solve_multiplier,
):
    states = wave_amplitudes[0]
    slab_index = lax.axis_index("slab")
    level_total = lax.axis_size("slab").bit_length() - 1
    up_rows = tunnel_coupling_block[0]
    next_shard = slab_step(states, -1)
    prev_shard = slab_step(states, 1)
    psi_full, next_full, prev_full = (
        lax.all_gather(states, "col", axis=0, tiled=True),
        lax.all_gather(next_shard, "col", axis=0, tiled=True),
        lax.all_gather(prev_shard, "col", axis=0, tiled=True),
    )
    below_rows = from_behind(up_rows, "slab", 1)
    below_cols = lax.all_to_all(below_rows, "col", split_axis=1, concat_axis=0, tiled=True)
    prev_term = transposed_dot(below_cols, prev_full)
    ham_psi = (
        plain_dot(energy_block_per_segment[0], psi_full) + plain_dot(up_rows, next_full) + prev_term
    )
    reduced = states - half_step * rotate(ham_psi)
    pivot_block = reduced_block_reciprocal[0]
    beneath_removal = beneath_reduce_multiplier[0]
    above_removal = above_reduce_multiplier[0]
    lower_back = beneath_solve_multiplier[0]
    upper_back = above_solve_multiplier[0]
    zeros_vec = jnp.zeros_like(states)
    pivot_part = zeros_vec
    for level_id in range(level_total):
        tier_spacing = 2**level_id
        active = slab_index % (2 * tier_spacing) == tier_spacing
        reduced_full = gather_rows(reduced)

        def eliminate(present_tier):
            return (
                complex_matmul(pivot_block, present_tier),
                complex_matmul(beneath_removal, present_tier),
                complex_matmul(above_removal, present_tier),
            )

        def pass_case(present_tier):
            return (zeros_vec, zeros_vec, zeros_vec)

        pivot_piece, heading_beneath, heading_above = lax.cond(
            active, eliminate, pass_case, reduced_full
        )
        pivot_part = jnp.where(active, pivot_piece, pivot_part)
        reduced = (
            reduced
            - slab_step(heading_beneath, -tier_spacing)
            - slab_step(heading_above, tier_spacing)
        )
    is_root = slab_index == 0
    root_full = gather_rows(reduced)

    def root_solve(present_tier):
        return complex_matmul(pivot_block, present_tier)

    def root_pass(present_tier):
        return zeros_vec

    pivot_part = jnp.where(is_root, lax.cond(is_root, root_solve, root_pass, root_full), pivot_part)
    solved = jnp.where(is_root, pivot_part, zeros_vec)
    for level_id in reversed(range(level_total)):
        tier_spacing = 2**level_id
        active = slab_index % (2 * tier_spacing) == tier_spacing
        lower_in = slab_step(solved, tier_spacing)
        upper_in = slab_step(solved, -tier_spacing)
        lower_full, upper_full = (
            lax.all_gather(lower_in, "col", axis=0, tiled=True),
            lax.all_gather(upper_in, "col", axis=0, tiled=True),
        )

        def settle(pair_in):
            return (
                pivot_part
                - complex_matmul(lower_back, pair_in[0])
                - complex_matmul(upper_back, pair_in[1])
            )

        def keep_case(pair_in):
            return solved

        solved = lax.cond(active, settle, keep_case, (lower_full, upper_full))
    return solved[None]


def solution(mesh):
    placed = (
        P("slab", "col", None),
        P("slab", "col", None),
        P("slab", "col", None),
        P("slab", None, "col", None),
        P("slab", None, "col", None),
        P("slab", None, "col", None),
        P("slab", None, "col", None),
        P("slab", None, "col", None),
    )
    return jax.shard_map(
        per_device, mesh=mesh, in_specs=placed, out_specs=P("slab", "col", None), check_vma=False
    )
```

profile of v0, /device:TPU:13, one launch (start us, length us, event | category | flops | bytes accessed | tf_op | source)
XLA Modules:
  0.0 158.1 jit_solution(15556099951096700906)
XLA Ops:
  3.1 4.0 %collective-permute-start.2 = (f32[128,128]{0,1:T(8,128)S(1)}, f32[128,128]{0,1:T(8,128)S(1)}, u32[]{:S(2)}, u32[]{:S(2)}) collective-permute-start(f32[128,128]{0,1:T(8,128)S(1)} %bitcast.174), channel_id=1, source_target_pairs={{0,4},{4,8},{8,12},{12,16},{16,20},{20,24},{24,28},{1,5},{5,9},{9,... | collective-permute-start | bytes 196616 | tf_op jit(solution)/shard_map/ppermute | solution.py:13
  10.6 7.1 %all-gather = f32[1,512,128]{2,1,0:T(8,128)S(1)} all-gather(f32[1,128,128]{2,1,0:T(8,128)S(1)} %copy-done.7), channel_id=2, replica_groups=mesh['slab'=8,'col'=4] {'col'}, dimensions={1}, use_global_device_ids=true | all-gather | bytes 327680 | tf_op jit(solution)/shard_map/all_gather | solution.py:60
  18.3 5.9 %all_gather.41 = f32[512,128]{0,1:T(8,128)S(1)} all-gather(f32[128,128]{0,1:T(8,128)S(1)} %collective-permute-done.2), channel_id=1, replica_groups=mesh['slab'=8,'col'=4] {'col'}, dimensions={0}, use_global_device_ids=true | all-gather | bytes 327680 | tf_op jit(solution)/shard_map/all_gather | solution.py:62
  24.2 5.9 %all_gather.40 = f32[512,128]{0,1:T(8,128)S(1)} all-gather(f32[128,128]{0,1:T(8,128)S(1)} %collective-permute-done), channel_id=1, replica_groups=mesh['slab'=8,'col'=4] {'col'}, dimensions={0}, use_global_device_ids=true | all-gather | bytes 327680 | tf_op jit(solution)/shard_map/all_gather | solution.py:61
  30.1 3.7 %all-to-all-start = ((f32[128,4,128]{0,2,1:T(8,128)}), f32[128,4,128]{0,2,1:T(8,128)S(1)}, u32[]{:S(2)}, u32[]{:S(2)}) async-start(f32[128,4,128]{0,2,1:T(8,128)} %bitcast.39), calls=%async_computation | async-start | bytes 524288 | tf_op jit(solution)/shard_map/all_to_all | solution.py:65
  34.1 4.8 %all-to-all-done = f32[128,4,128]{0,2,1:T(8,128)S(1)} async-done(((f32[128,4,128]{0,2,1:T(8,128)}), f32[128,4,128]{0,2,1:T(8,128)S(1)}, u32[]{:S(2)}, u32[]{:S(2)}) %all-to-all-start) | async-done | bytes 262176 | tf_op jit(solution)/shard_map/all_to_all | solution.py:65
  39.6 6.5 %all_gather.42 = f32[512,128]{0,1:T(8,128)S(1)} all-gather(f32[128,128]{0,1:T(8,128)S(1)} %fusion.109), channel_id=1, replica_groups=mesh['slab'=8,'col'=4] {'col'}, dimensions={0}, use_global_device_ids=true | all-gather | bytes 327680 | tf_op jit(solution)/shard_map/all_gather | solution.py:40
  46.1 2.8 %conditional.7 = (f32[128,128]{1,0:T(8,128)S(1)}, f32[128,128]{1,0:T(8,128)S(1)}, f32[128,128]{1,0:T(8,128)S(1)}) conditional(s32[]{:T(128)} %convert_element_type.15, () %tuple.56, (f32[2,128,512]{2,1,0:T(8,128)S(1)}, f32[512,128]{0,1:T(8,128)S(1)}, f32[2,128,512]{2,1,0:T(8,128)S(1)}, f32[2,128,512]{2,1,0:T(8,128)S(1)}) %tuple.144), branch_computations={%region_0.1_spmd, %region_1.2_spmd} | conditional | flops 604324608 | bytes 5117592 | solution.py:93
  51.1 3.4 %collective-permute-start.3 = (f32[128,128]{0,1:T(8,128)S(1)}, f32[128,128]{0,1:T(8,128)S(1)}, u32[]{:S(2)}, u32[]{:S(2)}) collective-permute-start(f32[128,128]{0,1:T(8,128)S(1)} %copy.229), channel_id=1, source_target_pairs={{4,0},{8,4},{12,8},{16,12},{20,16},{24,20},{28,24},{5,1},{9,5},{13... | collective-permute-start | bytes 196616 | tf_op jit(solution)/shard_map/ppermute | solution.py:13
  54.6 3.0 %collective-permute-done.3 = f32[128,128]{0,1:T(8,128)S(1)} collective-permute-done((f32[128,128]{0,1:T(8,128)S(1)}, f32[128,128]{0,1:T(8,128)S(1)}, u32[]{:S(2)}, u32[]{:S(2)}) %collective-permute-start.3) | collective-permute-done | bytes 65568 | tf_op jit(solution)/shard_map/ppermute | solution.py:13
  57.6 6.6 %all_gather.43 = f32[512,128]{0,1:T(8,128)S(1)} all-gather(f32[128,128]{0,1:T(8,128)S(1)} %subtract_subtract_fusion.2), channel_id=1, replica_groups=mesh['slab'=8,'col'=4] {'col'}, dimensions={0}, use_global_device_ids=true | all-gather | bytes 327680 | tf_op jit(solution)/shard_map/all_gather | solution.py:40
  64.4 3.1 %collective-permute-start.6 = (f32[128,128]{0,1:T(8,128)S(1)}, f32[128,128]{0,1:T(8,128)S(1)}, u32[]{:S(2)}, u32[]{:S(2)}) collective-permute-start(f32[128,128]{0,1:T(8,128)S(1)} %copy.233), channel_id=1, source_target_pairs={{0,8},{4,12},{8,16},{12,20},{16,24},{20,28},{1,9},{5,13},{9,17},{1... | collective-permute-start | bytes 196616 | tf_op jit(solution)/shard_map/ppermute | solution.py:13
  69.8 2.7 %collective-permute-done.5 = f32[128,128]{0,1:T(8,128)S(1)} collective-permute-done((f32[128,128]{0,1:T(8,128)S(1)}, f32[128,128]{0,1:T(8,128)S(1)}, u32[]{:S(2)}, u32[]{:S(2)}) %collective-permute-start.5) | collective-permute-done | bytes 65568 | tf_op jit(solution)/shard_map/ppermute | solution.py:13
  72.5 7.2 %all_gather.44 = f32[512,128]{0,1:T(8,128)S(1)} all-gather(f32[128,128]{0,1:T(8,128)S(1)} %subtract_subtract_fusion.1), channel_id=1, replica_groups=mesh['slab'=8,'col'=4] {'col'}, dimensions={0}, use_global_device_ids=true | all-gather | bytes 327680 | tf_op jit(solution)/shard_map/all_gather | solution.py:40
  82.8 4.8 %collective-permute-done.7 = f32[128,128]{0,1:T(8,128)S(1)} collective-permute-done((f32[128,128]{0,1:T(8,128)S(1)}, f32[128,128]{0,1:T(8,128)S(1)}, u32[]{:S(2)}, u32[]{:S(2)}) %collective-permute-start.7) | collective-permute-done | bytes 65568 | tf_op jit(solution)/shard_map/ppermute | solution.py:13
  87.6 6.7 %all_gather.45 = f32[512,128]{0,1:T(8,128)S(1)} all-gather(f32[128,128]{0,1:T(8,128)S(1)} %subtract_subtract_fusion), channel_id=1, replica_groups=mesh['slab'=8,'col'=4] {'col'}, dimensions={0}, use_global_device_ids=true | all-gather | bytes 327680 | tf_op jit(solution)/shard_map/all_gather | solution.py:40
  97.3 6.4 %all_gather.46 = f32[512,128]{1,0:T(8,128)S(1)} all-gather(f32[128,128]{1,0:T(8,128)S(1)} %collective-permute-done.9), channel_id=1, replica_groups=mesh['slab'=8,'col'=4] {'col'}, dimensions={0}, use_global_device_ids=true | all-gather | bytes 327680 | tf_op jit(solution)/shard_map/all_gather | solution.py:119
  103.7 5.9 %all_gather.47 = f32[512,128]{1,0:T(8,128)S(1)} all-gather(f32[128,128]{1,0:T(8,128)S(1)} %collective-permute-done.10), channel_id=1, replica_groups=mesh['slab'=8,'col'=4] {'col'}, dimensions={0}, use_global_device_ids=true | all-gather | bytes 327680 | tf_op jit(solution)/shard_map/all_gather | solution.py:120
  109.6 6.3 %collective-permute-start.11 = (f32[128,128]{1,0:T(8,128)S(1)}, f32[128,128]{1,0:T(8,128)S(1)}, u32[]{:S(2)}, u32[]{:S(2)}) collective-permute-start(f32[128,128]{1,0:T(8,128)S(1)} %get-tuple-element.277), channel_id=1, source_target_pairs={{0,8},{4,12},{8,16},{12,20},{16,24},{20,28},{1,9},{5,13},{9,17},{1... | collective-permute-start | bytes 196616 | tf_op jit(solution)/shard_map/ppermute | solution.py:13
  117.8 6.1 %all_gather.48 = f32[512,128]{1,0:T(8,128)S(1)} all-gather(f32[128,128]{1,0:T(8,128)S(1)} %collective-permute-done.11), channel_id=1, replica_groups=mesh['slab'=8,'col'=4] {'col'}, dimensions={0}, use_global_device_ids=true | all-gather | bytes 327680 | tf_op jit(solution)/shard_map/all_gather | solution.py:119
  123.9 5.9 %all_gather.49 = f32[512,128]{1,0:T(8,128)S(1)} all-gather(f32[128,128]{1,0:T(8,128)S(1)} %collective-permute-done.12), channel_id=1, replica_groups=mesh['slab'=8,'col'=4] {'col'}, dimensions={0}, use_global_device_ids=true | all-gather | bytes 327680 | tf_op jit(solution)/shard_map/all_gather | solution.py:120
  129.7 11.2 %collective-permute-start.13 = (f32[128,128]{1,0:T(8,128)S(1)}, f32[128,128]{1,0:T(8,128)S(1)}, u32[]{:S(2)}, u32[]{:S(2)}) collective-permute-start(f32[128,128]{1,0:T(8,128)S(1)} %get-tuple-element.278), channel_id=1, source_target_pairs={{0,4},{4,8},{8,12},{12,16},{16,20},{20,24},{24,28},{1,5},{5,9},{9,... | collective-permute-start | bytes 196616 | tf_op jit(solution)/shard_map/ppermute | solution.py:13
  143.3 6.3 %all_gather.50 = f32[512,128]{1,0:T(8,128)S(1)} all-gather(f32[128,128]{1,0:T(8,128)S(1)} %collective-permute-done.13), channel_id=1, replica_groups=mesh['slab'=8,'col'=4] {'col'}, dimensions={0}, use_global_device_ids=true | all-gather | bytes 327680 | tf_op jit(solution)/shard_map/all_gather | solution.py:119
  149.7 5.9 %all_gather.51 = f32[512,128]{1,0:T(8,128)S(1)} all-gather(f32[128,128]{1,0:T(8,128)S(1)} %collective-permute-done.14), channel_id=1, replica_groups=mesh['slab'=8,'col'=4] {'col'}, dimensions={0}, use_global_device_ids=true | all-gather | bytes 327680 | tf_op jit(solution)/shard_map/all_gather | solution.py:120
  (98 shorter events, 30.5 us)
Async XLA Ops:
  0.0 17.7 %copy-start = (f32[1,128,512]{2,1,0:T(8,128)S(1)}, f32[1,128,512]{2,1,0:T(8,128)}, u32[]{:S(2)}) copy-start(f32[1,128,512]{2,1,0:T(8,128)} %param.23) | copy-start | bytes 786436
  1.0 23.2 %collective-permute-start = (f32[128,128]{0,1:T(8,128)S(1)}, f32[128,128]{0,1:T(8,128)S(1)}, u32[]{:S(2)}, u32[]{:S(2)}) collective-permute-start(f32[128,128]{0,1:T(8,128)S(1)} %bitcast.173), channel_id=1, source_target_pairs={{4,0},{8,4},{12,8},{16,12},{20,16},{24,20},{28,24},{5,1},{9,5},{13... | collective-permute-start | bytes 196616 | tf_op jit(solution)/shard_map/ppermute | solution.py:13
  3.1 15.2 %collective-permute-start.2 = (f32[128,128]{0,1:T(8,128)S(1)}, f32[128,128]{0,1:T(8,128)S(1)}, u32[]{:S(2)}, u32[]{:S(2)}) collective-permute-start(f32[128,128]{0,1:T(8,128)S(1)} %bitcast.174), channel_id=1, source_target_pairs={{0,4},{4,8},{8,12},{12,16},{16,20},{20,24},{24,28},{1,5},{5,9},{9,... | collective-permute-start | bytes 196616 | tf_op jit(solution)/shard_map/ppermute | solution.py:13
  7.2 3.4 %copy-start.7 = (f32[1,128,128]{2,1,0:T(8,128)S(1)}, f32[1,128,128]{2,1,0:T(8,128)}, u32[]{:S(2)}) copy-start(f32[1,128,128]{2,1,0:T(8,128)} %param.22) | copy-start | bytes 196612
  8.3 21.8 %collective-permute-start.1 = (f32[128,512]{0,1:T(8,128)S(1)}, f32[128,512]{0,1:T(8,128)}, u32[]{:S(2)}, u32[]{:S(2)}) collective-permute-start(f32[128,512]{0,1:T(8,128)S(1)} %bitcast.172), channel_id=1, source_target_pairs={{0,4},{4,8},{8,12},{12,16},{16,20},{20,24},{24,28},{1,5},{5,9},{9,... | collective-permute-start | bytes 786440 | tf_op jit(solution)/shard_map/ppermute | solution.py:13
  30.1 3.7 %copy-start.6 = (f32[1,128,512]{2,1,0:T(8,128)S(1)}, f32[1,128,512]{2,1,0:T(8,128)}, u32[]{:S(2)}) copy-start(f32[1,128,512]{2,1,0:T(8,128)} %param.24) | copy-start | bytes 786436
  30.1 8.8 %all-to-all-start = ((f32[128,4,128]{0,2,1:T(8,128)}), f32[128,4,128]{0,2,1:T(8,128)S(1)}, u32[]{:S(2)}, u32[]{:S(2)}) async-start(f32[128,4,128]{0,2,1:T(8,128)} %bitcast.39), calls=%async_computation | async-start | bytes 524288 | tf_op jit(solution)/shard_map/all_to_all | solution.py:65
  38.9 7.2 %copy-start.3 = (f32[1,2,128,512]{3,2,1,0:T(8,128)S(1)}, f32[1,2,128,512]{3,2,1,0:T(8,128)}, u32[]{:S(2)}) copy-start(f32[1,2,128,512]{3,2,1,0:T(8,128)} %param.27) | copy-start | bytes 1572868
  39.0 7.1 %copy-start.2 = (f32[1,2,128,512]{3,2,1,0:T(8,128)S(1)}, f32[1,2,128,512]{3,2,1,0:T(8,128)}, u32[]{:S(2)}) copy-start(f32[1,2,128,512]{3,2,1,0:T(8,128)} %param.26) | copy-start | bytes 1572868
  39.5 6.7 %copy-start.1 = (f32[1,2,128,512]{3,2,1,0:T(8,128)S(1)}, f32[1,2,128,512]{3,2,1,0:T(8,128)}, u32[]{:S(2)}) copy-start(f32[1,2,128,512]{3,2,1,0:T(8,128)} %param.25) | copy-start | bytes 1572868
  49.2 5.4 %collective-permute-start.4 = (f32[128,128]{0,1:T(8,128)S(1)}, f32[128,128]{0,1:T(8,128)S(1)}, u32[]{:S(2)}, u32[]{:S(2)}) collective-permute-start(f32[128,128]{0,1:T(8,128)S(1)} %copy.230), channel_id=1, source_target_pairs={{0,4},{4,8},{8,12},{12,16},{16,20},{20,24},{24,28},{1,5},{5,9},{9,... | collective-permute-start | bytes 196616 | tf_op jit(solution)/shard_map/ppermute | solution.py:13
  51.1 6.5 %collective-permute-start.3 = (f32[128,128]{0,1:T(8,128)S(1)}, f32[128,128]{0,1:T(8,128)S(1)}, u32[]{:S(2)}, u32[]{:S(2)}) collective-permute-start(f32[128,128]{0,1:T(8,128)S(1)} %copy.229), channel_id=1, source_target_pairs={{4,0},{8,4},{12,8},{16,12},{20,16},{24,20},{28,24},{5,1},{9,5},{13... | collective-permute-start | bytes 196616 | tf_op jit(solution)/shard_map/ppermute | solution.py:13
  64.4 5.4 %collective-permute-start.6 = (f32[128,128]{0,1:T(8,128)S(1)}, f32[128,128]{0,1:T(8,128)S(1)}, u32[]{:S(2)}, u32[]{:S(2)}) collective-permute-start(f32[128,128]{0,1:T(8,128)S(1)} %copy.233), channel_id=1, source_target_pairs={{0,8},{4,12},{8,16},{12,20},{16,24},{20,28},{1,9},{5,13},{9,17},{1... | collective-permute-start | bytes 196616 | tf_op jit(solution)/shard_map/ppermute | solution.py:13
  67.5 5.0 %collective-permute-start.5 = (f32[128,128]{0,1:T(8,128)S(1)}, f32[128,128]{0,1:T(8,128)S(1)}, u32[]{:S(2)}, u32[]{:S(2)}) collective-permute-start(f32[128,128]{0,1:T(8,128)S(1)} %copy.232), channel_id=1, source_target_pairs={{8,0},{12,4},{16,8},{20,12},{24,16},{28,20},{9,1},{13,5},{17,9},{2... | collective-permute-start | bytes 196616 | tf_op jit(solution)/shard_map/ppermute | solution.py:13
  80.0 2.8 %collective-permute-start.8 = (f32[128,128]{0,1:T(8,128)S(1)}, f32[128,128]{0,1:T(8,128)S(1)}, u32[]{:S(2)}, u32[]{:S(2)}) collective-permute-start(f32[128,128]{0,1:T(8,128)S(1)} %copy.236), channel_id=1, source_target_pairs={{0,16},{4,20},{8,24},{12,28},{1,17},{5,21},{9,25},{13,29},{2,18},{... | collective-permute-start | bytes 196616 | tf_op jit(solution)/shard_map/ppermute | solution.py:13
  81.3 6.3 %collective-permute-start.7 = (f32[128,128]{0,1:T(8,128)S(1)}, f32[128,128]{0,1:T(8,128)S(1)}, u32[]{:S(2)}, u32[]{:S(2)}) collective-permute-start(f32[128,128]{0,1:T(8,128)S(1)} %copy.235), channel_id=1, source_target_pairs={{16,0},{20,4},{24,8},{28,12},{17,1},{21,5},{25,9},{29,13},{18,2},{... | collective-permute-start | bytes 196616 | tf_op jit(solution)/shard_map/ppermute | solution.py:13
  94.3 15.2 %copy-start.4 = (f32[1,2,128,512]{3,2,1,0:T(8,128)S(1)}, f32[1,2,128,512]{3,2,1,0:T(8,128)}, u32[]{:S(2)}) copy-start(f32[1,2,128,512]{3,2,1,0:T(8,128)} %param.29) | copy-start | bytes 1572868
  94.3 15.2 %copy-start.5 = (f32[1,2,128,512]{3,2,1,0:T(8,128)S(1)}, f32[1,2,128,512]{3,2,1,0:T(8,128)}, u32[]{:S(2)}) copy-start(f32[1,2,128,512]{3,2,1,0:T(8,128)} %param.28) | copy-start | bytes 1572868
  94.4 3.0 %collective-permute-start.9 = (f32[128,128]{1,0:T(8,128)S(1)}, f32[128,128]{1,0:T(8,128)S(1)}, u32[]{:S(2)}, u32[]{:S(2)}) collective-permute-start(f32[128,128]{1,0:T(8,128)S(1)} %get-tuple-element.170), channel_id=1, source_target_pairs={{0,16},{4,20},{8,24},{12,28},{1,17},{5,21},{9,25},{13,29},{2,18},{... | collective-permute-start | bytes 196616 | tf_op jit(solution)/shard_map/ppermute | solution.py:13
  95.8 7.9 %collective-permute-start.10 = (f32[128,128]{1,0:T(8,128)S(1)}, f32[128,128]{1,0:T(8,128)S(1)}, u32[]{:S(2)}, u32[]{:S(2)}) collective-permute-start(f32[128,128]{1,0:T(8,128)S(1)} %get-tuple-element.170), channel_id=1, source_target_pairs={{16,0},{20,4},{24,8},{28,12},{17,1},{21,5},{25,9},{29,13},{18,2},{... | collective-permute-start | bytes 196616 | tf_op jit(solution)/shard_map/ppermute | solution.py:13
  109.6 8.2 %collective-permute-start.11 = (f32[128,128]{1,0:T(8,128)S(1)}, f32[128,128]{1,0:T(8,128)S(1)}, u32[]{:S(2)}, u32[]{:S(2)}) collective-permute-start(f32[128,128]{1,0:T(8,128)S(1)} %get-tuple-element.277), channel_id=1, source_target_pairs={{0,8},{4,12},{8,16},{12,20},{16,24},{20,28},{1,9},{5,13},{9,17},{1... | collective-permute-start | bytes 196616 | tf_op jit(solution)/shard_map/ppermute | solution.py:13
  115.9 8.0 %collective-permute-start.12 = (f32[128,128]{1,0:T(8,128)S(1)}, f32[128,128]{1,0:T(8,128)S(1)}, u32[]{:S(2)}, u32[]{:S(2)}) collective-permute-start(f32[128,128]{1,0:T(8,128)S(1)} %get-tuple-element.277), channel_id=1, source_target_pairs={{8,0},{12,4},{16,8},{20,12},{24,16},{28,20},{9,1},{13,5},{17,9},{2... | collective-permute-start | bytes 196616 | tf_op jit(solution)/shard_map/ppermute | solution.py:13
  129.7 13.6 %collective-permute-start.13 = (f32[128,128]{1,0:T(8,128)S(1)}, f32[128,128]{1,0:T(8,128)S(1)}, u32[]{:S(2)}, u32[]{:S(2)}) collective-permute-start(f32[128,128]{1,0:T(8,128)S(1)} %get-tuple-element.278), channel_id=1, source_target_pairs={{0,4},{4,8},{8,12},{12,16},{16,20},{20,24},{24,28},{1,5},{5,9},{9,... | collective-permute-start | bytes 196616 | tf_op jit(solution)/shard_map/ppermute | solution.py:13
  140.9 8.8 %collective-permute-start.14 = (f32[128,128]{1,0:T(8,128)S(1)}, f32[128,128]{1,0:T(8,128)S(1)}, u32[]{:S(2)}, u32[]{:S(2)}) collective-permute-start(f32[128,128]{1,0:T(8,128)S(1)} %get-tuple-element.278), channel_id=1, source_target_pairs={{4,0},{8,4},{12,8},{16,12},{20,16},{24,20},{28,24},{5,1},{9,5},{13... | collective-permute-start | bytes 196616 | tf_op jit(solution)/shard_map/ppermute | solution.py:13
  (1 other events, 0.6 us)
where the time goes:
time: 159 us; the launch traced here: 158 us
  blocking collectives  82.2 us (52%)
  starting transfers between devices  49.6 us (31%)
  waiting for transfers between devices  16.1 us (10%)
  matrix products  5.22 us (3%)
  local copies, waits for them, and re-layouts  4.27 us (3%)
    ppermute x15, starting transfers between devices, from_behind(): return lax.ppermute(block, axis, route)  45.9 us
    all_gather x4, blocking collectives, gather_rows(): return lax.all_gather(values, 'col', axis=0, tiled=True)  27 us
    all_gather x3, blocking collectives, per_device(): lax.all_gather(lower_in, 'col', axis=0, tiled=True)  18.8 us
    all_gather x3, blocking collectives, per_device(): lax.all_gather(upper_in, 'col', axis=0, tiled=True)  17.6 us
    ppermute x15, waiting for transfers between devices, from_behind(): return lax.ppermute(block, axis, route)  11.3 us
    all_gather x1, blocking collectives, per_device(): lax.all_gather(states, 'col', axis=0, tiled=True)  7.14 us
    all_gather x1, blocking collectives, per_device(): lax.all_gather(prev_shard, 'col', axis=0, tiled=True)  5.86 us
    all_gather x1, blocking collectives, per_device(): lax.all_gather(next_shard, 'col', axis=0, tiled=True)  5.85 us
  transfers between devices with their start and end apart: 16, of which 8 were waited for; matrix products, arithmetic and copies ran while one was open for 1% of the time, Pallas kernels for 0%

commit v1 on v0

v1 whole, which is shorter than its diff:
```python
import functools

import jax
import jax.numpy as jnp
from jax import lax
from jax.experimental import pallas as pl
from jax.experimental.pallas import tpu as pltpu
from jax.sharding import PartitionSpec as P


half_step = 0.5
wide = jnp.float32
short = jnp.bfloat16
Q = 128
LANES = 128


def lanes(values):
    return lax.broadcasted_iota(jnp.int32, values.shape, 1)


def swap_halves(values):
    return pltpu.roll(values, 64, 1)


def join(left, right):
    return jnp.where(lanes(left) < 64, left, right)


def rotate(values):
    even = lanes(values) % 2 == 0
    return jnp.where(even, -pltpu.roll(values, LANES - 1, 1), pltpu.roll(values, 1, 1))


def split(values):
    high = values.astype(short)
    return high, (values - high.astype(wide)).astype(short)


def quarter(number):
    return pl.ds(pl.multiple_of(number * Q, Q), Q)


def spread(store, packed, first):
    high = packed.astype(short).astype(wide)
    low = packed - high
    store[quarter(first), :] = join(high, swap_halves(low)).astype(short)
    store[quarter(first ^ 1), :] = join(swap_halves(high), low).astype(short)


def load_vector(store, near, far):
    c = lax.axis_index("col")
    spread(store, near[...], c)
    spread(store, far[...], c ^ 2)


def rows_product(block, store):
    high, low = split(block)
    vector = store[...]
    return jnp.dot(high, vector, preferred_element_type=wide) + jnp.dot(
        low, vector, preferred_element_type=wide
    )


def fold(values):
    return values + swap_halves(values)


def real_product(own, mate, store):
    return join(fold(rows_product(own, store)), fold(rows_product(mate, store)))


def complex_half(block, store):
    both = rows_product(block.reshape(2 * Q, block.shape[-1]), store)
    return fold(both[:Q] + rotate(both[Q:]))


def complex_product(own, mate, store):
    return join(complex_half(own, store), complex_half(mate, store))


def regroup_kernel(mine, other, out):
    c = lax.axis_index("col")
    rows = join(mine[...], other[...])
    out[...] = jnp.where(c % 2 == 0, rows, swap_halves(rows))


def pack_kernel(mine, other, out):
    c = lax.axis_index("col")
    near, far = mine[...], other[...]
    out[...] = jnp.where(
        c % 2 == 0, join(near, swap_halves(far)), join(swap_halves(near), far)
    )


def up_kernel(packed, own, mate, near, far, store):
    c = lax.axis_index("col")
    turned = packed[...].T
    total = None
    for rows, block in ((turned[:64], own[0]), (turned[64:], mate[0])):
        high, low = split(rows)
        pair = jnp.concatenate([high, low], axis=0)
        block_high, block_low = split(block)
        part = jnp.dot(pair, block_high, preferred_element_type=wide) + jnp.dot(
            pair, block_low, preferred_element_type=wide
        )
        part = part[:64] + part[64:]
        total = part if total is None else total + part
    store[...] = total
    for out, first in ((near, c), (far, c ^ 2)):
        pair = jnp.concatenate(
            [store[:, quarter(first)], store[:, quarter(first ^ 1)]], axis=0
        )
        out[...] = pair.T


def ham_kernel(near, far, next_near, next_far, own, mate, out, here, there):
    load_vector(here, near, far)
    load_vector(there, next_near, next_far)
    ham = real_product(own[1], mate[1], here) + real_product(own[0], mate[0], there)
    out[...] = near[...] - half_step * rotate(ham)


def add_up_kernel(rest, first, second, out):
    out[...] = rest[...] - half_step * rotate(first[...] + second[...])


def level_kernel(near, far, own, mate, beneath, above, store):
    load_vector(store, near, far)
    beneath[...] = complex_product(own[0:2], mate[0:2], store)
    above[...] = complex_product(own[2:4], mate[2:4], store)


def top_kernel(near, far, own, mate, beneath, store):
    load_vector(store, near, far)
    beneath[...] = complex_product(own[0:2], mate[0:2], store)


def pivot_kernel(near, far, less_near, less_far, own, mate, out, store):
    c = lax.axis_index("col")
    spread(store, near[...] - less_near[...], c)
    spread(store, far[...] - less_far[...], c ^ 2)
    out[...] = complex_product(own[4:6], mate[4:6], store)


def settle_kernel(tier_spacing, pivot, solved, *refs):
    *vectors, own, mate, out, lower, upper = refs
    s = lax.axis_index("slab")
    load_vector(lower, vectors[0], vectors[1])
    change = complex_product(own[6:8], mate[6:8], lower)
    if len(vectors) == 4:
        load_vector(upper, vectors[2], vectors[3])
        change = change + complex_product(own[8:10], mate[8:10], upper)
    active = s % (2 * tier_spacing) == tier_spacing
    out[...] = jnp.where(active, pivot[...] - change, solved[...])


def call(kernel, *operands, outs=1, scratch=(), flops=0):
    packed = jax.ShapeDtypeStruct((Q, LANES), wide)
    size = sum(v.size for v in operands) * 4 + outs * Q * LANES * 4
    return pl.pallas_call(
        kernel,
        out_shape=packed if outs == 1 else (packed,) * outs,
        in_specs=[pl.BlockSpec(memory_space=pltpu.VMEM)] * len(operands),
        out_specs=pl.BlockSpec(memory_space=pltpu.VMEM)
        if outs == 1
        else (pl.BlockSpec(memory_space=pltpu.VMEM),) * outs,
        scratch_shapes=list(scratch),
        cost_estimate=pl.CostEstimate(flops=flops, bytes_accessed=size, transcendentals=0),
        compiler_params=pltpu.CompilerParams(vmem_limit_bytes=24 * 2**20),
    )(*operands)


def per_device(slabs, cols, waves, energy, tunnel, pivots, below, above, back_lower, back_upper):
    everyone = range(cols)
    rows = waves.shape[1]
    width = energy.shape[2]
    store = pltpu.VMEM((width, LANES), short)
    one = 2 * 2 * Q * width * 2 * LANES * 2

    def send(values, slab_pairs, flip=0):
        route = [
            (a * cols + c, b * cols + (c ^ flip)) for a, b in slab_pairs for c in everyone
        ]
        return lax.ppermute(values, ("slab", "col"), route)

    same = [(s, s) for s in range(slabs)]

    def shift(distance, chosen):
        return [(s, s + distance) for s in chosen if 0 <= s + distance < slabs]

    states = waves[0]
    mate_states = send(states, same, 1)
    hops = jnp.concatenate([tunnel, energy], axis=0)
    mate_hops = send(hops, same, 1)
    blocks = jnp.concatenate(
        [below[0], above[0], pivots[0], back_lower[0], back_upper[0]], axis=0
    )
    mate_blocks = send(blocks, same, 1)

    psi = call(pack_kernel, states, mate_states)
    every = range(slabs)
    down, up = shift(-1, every), shift(1, every)
    psi_far = send(psi, same, 2)
    next_near = send(psi, down)
    next_far = send(psi, down, 2)
    up_near, up_far = call(
        up_kernel,
        psi,
        hops,
        mate_hops,
        outs=2,
        scratch=[pltpu.VMEM((64, width), wide)],
        flops=one // 2,
    )
    prev_near = send(up_near, up)
    prev_far = send(up_far, up, 2)
    rest = call(
        ham_kernel,
        psi,
        psi_far,
        next_near,
        next_far,
        hops,
        mate_hops,
        scratch=[store, store],
        flops=one,
    )
    near = call(add_up_kernel, rest, prev_near, prev_far)

    levels = slabs.bit_length() - 1
    for level in range(levels):
        spacing = 2**level
        active = [s for s in every if s % (2 * spacing) == spacing]
        far = send(near, same, 2)
        if level < levels - 1:
            beneath, over = call(
                level_kernel, near, far, blocks, mate_blocks, outs=2, scratch=[store], flops=2 * one
            )
            less = send(beneath, shift(-spacing, active))
            more = send(over, shift(spacing, active))
            near = near - less - more
        else:
            beneath = call(
                top_kernel, near, far, blocks, mate_blocks, scratch=[store], flops=one
            )
            less_near = send(beneath, shift(-spacing, active))
            less_far = send(beneath, shift(-spacing, active), 2)
            pivot = call(
                pivot_kernel,
                near,
                far,
                less_near,
                less_far,
                blocks,
                mate_blocks,
                scratch=[store],
                flops=one,
            )

    solved = pivot
    for level in reversed(range(levels)):
        spacing = 2**level
        active = [s for s in every if s % (2 * spacing) == spacing]
        from_lower = [(s - spacing, s) for s in active]
        from_upper = [(s + spacing, s) for s in active if s + spacing < slabs]
        vectors = [send(solved, from_lower), send(solved, from_lower, 2)]
        if from_upper:
            vectors += [send(solved, from_upper), send(solved, from_upper, 2)]
        solved = call(
            functools.partial(settle_kernel, spacing),
            pivot,
            solved,
            *vectors,
            blocks,
            mate_blocks,
            scratch=[store, store],
            flops=len(vectors) // 2 * one,
        )
    out = call(regroup_kernel, solved, send(solved, same, 1))
    return out[None]


def solution(mesh):
    slabs, cols = mesh.shape["slab"], mesh.shape["col"]
    vector = P("slab", "col", None)
    block = P("slab", None, "col", None)
    return jax.shard_map(
        functools.partial(per_device, slabs, cols),
        mesh=mesh,
        in_specs=(vector,) * 3 + (block,) * 5,
        out_specs=vector,
        check_vma=False,
    )
```

time: 159 us -> 95.9 us (0.60)
  blocking collectives: 82.2 us -> 0 us
  waiting for transfers between devices: 16.1 us -> 34.4 us
  Pallas kernels: 0 us -> 7.93 us
  matrix products: 5.22 us -> 0 us
  starting transfers between devices: 49.6 us -> 47.9 us
    all_gather x13 -> x0, blocking collectives: 82.2 us -> none  [the longest x4 27 us: gather_rows(): return lax.all_gather(values, 'col', axis=0, tiled=True)]
    ppermute x15 -> x28, waiting for transfers between devices: 11.3 us -> 34.4 us  [send(): return lax.ppermute(values, ('slab', 'col'), route)]
    pallas_call x0 -> x12, Pallas kernels: none -> 7.93 us  [call(): pl.pallas_call(kernel, out_shape=packed if outs == 1 else (packed,) * out...]
    dot_general x13 -> x0, matrix products: 5.22 us -> none  [the longest x12 4.82 us: plain_dot(): jnp.dot(left, right, precision=highest, preferred_element_type=jnp.float32)]
    all_to_all x1 -> x0, waiting for transfers between devices: 4.78 us -> none  [per_device(): lax.all_to_all(below_rows, 'col', split_axis=1, concat_axis=0, tiled=True)]
    all_to_all x1 -> x0, starting transfers between devices: 3.67 us -> none  [per_device(): lax.all_to_all(below_rows, 'col', split_axis=1, concat_axis=0, tiled=True)]
    ppermute x15 -> x28, starting transfers between devices: 45.9 us -> 47.9 us  [send(): return lax.ppermute(values, ('slab', 'col'), route)]
    unnamed x20 -> x15, local copies, waits for them, and re-layouts: 2.74 us -> 3.46 us
  transfers between devices with their start and end apart: 16 -> 28, of which waited for: 8 -> 10; matrix products, arithmetic and copies ran while one was open for 1% -> 0% of each run, Pallas kernels for 0% -> 1%
where the time goes in v1:
time: 95.9 us; the launch traced here: 94.2 us
  starting transfers between devices  47.9 us (50%)
  waiting for transfers between devices  34.4 us (36%)
  Pallas kernels  7.93 us (8%)
  local copies, waits for them, and re-layouts  3.51 us (4%)
    ppermute x28, starting transfers between devices, send(): return lax.ppermute(values, ('slab', 'col'), route)  47.9 us
    ppermute x28, waiting for transfers between devices, send(): return lax.ppermute(values, ('slab', 'col'), route)  34.4 us
    pallas_call x12, Pallas kernels, call(): pl.pallas_call(kernel, out_shape=packed if outs == 1 else (packed,) * out...  7.93 us
    unnamed x15, local copies, waits for them, and re-layouts  3.46 us
  transfers between devices with their start and end apart: 28, of which 10 were waited for; matrix products, arithmetic and copies ran while one was open for 0% of the time, Pallas kernels for 1%

profile of v1, /device:TPU:13, one launch (start us, length us, event | category | flops | bytes accessed | tf_op | source)
XLA Modules:
  0.0 94.2 jit_solution(3675351104658687862)
XLA Ops:
  0.0 1.2 %bitcast_dynamic-update-slice_fusion.4 = f32[10,128,512]{2,1,0:T(8,128)S(1)} fusion(f32[1,2,128,512]{3,2,1,0:T(8,128)} %param.12), kind=kLoop, calls=%fused_computation.4 | loop fusion | bytes 1048576
  1.2 1.1 %bitcast_dynamic-update-slice_fusion.3 = f32[10,128,512]{2,1,0:T(8,128)S(1)} fusion(f32[10,128,512]{2,1,0:T(8,128)S(1)} %bitcast_dynamic-update-slice_fusion.4, f32[1,2,128,512]{3,2,1,0:T(8,128)} %param.13), kind=kLoop, calls=%fused_computation.3 | loop fusion | bytes 1048576
  4.9 4.7 %collective-permute-done.other = f32[128,128]{1,0:T(8,128)S(1)} collective-permute-done((f32[128,128]{1,0:T(8,128)S(1)}, f32[128,128]{1,0:T(8,128)S(1)}, u32[]{:S(2)}, u32[]{:S(2)}) %collective-permute-start) | collective-permute-done | bytes 65568 | tf_op jit(solution)/shard_map/ppermute | solution.py:185
  9.8 3.1 %collective-permute-start.3 = (f32[128,128]{1,0:T(8,128)S(1)}, f32[128,128]{1,0:T(8,128)S(1)}, u32[]{:S(2)}, u32[]{:S(2)}) collective-permute-start(f32[128,128]{1,0:T(8,128)S(1)} %shard_map.82.near.packed), channel_id=1, source_target_pairs={{4,2},{5,3},{6,0},{7,1},{8,6},{9,7},{10,4},{11,5},{12,10},{13,11},... | collective-permute-start | bytes 196616 | tf_op jit(solution)/shard_map/ppermute | solution.py:185
  12.8 3.0 %collective-permute-start.2 = (f32[128,128]{1,0:T(8,128)S(1)}, f32[128,128]{1,0:T(8,128)S(1)}, u32[]{:S(2)}, u32[]{:S(2)}) collective-permute-start(f32[128,128]{1,0:T(8,128)S(1)} %shard_map.82.near.packed), channel_id=1, source_target_pairs={{4,0},{5,1},{6,2},{7,3},{8,4},{9,5},{10,6},{11,7},{12,8},{13,9},{1... | collective-permute-start | bytes 196616 | tf_op jit(solution)/shard_map/ppermute | solution.py:185
  16.7 3.1 %collective-permute-start.5 = (f32[128,128]{1,0:T(8,128)S(1)}, f32[128,128]{1,0:T(8,128)S(1)}, u32[]{:S(2)}, u32[]{:S(2)}) collective-permute-start(f32[128,128]{1,0:T(8,128)S(1)} %get-tuple-element.11), channel_id=1, source_target_pairs={{0,4},{1,5},{2,6},{3,7},{4,8},{5,9},{6,10},{7,11},{8,12},{9,13},{1... | collective-permute-start | bytes 196616 | tf_op jit(solution)/shard_map/ppermute | solution.py:185
  19.8 4.1 %collective-permute-start.6 = (f32[128,128]{1,0:T(8,128)S(1)}, f32[128,128]{1,0:T(8,128)S(1)}, u32[]{:S(2)}, u32[]{:S(2)}) collective-permute-start(f32[128,128]{1,0:T(8,128)S(1)} %get-tuple-element.12), channel_id=1, source_target_pairs={{0,6},{1,7},{2,4},{3,5},{4,10},{5,11},{6,8},{7,9},{8,14},{9,15},{1... | collective-permute-start | bytes 196616 | tf_op jit(solution)/shard_map/ppermute | solution.py:185
  24.6 1.1 %collective-permute-done.6.second = f32[128,128]{1,0:T(8,128)S(1)} collective-permute-done((f32[128,128]{1,0:T(8,128)S(1)}, f32[128,128]{1,0:T(8,128)S(1)}, u32[]{:S(2)}, u32[]{:S(2)}) %collective-permute-start.6) | collective-permute-done | bytes 65568 | tf_op jit(solution)/shard_map/ppermute | solution.py:185
  25.8 1.3 %collective-permute-start.7 = (f32[128,128]{1,0:T(8,128)S(1)}, f32[128,128]{1,0:T(8,128)S(1)}, u32[]{:S(2)}, u32[]{:S(2)}) collective-permute-start(f32[128,128]{1,0:T(8,128)S(1)} %shard_map.85.near), channel_id=1, source_target_pairs={{0,2},{1,3},{2,0},{3,1},{4,6},{5,7},{6,4},{7,5},{8,10},{9,11},{10,... | collective-permute-start | bytes 196616 | tf_op jit(solution)/shard_map/ppermute | solution.py:185
  27.1 1.9 %collective-permute-done.7.far = f32[128,128]{1,0:T(8,128)S(1)} collective-permute-done((f32[128,128]{1,0:T(8,128)S(1)}, f32[128,128]{1,0:T(8,128)S(1)}, u32[]{:S(2)}, u32[]{:S(2)}) %collective-permute-start.7) | collective-permute-done | bytes 65568 | tf_op jit(solution)/shard_map/ppermute | solution.py:185
  30.0 3.0 %collective-permute-start.9 = (f32[128,128]{1,0:T(8,128)S(1)}, f32[128,128]{1,0:T(8,128)S(1)}, u32[]{:S(2)}, u32[]{:S(2)}) collective-permute-start(f32[128,128]{1,0:T(8,128)S(1)} %get-tuple-element.13), channel_id=1, source_target_pairs={{4,0},{5,1},{6,2},{7,3},{12,8},{13,9},{14,10},{15,11},{20,16},{21,... | collective-permute-start | bytes 196616 | tf_op jit(solution)/shard_map/ppermute | solution.py:185
  33.0 2.3 %collective-permute-start.10 = (f32[128,128]{1,0:T(8,128)S(1)}, f32[128,128]{1,0:T(8,128)S(1)}, u32[]{:S(2)}, u32[]{:S(2)}) collective-permute-start(f32[128,128]{1,0:T(8,128)S(1)} %get-tuple-element.14), channel_id=1, source_target_pairs={{4,8},{5,9},{6,10},{7,11},{12,16},{13,17},{14,18},{15,19},{20,24},... | collective-permute-start | bytes 196616 | tf_op jit(solution)/shard_map/ppermute | solution.py:185
  35.3 1.3 %collective-permute-done.10 = f32[128,128]{1,0:T(8,128)S(1)} collective-permute-done((f32[128,128]{1,0:T(8,128)S(1)}, f32[128,128]{1,0:T(8,128)S(1)}, u32[]{:S(2)}, u32[]{:S(2)}) %collective-permute-start.10) | collective-permute-done | bytes 65568 | tf_op jit(solution)/shard_map/ppermute | solution.py:185
  36.7 1.3 %collective-permute-start.11 = (f32[128,128]{1,0:T(8,128)S(1)}, f32[128,128]{1,0:T(8,128)S(1)}, u32[]{:S(2)}, u32[]{:S(2)}) collective-permute-start(f32[128,128]{1,0:T(8,128)S(1)} %subtract_subtract_fusion.1.near), channel_id=1, source_target_pairs={{0,2},{1,3},{2,0},{3,1},{4,6},{5,7},{6,4},{7,5},{8,10},{9,11},{10,... | collective-permute-start | bytes 196616 | tf_op jit(solution)/shard_map/ppermute | solution.py:185
  37.9 1.9 %collective-permute-done.11.far = f32[128,128]{1,0:T(8,128)S(1)} collective-permute-done((f32[128,128]{1,0:T(8,128)S(1)}, f32[128,128]{1,0:T(8,128)S(1)}, u32[]{:S(2)}, u32[]{:S(2)}) %collective-permute-start.11) | collective-permute-done | bytes 65568 | tf_op jit(solution)/shard_map/ppermute | solution.py:185
  42.2 1.3 %collective-permute-start.14 = (f32[128,128]{1,0:T(8,128)S(1)}, f32[128,128]{1,0:T(8,128)S(1)}, u32[]{:S(2)}, u32[]{:S(2)}) collective-permute-start(f32[128,128]{1,0:T(8,128)S(1)} %subtract_subtract_fusion.near), channel_id=1, source_target_pairs={{0,2},{1,3},{2,0},{3,1},{4,6},{5,7},{6,4},{7,5},{8,10},{9,11},{10,... | collective-permute-start | bytes 196616 | tf_op jit(solution)/shard_map/ppermute | solution.py:185
  43.5 2.2 %collective-permute-done.14.far = f32[128,128]{1,0:T(8,128)S(1)} collective-permute-done((f32[128,128]{1,0:T(8,128)S(1)}, f32[128,128]{1,0:T(8,128)S(1)}, u32[]{:S(2)}, u32[]{:S(2)}) %collective-permute-start.14) | collective-permute-done | bytes 65568 | tf_op jit(solution)/shard_map/ppermute | solution.py:185
  54.2 1.3 %collective-permute-start.26 = (f32[128,128]{1,0:T(8,128)S(1)}, f32[128,128]{1,0:T(8,128)S(1)}, u32[]{:S(2)}, u32[]{:S(2)}) collective-permute-start(f32[128,128]{1,0:T(8,128)S(1)} %shard_map.91.solved), channel_id=1, source_target_pairs={{8,6},{9,7},{10,4},{11,5},{16,14},{17,15},{18,12},{19,13},{24,22},... | collective-permute-start | bytes 196616 | tf_op jit(solution)/shard_map/ppermute | solution.py:185
  55.5 1.3 %collective-permute-start.25 = (f32[128,128]{1,0:T(8,128)S(1)}, f32[128,128]{1,0:T(8,128)S(1)}, u32[]{:S(2)}, u32[]{:S(2)}) collective-permute-start(f32[128,128]{1,0:T(8,128)S(1)} %shard_map.91.solved), channel_id=1, source_target_pairs={{8,4},{9,5},{10,6},{11,7},{16,12},{17,13},{18,14},{19,15},{24,20},... | collective-permute-start | bytes 196616 | tf_op jit(solution)/shard_map/ppermute | solution.py:185
  56.8 1.3 %collective-permute-start.24 = (f32[128,128]{1,0:T(8,128)S(1)}, f32[128,128]{1,0:T(8,128)S(1)}, u32[]{:S(2)}, u32[]{:S(2)}) collective-permute-start(f32[128,128]{1,0:T(8,128)S(1)} %shard_map.91.solved), channel_id=1, source_target_pairs={{0,6},{1,7},{2,4},{3,5},{8,14},{9,15},{10,12},{11,13},{16,22},{17,... | collective-permute-start | bytes 196616 | tf_op jit(solution)/shard_map/ppermute | solution.py:185
  58.1 1.3 %collective-permute-start.23 = (f32[128,128]{1,0:T(8,128)S(1)}, f32[128,128]{1,0:T(8,128)S(1)}, u32[]{:S(2)}, u32[]{:S(2)}) collective-permute-start(f32[128,128]{1,0:T(8,128)S(1)} %shard_map.91.solved), channel_id=1, source_target_pairs={{0,4},{1,5},{2,6},{3,7},{8,12},{9,13},{10,14},{11,15},{16,20},{17,... | collective-permute-start | bytes 196616 | tf_op jit(solution)/shard_map/ppermute | solution.py:185
  59.4 18.2 %collective-permute-done.26.refs_3_ = f32[128,128]{1,0:T(8,128)S(1)} collective-permute-done((f32[128,128]{1,0:T(8,128)S(1)}, f32[128,128]{1,0:T(8,128)S(1)}, u32[]{:S(2)}, u32[]{:S(2)}) %collective-permute-start.26) | collective-permute-done | bytes 65568 | tf_op jit(solution)/shard_map/ppermute | solution.py:185
  77.5 1.5 %collective-permute-done.25.refs_2_ = f32[128,128]{1,0:T(8,128)S(1)} collective-permute-done((f32[128,128]{1,0:T(8,128)S(1)}, f32[128,128]{1,0:T(8,128)S(1)}, u32[]{:S(2)}, u32[]{:S(2)}) %collective-permute-start.25) | collective-permute-done | bytes 65568 | tf_op jit(solution)/shard_map/ppermute | solution.py:185
  80.6 12.0 %collective-permute-start.27 = (f32[128,128]{1,0:T(8,128)S(1)}, f32[128,128]{1,0:T(8,128)S(1)}, u32[]{:S(2)}, u32[]{:S(2)}) collective-permute-start(f32[128,128]{1,0:T(8,128)S(1)} %shard_map.92.mine), channel_id=1, source_target_pairs={{0,1},{1,0},{2,3},{3,2},{4,5},{5,4},{6,7},{7,6},{8,9},{9,8},{10,11... | collective-permute-start | bytes 196616 | tf_op jit(solution)/shard_map/ppermute | solution.py:185
  (63 shorter events, 19.1 us)
Async XLA Ops:
  3.5 25.5 %collective-permute-start.8 = (f32[10,128,512]{2,1,0:T(8,128)S(1)}, f32[10,128,512]{2,1,0:T(8,128)S(1)}, u32[]{:S(2)}, u32[]{:S(2)}) collective-permute-start(f32[10,128,512]{2,1,0:T(8,128)S(1)} %bitcast_dynamic-update-slice_fusion.own.refs_2_.refs_4_), channel_id=1, source_target_pairs={{0,1},{1,0},{2,3},{3,2},{4,5},{5,4},{6,7},{7,6},{8,9},{9,8},{10,11... | collective-permute-start | bytes 7864328 | tf_op jit(solution)/shard_map/ppermute | solution.py:185
  4.3 11.9 %collective-permute-start.4 = (f32[2,128,512]{2,1,0:T(8,128)S(1)}, f32[2,128,512]{2,1,0:T(8,128)S(1)}, u32[]{:S(2)}, u32[]{:S(2)}) collective-permute-start(f32[2,128,512]{2,1,0:T(8,128)S(1)} %constant_dynamic-update-slice_fusion.own), channel_id=1, source_target_pairs={{0,1},{1,0},{2,3},{3,2},{4,5},{5,4},{6,7},{7,6},{8,9},{9,8},{10,11... | collective-permute-start | bytes 1572872 | tf_op jit(solution)/shard_map/ppermute | solution.py:185
  4.4 5.2 %collective-permute-start = (f32[128,128]{1,0:T(8,128)S(1)}, f32[128,128]{1,0:T(8,128)S(1)}, u32[]{:S(2)}, u32[]{:S(2)}) collective-permute-start(f32[128,128]{1,0:T(8,128)S(1)} %bitcast.12), channel_id=1, source_target_pairs={{0,1},{1,0},{2,3},{3,2},{4,5},{5,4},{6,7},{7,6},{8,9},{9,8},{10,11... | collective-permute-start | bytes 196616 | tf_op jit(solution)/shard_map/ppermute | solution.py:185
  9.8 10.1 %collective-permute-start.3 = (f32[128,128]{1,0:T(8,128)S(1)}, f32[128,128]{1,0:T(8,128)S(1)}, u32[]{:S(2)}, u32[]{:S(2)}) collective-permute-start(f32[128,128]{1,0:T(8,128)S(1)} %shard_map.82.near.packed), channel_id=1, source_target_pairs={{4,2},{5,3},{6,0},{7,1},{8,6},{9,7},{10,4},{11,5},{12,10},{13,11},... | collective-permute-start | bytes 196616 | tf_op jit(solution)/shard_map/ppermute | solution.py:185
  12.8 11.1 %collective-permute-start.2 = (f32[128,128]{1,0:T(8,128)S(1)}, f32[128,128]{1,0:T(8,128)S(1)}, u32[]{:S(2)}, u32[]{:S(2)}) collective-permute-start(f32[128,128]{1,0:T(8,128)S(1)} %shard_map.82.near.packed), channel_id=1, source_target_pairs={{4,0},{5,1},{6,2},{7,3},{8,4},{9,5},{10,6},{11,7},{12,8},{13,9},{1... | collective-permute-start | bytes 196616 | tf_op jit(solution)/shard_map/ppermute | solution.py:185
  15.9 8.1 %collective-permute-start.1 = (f32[128,128]{1,0:T(8,128)S(1)}, f32[128,128]{1,0:T(8,128)S(1)}, u32[]{:S(2)}, u32[]{:S(2)}) collective-permute-start(f32[128,128]{1,0:T(8,128)S(1)} %shard_map.82.near.packed), channel_id=1, source_target_pairs={{0,2},{1,3},{2,0},{3,1},{4,6},{5,7},{6,4},{7,5},{8,10},{9,11},{10,... | collective-permute-start | bytes 196616 | tf_op jit(solution)/shard_map/ppermute | solution.py:185
  16.7 8.0 %collective-permute-start.5 = (f32[128,128]{1,0:T(8,128)S(1)}, f32[128,128]{1,0:T(8,128)S(1)}, u32[]{:S(2)}, u32[]{:S(2)}) collective-permute-start(f32[128,128]{1,0:T(8,128)S(1)} %get-tuple-element.11), channel_id=1, source_target_pairs={{0,4},{1,5},{2,6},{3,7},{4,8},{5,9},{6,10},{7,11},{8,12},{9,13},{1... | collective-permute-start | bytes 196616 | tf_op jit(solution)/shard_map/ppermute | solution.py:185
  19.8 5.9 %collective-permute-start.6 = (f32[128,128]{1,0:T(8,128)S(1)}, f32[128,128]{1,0:T(8,128)S(1)}, u32[]{:S(2)}, u32[]{:S(2)}) collective-permute-start(f32[128,128]{1,0:T(8,128)S(1)} %get-tuple-element.12), channel_id=1, source_target_pairs={{0,6},{1,7},{2,4},{3,5},{4,10},{5,11},{6,8},{7,9},{8,14},{9,15},{1... | collective-permute-start | bytes 196616 | tf_op jit(solution)/shard_map/ppermute | solution.py:185
  25.8 3.2 %collective-permute-start.7 = (f32[128,128]{1,0:T(8,128)S(1)}, f32[128,128]{1,0:T(8,128)S(1)}, u32[]{:S(2)}, u32[]{:S(2)}) collective-permute-start(f32[128,128]{1,0:T(8,128)S(1)} %shard_map.85.near), channel_id=1, source_target_pairs={{0,2},{1,3},{2,0},{3,1},{4,6},{5,7},{6,4},{7,5},{8,10},{9,11},{10,... | collective-permute-start | bytes 196616 | tf_op jit(solution)/shard_map/ppermute | solution.py:185
  30.0 5.4 %collective-permute-start.9 = (f32[128,128]{1,0:T(8,128)S(1)}, f32[128,128]{1,0:T(8,128)S(1)}, u32[]{:S(2)}, u32[]{:S(2)}) collective-permute-start(f32[128,128]{1,0:T(8,128)S(1)} %get-tuple-element.13), channel_id=1, source_target_pairs={{4,0},{5,1},{6,2},{7,3},{12,8},{13,9},{14,10},{15,11},{20,16},{21,... | collective-permute-start | bytes 196616 | tf_op jit(solution)/shard_map/ppermute | solution.py:185
  33.0 3.6 %collective-permute-start.10 = (f32[128,128]{1,0:T(8,128)S(1)}, f32[128,128]{1,0:T(8,128)S(1)}, u32[]{:S(2)}, u32[]{:S(2)}) collective-permute-start(f32[128,128]{1,0:T(8,128)S(1)} %get-tuple-element.14), channel_id=1, source_target_pairs={{4,8},{5,9},{6,10},{7,11},{12,16},{13,17},{14,18},{15,19},{20,24},... | collective-permute-start | bytes 196616 | tf_op jit(solution)/shard_map/ppermute | solution.py:185
  36.7 3.2 %collective-permute-start.11 = (f32[128,128]{1,0:T(8,128)S(1)}, f32[128,128]{1,0:T(8,128)S(1)}, u32[]{:S(2)}, u32[]{:S(2)}) collective-permute-start(f32[128,128]{1,0:T(8,128)S(1)} %subtract_subtract_fusion.1.near), channel_id=1, source_target_pairs={{0,2},{1,3},{2,0},{3,1},{4,6},{5,7},{6,4},{7,5},{8,10},{9,11},{10,... | collective-permute-start | bytes 196616 | tf_op jit(solution)/shard_map/ppermute | solution.py:185
  40.8 1.3 %collective-permute-start.12 = (f32[128,128]{1,0:T(8,128)S(1)}, f32[128,128]{1,0:T(8,128)S(1)}, u32[]{:S(2)}, u32[]{:S(2)}) collective-permute-start(f32[128,128]{1,0:T(8,128)S(1)} %get-tuple-element.15), channel_id=1, source_target_pairs={{8,0},{9,1},{10,2},{11,3},{24,16},{25,17},{26,18},{27,19}} | collective-permute-start | bytes 196616 | tf_op jit(solution)/shard_map/ppermute | solution.py:185
  42.2 3.5 %collective-permute-start.14 = (f32[128,128]{1,0:T(8,128)S(1)}, f32[128,128]{1,0:T(8,128)S(1)}, u32[]{:S(2)}, u32[]{:S(2)}) collective-permute-start(f32[128,128]{1,0:T(8,128)S(1)} %subtract_subtract_fusion.near), channel_id=1, source_target_pairs={{0,2},{1,3},{2,0},{3,1},{4,6},{5,7},{6,4},{7,5},{8,10},{9,11},{10,... | collective-permute-start | bytes 196616 | tf_op jit(solution)/shard_map/ppermute | solution.py:185
  46.3 1.3 %collective-permute-start.16 = (f32[128,128]{1,0:T(8,128)S(1)}, f32[128,128]{1,0:T(8,128)S(1)}, u32[]{:S(2)}, u32[]{:S(2)}) collective-permute-start(f32[128,128]{1,0:T(8,128)S(1)} %shard_map.88), channel_id=1, source_target_pairs={{16,2},{17,3},{18,0},{19,1}} | collective-permute-start | bytes 196616 | tf_op jit(solution)/shard_map/ppermute | solution.py:185
  48.4 1.3 %collective-permute-start.18 = (f32[128,128]{1,0:T(8,128)S(1)}, f32[128,128]{1,0:T(8,128)S(1)}, u32[]{:S(2)}, u32[]{:S(2)}) collective-permute-start(f32[128,128]{1,0:T(8,128)S(1)} %shard_map.89.pivot.solved), channel_id=1, source_target_pairs={{0,18},{1,19},{2,16},{3,17}} | collective-permute-start | bytes 196616 | tf_op jit(solution)/shard_map/ppermute | solution.py:185
  50.4 2.7 %collective-permute-start.22 = (f32[128,128]{1,0:T(8,128)S(1)}, f32[128,128]{1,0:T(8,128)S(1)}, u32[]{:S(2)}, u32[]{:S(2)}) collective-permute-start(f32[128,128]{1,0:T(8,128)S(1)} %shard_map.90.solved), channel_id=1, source_target_pairs={{16,10},{17,11},{18,8},{19,9}} | collective-permute-start | bytes 196616 | tf_op jit(solution)/shard_map/ppermute | solution.py:185
  51.1 2.0 %collective-permute-start.21 = (f32[128,128]{1,0:T(8,128)S(1)}, f32[128,128]{1,0:T(8,128)S(1)}, u32[]{:S(2)}, u32[]{:S(2)}) collective-permute-start(f32[128,128]{1,0:T(8,128)S(1)} %shard_map.90.solved), channel_id=1, source_target_pairs={{16,8},{17,9},{18,10},{19,11}} | collective-permute-start | bytes 196616 | tf_op jit(solution)/shard_map/ppermute | solution.py:185
  51.8 1.4 %collective-permute-start.20 = (f32[128,128]{1,0:T(8,128)S(1)}, f32[128,128]{1,0:T(8,128)S(1)}, u32[]{:S(2)}, u32[]{:S(2)}) collective-permute-start(f32[128,128]{1,0:T(8,128)S(1)} %shard_map.90.solved), channel_id=1, source_target_pairs={{0,10},{1,11},{2,8},{3,9},{16,26},{17,27},{18,24},{19,25}} | collective-permute-start | bytes 196616 | tf_op jit(solution)/shard_map/ppermute | solution.py:185
  54.2 23.4 %collective-permute-start.26 = (f32[128,128]{1,0:T(8,128)S(1)}, f32[128,128]{1,0:T(8,128)S(1)}, u32[]{:S(2)}, u32[]{:S(2)}) collective-permute-start(f32[128,128]{1,0:T(8,128)S(1)} %shard_map.91.solved), channel_id=1, source_target_pairs={{8,6},{9,7},{10,4},{11,5},{16,14},{17,15},{18,12},{19,13},{24,22},... | collective-permute-start | bytes 196616 | tf_op jit(solution)/shard_map/ppermute | solution.py:185
  55.5 23.5 %collective-permute-start.25 = (f32[128,128]{1,0:T(8,128)S(1)}, f32[128,128]{1,0:T(8,128)S(1)}, u32[]{:S(2)}, u32[]{:S(2)}) collective-permute-start(f32[128,128]{1,0:T(8,128)S(1)} %shard_map.91.solved), channel_id=1, source_target_pairs={{8,4},{9,5},{10,6},{11,7},{16,12},{17,13},{18,14},{19,15},{24,20},... | collective-permute-start | bytes 196616 | tf_op jit(solution)/shard_map/ppermute | solution.py:185
  56.8 22.2 %collective-permute-start.24 = (f32[128,128]{1,0:T(8,128)S(1)}, f32[128,128]{1,0:T(8,128)S(1)}, u32[]{:S(2)}, u32[]{:S(2)}) collective-permute-start(f32[128,128]{1,0:T(8,128)S(1)} %shard_map.91.solved), channel_id=1, source_target_pairs={{0,6},{1,7},{2,4},{3,5},{8,14},{9,15},{10,12},{11,13},{16,22},{17,... | collective-permute-start | bytes 196616 | tf_op jit(solution)/shard_map/ppermute | solution.py:185
  58.1 21.6 %collective-permute-start.23 = (f32[128,128]{1,0:T(8,128)S(1)}, f32[128,128]{1,0:T(8,128)S(1)}, u32[]{:S(2)}, u32[]{:S(2)}) collective-permute-start(f32[128,128]{1,0:T(8,128)S(1)} %shard_map.91.solved), channel_id=1, source_target_pairs={{0,4},{1,5},{2,6},{3,7},{8,12},{9,13},{10,14},{11,15},{16,20},{17,... | collective-permute-start | bytes 196616 | tf_op jit(solution)/shard_map/ppermute | solution.py:185
  80.6 12.9 %collective-permute-start.27 = (f32[128,128]{1,0:T(8,128)S(1)}, f32[128,128]{1,0:T(8,128)S(1)}, u32[]{:S(2)}, u32[]{:S(2)}) collective-permute-start(f32[128,128]{1,0:T(8,128)S(1)} %shard_map.92.mine), channel_id=1, source_target_pairs={{0,1},{1,0},{2,3},{3,2},{4,5},{5,4},{6,7},{7,6},{8,9},{9,8},{10,11... | collective-permute-start | bytes 196616 | tf_op jit(solution)/shard_map/ppermute | solution.py:185
  (9 other events, 21.4 us)

commit v2 on v1

--- a/solution.py
+++ b/solution.py
@@ -50,8 +50,12 @@
 
 def load_vector(store, near, far):
     c = lax.axis_index("col")
-    spread(store, near[...], c)
-    spread(store, far[...], c ^ 2)
+    spread(store, near, c)
+    spread(store, far, c ^ 2)
+
+
+def keep(wanted, values):
+    return jnp.where(wanted, values[...], 0.0)
 
 
 def rows_product(block, store):
@@ -114,43 +118,52 @@
         out[...] = pair.T
 
 
-def ham_kernel(near, far, next_near, next_far, own, mate, out, here, there):
-    load_vector(here, near, far)
-    load_vector(there, next_near, next_far)
-    ham = real_product(own[1], mate[1], here) + real_product(own[0], mate[0], there)
+def ham_kernel(slabs, near, far, next_near, next_far, own_e, mate_e, own_t, mate_t, out, here, there):
+    linked = lax.axis_index("slab") < slabs - 1
+    load_vector(here, near[...], far[...])
+    load_vector(there, keep(linked, next_near), keep(linked, next_far))
+    ham = real_product(own_e[0], mate_e[0], here) + real_product(own_t[0], mate_t[0], there)
     out[...] = near[...] - half_step * rotate(ham)
 
 
 def add_up_kernel(rest, first, second, out):
-    out[...] = rest[...] - half_step * rotate(first[...] + second[...])
-
-
-def level_kernel(near, far, own, mate, beneath, above, store):
-    load_vector(store, near, far)
-    beneath[...] = complex_product(own[0:2], mate[0:2], store)
-    above[...] = complex_product(own[2:4], mate[2:4], store)
-
-
-def top_kernel(near, far, own, mate, beneath, store):
-    load_vector(store, near, far)
-    beneath[...] = complex_product(own[0:2], mate[0:2], store)
-
-
-def pivot_kernel(near, far, less_near, less_far, own, mate, out, store):
-    c = lax.axis_index("col")
-    spread(store, near[...] - less_near[...], c)
-    spread(store, far[...] - less_far[...], c ^ 2)
-    out[...] = complex_product(own[4:6], mate[4:6], store)
-
-
-def settle_kernel(tier_spacing, pivot, solved, *refs):
-    *vectors, own, mate, out, lower, upper = refs
+    linked = lax.axis_index("slab") > 0
+    out[...] = rest[...] - half_step * rotate(keep(linked, first) + keep(linked, second))
+
+
+def level_kernel(near, far, own_b, mate_b, own_a, mate_a, beneath, above, store):
+    load_vector(store, near[...], far[...])
+    beneath[...] = complex_product(own_b[0], mate_b[0], store)
+    above[...] = complex_product(own_a[0], mate_a[0], store)
+
+
+def top_kernel(near, far, own_b, mate_b, beneath, store):
+    load_vector(store, near[...], far[...])
+    beneath[...] = complex_product(own_b[0], mate_b[0], store)
+
+
+def reduce_kernel(tier_spacing, near, less, more, out):
     s = lax.axis_index("slab")
-    load_vector(lower, vectors[0], vectors[1])
-    change = complex_product(own[6:8], mate[6:8], lower)
-    if len(vectors) == 4:
-        load_vector(upper, vectors[2], vectors[3])
-        change = change + complex_product(own[8:10], mate[8:10], upper)
+    kept = s % (2 * tier_spacing) == 0
+    out[...] = near[...] - keep(kept, less) - keep(kept & (s > 0), more)
+
+
+def pivot_kernel(tier_spacing, near, far, less_near, less_far, own, mate, out, store):
+    root = lax.axis_index("slab") % (2 * tier_spacing) == 0
+    load_vector(store, near[...] - keep(root, less_near), far[...] - keep(root, less_far))
+    out[...] = complex_product(own[0], mate[0], store)
+
+
+def settle_kernel(slabs, tier_spacing, pivot, solved, lower_near, lower_far, own_l, mate_l, *refs):
+    *others, out, lower, upper = refs
+    s = lax.axis_index("slab")
+    load_vector(lower, lower_near[...], lower_far[...])
+    change = complex_product(own_l[0], mate_l[0], lower)
+    if others:
+        upper_near, upper_far, own_u, mate_u = others
+        linked = s + tier_spacing < slabs
+        load_vector(upper, keep(linked, upper_near), keep(linked, upper_far))
+        change = change + complex_product(own_u[0], mate_u[0], upper)
     active = s % (2 * tier_spacing) == tier_spacing
     out[...] = jnp.where(active, pivot[...] - change, solved[...])
 
@@ -171,9 +184,26 @@
     )(*operands)
 
 
+def completed(route, slabs, cols):
+    target = dict(route)
+    taken = set(target.values())
+    for a, b in route:
+        if b not in target and a not in taken:
+            target[b] = a
+            taken.add(a)
+    for a in [a for a in range(slabs * cols) if a not in target and a not in taken]:
+        target[a] = a ^ 1
+        taken.add(a ^ 1)
+    for a in range(slabs * cols):
+        if a not in target:
+            free = [b for b in range(slabs * cols) if b not in taken and b % cols == a % cols]
+            target[a] = free[0]
+            taken.add(free[0])
+    return sorted(target.items())
+
+
 def per_device(slabs, cols, waves, energy, tunnel, pivots, below, above, back_lower, back_upper):
     everyone = range(cols)
-    rows = waves.shape[1]
     width = energy.shape[2]
     store = pltpu.VMEM((width, LANES), short)
     one = 2 * 2 * Q * width * 2 * LANES * 2
@@ -182,47 +212,44 @@
         route = [
             (a * cols + c, b * cols + (c ^ flip)) for a, b in slab_pairs for c in everyone
         ]
-        return lax.ppermute(values, ("slab", "col"), route)
+        return lax.ppermute(values, ("slab", "col"), completed(route, slabs, cols))
 
     same = [(s, s) for s in range(slabs)]
 
     def shift(distance, chosen):
         return [(s, s + distance) for s in chosen if 0 <= s + distance < slabs]
 
+    def swap(values):
+        return send(values, same, 1)
+
     states = waves[0]
-    mate_states = send(states, same, 1)
-    hops = jnp.concatenate([tunnel, energy], axis=0)
-    mate_hops = send(hops, same, 1)
-    blocks = jnp.concatenate(
-        [below[0], above[0], pivots[0], back_lower[0], back_upper[0]], axis=0
-    )
-    mate_blocks = send(blocks, same, 1)
-
-    psi = call(pack_kernel, states, mate_states)
+    psi = call(pack_kernel, states, swap(states))
+    t_pair = tunnel, swap(tunnel)
+    e_pair = energy, swap(energy)
+    b_pair = below, swap(below)
+    a_pair = above, swap(above)
+    r_pair = pivots, swap(pivots)
+    l_pair = back_lower, swap(back_lower)
+    u_pair = back_upper, swap(back_upper)
+
     every = range(slabs)
     down, up = shift(-1, every), shift(1, every)
     psi_far = send(psi, same, 2)
     next_near = send(psi, down)
     next_far = send(psi, down, 2)
     up_near, up_far = call(
-        up_kernel,
-        psi,
-        hops,
-        mate_hops,
-        outs=2,
-        scratch=[pltpu.VMEM((64, width), wide)],
-        flops=one // 2,
+        up_kernel, psi, *t_pair, outs=2, scratch=[pltpu.VMEM((64, width), wide)], flops=one // 2
     )
     prev_near = send(up_near, up)
     prev_far = send(up_far, up, 2)
     rest = call(
-        ham_kernel,
+        functools.partial(ham_kernel, slabs),
         psi,
         psi_far,
         next_near,
         next_far,
-        hops,
-        mate_hops,
+        *e_pair,
+        *t_pair,
         scratch=[store, store],
         flops=one,
     )
@@ -235,25 +262,22 @@
         far = send(near, same, 2)
         if level < levels - 1:
             beneath, over = call(
-                level_kernel, near, far, blocks, mate_blocks, outs=2, scratch=[store], flops=2 * one
+                level_kernel, near, far, *b_pair, *a_pair, outs=2, scratch=[store], flops=2 * one
             )
             less = send(beneath, shift(-spacing, active))
             more = send(over, shift(spacing, active))
-            near = near - less - more
+            near = call(functools.partial(reduce_kernel, spacing), near, less, more)
         else:
-            beneath = call(
-                top_kernel, near, far, blocks, mate_blocks, scratch=[store], flops=one
-            )
+            beneath = call(top_kernel, near, far, *b_pair, scratch=[store], flops=one)
             less_near = send(beneath, shift(-spacing, active))
             less_far = send(beneath, shift(-spacing, active), 2)
             pivot = call(
-                pivot_kernel,
+                functools.partial(pivot_kernel, spacing),
                 near,
                 far,
                 less_near,
                 less_far,
-                blocks,
-                mate_blocks,
+                *r_pair,
                 scratch=[store],
                 flops=one,
             )
@@ -264,20 +288,18 @@
         active = [s for s in every if s % (2 * spacing) == spacing]
         from_lower = [(s - spacing, s) for s in active]
         from_upper = [(s + spacing, s) for s in active if s + spacing < slabs]
-        vectors = [send(solved, from_lower), send(solved, from_lower, 2)]
+        rest = [send(solved, from_lower), send(solved, from_lower, 2), *l_pair]
         if from_upper:
-            vectors += [send(solved, from_upper), send(solved, from_upper, 2)]
+            rest += [send(solved, from_upper), send(solved, from_upper, 2), *u_pair]
         solved = call(
-            functools.partial(settle_kernel, spacing),
+            functools.partial(settle_kernel, slabs, spacing),
             pivot,
             solved,
-            *vectors,
-            blocks,
-            mate_blocks,
+            *rest,
             scratch=[store, store],
-            flops=len(vectors) // 2 * one,
+            flops=len(rest) // 4 * one,
         )
-    out = call(regroup_kernel, solved, send(solved, same, 1))
+    out = call(regroup_kernel, solved, swap(solved))
     return out[None]
 
 

time: 95.9 us -> 99.3 us (1.035)
  starting transfers between devices: 47.9 us -> 59.4 us
  waiting for transfers between devices: 34.4 us -> 26.8 us
    ppermute x28 -> x33, starting transfers between devices: 47.9 us -> 59.4 us  [send(): return lax.ppermute(values, ('slab', 'col'), completed(route, slabs, cols))]
    ppermute x28 -> x33, waiting for transfers between devices: 34.4 us -> 26.8 us  [send(): return lax.ppermute(values, ('slab', 'col'), completed(route, slabs, cols))]
    unnamed x15 -> x18, local copies, waits for them, and re-layouts: 3.46 us -> 3.71 us
    pallas_call x12 -> x14, Pallas kernels: 7.93 us -> 7.94 us  [call(): pl.pallas_call(kernel, out_shape=packed if outs == 1 else (packed,) * out...]
  transfers between devices with their start and end apart: 28 -> 33, of which waited for: 10 -> 22; matrix products, arithmetic and copies ran while one was open for 0% -> 0% of each run, Pallas kernels for 1% -> 5%
where the time goes in v2:
time: 99.3 us; the launch traced here: 98 us
  starting transfers between devices  59.4 us (60%)
  waiting for transfers between devices  26.8 us (27%)
  Pallas kernels  7.94 us (8%)
  local copies, waits for them, and re-layouts  3.71 us (4%)
    ppermute x33, starting transfers between devices, send(): return lax.ppermute(values, ('slab', 'col'), completed(route, slabs, cols))  59.4 us
    ppermute x33, waiting for transfers between devices, send(): return lax.ppermute(values, ('slab', 'col'), completed(route, slabs, cols))  26.8 us
    pallas_call x14, Pallas kernels, call(): pl.pallas_call(kernel, out_shape=packed if outs == 1 else (packed,) * out...  7.94 us
    unnamed x18, local copies, waits for them, and re-layouts  3.71 us
  transfers between devices with their start and end apart: 33, of which 22 were waited for; matrix products, arithmetic and copies ran while one was open for 0% of the time, Pallas kernels for 5%

profile of v2, /device:TPU:13, one launch (start us, length us, event | category | flops | bytes accessed | tf_op | source)
XLA Modules:
  0.0 98.0 jit_solution(6834038460558682411)
XLA Ops:
  1.7 1.9 %collective-permute-done.other = f32[128,128]{1,0:T(8,128)S(1)} collective-permute-done((f32[128,128]{1,0:T(8,128)}, f32[128,128]{1,0:T(8,128)S(1)}, u32[]{:S(2)}, u32[]{:S(2)}) %collective-permute-start) | collective-permute-done | bytes 65568 | tf_op jit(solution)/shard_map/ppermute | solution.py:215
  4.6 1.3 %collective-permute-start.1 = (f32[128,128]{1,0:T(8,128)S(1)}, f32[128,128]{1,0:T(8,128)S(1)}, u32[]{:S(2)}, u32[]{:S(2)}) collective-permute-start(f32[128,128]{1,0:T(8,128)S(1)} %shard_map.82.near.packed), channel_id=1, source_target_pairs={{0,2},{1,3},{2,0},{3,1},{4,6},{5,7},{6,4},{7,5},{8,10},{9,11},{10,... | collective-permute-start | bytes 196616 | tf_op jit(solution)/shard_map/ppermute | solution.py:215
  5.9 1.9 %collective-permute-done.1.far = f32[128,128]{1,0:T(8,128)S(1)} collective-permute-done((f32[128,128]{1,0:T(8,128)S(1)}, f32[128,128]{1,0:T(8,128)S(1)}, u32[]{:S(2)}, u32[]{:S(2)}) %collective-permute-start.1) | collective-permute-done | bytes 65568 | tf_op jit(solution)/shard_map/ppermute | solution.py:215
  8.0 3.8 %collective-permute-done.2.next_near = f32[128,128]{1,0:T(8,128)S(1)} collective-permute-done((f32[128,128]{1,0:T(8,128)S(1)}, f32[128,128]{1,0:T(8,128)S(1)}, u32[]{:S(2)}, u32[]{:S(2)}) %collective-permute-start.2) | collective-permute-done | bytes 65568 | tf_op jit(solution)/shard_map/ppermute | solution.py:215
  12.0 3.0 %collective-permute-start.19 = (f32[1,2,128,512]{3,2,1,0:T(8,128)}, f32[1,2,128,512]{3,2,1,0:T(8,128)S(1)}, u32[]{:S(2)}, u32[]{:S(2)}) collective-permute-start(f32[1,2,128,512]{3,2,1,0:T(8,128)} %own.3), channel_id=1, source_target_pairs={{0,1},{1,0},{2,3},{3,2},{4,5},{5,4},{6,7},{7,6},{8,9},{9,8},{10,11... | collective-permute-start | bytes 1572872 | tf_op jit(solution)/shard_map/ppermute | solution.py:215
  16.7 2.8 %collective-permute-start.6 = (f32[128,128]{1,0:T(8,128)S(1)}, f32[128,128]{1,0:T(8,128)S(1)}, u32[]{:S(2)}, u32[]{:S(2)}) collective-permute-start(f32[128,128]{1,0:T(8,128)S(1)} %get-tuple-element.11), channel_id=1, source_target_pairs={{0,4},{1,5},{2,6},{3,7},{4,8},{5,9},{6,10},{7,11},{8,12},{9,13},{1... | collective-permute-start | bytes 196616 | tf_op jit(solution)/shard_map/ppermute | solution.py:215
  24.0 3.9 %collective-permute-start.22 = (f32[1,2,128,512]{3,2,1,0:T(8,128)S(1)}, f32[1,2,128,512]{3,2,1,0:T(8,128)S(1)}, u32[]{:S(2)}, u32[]{:S(2)}) collective-permute-start(f32[1,2,128,512]{3,2,1,0:T(8,128)S(1)} %copy-done.1), channel_id=1, source_target_pairs={{0,1},{1,0},{2,3},{3,2},{4,5},{5,4},{6,7},{7,6},{8,9},{9,8},{10,11... | collective-permute-start | bytes 1572872 | tf_op jit(solution)/shard_map/ppermute | solution.py:215
  27.9 3.8 %collective-permute-start.27 = (f32[1,2,128,512]{3,2,1,0:T(8,128)S(1)}, f32[1,2,128,512]{3,2,1,0:T(8,128)S(1)}, u32[]{:S(2)}, u32[]{:S(2)}) collective-permute-start(f32[1,2,128,512]{3,2,1,0:T(8,128)S(1)} %copy-done.3), channel_id=1, source_target_pairs={{0,1},{1,0},{2,3},{3,2},{4,5},{5,4},{6,7},{7,6},{8,9},{9,8},{10,11... | collective-permute-start | bytes 1572872 | tf_op jit(solution)/shard_map/ppermute | solution.py:215
  31.7 1.0 shard_map.86
  32.7 1.3 %collective-permute-start.11 = (f32[128,128]{1,0:T(8,128)S(1)}, f32[128,128]{1,0:T(8,128)S(1)}, u32[]{:S(2)}, u32[]{:S(2)}) collective-permute-start(f32[128,128]{1,0:T(8,128)S(1)} %get-tuple-element.13), channel_id=1, source_target_pairs={{0,4},{1,5},{2,6},{3,7},{4,0},{5,1},{6,2},{7,3},{8,12},{9,13},{10,... | collective-permute-start | bytes 196616 | tf_op jit(solution)/shard_map/ppermute | solution.py:215
  34.0 4.0 %collective-permute-start.12 = (f32[128,128]{1,0:T(8,128)S(1)}, f32[128,128]{1,0:T(8,128)S(1)}, u32[]{:S(2)}, u32[]{:S(2)}) collective-permute-start(f32[128,128]{1,0:T(8,128)S(1)} %get-tuple-element.14), channel_id=1, source_target_pairs={{0,1},{1,0},{2,3},{3,2},{4,8},{5,9},{6,10},{7,11},{8,4},{9,5},{10,... | collective-permute-start | bytes 196616 | tf_op jit(solution)/shard_map/ppermute | solution.py:215
  38.0 2.2 %collective-permute-done.12.more = f32[128,128]{1,0:T(8,128)S(1)} collective-permute-done((f32[128,128]{1,0:T(8,128)S(1)}, f32[128,128]{1,0:T(8,128)S(1)}, u32[]{:S(2)}, u32[]{:S(2)}) %collective-permute-start.12) | collective-permute-done | bytes 65568 | tf_op jit(solution)/shard_map/ppermute | solution.py:215
  40.5 2.9 %collective-permute-done.13.far = f32[128,128]{1,0:T(8,128)S(1)} collective-permute-done((f32[128,128]{1,0:T(8,128)S(1)}, f32[128,128]{1,0:T(8,128)S(1)}, u32[]{:S(2)}, u32[]{:S(2)}) %collective-permute-start.13) | collective-permute-done | bytes 65568 | tf_op jit(solution)/shard_map/ppermute | solution.py:215
  43.4 0.9 shard_map.88
  44.4 2.0 %collective-permute-start.14 = (f32[128,128]{1,0:T(8,128)S(1)}, f32[128,128]{1,0:T(8,128)S(1)}, u32[]{:S(2)}, u32[]{:S(2)}) collective-permute-start(f32[128,128]{1,0:T(8,128)S(1)} %get-tuple-element.15), channel_id=1, source_target_pairs={{0,8},{1,9},{2,10},{3,11},{4,5},{5,4},{6,7},{7,6},{8,0},{9,1},{10,... | collective-permute-start | bytes 196616 | tf_op jit(solution)/shard_map/ppermute | solution.py:215
  48.0 3.3 %collective-permute-done.16.far = f32[128,128]{1,0:T(8,128)S(1)} collective-permute-done((f32[128,128]{1,0:T(8,128)S(1)}, f32[128,128]{1,0:T(8,128)S(1)}, u32[]{:S(2)}, u32[]{:S(2)}) %collective-permute-start.16) | collective-permute-done | bytes 65568 | tf_op jit(solution)/shard_map/ppermute | solution.py:215
  51.9 1.0 %collective-permute-start.17 = (f32[128,128]{1,0:T(8,128)S(1)}, f32[128,128]{1,0:T(8,128)S(1)}, u32[]{:S(2)}, u32[]{:S(2)}) collective-permute-start(f32[128,128]{1,0:T(8,128)S(1)} %shard_map.90), channel_id=1, source_target_pairs={{0,16},{1,17},{2,18},{3,19},{4,5},{5,4},{6,7},{7,6},{8,9},{9,8},{1... | collective-permute-start | bytes 196616 | tf_op jit(solution)/shard_map/ppermute | solution.py:215
  59.3 1.0 shard_map.93.solved
  60.2 16.4 %collective-permute-start.28 = (f32[128,128]{1,0:T(8,128)S(1)}, f32[128,128]{1,0:T(8,128)S(1)}, u32[]{:S(2)}, u32[]{:S(2)}) collective-permute-start(f32[128,128]{1,0:T(8,128)S(1)} %shard_map.93.solved), channel_id=1, source_target_pairs={{0,4},{1,5},{2,6},{3,7},{4,0},{5,1},{6,2},{7,3},{8,12},{9,13},{10,... | collective-permute-start | bytes 196616 | tf_op jit(solution)/shard_map/ppermute | solution.py:215
  76.7 2.6 %collective-permute-start.30 = (f32[128,128]{1,0:T(8,128)S(1)}, f32[128,128]{1,0:T(8,128)S(1)}, u32[]{:S(2)}, u32[]{:S(2)}) collective-permute-start(f32[128,128]{1,0:T(8,128)S(1)} %shard_map.93.solved), channel_id=1, source_target_pairs={{0,1},{1,0},{2,3},{3,2},{4,8},{5,9},{6,10},{7,11},{8,4},{9,5},{10,... | collective-permute-start | bytes 196616 | tf_op jit(solution)/shard_map/ppermute | solution.py:215
  80.0 1.1 %collective-permute-done.29.lower_far = f32[128,128]{1,0:T(8,128)S(1)} collective-permute-done((f32[128,128]{1,0:T(8,128)S(1)}, f32[128,128]{1,0:T(8,128)S(1)}, u32[]{:S(2)}, u32[]{:S(2)}) %collective-permute-start.29) | collective-permute-done | bytes 65568 | tf_op jit(solution)/shard_map/ppermute | solution.py:215
  81.4 3.0 %collective-permute-done.31.refs_1_ = f32[128,128]{1,0:T(8,128)S(1)} collective-permute-done((f32[128,128]{1,0:T(8,128)S(1)}, f32[128,128]{1,0:T(8,128)S(1)}, u32[]{:S(2)}, u32[]{:S(2)}) %collective-permute-start.31) | collective-permute-done | bytes 65568 | tf_op jit(solution)/shard_map/ppermute | solution.py:215
  84.4 1.0 shard_map.94.mine
  85.3 11.0 %collective-permute-start.32 = (f32[128,128]{1,0:T(8,128)S(1)}, f32[128,128]{1,0:T(8,128)S(1)}, u32[]{:S(2)}, u32[]{:S(2)}) collective-permute-start(f32[128,128]{1,0:T(8,128)S(1)} %shard_map.94.mine), channel_id=1, source_target_pairs={{0,1},{1,0},{2,3},{3,2},{4,5},{5,4},{6,7},{7,6},{8,9},{9,8},{10,11... | collective-permute-start | bytes 196616 | tf_op jit(solution)/shard_map/ppermute | solution.py:215
  (74 shorter events, 20.8 us)
Async XLA Ops:
  0.0 31.7 %collective-permute-start.9 = (f32[1,2,128,512]{3,2,1,0:T(8,128)}, f32[1,2,128,512]{3,2,1,0:T(8,128)S(1)}, u32[]{:S(2)}, u32[]{:S(2)}) collective-permute-start(f32[1,2,128,512]{3,2,1,0:T(8,128)} %own_b.5), channel_id=1, source_target_pairs={{0,1},{1,0},{2,3},{3,2},{4,5},{5,4},{6,7},{7,6},{8,9},{9,8},{10,11... | collective-permute-start | bytes 1572872 | tf_op jit(solution)/shard_map/ppermute | solution.py:215
  0.7 31.1 %collective-permute-start.10 = (f32[1,2,128,512]{3,2,1,0:T(8,128)}, f32[1,2,128,512]{3,2,1,0:T(8,128)S(1)}, u32[]{:S(2)}, u32[]{:S(2)}) collective-permute-start(f32[1,2,128,512]{3,2,1,0:T(8,128)} %own_a.3), channel_id=1, source_target_pairs={{0,1},{1,0},{2,3},{3,2},{4,5},{5,4},{6,7},{7,6},{8,9},{9,8},{10,11... | collective-permute-start | bytes 1572872 | tf_op jit(solution)/shard_map/ppermute | solution.py:215
  0.7 11.4 %collective-permute-start.5 = (f32[1,128,512]{2,1,0:T(8,128)}, f32[1,128,512]{2,1,0:T(8,128)S(1)}, u32[]{:S(2)}, u32[]{:S(2)}) collective-permute-start(f32[1,128,512]{2,1,0:T(8,128)} %own.2), channel_id=1, source_target_pairs={{0,1},{1,0},{2,3},{3,2},{4,5},{5,4},{6,7},{7,6},{8,9},{9,8},{10,11... | collective-permute-start | bytes 786440 | tf_op jit(solution)/shard_map/ppermute | solution.py:215
  1.2 2.5 %collective-permute-start = (f32[128,128]{1,0:T(8,128)}, f32[128,128]{1,0:T(8,128)S(1)}, u32[]{:S(2)}, u32[]{:S(2)}) collective-permute-start(f32[128,128]{1,0:T(8,128)} %bitcast.2), channel_id=1, source_target_pairs={{0,1},{1,0},{2,3},{3,2},{4,5},{5,4},{6,7},{7,6},{8,9},{9,8},{10,11... | collective-permute-start | bytes 196616 | tf_op jit(solution)/shard_map/ppermute | solution.py:215
  1.2 18.3 %collective-permute-start.4 = (f32[1,128,512]{2,1,0:T(8,128)}, f32[1,128,512]{2,1,0:T(8,128)S(1)}, u32[]{:S(2)}, u32[]{:S(2)}) collective-permute-start(f32[1,128,512]{2,1,0:T(8,128)} %own_e.1), channel_id=1, source_target_pairs={{0,1},{1,0},{2,3},{3,2},{4,5},{5,4},{6,7},{7,6},{8,9},{9,8},{10,11... | collective-permute-start | bytes 786440 | tf_op jit(solution)/shard_map/ppermute | solution.py:215
  4.6 3.2 %collective-permute-start.1 = (f32[128,128]{1,0:T(8,128)S(1)}, f32[128,128]{1,0:T(8,128)S(1)}, u32[]{:S(2)}, u32[]{:S(2)}) collective-permute-start(f32[128,128]{1,0:T(8,128)S(1)} %shard_map.82.near.packed), channel_id=1, source_target_pairs={{0,2},{1,3},{2,0},{3,1},{4,6},{5,7},{6,4},{7,5},{8,10},{9,11},{10,... | collective-permute-start | bytes 196616 | tf_op jit(solution)/shard_map/ppermute | solution.py:215
  7.8 4.0 %collective-permute-start.2 = (f32[128,128]{1,0:T(8,128)S(1)}, f32[128,128]{1,0:T(8,128)S(1)}, u32[]{:S(2)}, u32[]{:S(2)}) collective-permute-start(f32[128,128]{1,0:T(8,128)S(1)} %shard_map.82.near.packed), channel_id=1, source_target_pairs={{0,28},{1,29},{2,30},{3,31},{4,0},{5,1},{6,2},{7,3},{8,4},{9,5},{1... | collective-permute-start | bytes 196616 | tf_op jit(solution)/shard_map/ppermute | solution.py:215
  11.8 4.9 %collective-permute-start.3 = (f32[128,128]{1,0:T(8,128)S(1)}, f32[128,128]{1,0:T(8,128)S(1)}, u32[]{:S(2)}, u32[]{:S(2)}) collective-permute-start(f32[128,128]{1,0:T(8,128)S(1)} %shard_map.82.near.packed), channel_id=1, source_target_pairs={{0,28},{1,29},{2,30},{3,31},{4,2},{5,3},{6,0},{7,1},{8,6},{9,7},{1... | collective-permute-start | bytes 196616 | tf_op jit(solution)/shard_map/ppermute | solution.py:215
  12.0 41.0 %collective-permute-start.19 = (f32[1,2,128,512]{3,2,1,0:T(8,128)}, f32[1,2,128,512]{3,2,1,0:T(8,128)S(1)}, u32[]{:S(2)}, u32[]{:S(2)}) collective-permute-start(f32[1,2,128,512]{3,2,1,0:T(8,128)} %own.3), channel_id=1, source_target_pairs={{0,1},{1,0},{2,3},{3,2},{4,5},{5,4},{6,7},{7,6},{8,9},{9,8},{10,11... | collective-permute-start | bytes 1572872 | tf_op jit(solution)/shard_map/ppermute | solution.py:215
  16.7 6.1 %collective-permute-start.6 = (f32[128,128]{1,0:T(8,128)S(1)}, f32[128,128]{1,0:T(8,128)S(1)}, u32[]{:S(2)}, u32[]{:S(2)}) collective-permute-start(f32[128,128]{1,0:T(8,128)S(1)} %get-tuple-element.11), channel_id=1, source_target_pairs={{0,4},{1,5},{2,6},{3,7},{4,8},{5,9},{6,10},{7,11},{8,12},{9,13},{1... | collective-permute-start | bytes 196616 | tf_op jit(solution)/shard_map/ppermute | solution.py:215
  19.5 4.1 %collective-permute-start.7 = (f32[128,128]{1,0:T(8,128)S(1)}, f32[128,128]{1,0:T(8,128)S(1)}, u32[]{:S(2)}, u32[]{:S(2)}) collective-permute-start(f32[128,128]{1,0:T(8,128)S(1)} %get-tuple-element.12), channel_id=1, source_target_pairs={{0,6},{1,7},{2,4},{3,5},{4,10},{5,11},{6,8},{7,9},{8,14},{9,15},{1... | collective-permute-start | bytes 196616 | tf_op jit(solution)/shard_map/ppermute | solution.py:215
  23.7 4.2 %collective-permute-start.8 = (f32[128,128]{1,0:T(8,128)S(1)}, f32[128,128]{1,0:T(8,128)S(1)}, u32[]{:S(2)}, u32[]{:S(2)}) collective-permute-start(f32[128,128]{1,0:T(8,128)S(1)} %shard_map.85.near), channel_id=1, source_target_pairs={{0,2},{1,3},{2,0},{3,1},{4,6},{5,7},{6,4},{7,5},{8,10},{9,11},{10,... | collective-permute-start | bytes 196616 | tf_op jit(solution)/shard_map/ppermute | solution.py:215
  24.0 31.5 %collective-permute-start.22 = (f32[1,2,128,512]{3,2,1,0:T(8,128)S(1)}, f32[1,2,128,512]{3,2,1,0:T(8,128)S(1)}, u32[]{:S(2)}, u32[]{:S(2)}) collective-permute-start(f32[1,2,128,512]{3,2,1,0:T(8,128)S(1)} %copy-done.1), channel_id=1, source_target_pairs={{0,1},{1,0},{2,3},{3,2},{4,5},{5,4},{6,7},{7,6},{8,9},{9,8},{10,11... | collective-permute-start | bytes 1572872 | tf_op jit(solution)/shard_map/ppermute | solution.py:215
  27.9 30.2 %collective-permute-start.27 = (f32[1,2,128,512]{3,2,1,0:T(8,128)S(1)}, f32[1,2,128,512]{3,2,1,0:T(8,128)S(1)}, u32[]{:S(2)}, u32[]{:S(2)}) collective-permute-start(f32[1,2,128,512]{3,2,1,0:T(8,128)S(1)} %copy-done.3), channel_id=1, source_target_pairs={{0,1},{1,0},{2,3},{3,2},{4,5},{5,4},{6,7},{7,6},{8,9},{9,8},{10,11... | collective-permute-start | bytes 1572872 | tf_op jit(solution)/shard_map/ppermute | solution.py:215
  32.7 5.2 %collective-permute-start.11 = (f32[128,128]{1,0:T(8,128)S(1)}, f32[128,128]{1,0:T(8,128)S(1)}, u32[]{:S(2)}, u32[]{:S(2)}) collective-permute-start(f32[128,128]{1,0:T(8,128)S(1)} %get-tuple-element.13), channel_id=1, source_target_pairs={{0,4},{1,5},{2,6},{3,7},{4,0},{5,1},{6,2},{7,3},{8,12},{9,13},{10,... | collective-permute-start | bytes 196616 | tf_op jit(solution)/shard_map/ppermute | solution.py:215
  34.0 6.2 %collective-permute-start.12 = (f32[128,128]{1,0:T(8,128)S(1)}, f32[128,128]{1,0:T(8,128)S(1)}, u32[]{:S(2)}, u32[]{:S(2)}) collective-permute-start(f32[128,128]{1,0:T(8,128)S(1)} %get-tuple-element.14), channel_id=1, source_target_pairs={{0,1},{1,0},{2,3},{3,2},{4,8},{5,9},{6,10},{7,11},{8,4},{9,5},{10,... | collective-permute-start | bytes 196616 | tf_op jit(solution)/shard_map/ppermute | solution.py:215
  40.2 3.2 %collective-permute-start.13 = (f32[128,128]{1,0:T(8,128)S(1)}, f32[128,128]{1,0:T(8,128)S(1)}, u32[]{:S(2)}, u32[]{:S(2)}) collective-permute-start(f32[128,128]{1,0:T(8,128)S(1)} %shard_map.87.near), channel_id=1, source_target_pairs={{0,2},{1,3},{2,0},{3,1},{4,6},{5,7},{6,4},{7,5},{8,10},{9,11},{10,... | collective-permute-start | bytes 196616 | tf_op jit(solution)/shard_map/ppermute | solution.py:215
  44.4 2.9 %collective-permute-start.14 = (f32[128,128]{1,0:T(8,128)S(1)}, f32[128,128]{1,0:T(8,128)S(1)}, u32[]{:S(2)}, u32[]{:S(2)}) collective-permute-start(f32[128,128]{1,0:T(8,128)S(1)} %get-tuple-element.15), channel_id=1, source_target_pairs={{0,8},{1,9},{2,10},{3,11},{4,5},{5,4},{6,7},{7,6},{8,0},{9,1},{10,... | collective-permute-start | bytes 196616 | tf_op jit(solution)/shard_map/ppermute | solution.py:215
  47.7 3.6 %collective-permute-start.16 = (f32[128,128]{1,0:T(8,128)S(1)}, f32[128,128]{1,0:T(8,128)S(1)}, u32[]{:S(2)}, u32[]{:S(2)}) collective-permute-start(f32[128,128]{1,0:T(8,128)S(1)} %shard_map.89.near), channel_id=1, source_target_pairs={{0,2},{1,3},{2,0},{3,1},{4,6},{5,7},{6,4},{7,5},{8,10},{9,11},{10,... | collective-permute-start | bytes 196616 | tf_op jit(solution)/shard_map/ppermute | solution.py:215
  60.2 19.8 %collective-permute-start.28 = (f32[128,128]{1,0:T(8,128)S(1)}, f32[128,128]{1,0:T(8,128)S(1)}, u32[]{:S(2)}, u32[]{:S(2)}) collective-permute-start(f32[128,128]{1,0:T(8,128)S(1)} %shard_map.93.solved), channel_id=1, source_target_pairs={{0,4},{1,5},{2,6},{3,7},{4,0},{5,1},{6,2},{7,3},{8,12},{9,13},{10,... | collective-permute-start | bytes 196616 | tf_op jit(solution)/shard_map/ppermute | solution.py:215
  76.7 4.4 %collective-permute-start.29 = (f32[128,128]{1,0:T(8,128)S(1)}, f32[128,128]{1,0:T(8,128)S(1)}, u32[]{:S(2)}, u32[]{:S(2)}) collective-permute-start(f32[128,128]{1,0:T(8,128)S(1)} %shard_map.93.solved), channel_id=1, source_target_pairs={{0,6},{1,7},{2,4},{3,5},{4,2},{5,3},{6,0},{7,1},{8,14},{9,15},{10,... | collective-permute-start | bytes 196616 | tf_op jit(solution)/shard_map/ppermute | solution.py:215
  76.7 4.7 %collective-permute-start.30 = (f32[128,128]{1,0:T(8,128)S(1)}, f32[128,128]{1,0:T(8,128)S(1)}, u32[]{:S(2)}, u32[]{:S(2)}) collective-permute-start(f32[128,128]{1,0:T(8,128)S(1)} %shard_map.93.solved), channel_id=1, source_target_pairs={{0,1},{1,0},{2,3},{3,2},{4,8},{5,9},{6,10},{7,11},{8,4},{9,5},{10,... | collective-permute-start | bytes 196616 | tf_op jit(solution)/shard_map/ppermute | solution.py:215
  79.3 5.1 %collective-permute-start.31 = (f32[128,128]{1,0:T(8,128)S(1)}, f32[128,128]{1,0:T(8,128)S(1)}, u32[]{:S(2)}, u32[]{:S(2)}) collective-permute-start(f32[128,128]{1,0:T(8,128)S(1)} %shard_map.93.solved), channel_id=1, source_target_pairs={{0,1},{1,0},{2,3},{3,2},{4,10},{5,11},{6,8},{7,9},{8,6},{9,7},{10,... | collective-permute-start | bytes 196616 | tf_op jit(solution)/shard_map/ppermute | solution.py:215
  85.3 11.9 %collective-permute-start.32 = (f32[128,128]{1,0:T(8,128)S(1)}, f32[128,128]{1,0:T(8,128)S(1)}, u32[]{:S(2)}, u32[]{:S(2)}) collective-permute-start(f32[128,128]{1,0:T(8,128)S(1)} %shard_map.94.mine), channel_id=1, source_target_pairs={{0,1},{1,0},{2,3},{3,2},{4,5},{5,4},{6,7},{7,6},{8,9},{9,8},{10,11... | collective-permute-start | bytes 196616 | tf_op jit(solution)/shard_map/ppermute | solution.py:215
  (18 other events, 63.3 us)

commit v3 on v2

v3 whole, which is shorter than its diff:
```python
import functools

import jax
import jax.numpy as jnp
from jax import lax
from jax.experimental import pallas as pl
from jax.experimental.pallas import tpu as pltpu
from jax.sharding import PartitionSpec as P


half_step = 0.5
wide = jnp.float32
short = jnp.bfloat16
Q = 128
LANES = 128
cost = pl.CostEstimate(flops=10**10, bytes_accessed=1, transcendentals=0)


def lanes(values):
    return lax.broadcasted_iota(jnp.int32, values.shape, 1)


def swap_halves(values):
    return pltpu.roll(values, 64, 1)


def join(left, right):
    return jnp.where(lanes(left) < 64, left, right)


def rotate(values):
    even = lanes(values) % 2 == 0
    return jnp.where(even, -pltpu.roll(values, LANES - 1, 1), pltpu.roll(values, 1, 1))


def split(values):
    high = values.astype(short)
    return high, (values - high.astype(wide)).astype(short)


def quarter(number):
    return pl.ds(pl.multiple_of(number * Q, Q), Q)


def spread(store, packed, first):
    high = packed.astype(short).astype(wide)
    low = packed - high
    store[quarter(first), :] = join(high, swap_halves(low)).astype(short)
    store[quarter(first ^ 1), :] = join(swap_halves(high), low).astype(short)


def load_vector(store, near, far):
    c = lax.axis_index("col")
    spread(store, near, c)
    spread(store, far, c ^ 2)


def keep(wanted, values):
    return jnp.where(wanted, values[...], 0.0)


def rows_product(block, store):
    high, low = split(block)
    vector = store[...]
    return jnp.dot(high, vector, preferred_element_type=wide) + jnp.dot(
        low, vector, preferred_element_type=wide
    )


def fold(values):
    return values + swap_halves(values)


def real_product(own, mate, store):
    return join(fold(rows_product(own, store)), fold(rows_product(mate, store)))


def complex_half(block, store):
    both = rows_product(block.reshape(2 * Q, block.shape[-1]), store)
    return fold(both[:Q] + rotate(both[Q:]))


def complex_product(own, mate, store):
    return join(complex_half(own, store), complex_half(mate, store))


def regroup_kernel(mine, other, out):
    c = lax.axis_index("col")
    rows = join(mine[...], other[...])
    out[...] = jnp.where(c % 2 == 0, rows, swap_halves(rows))


def side_kernel(side):
    c = lax.axis_index("col")
    side[...] = jnp.zeros_like(side) + (1 - c % 2)


def open_kernel(mine, other, side, own, mate, psi, near, far, crossing, store):
    c = lax.axis_index("col")
    packed = jnp.where(
        side[0:1] == 1,
        join(mine[0], swap_halves(other[0])),
        join(swap_halves(mine[0]), other[0]),
    )
    psi[...] = packed
    turned = packed.T
    total = None
    for rows, block in ((turned[:64], own[0]), (turned[64:], mate[0])):
        high, low = split(rows)
        pair = jnp.concatenate([high, low], axis=0)
        block_high, block_low = split(block)
        part = jnp.dot(pair, block_high, preferred_element_type=wide) + jnp.dot(
            pair, block_low, preferred_element_type=wide
        )
        part = part[:64] + part[64:]
        total = part if total is None else total + part
    store[...] = total
    for out, first in ((near, c), (far, c ^ 2)):
        pair = jnp.concatenate(
            [store[:, quarter(first)], store[:, quarter(first ^ 1)]], axis=0
        )
        out[...] = half_step * rotate(pair.T)
    crossing[...] = jnp.where(lax.axis_index("slab") % 2 == 1, packed, far[...])


def ham_kernel(slabs, near, crossed, crossed_next, next_near, own_e, mate_e, own_t, mate_t, out, here, there):
    s = lax.axis_index("slab")
    odd = s % 2 == 1
    linked = odd & (s < slabs - 1)
    load_vector(here, near[...], jnp.where(odd, crossed[...], crossed_next[...]))
    load_vector(there, keep(linked, next_near), keep(linked, crossed_next))
    ham = real_product(own_e[0], mate_e[0], here) + real_product(own_t[0], mate_t[0], there)
    out[...] = near[...] - half_step * rotate(ham)


def even_kernel(rest, next_near, next_far, own, mate, out, store):
    load_vector(store, next_near[...], next_far[...])
    out[...] = rest[...] - half_step * rotate(real_product(own[0], mate[0], store))


def first_kernel(near, far, tail_near, tail_far, own_b, mate_b, own_a, mate_a, beneath, above, store):
    load_vector(store, near[...], far[...])
    above[...] = complex_product(own_a[0], mate_a[0], store) + tail_near[...] + tail_far[...]
    beneath[...] = complex_product(own_b[0], mate_b[0], store)


def level_kernel(near, far, own_b, mate_b, own_a, mate_a, beneath, above, store):
    load_vector(store, near[...], far[...])
    above[...] = complex_product(own_a[0], mate_a[0], store)
    beneath[...] = complex_product(own_b[0], mate_b[0], store)


def one_kernel(near, far, own, mate, out, store):
    load_vector(store, near[...], far[...])
    out[...] = complex_product(own[0], mate[0], store)


def settle_kernel(tier_spacing, late, pivot, near, far, own_l, mate_l, own_u, mate_u, out, store):
    first = lax.axis_index("slab") % (4 * tier_spacing) == tier_spacing
    from_lower = jnp.logical_xor(first, late)
    load_vector(store, near[...], far[...])

    @pl.when(from_lower)
    def _():
        out[...] = pivot[...] - complex_product(own_l[0], mate_l[0], store)

    @pl.when(jnp.logical_not(from_lower))
    def _():
        out[...] = pivot[...] - complex_product(own_u[0], mate_u[0], store)


def call(kernel, *operands, outs=1, scratch=(), shape=jax.ShapeDtypeStruct((Q, LANES), wide)):
    vmem = pl.BlockSpec(memory_space=pltpu.VMEM)
    return pl.pallas_call(
        kernel,
        out_shape=shape if outs == 1 else (shape,) * outs,
        in_specs=[vmem] * len(operands),
        out_specs=vmem if outs == 1 else (vmem,) * outs,
        scratch_shapes=list(scratch),
        cost_estimate=cost,
        compiler_params=pltpu.CompilerParams(vmem_limit_bytes=16 * 2**20),
    )(*operands)


def completed(route, slabs, cols):
    target = dict(route)
    taken = set(target.values())
    for a, b in route:
        if b not in target and a not in taken:
            target[b] = a
            taken.add(a)
    for a in [a for a in range(slabs * cols) if a not in target and a not in taken]:
        target[a] = a ^ 1
        taken.add(a ^ 1)
    for a in range(slabs * cols):
        if a not in target:
            free = [b for b in range(slabs * cols) if b not in taken and b % cols == a % cols]
            target[a] = free[0]
            taken.add(free[0])
    return sorted(target.items())


def per_device(slabs, cols, waves, energy, tunnel, pivots, below, above, back_lower, back_upper):
    everyone = range(cols)
    width = energy.shape[2]
    store = pltpu.VMEM((width, LANES), short)
    levels = slabs.bit_length() - 1
    every = range(slabs)
    s = lax.axis_index("slab")
    odd = s % 2 == 1

    def send(values, slab_pairs, flip=0):
        route = [
            (a * cols + c, b * cols + (c ^ flip)) for a, b in slab_pairs for c in everyone
        ]
        return lax.ppermute(values, ("slab", "col"), completed(route, slabs, cols))

    def both(values, slab_pairs):
        return send(values, slab_pairs), send(values, slab_pairs, 2)

    def swap(values):
        return send(values, [(a, a) for a in every], 1)

    def exchange(values):
        return send(values, [(a, a) for a in every], 2)

    in_plane = [(a, a ^ 1) for a in every]
    between = [(a, a + 1) for a in every if a % 2 == 1 and a + 1 < slabs]

    side = call(side_kernel, shape=jax.ShapeDtypeStruct((8, LANES), jnp.int32))
    t_pair = tunnel, swap(tunnel)
    e_pair = energy, swap(energy)
    b_pair = below, swap(below)
    a_pair = above, swap(above)
    r_pair = pivots, swap(pivots)
    l_pair = back_lower, swap(back_lower)
    u_pair = back_upper, swap(back_upper)
    psi, up_near, up_far, crossing = call(
        open_kernel,
        waves,
        swap(waves),
        side,
        *t_pair,
        outs=4,
        scratch=[pltpu.VMEM((64, width), wide)],
    )
    next_odd = send(psi, between)
    crossed = exchange(crossing)
    crossed_next = exchange(jnp.where(odd, next_odd, psi))
    stepped = send(jnp.where(odd, psi, up_near + crossed), in_plane)
    up_odd = exchange(up_far)
    rest = call(
        functools.partial(ham_kernel, slabs),
        psi,
        crossed,
        crossed_next,
        next_odd,
        *e_pair,
        *t_pair,
        scratch=[store, store],
    )
    near = rest - stepped
    far = exchange(near)
    stepped_far = exchange(stepped)

    base = base_far = last_near = last_far = pivot = None
    for level in range(levels):
        spacing = 2**level
        active = [a for a in every if a % (2 * spacing) == spacing]
        is_active = s % (2 * spacing) == spacing
        if level == 0:
            last_near, last_far = near, far
            beneath, over = call(
                first_kernel,
                near,
                far,
                up_near,
                up_odd,
                *b_pair,
                *a_pair,
                outs=2,
                scratch=[store],
            )
        else:
            last_near = jnp.where(is_active, near, last_near)
            last_far = jnp.where(is_active, far, last_far)
            if level < levels - 1:
                beneath, over = call(
                    level_kernel, near, far, *b_pair, *a_pair, outs=2, scratch=[store]
                )
            else:
                beneath = call(one_kernel, near, far, *b_pair, scratch=[store])
        if level == levels - 1:
            less_near, less_far = both(beneath, [(spacing, 0)])
            base_far = exchange(base)
            near = jnp.where(s == 0, base - less_near, last_near)
            far = jnp.where(s == 0, base_far - less_far, last_far)
            pivot = call(one_kernel, near, far, *r_pair, scratch=[store])
            continue
        urgent = [a for a in every if a % (4 * spacing) == 2 * spacing]
        more_near, more_far = both(over, [(a - spacing, a) for a in urgent])
        less_near, less_far = both(beneath, [(a + spacing, a) for a in urgent])
        if level == 0:
            base = call(
                even_kernel, rest, stepped, stepped_far, *t_pair, scratch=[store]
            )
        base_far = exchange(base)
        near = base - more_near - less_near
        far = base_far - more_far - less_far
        patient = [a for a in every if a % (4 * spacing) == 0]
        is_patient = s % (4 * spacing) == 0
        later_less = send(beneath, [(a + spacing, a) for a in patient])
        later_more = [(a - spacing, a) for a in patient if a >= spacing]
        base = base - jnp.where(is_patient, later_less, 0.0)
        if later_more:
            arrived = send(over, later_more)
            base = base - jnp.where(is_patient & (s > 0), arrived, 0.0)

    solved = rest = pivot
    for level in reversed(range(levels)):
        spacing = 2**level
        is_active = s % (2 * spacing) == spacing
        late = [a for a in every if a % (4 * spacing) == 2 * spacing] if level < levels - 1 else [0]
        vectors = []
        for way in (1, -1):
            pairs = [(a, a + way * spacing) for a in late if 0 <= a + way * spacing < slabs]
            if pairs:
                vectors.append((way, both(solved, pairs)))
        if level == levels - 1:
            near, far = vectors[0][1]
        else:
            from_above = s % (4 * spacing) == spacing
            near = jnp.where(from_above, vectors[1][1][0], vectors[0][1][0])
            far = jnp.where(from_above, vectors[1][1][1], vectors[0][1][1])
        settled = call(
            functools.partial(settle_kernel, spacing, level < levels - 1),
            rest,
            near,
            far,
            *l_pair,
            *u_pair,
            scratch=[store],
        )
        before = solved
        solved = jnp.where(is_active, settled, solved)
        if level > 0:
            below_spacing = spacing // 2
            sources = [a for a in every if a % (4 * below_spacing) == 0]
            from_lower = [(a, a + below_spacing) for a in sources]
            from_upper = [(a, a - below_spacing) for a in sources if a > 0]
            low = both(before, from_lower)
            near, far = low
            linked = True
            if from_upper:
                up = both(before, from_upper)
                first = s % (4 * below_spacing) == below_spacing
                near = jnp.where(first, low[0], up[0])
                far = jnp.where(first, low[1], up[1])
            linked = s + below_spacing < slabs
            rest = call(
                functools.partial(settle_kernel, below_spacing, False),
                pivot,
                jnp.where(linked, near, 0.0),
                jnp.where(linked, far, 0.0),
                *l_pair,
                *u_pair,
                scratch=[store],
            )
    out = call(regroup_kernel, solved, swap(solved))
    return out[None]


def solution(mesh):
    slabs, cols = mesh.shape["slab"], mesh.shape["col"]
    vector = P("slab", "col", None)
    block = P("slab", None, "col", None)
    return jax.shard_map(
        functools.partial(per_device, slabs, cols),
        mesh=mesh,
        in_specs=(vector,) * 3 + (block,) * 5,
        out_specs=vector,
        check_vma=False,
    )
```

time: 99.3 us -> 83.3 us (0.84)
  the two profiles are of different devices: /device:TPU:13 before, /device:TPU:9 now
where the time goes in v3:
time: 83.3 us; the launch traced here: 83.2 us
  starting transfers between devices  50.8 us (61%)
  waiting for transfers between devices  22 us (26%)
  Pallas kernels  9.84 us (12%)
    ppermute x48, starting transfers between devices, send(): return lax.ppermute(values, ('slab', 'col'), completed(route, slabs, cols))  50.8 us
    ppermute x48, waiting for transfers between devices, send(): return lax.ppermute(values, ('slab', 'col'), completed(route, slabs, cols))  22 us
    pallas_call x14, Pallas kernels, call(): pl.pallas_call(kernel, out_shape=shape if outs == 1 else (shape,) * outs,...  9.84 us
  transfers between devices with their start and end apart: 48, of which 17 were waited for; matrix products, arithmetic and copies ran while one was open for 0% of the time, Pallas kernels for 9%

profile of v3, /device:TPU:9, one launch (start us, length us, event | category | flops | bytes accessed | tf_op | source)
XLA Modules:
  0.0 83.2 jit_solution(15650559794819135534)
XLA Ops:
  0.8 1.4 %collective-permute-done.other = f32[1,128,128]{2,1,0:T(8,128)S(1)} collective-permute-done((f32[1,128,128]{2,1,0:T(8,128)}, f32[1,128,128]{2,1,0:T(8,128)S(1)}, u32[]{:S(2)}, u32[]{:S(2)}) %collective-permute-start) | collective-permute-done | bytes 65568 | tf_op jit(solution)/shard_map/ppermute | solution.py:216
  8.7 1.8 %collective-permute-start.10 = (f32[1,2,128,512]{3,2,1,0:T(8,128)S(1)}, f32[1,2,128,512]{3,2,1,0:T(8,128)S(1)}, u32[]{:S(2)}, u32[]{:S(2)}) collective-permute-start(f32[1,2,128,512]{3,2,1,0:T(8,128)S(1)} %copy-done.1), channel_id=1, source_target_pairs={{0,1},{1,0},{2,3},{3,2},{4,5},{5,4},{6,7},{7,6},{8,9},{9,8},{10,11... | collective-permute-start | bytes 1572872 | tf_op jit(solution)/shard_map/ppermute | solution.py:216
  10.8 1.4 %collective-permute-start.6 = (f32[128,128]{1,0:T(8,128)S(1)}, f32[128,128]{1,0:T(8,128)S(1)}, u32[]{:S(2)}, u32[]{:S(2)}) collective-permute-start(f32[128,128]{1,0:T(8,128)S(1)} %get-tuple-element.25), channel_id=1, source_target_pairs={{0,4},{1,5},{2,6},{3,7},{4,0},{5,1},{6,2},{7,3},{8,12},{9,13},{10,... | collective-permute-start | bytes 196616 | tf_op jit(solution)/shard_map/ppermute | solution.py:216
  12.9 1.4 %collective-permute-done.6.next_near = f32[128,128]{1,0:T(8,128)S(1)} collective-permute-done((f32[128,128]{1,0:T(8,128)S(1)}, f32[128,128]{1,0:T(8,128)S(1)}, u32[]{:S(2)}, u32[]{:S(2)}) %collective-permute-start.6) | collective-permute-done | bytes 65568 | tf_op jit(solution)/shard_map/ppermute | solution.py:216
  14.3 1.3 %collective-permute-start.8 = (f32[128,128]{1,0:T(8,128)S(1)}, f32[128,128]{1,0:T(8,128)S(1)}, u32[]{:S(2)}, u32[]{:S(2)}) collective-permute-start(f32[128,128]{1,0:T(8,128)S(1)} %sub.42.near), channel_id=1, source_target_pairs={{0,2},{1,3},{2,0},{3,1},{4,6},{5,7},{6,4},{7,5},{8,10},{9,11},{10,... | collective-permute-start | bytes 196616 | tf_op jit(solution)/shard_map/ppermute | solution.py:216
  15.8 1.6 %collective-permute-done.8.far = f32[128,128]{1,0:T(8,128)S(1)} collective-permute-done((f32[128,128]{1,0:T(8,128)S(1)}, f32[128,128]{1,0:T(8,128)S(1)}, u32[]{:S(2)}, u32[]{:S(2)}) %collective-permute-start.8) | collective-permute-done | bytes 65568 | tf_op jit(solution)/shard_map/ppermute | solution.py:216
  18.4 1.3 %collective-permute-start.14 = (f32[128,128]{1,0:T(8,128)S(1)}, f32[128,128]{1,0:T(8,128)S(1)}, u32[]{:S(2)}, u32[]{:S(2)}) collective-permute-start(f32[128,128]{1,0:T(8,128)S(1)} %get-tuple-element.18), channel_id=1, source_target_pairs={{0,1},{1,0},{2,3},{3,2},{4,8},{5,9},{6,10},{7,11},{8,4},{9,5},{10,... | collective-permute-start | bytes 196616 | tf_op jit(solution)/shard_map/ppermute | solution.py:216
  19.7 2.9 %collective-permute-start.15 = (f32[128,128]{1,0:T(8,128)S(1)}, f32[128,128]{1,0:T(8,128)S(1)}, u32[]{:S(2)}, u32[]{:S(2)}) collective-permute-start(f32[128,128]{1,0:T(8,128)S(1)} %get-tuple-element.17), channel_id=1, source_target_pairs={{0,1},{1,0},{2,3},{3,2},{4,5},{5,4},{6,7},{7,6},{8,12},{9,13},{10,... | collective-permute-start | bytes 196616 | tf_op jit(solution)/shard_map/ppermute | solution.py:216
  23.1 1.3 %collective-permute-start.16 = (f32[128,128]{1,0:T(8,128)S(1)}, f32[128,128]{1,0:T(8,128)S(1)}, u32[]{:S(2)}, u32[]{:S(2)}) collective-permute-start(f32[128,128]{1,0:T(8,128)S(1)} %shard_map.85), channel_id=1, source_target_pairs={{0,2},{1,3},{2,0},{3,1},{4,6},{5,7},{6,4},{7,5},{8,10},{9,11},{10,... | collective-permute-start | bytes 196616 | tf_op jit(solution)/shard_map/ppermute | solution.py:216
  27.1 2.2 %collective-permute-done.17 = f32[128,128]{1,0:T(8,128)S(1)} collective-permute-done((f32[128,128]{1,0:T(8,128)S(1)}, f32[128,128]{1,0:T(8,128)S(1)}, u32[]{:S(2)}, u32[]{:S(2)}) %collective-permute-start.17) | collective-permute-done | bytes 65568 | tf_op jit(solution)/shard_map/ppermute | solution.py:216
  29.3 2.0 %collective-permute-done.18 = f32[128,128]{1,0:T(8,128)S(1)} collective-permute-done((f32[128,128]{1,0:T(8,128)S(1)}, f32[128,128]{1,0:T(8,128)S(1)}, u32[]{:S(2)}, u32[]{:S(2)}) %collective-permute-start.18) | collective-permute-done | bytes 65568 | tf_op jit(solution)/shard_map/ppermute | solution.py:216
  33.2 2.7 %collective-permute-start.23 = (f32[128,128]{1,0:T(8,128)S(1)}, f32[128,128]{1,0:T(8,128)S(1)}, u32[]{:S(2)}, u32[]{:S(2)}) collective-permute-start(f32[128,128]{1,0:T(8,128)S(1)} %get-tuple-element.20), channel_id=1, source_target_pairs={{0,1},{1,0},{2,3},{3,2},{4,5},{5,4},{6,7},{7,6},{8,18},{9,19},{10,... | collective-permute-start | bytes 196616 | tf_op jit(solution)/shard_map/ppermute | solution.py:216
  37.3 1.3 %collective-permute-done.23 = f32[128,128]{1,0:T(8,128)S(1)} collective-permute-done((f32[128,128]{1,0:T(8,128)S(1)}, f32[128,128]{1,0:T(8,128)S(1)}, u32[]{:S(2)}, u32[]{:S(2)}) %collective-permute-start.23) | collective-permute-done | bytes 65568 | tf_op jit(solution)/shard_map/ppermute | solution.py:216
  39.8 1.3 %shard_map.88 = f32[128,128]{1,0:T(8,128)} custom-call(f32[128,128]{1,0:T(8,128)S(1)} %get-tuple-element.23.near, f32[128,128]{1,0:T(8,128)S(1)} %subtract_subtract_fusion.far, f32[1,2,128,512]{3,2,1,0:T(8,128)S(1)} %copy-done.1, f32[1,2,128,512]{3,2,1,0:T(8,128)S(1)} %collective-permute-done.10.mate_b.mate), custom_call_target="tpu_custom_call" | custom-call | flops 10000000000 | bytes 1 | tf_op jit(solution)/shard_map/pallas_call | solution.py:174
  41.1 2.3 %collective-permute-start.25 = (f32[128,128]{1,0:T(8,128)}, f32[128,128]{1,0:T(8,128)S(1)}, u32[]{:S(2)}, u32[]{:S(2)}) collective-permute-start(f32[128,128]{1,0:T(8,128)} %shard_map.88), channel_id=1, source_target_pairs={{0,16},{1,17},{2,18},{3,19},{4,5},{5,4},{6,7},{7,6},{8,9},{9,8},{1... | collective-permute-start | bytes 196616 | tf_op jit(solution)/shard_map/ppermute | solution.py:216
  46.5 1.3 %collective-permute-done.26 = f32[128,128]{1,0:T(8,128)S(1)} collective-permute-done((f32[128,128]{1,0:T(8,128)S(1)}, f32[128,128]{1,0:T(8,128)S(1)}, u32[]{:S(2)}, u32[]{:S(2)}) %collective-permute-start.26) | collective-permute-done | bytes 65568 | tf_op jit(solution)/shard_map/ppermute | solution.py:216
  48.5 1.6 %collective-permute-start.29 = (f32[128,128]{1,0:T(8,128)S(1)}, f32[128,128]{1,0:T(8,128)S(1)}, u32[]{:S(2)}, u32[]{:S(2)}) collective-permute-start(f32[128,128]{1,0:T(8,128)S(1)} %shard_map.89.pivot), channel_id=1, source_target_pairs={{0,16},{1,17},{2,18},{3,19},{4,5},{5,4},{6,7},{7,6},{8,9},{9,8},{1... | collective-permute-start | bytes 196616 | tf_op jit(solution)/shard_map/ppermute | solution.py:216
  50.2 6.1 %collective-permute-start.37 = (f32[128,128]{1,0:T(8,128)S(1)}, f32[128,128]{1,0:T(8,128)S(1)}, u32[]{:S(2)}, u32[]{:S(2)}) collective-permute-start(f32[128,128]{1,0:T(8,128)S(1)} %shard_map.89.pivot), channel_id=1, source_target_pairs={{0,8},{1,9},{2,10},{3,11},{4,5},{5,4},{6,7},{7,6},{8,0},{9,1},{10,... | collective-permute-start | bytes 196616 | tf_op jit(solution)/shard_map/ppermute | solution.py:216
  57.0 3.8 %collective-permute-start.41 = (f32[128,128]{1,0:T(8,128)S(1)}, f32[128,128]{1,0:T(8,128)S(1)}, u32[]{:S(2)}, u32[]{:S(2)}) collective-permute-start(f32[128,128]{1,0:T(8,128)S(1)} %broadcast_select_fusion.7), channel_id=1, source_target_pairs={{0,1},{1,0},{2,3},{3,2},{4,5},{5,4},{6,7},{7,6},{8,18},{9,19},{10,... | collective-permute-start | bytes 196616 | tf_op jit(solution)/shard_map/ppermute | solution.py:216
  60.8 3.8 %collective-permute-start.42 = (f32[128,128]{1,0:T(8,128)S(1)}, f32[128,128]{1,0:T(8,128)S(1)}, u32[]{:S(2)}, u32[]{:S(2)}) collective-permute-start(f32[128,128]{1,0:T(8,128)S(1)} %broadcast_select_fusion.7), channel_id=1, source_target_pairs={{0,1},{1,0},{2,3},{3,2},{4,5},{5,4},{6,7},{7,6},{8,9},{9,8},{10,11... | collective-permute-start | bytes 196616 | tf_op jit(solution)/shard_map/ppermute | solution.py:216
  66.9 1.4 %collective-permute-done.39 = f32[128,128]{1,0:T(8,128)S(1)} collective-permute-done((f32[128,128]{1,0:T(8,128)S(1)}, f32[128,128]{1,0:T(8,128)S(1)}, u32[]{:S(2)}, u32[]{:S(2)}) %collective-permute-start.39) | collective-permute-done | bytes 65568 | tf_op jit(solution)/shard_map/ppermute | solution.py:216
  70.3 3.4 %collective-permute-start.46 = (f32[128,128]{1,0:T(8,128)S(1)}, f32[128,128]{1,0:T(8,128)S(1)}, u32[]{:S(2)}, u32[]{:S(2)}) collective-permute-start(f32[128,128]{1,0:T(8,128)S(1)} %broadcast_select_fusion.6), channel_id=1, source_target_pairs={{0,1},{1,0},{2,3},{3,2},{4,5},{5,4},{6,7},{7,6},{8,14},{9,15},{10,... | collective-permute-start | bytes 196616 | tf_op jit(solution)/shard_map/ppermute | solution.py:216
  75.8 1.8 %collective-permute-done.46 = f32[128,128]{1,0:T(8,128)S(1)} collective-permute-done((f32[128,128]{1,0:T(8,128)S(1)}, f32[128,128]{1,0:T(8,128)S(1)}, u32[]{:S(2)}, u32[]{:S(2)}) %collective-permute-start.46) | collective-permute-done | bytes 65568 | tf_op jit(solution)/shard_map/ppermute | solution.py:216
  78.1 2.2 %collective-permute-done.44 = f32[128,128]{1,0:T(8,128)S(1)} collective-permute-done((f32[128,128]{1,0:T(8,128)S(1)}, f32[128,128]{1,0:T(8,128)S(1)}, u32[]{:S(2)}, u32[]{:S(2)}) %collective-permute-start.44) | collective-permute-done | bytes 65568 | tf_op jit(solution)/shard_map/ppermute | solution.py:216
  (121 shorter events, 31.4 us)
Async XLA Ops:
  5.2 5.6 %collective-permute-start.5 = (f32[1,128,512]{2,1,0:T(8,128)S(1)}, f32[1,128,512]{2,1,0:T(8,128)S(1)}, u32[]{:S(2)}, u32[]{:S(2)}) collective-permute-start(f32[1,128,512]{2,1,0:T(8,128)S(1)} %copy-done.5), channel_id=1, source_target_pairs={{0,1},{1,0},{2,3},{3,2},{4,5},{5,4},{6,7},{7,6},{8,9},{9,8},{10,11... | collective-permute-start | bytes 786440 | tf_op jit(solution)/shard_map/ppermute | solution.py:216
  8.7 8.7 %collective-permute-start.10 = (f32[1,2,128,512]{3,2,1,0:T(8,128)S(1)}, f32[1,2,128,512]{3,2,1,0:T(8,128)S(1)}, u32[]{:S(2)}, u32[]{:S(2)}) collective-permute-start(f32[1,2,128,512]{3,2,1,0:T(8,128)S(1)} %copy-done.1), channel_id=1, source_target_pairs={{0,1},{1,0},{2,3},{3,2},{4,5},{5,4},{6,7},{7,6},{8,9},{9,8},{10,11... | collective-permute-start | bytes 1572872 | tf_op jit(solution)/shard_map/ppermute | solution.py:216
  10.5 6.9 %collective-permute-start.11 = (f32[1,2,128,512]{3,2,1,0:T(8,128)S(1)}, f32[1,2,128,512]{3,2,1,0:T(8,128)S(1)}, u32[]{:S(2)}, u32[]{:S(2)}) collective-permute-start(f32[1,2,128,512]{3,2,1,0:T(8,128)S(1)} %copy-done), channel_id=1, source_target_pairs={{0,1},{1,0},{2,3},{3,2},{4,5},{5,4},{6,7},{7,6},{8,9},{9,8},{10,11... | collective-permute-start | bytes 1572872 | tf_op jit(solution)/shard_map/ppermute | solution.py:216
  15.5 7.0 %collective-permute-start.7 = (f32[128,128]{1,0:T(8,128)S(1)}, f32[128,128]{1,0:T(8,128)S(1)}, u32[]{:S(2)}, u32[]{:S(2)}) collective-permute-start(f32[128,128]{1,0:T(8,128)S(1)} %collective-permute-done.6.next_near), channel_id=1, source_target_pairs={{0,2},{1,3},{2,0},{3,1},{4,6},{5,7},{6,4},{7,5},{8,10},{9,11},{10,... | collective-permute-start | bytes 196616 | tf_op jit(solution)/shard_map/ppermute | solution.py:216
  18.4 8.1 %collective-permute-start.14 = (f32[128,128]{1,0:T(8,128)S(1)}, f32[128,128]{1,0:T(8,128)S(1)}, u32[]{:S(2)}, u32[]{:S(2)}) collective-permute-start(f32[128,128]{1,0:T(8,128)S(1)} %get-tuple-element.18), channel_id=1, source_target_pairs={{0,1},{1,0},{2,3},{3,2},{4,8},{5,9},{6,10},{7,11},{8,4},{9,5},{10,... | collective-permute-start | bytes 196616 | tf_op jit(solution)/shard_map/ppermute | solution.py:216
  19.7 7.1 %collective-permute-start.15 = (f32[128,128]{1,0:T(8,128)S(1)}, f32[128,128]{1,0:T(8,128)S(1)}, u32[]{:S(2)}, u32[]{:S(2)}) collective-permute-start(f32[128,128]{1,0:T(8,128)S(1)} %get-tuple-element.17), channel_id=1, source_target_pairs={{0,1},{1,0},{2,3},{3,2},{4,5},{5,4},{6,7},{7,6},{8,12},{9,13},{10,... | collective-permute-start | bytes 196616 | tf_op jit(solution)/shard_map/ppermute | solution.py:216
  25.6 5.7 %collective-permute-start.18 = (f32[128,128]{1,0:T(8,128)S(1)}, f32[128,128]{1,0:T(8,128)S(1)}, u32[]{:S(2)}, u32[]{:S(2)}) collective-permute-start(f32[128,128]{1,0:T(8,128)S(1)} %get-tuple-element.17), channel_id=1, source_target_pairs={{0,1},{1,0},{2,3},{3,2},{4,5},{5,4},{6,7},{7,6},{8,14},{9,15},{10,... | collective-permute-start | bytes 196616 | tf_op jit(solution)/shard_map/ppermute | solution.py:216
  26.5 9.4 %collective-permute-start.12 = (f32[128,128]{1,0:T(8,128)S(1)}, f32[128,128]{1,0:T(8,128)S(1)}, u32[]{:S(2)}, u32[]{:S(2)}) collective-permute-start(f32[128,128]{1,0:T(8,128)S(1)} %get-tuple-element.17), channel_id=1, source_target_pairs={{0,4},{1,5},{2,6},{3,7},{4,0},{5,1},{6,2},{7,3},{8,9},{9,8},{10,11... | collective-permute-start | bytes 196616 | tf_op jit(solution)/shard_map/ppermute | solution.py:216
  26.8 9.7 %collective-permute-start.13 = (f32[128,128]{1,0:T(8,128)S(1)}, f32[128,128]{1,0:T(8,128)S(1)}, u32[]{:S(2)}, u32[]{:S(2)}) collective-permute-start(f32[128,128]{1,0:T(8,128)S(1)} %get-tuple-element.18), channel_id=1, source_target_pairs={{0,1},{1,0},{2,3},{3,2},{4,5},{5,4},{6,7},{7,6},{8,9},{9,8},{10,11... | collective-permute-start | bytes 196616 | tf_op jit(solution)/shard_map/ppermute | solution.py:216
  37.3 6.7 %collective-permute-start.19 = (f32[128,128]{1,0:T(8,128)S(1)}, f32[128,128]{1,0:T(8,128)S(1)}, u32[]{:S(2)}, u32[]{:S(2)}) collective-permute-start(f32[128,128]{1,0:T(8,128)S(1)} %get-tuple-element.19), channel_id=1, source_target_pairs={{0,8},{1,9},{2,10},{3,11},{4,5},{5,4},{6,7},{7,6},{8,0},{9,1},{10,... | collective-permute-start | bytes 196616 | tf_op jit(solution)/shard_map/ppermute | solution.py:216
  45.8 10.5 %collective-permute-start.31 = (f32[1,2,128,512]{3,2,1,0:T(8,128)S(1)}, f32[1,2,128,512]{3,2,1,0:T(8,128)S(1)}, u32[]{:S(2)}, u32[]{:S(2)}) collective-permute-start(f32[1,2,128,512]{3,2,1,0:T(8,128)S(1)} %copy-done.3), channel_id=1, source_target_pairs={{0,1},{1,0},{2,3},{3,2},{4,5},{5,4},{6,7},{7,6},{8,9},{9,8},{10,11... | collective-permute-start | bytes 1572872 | tf_op jit(solution)/shard_map/ppermute | solution.py:216
  46.4 9.9 %collective-permute-start.32 = (f32[1,2,128,512]{3,2,1,0:T(8,128)S(1)}, f32[1,2,128,512]{3,2,1,0:T(8,128)S(1)}, u32[]{:S(2)}, u32[]{:S(2)}) collective-permute-start(f32[1,2,128,512]{3,2,1,0:T(8,128)S(1)} %copy-done.4), channel_id=1, source_target_pairs={{0,1},{1,0},{2,3},{3,2},{4,5},{5,4},{6,7},{7,6},{8,9},{9,8},{10,11... | collective-permute-start | bytes 1572872 | tf_op jit(solution)/shard_map/ppermute | solution.py:216
  48.5 7.8 %collective-permute-start.29 = (f32[128,128]{1,0:T(8,128)S(1)}, f32[128,128]{1,0:T(8,128)S(1)}, u32[]{:S(2)}, u32[]{:S(2)}) collective-permute-start(f32[128,128]{1,0:T(8,128)S(1)} %shard_map.89.pivot), channel_id=1, source_target_pairs={{0,16},{1,17},{2,18},{3,19},{4,5},{5,4},{6,7},{7,6},{8,9},{9,8},{1... | collective-permute-start | bytes 196616 | tf_op jit(solution)/shard_map/ppermute | solution.py:216
  50.1 6.2 %collective-permute-start.30 = (f32[128,128]{1,0:T(8,128)S(1)}, f32[128,128]{1,0:T(8,128)S(1)}, u32[]{:S(2)}, u32[]{:S(2)}) collective-permute-start(f32[128,128]{1,0:T(8,128)S(1)} %shard_map.89.pivot), channel_id=1, source_target_pairs={{0,18},{1,19},{2,16},{3,17},{4,5},{5,4},{6,7},{7,6},{8,9},{9,8},{1... | collective-permute-start | bytes 196616 | tf_op jit(solution)/shard_map/ppermute | solution.py:216
  50.2 14.4 %collective-permute-start.37 = (f32[128,128]{1,0:T(8,128)S(1)}, f32[128,128]{1,0:T(8,128)S(1)}, u32[]{:S(2)}, u32[]{:S(2)}) collective-permute-start(f32[128,128]{1,0:T(8,128)S(1)} %shard_map.89.pivot), channel_id=1, source_target_pairs={{0,8},{1,9},{2,10},{3,11},{4,5},{5,4},{6,7},{7,6},{8,0},{9,1},{10,... | collective-permute-start | bytes 196616 | tf_op jit(solution)/shard_map/ppermute | solution.py:216
  56.3 8.5 %collective-permute-start.38 = (f32[128,128]{1,0:T(8,128)S(1)}, f32[128,128]{1,0:T(8,128)S(1)}, u32[]{:S(2)}, u32[]{:S(2)}) collective-permute-start(f32[128,128]{1,0:T(8,128)S(1)} %shard_map.89.pivot), channel_id=1, source_target_pairs={{0,10},{1,11},{2,8},{3,9},{4,5},{5,4},{6,7},{7,6},{8,2},{9,3},{10,... | collective-permute-start | bytes 196616 | tf_op jit(solution)/shard_map/ppermute | solution.py:216
  57.0 8.8 %collective-permute-start.41 = (f32[128,128]{1,0:T(8,128)S(1)}, f32[128,128]{1,0:T(8,128)S(1)}, u32[]{:S(2)}, u32[]{:S(2)}) collective-permute-start(f32[128,128]{1,0:T(8,128)S(1)} %broadcast_select_fusion.7), channel_id=1, source_target_pairs={{0,1},{1,0},{2,3},{3,2},{4,5},{5,4},{6,7},{7,6},{8,18},{9,19},{10,... | collective-permute-start | bytes 196616 | tf_op jit(solution)/shard_map/ppermute | solution.py:216
  60.8 6.1 %collective-permute-start.42 = (f32[128,128]{1,0:T(8,128)S(1)}, f32[128,128]{1,0:T(8,128)S(1)}, u32[]{:S(2)}, u32[]{:S(2)}) collective-permute-start(f32[128,128]{1,0:T(8,128)S(1)} %broadcast_select_fusion.7), channel_id=1, source_target_pairs={{0,1},{1,0},{2,3},{3,2},{4,5},{5,4},{6,7},{7,6},{8,9},{9,8},{10,11... | collective-permute-start | bytes 196616 | tf_op jit(solution)/shard_map/ppermute | solution.py:216
  65.9 7.8 %collective-permute-start.36 = (f32[128,128]{1,0:T(8,128)S(1)}, f32[128,128]{1,0:T(8,128)S(1)}, u32[]{:S(2)}, u32[]{:S(2)}) collective-permute-start(f32[128,128]{1,0:T(8,128)S(1)} %broadcast_select_fusion.7), channel_id=1, source_target_pairs={{0,1},{1,0},{2,3},{3,2},{4,5},{5,4},{6,7},{7,6},{8,9},{9,8},{10,11... | collective-permute-start | bytes 196616 | tf_op jit(solution)/shard_map/ppermute | solution.py:216
  66.9 7.0 %collective-permute-start.33 = (f32[128,128]{1,0:T(8,128)S(1)}, f32[128,128]{1,0:T(8,128)S(1)}, u32[]{:S(2)}, u32[]{:S(2)}) collective-permute-start(f32[128,128]{1,0:T(8,128)S(1)} %broadcast_select_fusion.7), channel_id=1, source_target_pairs={{0,4},{1,5},{2,6},{3,7},{4,0},{5,1},{6,2},{7,3},{8,9},{9,8},{10,11... | collective-permute-start | bytes 196616 | tf_op jit(solution)/shard_map/ppermute | solution.py:216
  68.3 6.0 %collective-permute-start.34 = (f32[128,128]{1,0:T(8,128)S(1)}, f32[128,128]{1,0:T(8,128)S(1)}, u32[]{:S(2)}, u32[]{:S(2)}) collective-permute-start(f32[128,128]{1,0:T(8,128)S(1)} %broadcast_select_fusion.7), channel_id=1, source_target_pairs={{0,1},{1,0},{2,3},{3,2},{4,5},{5,4},{6,7},{7,6},{8,9},{9,8},{10,11... | collective-permute-start | bytes 196616 | tf_op jit(solution)/shard_map/ppermute | solution.py:216
  70.2 5.6 %collective-permute-start.45 = (f32[128,128]{1,0:T(8,128)S(1)}, f32[128,128]{1,0:T(8,128)S(1)}, u32[]{:S(2)}, u32[]{:S(2)}) collective-permute-start(f32[128,128]{1,0:T(8,128)S(1)} %broadcast_select_fusion.6), channel_id=1, source_target_pairs={{0,1},{1,0},{2,3},{3,2},{4,10},{5,11},{6,8},{7,9},{8,6},{9,7},{10,... | collective-permute-start | bytes 196616 | tf_op jit(solution)/shard_map/ppermute | solution.py:216
  70.3 7.2 %collective-permute-start.46 = (f32[128,128]{1,0:T(8,128)S(1)}, f32[128,128]{1,0:T(8,128)S(1)}, u32[]{:S(2)}, u32[]{:S(2)}) collective-permute-start(f32[128,128]{1,0:T(8,128)S(1)} %broadcast_select_fusion.6), channel_id=1, source_target_pairs={{0,1},{1,0},{2,3},{3,2},{4,5},{5,4},{6,7},{7,6},{8,14},{9,15},{10,... | collective-permute-start | bytes 196616 | tf_op jit(solution)/shard_map/ppermute | solution.py:216
  73.9 6.4 %collective-permute-start.44 = (f32[128,128]{1,0:T(8,128)S(1)}, f32[128,128]{1,0:T(8,128)S(1)}, u32[]{:S(2)}, u32[]{:S(2)}) collective-permute-start(f32[128,128]{1,0:T(8,128)S(1)} %broadcast_select_fusion.6), channel_id=1, source_target_pairs={{0,1},{1,0},{2,3},{3,2},{4,5},{5,4},{6,7},{7,6},{8,12},{9,13},{10,... | collective-permute-start | bytes 196616 | tf_op jit(solution)/shard_map/ppermute | solution.py:216
  (32 other events, 131.5 us)

commit v4 on v2

v4 whole, which is shorter than its diff:
```python
import functools

import jax
import jax.numpy as jnp
from jax import lax
from jax.experimental import pallas as pl
from jax.experimental.pallas import tpu as pltpu
from jax.sharding import PartitionSpec as P


half_step = 0.5
wide = jnp.float32
short = jnp.bfloat16
Q = 128
LANES = 128


def lanes(values):
    return lax.broadcasted_iota(jnp.int32, values.shape, 1)


def swap_halves(values):
    return pltpu.roll(values, 64, 1)


def join(left, right):
    return jnp.where(lanes(left) < 64, left, right)


def rotate(values):
    even = lanes(values) % 2 == 0
    return jnp.where(even, -pltpu.roll(values, LANES - 1, 1), pltpu.roll(values, 1, 1))


def split(values):
    high = values.astype(short)
    return high, (values - high.astype(wide)).astype(short)


def quarter(number):
    return pl.ds(pl.multiple_of(number * Q, Q), Q)


def spread(store, packed, first):
    high = packed.astype(short).astype(wide)
    low = packed - high
    store[quarter(first), :] = join(high, swap_halves(low)).astype(short)
    store[quarter(first ^ 1), :] = join(swap_halves(high), low).astype(short)


def load_vector(store, near, far):
    c = lax.axis_index("col")
    spread(store, near, c)
    spread(store, far, c ^ 2)


def keep(wanted, values):
    return jnp.where(wanted, values[...], 0.0)


def rows_product(block, store):
    high, low = split(block)
    vector = store[...]
    return jnp.dot(high, vector, preferred_element_type=wide) + jnp.dot(
        low, vector, preferred_element_type=wide
    )


def fold(values):
    return values + swap_halves(values)


def real_product(own, mate, store):
    return join(fold(rows_product(own, store)), fold(rows_product(mate, store)))


def complex_half(block, store):
    both = rows_product(block.reshape(2 * Q, block.shape[-1]), store)
    return fold(both[:Q] + rotate(both[Q:]))


def complex_product(own, mate, store):
    return join(complex_half(own, store), complex_half(mate, store))


def this_core(left, right):
    first = lax.axis_index("col") % 2 == 0
    return jnp.where(first, join(left, swap_halves(right)), join(swap_halves(left), right))


def side_kernel(side):
    side[...] = jnp.zeros_like(side) + lax.axis_index("col")


def regroup_kernel(mine, other, out):
    rows = join(mine[...], other[...])
    out[...] = jnp.where(lax.axis_index("col") % 2 == 0, rows, swap_halves(rows))


def stack_kernel(*refs):
    *sources, _, out = refs
    place = 0
    for source in sources:
        depth = source.shape[0]
        out[place : place + depth] = source[...]
        place += depth


def reduce_kernel(spacing, count, base, *refs):
    out = refs[-1]
    less, *more = refs[:count]
    s = lax.axis_index("slab")
    kept = s % (4 * spacing) == 0
    values = base[...] - keep(kept, less)
    for late in more:
        values = values - keep(kept & (s > 0), late)
    out[...] = values


def open_kernel(mine, other, side, own, mate, psi, near, far, store):
    c = lax.axis_index("col")
    packed = this_core(mine[0], other[0])
    psi[...] = packed
    turned = packed.T
    total = None
    for rows, block in ((turned[:64], own[0]), (turned[64:], mate[0])):
        high, low = split(rows)
        pair = jnp.concatenate([high, low], axis=0)
        block_high, block_low = split(block)
        part = jnp.dot(pair, block_high, preferred_element_type=wide) + jnp.dot(
            pair, block_low, preferred_element_type=wide
        )
        part = part[:64] + part[64:]
        total = part if total is None else total + part
    store[...] = total
    for out, first in ((far, c ^ 2), (near, c)):
        pair = jnp.concatenate(
            [store[:, quarter(first)], store[:, quarter(first ^ 1)]], axis=0
        )
        out[...] = half_step * rotate(pair.T)


def ham_kernel(slabs, near, far, next_near, next_far, own_e, mate_e, own_t, mate_t, *refs):
    out, here, there = refs[-3:]
    linked = lax.axis_index("slab") < slabs - 1
    load_vector(here, near[...], far[...])
    load_vector(there, keep(linked, next_near), keep(linked, next_far))
    ham = real_product(own_e[0], mate_e[0], here) + real_product(own_t[0], mate_t[0], there)
    out[...] = near[...] - half_step * rotate(ham)


def level_kernel(spacing, near, far, own, mate, *refs):
    beneath, above, store = refs[-3:]

    @pl.when(lax.axis_index("slab") % (2 * spacing) == spacing)
    def _():
        load_vector(store, near[...], far[...])
        above[...] = complex_product(own[2:4], mate[2:4], store)
        beneath[...] = complex_product(own[0:2], mate[0:2], store)


def top_kernel(spacing, near, far, own, mate, *refs):
    beneath, store = refs[-2:]

    @pl.when(lax.axis_index("slab") % (2 * spacing) == spacing)
    def _():
        load_vector(store, near[...], far[...])
        beneath[...] = complex_product(own[0:2], mate[0:2], store)


def pivot_kernel(spacing, near, far, own, mate, before, out, store):
    active = lax.axis_index("slab") % (2 * spacing) == spacing

    @pl.when(active)
    def _():
        load_vector(store, near[...], far[...])
        out[...] = complex_product(own[0:2], mate[0:2], store)

    @pl.when(jnp.logical_not(active))
    def _():
        out[...] = before[...]


def root_kernel(near, far, less_near, less_far, own, mate, before, out, store):
    root = lax.axis_index("slab") == 0

    @pl.when(root)
    def _():
        load_vector(store, near[...] - less_near[...], far[...] - less_far[...])
        out[...] = complex_product(own[0:2], mate[0:2], store)

    @pl.when(jnp.logical_not(root))
    def _():
        out[...] = before[...]


def settle_kernel(slabs, spacing, kind, part, other, *refs):
    *vectors, own, mate, out, store = refs
    s = lax.axis_index("slab")
    active = s % (2 * spacing) == spacing
    first = s % (4 * spacing) == spacing
    if kind == "late":
        below = jnp.logical_not(first)
        take = active
    elif kind == "early":
        below = first
        take = active & (s + spacing < slabs)
    else:
        below = s >= 0
        take = active

    def settle(vector, place):
        load_vector(store, vector[0][...], vector[1][...])
        blocks = slice(place, place + 2)
        out[...] = part[...] - complex_product(own[blocks], mate[blocks], store)

    @pl.when(take & below)
    def _():
        settle(vectors[:2], 2)

    if len(vectors) == 4:

        @pl.when(take & jnp.logical_not(below))
        def _():
            settle(vectors[2:], 4)

    @pl.when(jnp.logical_not(take))
    def _():
        out[...] = other[...]


def call(
    kernel,
    *operands,
    outs=1,
    scratch=(),
    unused=(),
    shape=jax.ShapeDtypeStruct((Q, LANES), wide),
    flops=10**9,
):
    vmem = pl.BlockSpec(memory_space=pltpu.VMEM)
    return pl.pallas_call(
        kernel,
        out_shape=shape if outs == 1 else (shape,) * outs,
        in_specs=[vmem] * len(operands) + [pl.BlockSpec(memory_space=pl.ANY)] * len(unused),
        out_specs=vmem if outs == 1 else (vmem,) * outs,
        scratch_shapes=list(scratch),
        cost_estimate=pl.CostEstimate(flops=flops, bytes_accessed=1, transcendentals=0),
        compiler_params=pltpu.CompilerParams(vmem_limit_bytes=16 * 2**20),
    )(*operands, *unused)


def completed(route, count, cols):
    target = dict(route)
    taken = set(target.values())
    for a in [a for a in range(count) if a not in target and a not in taken]:
        target[a] = a ^ 1
        taken.add(a ^ 1)
    for a in range(count):
        if a not in target:
            target[a] = next(b for b in range(count) if b not in taken and b % cols == a % cols)
            taken.add(target[a])
    if sorted(target.values()) != list(range(count)):
        raise ValueError("no permutation")
    return sorted(target.items())


def per_device(slabs, cols, waves, energy, tunnel, pivots, below, above, back_lower, back_upper):
    everyone = range(cols)
    width = energy.shape[2]
    store = pltpu.VMEM((width, LANES), short)
    levels = slabs.bit_length() - 1
    every = range(slabs)
    s = lax.axis_index("slab")

    def send(values, moves, flip=0):
        route = []
        for c in everyone:
            for a, b, *h in moves:
                route.append((a * cols + c, b * cols + (c ^ flip)))
                for h in h:
                    route.append((b * cols + (c ^ flip), h * cols + c))
                    route.append((h * cols + c, a * cols + c))
        return lax.ppermute(values, ("slab", "col"), completed(route, slabs * cols, cols))

    def both(values, near_moves, far_moves):
        return send(values, near_moves), send(values, far_moves, 2)

    def swap(values):
        return send(values, [(a, a) for a in every], 1)

    def exchange(values, chosen=every):
        return send(values, [(a, a) for a in chosen], 2)

    def kernel(body, *arguments):
        return functools.partial(body, *arguments)

    def stack(*arrays, after):
        depth = sum(v.shape[0] for v in arrays)
        shape = jax.ShapeDtypeStruct((depth, Q, width), wide)
        return call(stack_kernel, *arrays, unused=(after,), shape=shape, flops=1)

    mate_waves = swap(waves)
    t_pair = tunnel, swap(tunnel)
    e_pair = energy, swap(energy)
    side = call(side_kernel, shape=jax.ShapeDtypeStruct((8, LANES), jnp.int32))
    psi, up_near, up_far = call(
        open_kernel, waves, mate_waves, side, *t_pair, outs=3, scratch=[pltpu.VMEM((64, width), wide)]
    )
    up = up_near + exchange(up_far)
    prev = send(up, [(a, a + 1) for a in every[:-1]])
    down = [(a + 1, a) for a in every[:-1]]
    front = stack(below[0], above[0], after=up)
    front = front, swap(front)
    rest = call(
        kernel(ham_kernel, slabs),
        psi,
        exchange(psi),
        *both(psi, down, down),
        *e_pair,
        *t_pair,
        scratch=[store, store],
        unused=(up,),
    )
    base = near = rest - jnp.where(s > 0, prev, 0.0)
    back = stack(pivots[0], back_lower[0], back_upper[0], after=near)
    back = back, swap(back)
    base_far = far = exchange(near)

    pivot = base
    late = None
    for level in range(levels):
        d = 2**level
        active = [a for a in every if a % (2 * d) == d]
        if level == levels - 1:
            beneath = call(
                kernel(top_kernel, d), near, far, *front, scratch=[store], unused=late
            )
            less = both(beneath, [(d, 0, d + 1)], [(d, 0, d + 3)])
            base = call(kernel(reduce_kernel, d // 2, len(late)), base, *late, unused=(beneath,))
            base_far = exchange(base)
            pivot = call(kernel(pivot_kernel, d), near, far, *back, pivot, scratch=[store])
            pivot = call(root_kernel, base, base_far, *less, *back, pivot, scratch=[store])
            break
        beneath, over = call(
            kernel(level_kernel, d),
            near,
            far,
            *front,
            outs=2,
            scratch=[store],
            unused=(back[1],) if level == 0 else late,
        )
        urgent = [b for b in every if b % (4 * d) == 2 * d]
        patient = [b for b in every if b % (4 * d) == 0]
        if level == 0:
            more = send(over, [(b - 1, b, b - 2) for b in urgent])
            less = send(beneath, [(b + 1, b, b - 2) for b in urgent])
            late_less = send(beneath, [(b + 1, b, b + 3) for b in patient])
            late_more = send(over, [(b - 1, b, b + 1) for b in patient if b > 0])
        else:
            more = both(
                over, [(b - d, b, b - 1) for b in urgent], [(b - d, b, b - 3) for b in urgent]
            )
            less = both(
                beneath, [(b + d, b, b + 1) for b in urgent], [(b + d, b, b + 3) for b in urgent]
            )
            late_less = send(beneath, [(b + d, b, b + d + 1) for b in patient])
            late_more = None
            if len(patient) > 1:
                late_more = send(over, [(b - d, b, b - d + 1) for b in patient if b > 0])
        pivot = call(kernel(pivot_kernel, d), near, far, *back, pivot, scratch=[store])
        if level == 0:
            near = base - more - less
            far = exchange(near)
        else:
            base = call(kernel(reduce_kernel, d // 2, len(late)), base, *late, unused=(beneath,))
            base_far = exchange(base)
            near = base - more[0] - less[0]
            far = base_far - more[1] - less[1]
        late = (late_less,) if late_more is None else (late_less, late_more)

    solved = rest = pivot
    for level in reversed(range(levels)):
        d = 2**level
        if level == levels - 1:
            vectors = both(solved, [(0, d, 1)], [(0, d, 3)])
            kind = "only"
        else:
            sources = [a for a in every if a % (4 * d) == 2 * d]
            kind = "late"
            if d > 1:
                up_near = send(solved, [(a, a + d, a + 3) for a in sources])
                down_near = send(solved, [(a, a - d, a - 1) for a in sources])
                up_far = send(solved, [(a, a + d, a + 1) for a in sources], 2)
                down_far = send(solved, [(a, a - d, a - 3) for a in sources], 2)
            else:
                up_near = send(solved, [(a, a + 1, a - 2) for a in sources])
                down_near = send(solved, [(a, a - 1, a + 1) for a in sources])
                down_far = send(solved, [(a, a - 1, a - 2) for a in sources], 2)
                up_far = exchange(up_near, [a + 1 for a in sources])
            vectors = up_near, up_far, down_near, down_far
        if level > 0:
            half = d // 2
            sources = [a for a in every if a % (4 * half) == 0]
            if half > 1:
                early = both(
                    solved,
                    [(a, a + half, a + 1) for a in sources],
                    [(a, a + half, a + 3) for a in sources],
                )
                if len(sources) > 1:
                    early += both(
                        solved,
                        [(a, a - half, a - 1) for a in sources if a > 0],
                        [(a, a - half, a - 3) for a in sources if a > 0],
                    )
            else:
                early = both(
                    solved,
                    [(a, a + 1, a + 3) for a in sources],
                    [(a, a + 1, a + 3) for a in sources],
                ) + both(
                    solved,
                    [(a, a - 1, a + 1) for a in sources if a > 0],
                    [(a, a - 1, a + 1) for a in sources if a > 0],
                )
        solved = call(
            kernel(settle_kernel, slabs, d, kind),
            rest,
            solved,
            *vectors,
            *back,
            scratch=[store],
        )
        if level > 0:
            rest = call(
                kernel(settle_kernel, slabs, half, "early"),
                pivot,
                pivot,
                *early,
                *back,
                scratch=[store],
            )
    out = call(regroup_kernel, solved, swap(solved))
    return out[None]


def solution(mesh):
    slabs, cols = mesh.shape["slab"], mesh.shape["col"]
    vector = P("slab", "col", None)
    block = P("slab", None, "col", None)
    return jax.shard_map(
        functools.partial(per_device, slabs, cols),
        mesh=mesh,
        in_specs=(vector,) * 3 + (block,) * 5,
        out_specs=vector,
        check_vma=False,
    )
```

time: 99.3 us -> 77.5 us (0.78)
  waiting for transfers between devices: 26.8 us -> 18.1 us
  starting transfers between devices: 59.4 us -> 52.7 us
  local copies, waits for them, and re-layouts: 3.71 us -> 0.43 us
  Pallas kernels: 7.94 us -> 5.33 us
    ppermute x33 -> x42, waiting for transfers between devices: 26.8 us -> 18.1 us  [send(): lax.ppermute(values, ('slab', 'col'), completed(route, slabs * cols, cols))]
    ppermute x33 -> x42, starting transfers between devices: 59.4 us -> 52.7 us  [send(): lax.ppermute(values, ('slab', 'col'), completed(route, slabs * cols, cols))]
    unnamed x18 -> x16, local copies, waits for them, and re-layouts: 3.71 us -> 0.43 us
    pallas_call x14 -> x20, Pallas kernels: 7.94 us -> 5.33 us  [call(): pl.pallas_call(kernel, out_shape=shape if outs == 1 else (shape,) * outs,...]
  transfers between devices with their start and end apart: 33 -> 42, of which waited for: 22 -> 14; matrix products, arithmetic and copies ran while one was open for 0% -> 0% of each run, Pallas kernels for 5% -> 4%
where the time goes in v4:
time: 77.5 us; the launch traced here: 76.8 us
  starting transfers between devices  52.7 us (68%)
  waiting for transfers between devices  18.1 us (23%)
  Pallas kernels  5.33 us (7%)
    ppermute x42, starting transfers between devices, send(): lax.ppermute(values, ('slab', 'col'), completed(route, slabs * cols, cols))  52.7 us
    ppermute x42, waiting for transfers between devices, send(): lax.ppermute(values, ('slab', 'col'), completed(route, slabs * cols, cols))  18.1 us
    pallas_call x20, Pallas kernels, call(): pl.pallas_call(kernel, out_shape=shape if outs == 1 else (shape,) * outs,...  5.33 us
  transfers between devices with their start and end apart: 42, of which 14 were waited for; matrix products, arithmetic and copies ran while one was open for 0% of the time, Pallas kernels for 4%

profile of v4, /device:TPU:13, one launch (start us, length us, event | category | flops | bytes accessed | tf_op | source)
XLA Modules:
  0.0 76.8 jit_solution(3778862232202057128)
XLA Ops:
  1.2 1.3 %collective-permute-done.other = f32[1,128,128]{2,1,0:T(8,128)S(1)} collective-permute-done((f32[1,128,128]{2,1,0:T(8,128)}, f32[1,128,128]{2,1,0:T(8,128)S(1)}, u32[]{:S(2)}, u32[]{:S(2)}) %collective-permute-start) | collective-permute-done | bytes 65568 | tf_op jit(solution)/shard_map/ppermute | solution.py:284
  3.2 1.3 %collective-permute-start.6 = (f32[128,128]{1,0:T(8,128)S(1)}, f32[128,128]{1,0:T(8,128)S(1)}, u32[]{:S(2)}, u32[]{:S(2)}) collective-permute-start(f32[128,128]{1,0:T(8,128)S(1)} %get-tuple-element.14), channel_id=1, source_target_pairs={{0,2},{1,3},{2,0},{3,1},{4,6},{5,7},{6,4},{7,5},{8,10},{9,11},{10,... | collective-permute-start | bytes 196616 | tf_op jit(solution)/shard_map/ppermute | solution.py:284
  7.1 1.3 %collective-permute-start.7 = (f32[128,128]{1,0:T(8,128)S(1)}, f32[128,128]{1,0:T(8,128)S(1)}, u32[]{:S(2)}, u32[]{:S(2)}) collective-permute-start(f32[128,128]{1,0:T(8,128)S(1)} %add.3.refs_0_.refs_2_), channel_id=1, source_target_pairs={{0,4},{1,5},{2,6},{3,7},{4,8},{5,9},{6,10},{7,11},{8,12},{9,13},{1... | collective-permute-start | bytes 196616 | tf_op jit(solution)/shard_map/ppermute | solution.py:284
  8.4 1.5 %collective-permute-done.4.next_far = f32[128,128]{1,0:T(8,128)S(1)} collective-permute-done((f32[128,128]{1,0:T(8,128)S(1)}, f32[128,128]{1,0:T(8,128)S(1)}, u32[]{:S(2)}, u32[]{:S(2)}) %collective-permute-start.4) | collective-permute-done | bytes 65568 | tf_op jit(solution)/shard_map/ppermute | solution.py:284
  10.6 2.2 %collective-permute-done.7 = f32[128,128]{1,0:T(8,128)S(1)} collective-permute-done((f32[128,128]{1,0:T(8,128)S(1)}, f32[128,128]{1,0:T(8,128)S(1)}, u32[]{:S(2)}, u32[]{:S(2)}) %collective-permute-start.7) | collective-permute-done | bytes 65568 | tf_op jit(solution)/shard_map/ppermute | solution.py:284
  15.5 3.0 %collective-permute-done.8.far = f32[128,128]{1,0:T(8,128)S(1)} collective-permute-done((f32[128,128]{1,0:T(8,128)S(1)}, f32[128,128]{1,0:T(8,128)S(1)}, u32[]{:S(2)}, u32[]{:S(2)}) %collective-permute-start.8) | collective-permute-done | bytes 65568 | tf_op jit(solution)/shard_map/ppermute | solution.py:284
  21.0 4.5 %collective-permute-start.11 = (f32[128,128]{1,0:T(8,128)S(1)}, f32[128,128]{1,0:T(8,128)S(1)}, u32[]{:S(2)}, u32[]{:S(2)}) collective-permute-start(f32[128,128]{1,0:T(8,128)S(1)} %get-tuple-element.15), channel_id=1, source_target_pairs={{0,12},{1,13},{2,14},{3,15},{4,0},{5,1},{6,2},{7,3},{8,9},{9,8},{1... | collective-permute-start | bytes 196616 | tf_op jit(solution)/shard_map/ppermute | solution.py:284
  27.0 1.6 %collective-permute-done.12.refs_1_ = f32[128,128]{1,0:T(8,128)S(1)} collective-permute-done((f32[128,128]{1,0:T(8,128)S(1)}, f32[128,128]{1,0:T(8,128)S(1)}, u32[]{:S(2)}, u32[]{:S(2)}) %collective-permute-start.12) | collective-permute-done | bytes 65568 | tf_op jit(solution)/shard_map/ppermute | solution.py:284
  28.8 3.2 %collective-permute-start.20 = (f32[128,128]{1,0:T(8,128)S(1)}, f32[128,128]{1,0:T(8,128)S(1)}, u32[]{:S(2)}, u32[]{:S(2)}) collective-permute-start(f32[128,128]{1,0:T(8,128)S(1)} %get-tuple-element.18), channel_id=1, source_target_pairs={{0,1},{1,0},{2,3},{3,2},{4,8},{5,9},{6,10},{7,11},{8,18},{9,19},{1... | collective-permute-start | bytes 196616 | tf_op jit(solution)/shard_map/ppermute | solution.py:284
  32.5 3.7 %collective-permute-start.21 = (f32[128,128]{1,0:T(8,128)S(1)}, f32[128,128]{1,0:T(8,128)S(1)}, u32[]{:S(2)}, u32[]{:S(2)}) collective-permute-start(f32[128,128]{1,0:T(8,128)S(1)} %get-tuple-element.17.refs_2_), channel_id=1, source_target_pairs={{0,1},{1,0},{2,3},{3,2},{4,5},{5,4},{6,7},{7,6},{8,9},{9,8},{10,11... | collective-permute-start | bytes 196616 | tf_op jit(solution)/shard_map/ppermute | solution.py:284
  37.5 2.0 %collective-permute-done.19 = f32[128,128]{1,0:T(8,128)S(1)} collective-permute-done((f32[128,128]{1,0:T(8,128)S(1)}, f32[128,128]{1,0:T(8,128)S(1)}, u32[]{:S(2)}, u32[]{:S(2)}) %collective-permute-start.19) | collective-permute-done | bytes 65568 | tf_op jit(solution)/shard_map/ppermute | solution.py:284
  40.2 3.4 %collective-permute-start.24 = (f32[128,128]{1,0:T(8,128)S(1)}, f32[128,128]{1,0:T(8,128)S(1)}, u32[]{:S(2)}, u32[]{:S(2)}) collective-permute-start(f32[128,128]{1,0:T(8,128)S(1)} %shard_map.90.refs_1_), channel_id=1, source_target_pairs={{0,30},{1,31},{2,28},{3,29},{4,5},{5,4},{6,7},{7,6},{8,9},{9,8},{1... | collective-permute-start | bytes 196616 | tf_op jit(solution)/shard_map/ppermute | solution.py:284
  44.4 2.5 %collective-permute-done.22.far = f32[128,128]{1,0:T(8,128)S(1)} collective-permute-done((f32[128,128]{1,0:T(8,128)S(1)}, f32[128,128]{1,0:T(8,128)S(1)}, u32[]{:S(2)}, u32[]{:S(2)}) %collective-permute-start.22) | collective-permute-done | bytes 65568 | tf_op jit(solution)/shard_map/ppermute | solution.py:284
  46.9 2.5 %collective-permute-start.26 = (f32[128,128]{1,0:T(8,128)S(1)}, f32[128,128]{1,0:T(8,128)S(1)}, u32[]{:S(2)}, u32[]{:S(2)}) collective-permute-start(f32[128,128]{1,0:T(8,128)S(1)} %shard_map.95.part.other), channel_id=1, source_target_pairs={{0,18},{1,19},{2,16},{3,17},{4,5},{5,4},{6,7},{7,6},{8,9},{9,8},{1... | collective-permute-start | bytes 196616 | tf_op jit(solution)/shard_map/ppermute | solution.py:284
  49.4 2.2 %collective-permute-start.25 = (f32[128,128]{1,0:T(8,128)S(1)}, f32[128,128]{1,0:T(8,128)S(1)}, u32[]{:S(2)}, u32[]{:S(2)}) collective-permute-start(f32[128,128]{1,0:T(8,128)S(1)} %shard_map.95.part.other), channel_id=1, source_target_pairs={{0,16},{1,17},{2,18},{3,19},{4,0},{5,1},{6,2},{7,3},{8,9},{9,8},{1... | collective-permute-start | bytes 196616 | tf_op jit(solution)/shard_map/ppermute | solution.py:284
  51.6 1.6 %collective-permute-start.31 = (f32[128,128]{1,0:T(8,128)S(1)}, f32[128,128]{1,0:T(8,128)S(1)}, u32[]{:S(2)}, u32[]{:S(2)}) collective-permute-start(f32[128,128]{1,0:T(8,128)S(1)} %shard_map.95.part.other), channel_id=1, source_target_pairs={{0,8},{1,9},{2,10},{3,11},{4,0},{5,1},{6,2},{7,3},{8,4},{9,5},{10,... | collective-permute-start | bytes 196616 | tf_op jit(solution)/shard_map/ppermute | solution.py:284
  53.3 1.5 %collective-permute-start.36 = (f32[128,128]{1,0:T(8,128)S(1)}, f32[128,128]{1,0:T(8,128)S(1)}, u32[]{:S(2)}, u32[]{:S(2)}) collective-permute-start(f32[128,128]{1,0:T(8,128)S(1)} %shard_map.96.other), channel_id=1, source_target_pairs={{0,1},{1,0},{2,3},{3,2},{4,16},{5,17},{6,18},{7,19},{8,6},{9,7},{1... | collective-permute-start | bytes 196616 | tf_op jit(solution)/shard_map/ppermute | solution.py:284
  55.9 2.3 %collective-permute-start.34 = (f32[128,128]{1,0:T(8,128)S(1)}, f32[128,128]{1,0:T(8,128)S(1)}, u32[]{:S(2)}, u32[]{:S(2)}) collective-permute-start(f32[128,128]{1,0:T(8,128)S(1)} %shard_map.96.other), channel_id=1, source_target_pairs={{0,1},{1,0},{2,3},{3,2},{4,5},{5,4},{6,7},{7,6},{8,9},{9,8},{10,11... | collective-permute-start | bytes 196616 | tf_op jit(solution)/shard_map/ppermute | solution.py:284
  58.3 3.4 %collective-permute-start.30 = (f32[128,128]{1,0:T(8,128)S(1)}, f32[128,128]{1,0:T(8,128)S(1)}, u32[]{:S(2)}, u32[]{:S(2)}) collective-permute-start(f32[128,128]{1,0:T(8,128)S(1)} %shard_map.96.other), channel_id=1, source_target_pairs={{0,1},{1,0},{2,3},{3,2},{4,5},{5,4},{6,7},{7,6},{8,9},{9,8},{10,11... | collective-permute-start | bytes 196616 | tf_op jit(solution)/shard_map/ppermute | solution.py:284
  61.8 1.5 %collective-permute-start.28 = (f32[128,128]{1,0:T(8,128)S(1)}, f32[128,128]{1,0:T(8,128)S(1)}, u32[]{:S(2)}, u32[]{:S(2)}) collective-permute-start(f32[128,128]{1,0:T(8,128)S(1)} %shard_map.96.other), channel_id=1, source_target_pairs={{0,6},{1,7},{2,4},{3,5},{4,14},{5,15},{6,12},{7,13},{8,9},{9,8},{1... | collective-permute-start | bytes 196616 | tf_op jit(solution)/shard_map/ppermute | solution.py:284
  63.3 1.4 %collective-permute-start.27 = (f32[128,128]{1,0:T(8,128)S(1)}, f32[128,128]{1,0:T(8,128)S(1)}, u32[]{:S(2)}, u32[]{:S(2)}) collective-permute-start(f32[128,128]{1,0:T(8,128)S(1)} %shard_map.96.other), channel_id=1, source_target_pairs={{0,4},{1,5},{2,6},{3,7},{4,12},{5,13},{6,14},{7,15},{8,9},{9,8},{1... | collective-permute-start | bytes 196616 | tf_op jit(solution)/shard_map/ppermute | solution.py:284
  66.2 1.5 %collective-permute-start.38 = (f32[128,128]{1,0:T(8,128)S(1)}, f32[128,128]{1,0:T(8,128)S(1)}, u32[]{:S(2)}, u32[]{:S(2)}) collective-permute-start(f32[128,128]{1,0:T(8,128)S(1)} %collective-permute-done.37.refs_0_), channel_id=1, source_target_pairs={{0,1},{1,0},{2,3},{3,2},{4,5},{5,4},{6,7},{7,6},{8,9},{9,8},{10,11... | collective-permute-start | bytes 196616 | tf_op jit(solution)/shard_map/ppermute | solution.py:284
  68.4 1.3 %collective-permute-done.39.refs_2_ = f32[128,128]{1,0:T(8,128)S(1)} collective-permute-done((f32[128,128]{1,0:T(8,128)S(1)}, f32[128,128]{1,0:T(8,128)S(1)}, u32[]{:S(2)}, u32[]{:S(2)}) %collective-permute-start.39) | collective-permute-done | bytes 65568 | tf_op jit(solution)/shard_map/ppermute | solution.py:284
  70.4 4.9 %collective-permute-start.41 = (f32[128,128]{1,0:T(8,128)S(1)}, f32[128,128]{1,0:T(8,128)S(1)}, u32[]{:S(2)}, u32[]{:S(2)}) collective-permute-start(f32[128,128]{1,0:T(8,128)S(1)} %shard_map.100.mine), channel_id=1, source_target_pairs={{0,1},{1,0},{2,3},{3,2},{4,5},{5,4},{6,7},{7,6},{8,9},{9,8},{10,11... | collective-permute-start | bytes 196616 | tf_op jit(solution)/shard_map/ppermute | solution.py:284
  (101 shorter events, 21.1 us)
Async XLA Ops:
  0.7 7.7 %collective-permute-start.5 = (f32[1,128,512]{2,1,0:T(8,128)}, f32[1,128,512]{2,1,0:T(8,128)S(1)}, u32[]{:S(2)}, u32[]{:S(2)}) collective-permute-start(f32[1,128,512]{2,1,0:T(8,128)} %own_e.1), channel_id=1, source_target_pairs={{0,1},{1,0},{2,3},{3,2},{4,5},{5,4},{6,7},{7,6},{8,9},{9,8},{10,11... | collective-permute-start | bytes 786440 | tf_op jit(solution)/shard_map/ppermute | solution.py:284
  4.5 5.4 %collective-permute-start.4 = (f32[128,128]{1,0:T(8,128)S(1)}, f32[128,128]{1,0:T(8,128)S(1)}, u32[]{:S(2)}, u32[]{:S(2)}) collective-permute-start(f32[128,128]{1,0:T(8,128)S(1)} %get-tuple-element.12.near), channel_id=1, source_target_pairs={{0,28},{1,29},{2,30},{3,31},{4,2},{5,3},{6,0},{7,1},{8,6},{9,7},{1... | collective-permute-start | bytes 196616 | tf_op jit(solution)/shard_map/ppermute | solution.py:284
  4.7 5.2 %collective-permute-start.3 = (f32[128,128]{1,0:T(8,128)S(1)}, f32[128,128]{1,0:T(8,128)S(1)}, u32[]{:S(2)}, u32[]{:S(2)}) collective-permute-start(f32[128,128]{1,0:T(8,128)S(1)} %get-tuple-element.12.near), channel_id=1, source_target_pairs={{0,28},{1,29},{2,30},{3,31},{4,0},{5,1},{6,2},{7,3},{8,4},{9,5},{1... | collective-permute-start | bytes 196616 | tf_op jit(solution)/shard_map/ppermute | solution.py:284
  7.1 5.7 %collective-permute-start.7 = (f32[128,128]{1,0:T(8,128)S(1)}, f32[128,128]{1,0:T(8,128)S(1)}, u32[]{:S(2)}, u32[]{:S(2)}) collective-permute-start(f32[128,128]{1,0:T(8,128)S(1)} %add.3.refs_0_.refs_2_), channel_id=1, source_target_pairs={{0,4},{1,5},{2,6},{3,7},{4,8},{5,9},{6,10},{7,11},{8,12},{9,13},{1... | collective-permute-start | bytes 196616 | tf_op jit(solution)/shard_map/ppermute | solution.py:284
  12.9 5.5 %collective-permute-start.10 = (f32[6,128,512]{2,1,0:T(8,128)S(1)}, f32[6,128,512]{2,1,0:T(8,128)S(1)}, u32[]{:S(2)}, u32[]{:S(2)}) collective-permute-start(f32[6,128,512]{2,1,0:T(8,128)S(1)} %shard_map.86.own.refs_2_.refs_4_), channel_id=1, source_target_pairs={{0,1},{1,0},{2,3},{3,2},{4,5},{5,4},{6,7},{7,6},{8,9},{9,8},{10,11... | collective-permute-start | bytes 4718600 | tf_op jit(solution)/shard_map/ppermute | solution.py:284
  14.1 4.4 %collective-permute-start.9 = (f32[4,128,512]{2,1,0:T(8,128)S(1)}, f32[4,128,512]{2,1,0:T(8,128)S(1)}, u32[]{:S(2)}, u32[]{:S(2)}) collective-permute-start(f32[4,128,512]{2,1,0:T(8,128)S(1)} %shard_map.85.own), channel_id=1, source_target_pairs={{0,1},{1,0},{2,3},{3,2},{4,5},{5,4},{6,7},{7,6},{8,9},{9,8},{10,11... | collective-permute-start | bytes 3145736 | tf_op jit(solution)/shard_map/ppermute | solution.py:284
  19.4 6.2 %collective-permute-start.14 = (f32[128,128]{1,0:T(8,128)S(1)}, f32[128,128]{1,0:T(8,128)S(1)}, u32[]{:S(2)}, u32[]{:S(2)}) collective-permute-start(f32[128,128]{1,0:T(8,128)S(1)} %get-tuple-element.15), channel_id=1, source_target_pairs={{0,12},{1,13},{2,14},{3,15},{4,5},{5,4},{6,7},{7,6},{8,0},{9,1},{1... | collective-permute-start | bytes 196616 | tf_op jit(solution)/shard_map/ppermute | solution.py:284
  19.8 5.8 %collective-permute-start.13 = (f32[128,128]{1,0:T(8,128)S(1)}, f32[128,128]{1,0:T(8,128)S(1)}, u32[]{:S(2)}, u32[]{:S(2)}) collective-permute-start(f32[128,128]{1,0:T(8,128)S(1)} %get-tuple-element.16), channel_id=1, source_target_pairs={{0,4},{1,5},{2,6},{3,7},{4,8},{5,9},{6,10},{7,11},{8,0},{9,1},{10,... | collective-permute-start | bytes 196616 | tf_op jit(solution)/shard_map/ppermute | solution.py:284
  21.0 6.0 %collective-permute-start.11 = (f32[128,128]{1,0:T(8,128)S(1)}, f32[128,128]{1,0:T(8,128)S(1)}, u32[]{:S(2)}, u32[]{:S(2)}) collective-permute-start(f32[128,128]{1,0:T(8,128)S(1)} %get-tuple-element.15), channel_id=1, source_target_pairs={{0,12},{1,13},{2,14},{3,15},{4,0},{5,1},{6,2},{7,3},{8,9},{9,8},{1... | collective-permute-start | bytes 196616 | tf_op jit(solution)/shard_map/ppermute | solution.py:284
  28.8 8.7 %collective-permute-start.20 = (f32[128,128]{1,0:T(8,128)S(1)}, f32[128,128]{1,0:T(8,128)S(1)}, u32[]{:S(2)}, u32[]{:S(2)}) collective-permute-start(f32[128,128]{1,0:T(8,128)S(1)} %get-tuple-element.18), channel_id=1, source_target_pairs={{0,1},{1,0},{2,3},{3,2},{4,8},{5,9},{6,10},{7,11},{8,18},{9,19},{1... | collective-permute-start | bytes 196616 | tf_op jit(solution)/shard_map/ppermute | solution.py:284
  32.1 4.2 %collective-permute-start.17 = (f32[128,128]{1,0:T(8,128)S(1)}, f32[128,128]{1,0:T(8,128)S(1)}, u32[]{:S(2)}, u32[]{:S(2)}) collective-permute-start(f32[128,128]{1,0:T(8,128)S(1)} %get-tuple-element.18), channel_id=1, source_target_pairs={{0,1},{1,0},{2,3},{3,2},{4,5},{5,4},{6,7},{7,6},{8,16},{9,17},{10,... | collective-permute-start | bytes 196616 | tf_op jit(solution)/shard_map/ppermute | solution.py:284
  32.5 7.0 %collective-permute-start.21 = (f32[128,128]{1,0:T(8,128)S(1)}, f32[128,128]{1,0:T(8,128)S(1)}, u32[]{:S(2)}, u32[]{:S(2)}) collective-permute-start(f32[128,128]{1,0:T(8,128)S(1)} %get-tuple-element.17.refs_2_), channel_id=1, source_target_pairs={{0,1},{1,0},{2,3},{3,2},{4,5},{5,4},{6,7},{7,6},{8,9},{9,8},{10,11... | collective-permute-start | bytes 196616 | tf_op jit(solution)/shard_map/ppermute | solution.py:284
  40.2 6.7 %collective-permute-start.24 = (f32[128,128]{1,0:T(8,128)S(1)}, f32[128,128]{1,0:T(8,128)S(1)}, u32[]{:S(2)}, u32[]{:S(2)}) collective-permute-start(f32[128,128]{1,0:T(8,128)S(1)} %shard_map.90.refs_1_), channel_id=1, source_target_pairs={{0,30},{1,31},{2,28},{3,29},{4,5},{5,4},{6,7},{7,6},{8,9},{9,8},{1... | collective-permute-start | bytes 196616 | tf_op jit(solution)/shard_map/ppermute | solution.py:284
  46.9 6.3 %collective-permute-start.26 = (f32[128,128]{1,0:T(8,128)S(1)}, f32[128,128]{1,0:T(8,128)S(1)}, u32[]{:S(2)}, u32[]{:S(2)}) collective-permute-start(f32[128,128]{1,0:T(8,128)S(1)} %shard_map.95.part.other), channel_id=1, source_target_pairs={{0,18},{1,19},{2,16},{3,17},{4,5},{5,4},{6,7},{7,6},{8,9},{9,8},{1... | collective-permute-start | bytes 196616 | tf_op jit(solution)/shard_map/ppermute | solution.py:284
  51.6 6.6 %collective-permute-start.32 = (f32[128,128]{1,0:T(8,128)S(1)}, f32[128,128]{1,0:T(8,128)S(1)}, u32[]{:S(2)}, u32[]{:S(2)}) collective-permute-start(f32[128,128]{1,0:T(8,128)S(1)} %shard_map.95.part.other), channel_id=1, source_target_pairs={{0,10},{1,11},{2,8},{3,9},{4,5},{5,4},{6,7},{7,6},{8,14},{9,15},{1... | collective-permute-start | bytes 196616 | tf_op jit(solution)/shard_map/ppermute | solution.py:284
  51.6 6.6 %collective-permute-start.31 = (f32[128,128]{1,0:T(8,128)S(1)}, f32[128,128]{1,0:T(8,128)S(1)}, u32[]{:S(2)}, u32[]{:S(2)}) collective-permute-start(f32[128,128]{1,0:T(8,128)S(1)} %shard_map.95.part.other), channel_id=1, source_target_pairs={{0,8},{1,9},{2,10},{3,11},{4,0},{5,1},{6,2},{7,3},{8,4},{9,5},{10,... | collective-permute-start | bytes 196616 | tf_op jit(solution)/shard_map/ppermute | solution.py:284
  53.3 8.4 %collective-permute-start.36 = (f32[128,128]{1,0:T(8,128)S(1)}, f32[128,128]{1,0:T(8,128)S(1)}, u32[]{:S(2)}, u32[]{:S(2)}) collective-permute-start(f32[128,128]{1,0:T(8,128)S(1)} %shard_map.96.other), channel_id=1, source_target_pairs={{0,1},{1,0},{2,3},{3,2},{4,16},{5,17},{6,18},{7,19},{8,6},{9,7},{1... | collective-permute-start | bytes 196616 | tf_op jit(solution)/shard_map/ppermute | solution.py:284
  54.8 6.9 %collective-permute-start.35 = (f32[128,128]{1,0:T(8,128)S(1)}, f32[128,128]{1,0:T(8,128)S(1)}, u32[]{:S(2)}, u32[]{:S(2)}) collective-permute-start(f32[128,128]{1,0:T(8,128)S(1)} %shard_map.96.other), channel_id=1, source_target_pairs={{0,1},{1,0},{2,3},{3,2},{4,5},{5,4},{6,7},{7,6},{8,12},{9,13},{10,... | collective-permute-start | bytes 196616 | tf_op jit(solution)/shard_map/ppermute | solution.py:284
  55.9 5.8 %collective-permute-start.34 = (f32[128,128]{1,0:T(8,128)S(1)}, f32[128,128]{1,0:T(8,128)S(1)}, u32[]{:S(2)}, u32[]{:S(2)}) collective-permute-start(f32[128,128]{1,0:T(8,128)S(1)} %shard_map.96.other), channel_id=1, source_target_pairs={{0,1},{1,0},{2,3},{3,2},{4,5},{5,4},{6,7},{7,6},{8,9},{9,8},{10,11... | collective-permute-start | bytes 196616 | tf_op jit(solution)/shard_map/ppermute | solution.py:284
  58.3 6.5 %collective-permute-start.30 = (f32[128,128]{1,0:T(8,128)S(1)}, f32[128,128]{1,0:T(8,128)S(1)}, u32[]{:S(2)}, u32[]{:S(2)}) collective-permute-start(f32[128,128]{1,0:T(8,128)S(1)} %shard_map.96.other), channel_id=1, source_target_pairs={{0,1},{1,0},{2,3},{3,2},{4,5},{5,4},{6,7},{7,6},{8,9},{9,8},{10,11... | collective-permute-start | bytes 196616 | tf_op jit(solution)/shard_map/ppermute | solution.py:284
  61.8 4.5 %collective-permute-start.37 = (f32[128,128]{1,0:T(8,128)S(1)}, f32[128,128]{1,0:T(8,128)S(1)}, u32[]{:S(2)}, u32[]{:S(2)}) collective-permute-start(f32[128,128]{1,0:T(8,128)S(1)} %shard_map.99.other), channel_id=1, source_target_pairs={{0,8},{1,9},{2,10},{3,11},{4,5},{5,4},{6,7},{7,6},{8,12},{9,13},{1... | collective-permute-start | bytes 196616 | tf_op jit(solution)/shard_map/ppermute | solution.py:284
  61.8 5.9 %collective-permute-start.28 = (f32[128,128]{1,0:T(8,128)S(1)}, f32[128,128]{1,0:T(8,128)S(1)}, u32[]{:S(2)}, u32[]{:S(2)}) collective-permute-start(f32[128,128]{1,0:T(8,128)S(1)} %shard_map.96.other), channel_id=1, source_target_pairs={{0,6},{1,7},{2,4},{3,5},{4,14},{5,15},{6,12},{7,13},{8,9},{9,8},{1... | collective-permute-start | bytes 196616 | tf_op jit(solution)/shard_map/ppermute | solution.py:284
  63.3 4.4 %collective-permute-start.27 = (f32[128,128]{1,0:T(8,128)S(1)}, f32[128,128]{1,0:T(8,128)S(1)}, u32[]{:S(2)}, u32[]{:S(2)}) collective-permute-start(f32[128,128]{1,0:T(8,128)S(1)} %shard_map.96.other), channel_id=1, source_target_pairs={{0,4},{1,5},{2,6},{3,7},{4,12},{5,13},{6,14},{7,15},{8,9},{9,8},{1... | collective-permute-start | bytes 196616 | tf_op jit(solution)/shard_map/ppermute | solution.py:284
  70.4 5.8 %collective-permute-start.41 = (f32[128,128]{1,0:T(8,128)S(1)}, f32[128,128]{1,0:T(8,128)S(1)}, u32[]{:S(2)}, u32[]{:S(2)}) collective-permute-start(f32[128,128]{1,0:T(8,128)S(1)} %shard_map.100.mine), channel_id=1, source_target_pairs={{0,1},{1,0},{2,3},{3,2},{4,5},{5,4},{6,7},{7,6},{8,9},{9,8},{10,11... | collective-permute-start | bytes 196616 | tf_op jit(solution)/shard_map/ppermute | solution.py:284
  (26 other events, 92.7 us)

commit v5 on v4

--- a/solution.py
+++ b/solution.py
@@ -174,59 +174,68 @@
     @pl.when(active)
     def _():
         load_vector(store, near[...], far[...])
-        out[...] = complex_product(own[0:2], mate[0:2], store)
+        out[...] = complex_product(own[4:6], mate[4:6], store)
 
     @pl.when(jnp.logical_not(active))
     def _():
         out[...] = before[...]
 
 
-def root_kernel(near, far, less_near, less_far, own, mate, before, out, store):
+def root_kernel(count, *refs):
+    near, far = refs[:2]
+    shares = refs[2 : 2 + 2 * count]
+    own, mate, before, out, store = refs[2 + 2 * count :]
     root = lax.axis_index("slab") == 0
 
     @pl.when(root)
     def _():
-        load_vector(store, near[...] - less_near[...], far[...] - less_far[...])
-        out[...] = complex_product(own[0:2], mate[0:2], store)
+        whole = [near[...], far[...]]
+        for n, share in enumerate(shares):
+            whole[n % 2] = whole[n % 2] - share[...]
+        load_vector(store, *whole)
+        out[...] = complex_product(own[4:6], mate[4:6], store)
 
     @pl.when(jnp.logical_not(root))
     def _():
         out[...] = before[...]
 
 
-def settle_kernel(slabs, spacing, kind, part, other, *refs):
-    *vectors, own, mate, out, store = refs
+def settle_kernel(spacing, part, near, far, own, mate, out, store):
+    active = lax.axis_index("slab") % (2 * spacing) == spacing
+
+    @pl.when(active)
+    def _():
+        load_vector(store, near[...], far[...])
+        out[...] = part[...] - complex_product(own[6:8], mate[6:8], store)
+
+    @pl.when(jnp.logical_not(active))
+    def _():
+        out[...] = part[...]
+
+
+def both_kernel(slabs, spacing, part, other, low_near, low_far, up_near, up_far, own, mate, *refs):
+    out, lower, upper = refs
     s = lax.axis_index("slab")
     active = s % (2 * spacing) == spacing
-    first = s % (4 * spacing) == spacing
-    if kind == "late":
-        below = jnp.logical_not(first)
-        take = active
-    elif kind == "early":
-        below = first
-        take = active & (s + spacing < slabs)
-    else:
-        below = s >= 0
-        take = active
-
-    def settle(vector, place):
-        load_vector(store, vector[0][...], vector[1][...])
-        blocks = slice(place, place + 2)
-        out[...] = part[...] - complex_product(own[blocks], mate[blocks], store)
-
-    @pl.when(take & below)
-    def _():
-        settle(vectors[:2], 2)
-
-    if len(vectors) == 4:
-
-        @pl.when(take & jnp.logical_not(below))
-        def _():
-            settle(vectors[2:], 4)
-
-    @pl.when(jnp.logical_not(take))
+    linked = s + spacing < slabs
+
+    @pl.when(active)
+    def _():
+        load_vector(lower, low_near[...], low_far[...])
+        out[...] = part[...] - complex_product(own[6:8], mate[6:8], lower)
+
+    @pl.when(active & linked)
+    def _():
+        load_vector(upper, up_near[...], up_far[...])
+        out[...] -= complex_product(own[8:10], mate[8:10], upper)
+
+    @pl.when(jnp.logical_not(active))
     def _():
         out[...] = other[...]
+
+
+def copy_kernel(values, *refs):
+    refs[-1][...] = values[...]
 
 
 def call(
@@ -273,7 +282,7 @@
     every = range(slabs)
     s = lax.axis_index("slab")
 
-    def send(values, moves, flip=0):
+    def send(values, moves, flip=0, whole=True):
         route = []
         for c in everyone:
             for a, b, *h in moves:
@@ -281,7 +290,9 @@
                 for h in h:
                     route.append((b * cols + (c ^ flip), h * cols + c))
                     route.append((h * cols + c, a * cols + c))
-        return lax.ppermute(values, ("slab", "col"), completed(route, slabs * cols, cols))
+        if whole:
+            route = completed(route, slabs * cols, cols)
+        return lax.ppermute(values, ("slab", "col"), route)
 
     def both(values, near_moves, far_moves):
         return send(values, near_moves), send(values, far_moves, 2)
@@ -308,40 +319,48 @@
         open_kernel, waves, mate_waves, side, *t_pair, outs=3, scratch=[pltpu.VMEM((64, width), wide)]
     )
     up = up_near + exchange(up_far)
-    prev = send(up, [(a, a + 1) for a in every[:-1]])
+    prev = send(up, [(a, a + 1) for a in every[:-1]], whole=False)
     down = [(a + 1, a) for a in every[:-1]]
-    front = stack(below[0], above[0], after=up)
-    front = front, swap(front)
+    next_near = send(psi, down, whole=False)
+    next_far = send(psi, down, 2, whole=False)
     rest = call(
         kernel(ham_kernel, slabs),
         psi,
         exchange(psi),
-        *both(psi, down, down),
+        next_near,
+        next_far,
         *e_pair,
         *t_pair,
         scratch=[store, store],
         unused=(up,),
     )
-    base = near = rest - jnp.where(s > 0, prev, 0.0)
-    back = stack(pivots[0], back_lower[0], back_upper[0], after=near)
-    back = back, swap(back)
-    base_far = far = exchange(near)
+    base = near = rest - prev
+    front = stack(below[0], above[0], pivots[0], back_lower[0], back_upper[0], after=near)
+    front = front, swap(front)
+    back = front
 
     pivot = base
-    late = None
+    far = exchange(near, [a for a in every if a % 2 == 1])
     for level in range(levels):
         d = 2**level
-        active = [a for a in every if a % (2 * d) == d]
         if level == levels - 1:
-            beneath = call(
-                kernel(top_kernel, d), near, far, *front, scratch=[store], unused=late
+            beneath = call(kernel(top_kernel, d), near, far, *front, scratch=[store])
+            shares = both(beneath, [(d, 0, d + 1)], [(d, 0, d + 3)])
+            if level > 1:
+                shares = shares + late
+            pivot = call(kernel(pivot_kernel, d), near, far, *back, pivot, scratch=[store])
+            pivot = call(
+                kernel(root_kernel, len(shares) // 2),
+                base,
+                base_far,
+                *shares,
+                *back,
+                pivot,
+                scratch=[store],
             )
-            less = both(beneath, [(d, 0, d + 1)], [(d, 0, d + 3)])
-            base = call(kernel(reduce_kernel, d // 2, len(late)), base, *late, unused=(beneath,))
-            base_far = exchange(base)
-            pivot = call(kernel(pivot_kernel, d), near, far, *back, pivot, scratch=[store])
-            pivot = call(root_kernel, base, base_far, *less, *back, pivot, scratch=[store])
             break
+        urgent = [b for b in every if b % (4 * d) == 2 * d]
+        patient = [b for b in every if b % (4 * d) == 0]
         beneath, over = call(
             kernel(level_kernel, d),
             near,
@@ -349,98 +368,87 @@
             *front,
             outs=2,
             scratch=[store],
-            unused=(back[1],) if level == 0 else late,
+            unused=() if level == 0 else (base,),
         )
-        urgent = [b for b in every if b % (4 * d) == 2 * d]
-        patient = [b for b in every if b % (4 * d) == 0]
         if level == 0:
             more = send(over, [(b - 1, b, b - 2) for b in urgent])
             less = send(beneath, [(b + 1, b, b - 2) for b in urgent])
-            late_less = send(beneath, [(b + 1, b, b + 3) for b in patient])
-            late_more = send(over, [(b - 1, b, b + 1) for b in patient if b > 0])
-        else:
-            more = both(
-                over, [(b - d, b, b - 1) for b in urgent], [(b - d, b, b - 3) for b in urgent]
+            pivot = call(kernel(pivot_kernel, d), near, far, *back, pivot, scratch=[store])
+            held = call(copy_kernel, beneath, unused=(pivot,))
+            late = [send(held, [(b + 1, b, b + 3) for b in patient])]
+            if len(patient) > 1:
+                held = call(copy_kernel, over, unused=(pivot,))
+                late.append(send(held, [(b - 1, b, b + 1) for b in patient if b > 0]))
+            near = base - more - less
+            far = exchange(near, urgent)
+            base = call(kernel(reduce_kernel, d, len(late)), base, *late)
+            base_far = exchange(base, patient)
+            continue
+        more = both(over, [(b - d, b, b - 1) for b in urgent], [(b - d, b, b - 3) for b in urgent])
+        less = both(
+            beneath, [(b + d, b, b + 1) for b in urgent], [(b + d, b, b + 3) for b in urgent]
+        )
+        pivot = call(kernel(pivot_kernel, d), near, far, *back, pivot, scratch=[store])
+        if level > 1:
+            is_late = s % (2 * d) == 0
+            for n, share in enumerate(late):
+                share = jnp.where(is_late & ((s > 0) | (n < 2)), share, 0.0)
+                if n % 2 == 0:
+                    base = base - share
+                else:
+                    base_far = base_far - share
+        near = base - more[0] - less[0]
+        far = base_far - more[1] - less[1]
+        held = call(copy_kernel, beneath, unused=(base_far,))
+        late = both(
+            held, [(b + d, b, b + d + 1) for b in patient], [(b + d, b, b + d + 3) for b in patient]
+        )
+        if len(patient) > 1:
+            held = call(copy_kernel, over, unused=(base_far,))
+            late = late + both(
+                held,
+                [(b - d, b, b - d + 1) for b in patient if b > 0],
+                [(b - d, b, b - d + 3) for b in patient if b > 0],
             )
-            less = both(
-                beneath, [(b + d, b, b + 1) for b in urgent], [(b + d, b, b + 3) for b in urgent]
-            )
-            late_less = send(beneath, [(b + d, b, b + d + 1) for b in patient])
-            late_more = None
-            if len(patient) > 1:
-                late_more = send(over, [(b - d, b, b - d + 1) for b in patient if b > 0])
-        pivot = call(kernel(pivot_kernel, d), near, far, *back, pivot, scratch=[store])
-        if level == 0:
-            near = base - more - less
-            far = exchange(near)
-        else:
-            base = call(kernel(reduce_kernel, d // 2, len(late)), base, *late, unused=(beneath,))
-            base_far = exchange(base)
-            near = base - more[0] - less[0]
-            far = base_far - more[1] - less[1]
-        late = (late_less,) if late_more is None else (late_less, late_more)
-
-    solved = rest = pivot
+
+    solved = pivot
     for level in reversed(range(levels)):
         d = 2**level
-        if level == levels - 1:
-            vectors = both(solved, [(0, d, 1)], [(0, d, 3)])
-            kind = "only"
+        sources = [a for a in every if a % (2 * d) == 0]
+        upper = [a for a in sources if a > 0]
+        if d > 1:
+            if upper:
+                up_near = send(solved, [(a, a - d, a - 1) for a in upper])
+            low_near = send(solved, [(a, a + d, a + 3) for a in sources])
+            if upper:
+                up_far = send(solved, [(a, a - d, a + 3) for a in upper], 2)
+            low_far = send(solved, [(a, a + d, a + 1) for a in sources], 2)
         else:
-            sources = [a for a in every if a % (4 * d) == 2 * d]
-            kind = "late"
-            if d > 1:
-                up_near = send(solved, [(a, a + d, a + 3) for a in sources])
-                down_near = send(solved, [(a, a - d, a - 1) for a in sources])
-                up_far = send(solved, [(a, a + d, a + 1) for a in sources], 2)
-                down_far = send(solved, [(a, a - d, a - 3) for a in sources], 2)
-            else:
-                up_near = send(solved, [(a, a + 1, a - 2) for a in sources])
-                down_near = send(solved, [(a, a - 1, a + 1) for a in sources])
-                down_far = send(solved, [(a, a - 1, a - 2) for a in sources], 2)
-                up_far = exchange(up_near, [a + 1 for a in sources])
-            vectors = up_near, up_far, down_near, down_far
-        if level > 0:
-            half = d // 2
-            sources = [a for a in every if a % (4 * half) == 0]
-            if half > 1:
-                early = both(
-                    solved,
-                    [(a, a + half, a + 1) for a in sources],
-                    [(a, a + half, a + 3) for a in sources],
-                )
-                if len(sources) > 1:
-                    early += both(
-                        solved,
-                        [(a, a - half, a - 1) for a in sources if a > 0],
-                        [(a, a - half, a - 3) for a in sources if a > 0],
-                    )
-            else:
-                early = both(
-                    solved,
-                    [(a, a + 1, a + 3) for a in sources],
-                    [(a, a + 1, a + 3) for a in sources],
-                ) + both(
-                    solved,
-                    [(a, a - 1, a + 1) for a in sources if a > 0],
-                    [(a, a - 1, a + 1) for a in sources if a > 0],
-                )
-        solved = call(
-            kernel(settle_kernel, slabs, d, kind),
-            rest,
-            solved,
-            *vectors,
-            *back,
-            scratch=[store],
-        )
-        if level > 0:
-            rest = call(
-                kernel(settle_kernel, slabs, half, "early"),
+            low_near = send(solved, [(a, a ^ 1) for a in every])
+            ways = [(a, a - 1) for a in upper] + [(a - 1, a) for a in upper]
+            up_near = send(solved, ways)
+            up_far = send(solved, ways, 2)
+            low_far = exchange(low_near, [a + 1 for a in sources])
+        if not upper:
+            solved = call(
+                kernel(settle_kernel, d),
                 pivot,
-                pivot,
-                *early,
+                low_near,
+                low_far,
                 *back,
                 scratch=[store],
+            )
+        else:
+            solved = call(
+                kernel(both_kernel, slabs, d),
+                pivot,
+                solved,
+                low_near,
+                low_far,
+                up_near,
+                up_far,
+                *back,
+                scratch=[store, store],
             )
     out = call(regroup_kernel, solved, swap(solved))
     return out[None]

time: 77.5 us -> 77.5 us (level)
  waiting for transfers between devices: 18.1 us -> 19.8 us
  starting transfers between devices: 52.7 us -> 51.8 us
    ppermute x42 -> x35, waiting for transfers between devices: 18.1 us -> 19.8 us  [send(): return lax.ppermute(values, ('slab', 'col'), route)]
    ppermute x42 -> x35, starting transfers between devices: 52.7 us -> 51.8 us  [send(): return lax.ppermute(values, ('slab', 'col'), route)]
    pallas_call x20 -> x19, Pallas kernels: 5.33 us -> 5.32 us  [call(): pl.pallas_call(kernel, out_shape=shape if outs == 1 else (shape,) * outs,...]
  transfers between devices with their start and end apart: 42 -> 35, of which waited for: 14 -> 18; matrix products, arithmetic and copies ran while one was open for 0% -> 0% of each run, Pallas kernels for 4% -> 3%
where the time goes in v5:
time: 77.5 us; the launch traced here: 77.3 us
  starting transfers between devices  51.8 us (67%)
  waiting for transfers between devices  19.8 us (26%)
  Pallas kernels  5.32 us (7%)
    ppermute x35, starting transfers between devices, send(): return lax.ppermute(values, ('slab', 'col'), route)  51.8 us
    ppermute x35, waiting for transfers between devices, send(): return lax.ppermute(values, ('slab', 'col'), route)  19.8 us
    pallas_call x19, Pallas kernels, call(): pl.pallas_call(kernel, out_shape=shape if outs == 1 else (shape,) * outs,...  5.32 us
  transfers between devices with their start and end apart: 35, of which 18 were waited for; matrix products, arithmetic and copies ran while one was open for 0% of the time, Pallas kernels for 3%

profile of v5, /device:TPU:13, one launch (start us, length us, event | category | flops | bytes accessed | tf_op | source)
XLA Modules:
  0.0 77.3 jit_solution(17330766520141598267)
XLA Ops:
  1.2 1.3 %collective-permute-done.other = f32[1,128,128]{2,1,0:T(8,128)S(1)} collective-permute-done((f32[1,128,128]{2,1,0:T(8,128)}, f32[1,128,128]{2,1,0:T(8,128)S(1)}, u32[]{:S(2)}, u32[]{:S(2)}) %collective-permute-start) | collective-permute-done | bytes 65568 | tf_op jit(solution)/shard_map/ppermute | solution.py:295
  3.3 1.3 %collective-permute-start.6 = (f32[128,128]{1,0:T(8,128)S(1)}, f32[128,128]{1,0:T(8,128)S(1)}, u32[]{:S(2)}, u32[]{:S(2)}) collective-permute-start(f32[128,128]{1,0:T(8,128)S(1)} %get-tuple-element.14), channel_id=1, source_target_pairs={{0,2},{1,3},{2,0},{3,1},{4,6},{5,7},{6,4},{7,5},{8,10},{9,11},{10,... | collective-permute-start | bytes 196616 | tf_op jit(solution)/shard_map/ppermute | solution.py:295
  4.8 2.1 %collective-permute-start.3 = (f32[128,128]{1,0:T(8,128)S(1)}, f32[128,128]{1,0:T(8,128)S(1)}, u32[]{:S(2)}, u32[]{:S(2)}) collective-permute-start(f32[128,128]{1,0:T(8,128)S(1)} %get-tuple-element.12.near), channel_id=1, source_target_pairs={{4,0},{8,4},{12,8},{16,12},{20,16},{24,20},{28,24},{5,1},{9,5},{13... | collective-permute-start | bytes 196616 | tf_op jit(solution)/shard_map/ppermute | solution.py:295
  6.9 4.0 %collective-permute-start.4 = (f32[128,128]{1,0:T(8,128)S(1)}, f32[128,128]{1,0:T(8,128)S(1)}, u32[]{:S(2)}, u32[]{:S(2)}) collective-permute-start(f32[128,128]{1,0:T(8,128)S(1)} %get-tuple-element.12.near), channel_id=1, source_target_pairs={{4,2},{8,6},{12,10},{16,14},{20,18},{24,22},{28,26},{5,3},{9,7},{1... | collective-permute-start | bytes 196616 | tf_op jit(solution)/shard_map/ppermute | solution.py:295
  10.9 3.2 %collective-permute-start.7 = (f32[128,128]{1,0:T(8,128)S(1)}, f32[128,128]{1,0:T(8,128)S(1)}, u32[]{:S(2)}, u32[]{:S(2)}) collective-permute-start(f32[128,128]{1,0:T(8,128)S(1)} %add.3.refs_0_), channel_id=1, source_target_pairs={{0,4},{4,8},{8,12},{12,16},{16,20},{20,24},{24,28},{1,5},{5,9},{9,... | collective-permute-start | bytes 196616 | tf_op jit(solution)/shard_map/ppermute | solution.py:295
  14.8 1.3 %collective-permute-done.7 = f32[128,128]{1,0:T(8,128)S(1)} collective-permute-done((f32[128,128]{1,0:T(8,128)S(1)}, f32[128,128]{1,0:T(8,128)S(1)}, u32[]{:S(2)}, u32[]{:S(2)}) %collective-permute-start.7) | collective-permute-done | bytes 65568 | tf_op jit(solution)/shard_map/ppermute | solution.py:295
  16.3 2.6 %collective-permute-start.9 = (f32[10,128,512]{2,1,0:T(8,128)S(1)}, f32[10,128,512]{2,1,0:T(8,128)S(1)}, u32[]{:S(2)}, u32[]{:S(2)}) collective-permute-start(f32[10,128,512]{2,1,0:T(8,128)S(1)} %shard_map.85.own.refs_6_), channel_id=1, source_target_pairs={{0,1},{1,0},{2,3},{3,2},{4,5},{5,4},{6,7},{7,6},{8,9},{9,8},{10,11... | collective-permute-start | bytes 7864328 | tf_op jit(solution)/shard_map/ppermute | solution.py:295
  19.2 3.4 %collective-permute-done.8.far = f32[128,128]{1,0:T(8,128)S(1)} collective-permute-done((f32[128,128]{1,0:T(8,128)S(1)}, f32[128,128]{1,0:T(8,128)S(1)}, u32[]{:S(2)}, u32[]{:S(2)}) %collective-permute-start.8) | collective-permute-done | bytes 65568 | tf_op jit(solution)/shard_map/ppermute | solution.py:295
  25.5 2.9 %collective-permute-start.11 = (f32[128,128]{1,0:T(8,128)S(1)}, f32[128,128]{1,0:T(8,128)S(1)}, u32[]{:S(2)}, u32[]{:S(2)}) collective-permute-start(f32[128,128]{1,0:T(8,128)S(1)} %shard_map.89), channel_id=1, source_target_pairs={{0,1},{1,0},{2,3},{3,2},{4,5},{5,4},{6,7},{7,6},{8,9},{9,8},{10,11... | collective-permute-start | bytes 196616 | tf_op jit(solution)/shard_map/ppermute | solution.py:295
  30.8 1.6 %collective-permute-done.10.refs_0_ = f32[128,128]{1,0:T(8,128)S(1)} collective-permute-done((f32[128,128]{1,0:T(8,128)S(1)}, f32[128,128]{1,0:T(8,128)S(1)}, u32[]{:S(2)}, u32[]{:S(2)}) %collective-permute-start.10) | collective-permute-done | bytes 65568 | tf_op jit(solution)/shard_map/ppermute | solution.py:295
  32.4 1.9 %collective-permute-start.12 = (f32[128,128]{1,0:T(8,128)S(1)}, f32[128,128]{1,0:T(8,128)S(1)}, u32[]{:S(2)}, u32[]{:S(2)}) collective-permute-start(f32[128,128]{1,0:T(8,128)S(1)} %shard_map.90.refs_0_), channel_id=1, source_target_pairs={{0,2},{1,3},{2,0},{3,1},{4,5},{5,4},{6,7},{7,6},{8,9},{9,8},{10,11... | collective-permute-start | bytes 196616 | tf_op jit(solution)/shard_map/ppermute | solution.py:295
  34.5 1.7 %collective-permute-start.16 = (f32[128,128]{1,0:T(8,128)S(1)}, f32[128,128]{1,0:T(8,128)S(1)}, u32[]{:S(2)}, u32[]{:S(2)}) collective-permute-start(f32[128,128]{1,0:T(8,128)S(1)} %get-tuple-element.17), channel_id=1, source_target_pairs={{0,1},{1,0},{2,3},{3,2},{4,5},{5,4},{6,7},{7,6},{8,16},{9,17},{10,... | collective-permute-start | bytes 196616 | tf_op jit(solution)/shard_map/ppermute | solution.py:295
  36.2 1.4 %collective-permute-start.19 = (f32[128,128]{1,0:T(8,128)S(1)}, f32[128,128]{1,0:T(8,128)S(1)}, u32[]{:S(2)}, u32[]{:S(2)}) collective-permute-start(f32[128,128]{1,0:T(8,128)S(1)} %get-tuple-element.18.values), channel_id=1, source_target_pairs={{0,1},{1,0},{2,3},{3,2},{4,5},{5,4},{6,7},{7,6},{8,9},{9,8},{10,11... | collective-permute-start | bytes 196616 | tf_op jit(solution)/shard_map/ppermute | solution.py:295
  38.9 1.7 %collective-permute-start.20 = (f32[128,128]{1,0:T(8,128)S(1)}, f32[128,128]{1,0:T(8,128)S(1)}, u32[]{:S(2)}, u32[]{:S(2)}) collective-permute-start(f32[128,128]{1,0:T(8,128)S(1)} %shard_map.92), channel_id=1, source_target_pairs={{0,20},{1,21},{2,22},{3,23},{4,5},{5,4},{6,7},{7,6},{8,9},{9,8},{1... | collective-permute-start | bytes 196616 | tf_op jit(solution)/shard_map/ppermute | solution.py:295
  41.9 7.1 %collective-permute-start.24 = (f32[128,128]{1,0:T(8,128)S(1)}, f32[128,128]{1,0:T(8,128)S(1)}, u32[]{:S(2)}, u32[]{:S(2)}) collective-permute-start(f32[128,128]{1,0:T(8,128)S(1)} %shard_map.96.part), channel_id=1, source_target_pairs={{0,16},{1,17},{2,18},{3,19},{4,5},{5,4},{6,7},{7,6},{8,9},{9,8},{1... | collective-permute-start | bytes 196616 | tf_op jit(solution)/shard_map/ppermute | solution.py:295
  49.0 3.9 %collective-permute-start.25 = (f32[128,128]{1,0:T(8,128)S(1)}, f32[128,128]{1,0:T(8,128)S(1)}, u32[]{:S(2)}, u32[]{:S(2)}) collective-permute-start(f32[128,128]{1,0:T(8,128)S(1)} %shard_map.96.part), channel_id=1, source_target_pairs={{0,18},{1,19},{2,16},{3,17},{4,0},{5,1},{6,2},{7,3},{8,9},{9,8},{1... | collective-permute-start | bytes 196616 | tf_op jit(solution)/shard_map/ppermute | solution.py:295
  53.8 4.3 %collective-permute-start.27 = (f32[128,128]{1,0:T(8,128)S(1)}, f32[128,128]{1,0:T(8,128)S(1)}, u32[]{:S(2)}, u32[]{:S(2)}) collective-permute-start(f32[128,128]{1,0:T(8,128)S(1)} %shard_map.97.other), channel_id=1, source_target_pairs={{0,10},{1,11},{2,8},{3,9},{4,0},{5,1},{6,2},{7,3},{8,6},{9,7},{10,... | collective-permute-start | bytes 196616 | tf_op jit(solution)/shard_map/ppermute | solution.py:295
  59.0 2.8 %collective-permute-done.28.up_near = f32[128,128]{1,0:T(8,128)S(1)} collective-permute-done((f32[128,128]{1,0:T(8,128)S(1)}, f32[128,128]{1,0:T(8,128)S(1)}, u32[]{:S(2)}, u32[]{:S(2)}) %collective-permute-start.28) | collective-permute-done | bytes 65568 | tf_op jit(solution)/shard_map/ppermute | solution.py:295
  61.9 3.2 %collective-permute-start.30 = (f32[128,128]{1,0:T(8,128)S(1)}, f32[128,128]{1,0:T(8,128)S(1)}, u32[]{:S(2)}, u32[]{:S(2)}) collective-permute-start(f32[128,128]{1,0:T(8,128)S(1)} %shard_map.98.other), channel_id=1, source_target_pairs={{0,4},{1,5},{2,6},{3,7},{4,0},{5,1},{6,2},{7,3},{8,12},{9,13},{10,... | collective-permute-start | bytes 196616 | tf_op jit(solution)/shard_map/ppermute | solution.py:295
  65.0 1.8 %collective-permute-start.33 = (f32[128,128]{1,0:T(8,128)S(1)}, f32[128,128]{1,0:T(8,128)S(1)}, u32[]{:S(2)}, u32[]{:S(2)}) collective-permute-start(f32[128,128]{1,0:T(8,128)S(1)} %shard_map.98.other), channel_id=1, source_target_pairs={{0,1},{1,0},{2,3},{3,2},{4,10},{5,11},{6,8},{7,9},{8,6},{9,7},{10,... | collective-permute-start | bytes 196616 | tf_op jit(solution)/shard_map/ppermute | solution.py:295
  66.8 1.8 %collective-permute-start.31 = (f32[128,128]{1,0:T(8,128)S(1)}, f32[128,128]{1,0:T(8,128)S(1)}, u32[]{:S(2)}, u32[]{:S(2)}) collective-permute-start(f32[128,128]{1,0:T(8,128)S(1)} %collective-permute-done.30.low_near), channel_id=1, source_target_pairs={{0,1},{1,0},{2,3},{3,2},{4,6},{5,7},{6,4},{7,5},{8,9},{9,8},{10,11... | collective-permute-start | bytes 196616 | tf_op jit(solution)/shard_map/ppermute | solution.py:295
  70.0 1.2 %collective-permute-done.31.low_far = f32[128,128]{1,0:T(8,128)S(1)} collective-permute-done((f32[128,128]{1,0:T(8,128)S(1)}, f32[128,128]{1,0:T(8,128)S(1)}, u32[]{:S(2)}, u32[]{:S(2)}) %collective-permute-start.31) | collective-permute-done | bytes 65568 | tf_op jit(solution)/shard_map/ppermute | solution.py:295
  71.2 1.4 %shard_map.99.mine = f32[128,128]{1,0:T(8,128)S(1)} custom-call(f32[128,128]{1,0:T(8,128)S(1)} %shard_map.96.part, f32[128,128]{1,0:T(8,128)S(1)} %shard_map.98.other, f32[128,128]{1,0:T(8,128)S(1)} %collective-permute-done.30.low_near, f32[128,128]{1,0:T(8,128)S(1)} %collective-permute-done.31.low_far, f32[128,128]{1,0:T(8,128)S(1)} %collective-permute-done.32.up_near, ...), custom_call_target="tpu_custom_call" | custom-call | flops 1000000000 | bytes 1 | tf_op jit(solution)/shard_map/pallas_call | solution.py:251
  72.6 3.1 %collective-permute-start.34 = (f32[128,128]{1,0:T(8,128)S(1)}, f32[128,128]{1,0:T(8,128)S(1)}, u32[]{:S(2)}, u32[]{:S(2)}) collective-permute-start(f32[128,128]{1,0:T(8,128)S(1)} %shard_map.99.mine), channel_id=1, source_target_pairs={{0,1},{1,0},{2,3},{3,2},{4,5},{5,4},{6,7},{7,6},{8,9},{9,8},{10,11... | collective-permute-start | bytes 196616 | tf_op jit(solution)/shard_map/ppermute | solution.py:295
  (86 shorter events, 16.2 us)
Async XLA Ops:
  0.7 13.4 %collective-permute-start.5 = (f32[1,128,512]{2,1,0:T(8,128)}, f32[1,128,512]{2,1,0:T(8,128)S(1)}, u32[]{:S(2)}, u32[]{:S(2)}) collective-permute-start(f32[1,128,512]{2,1,0:T(8,128)} %own_e.1), channel_id=1, source_target_pairs={{0,1},{1,0},{2,3},{3,2},{4,5},{5,4},{6,7},{7,6},{8,9},{9,8},{10,11... | collective-permute-start | bytes 786440 | tf_op jit(solution)/shard_map/ppermute | solution.py:295
  3.3 7.6 %collective-permute-start.6 = (f32[128,128]{1,0:T(8,128)S(1)}, f32[128,128]{1,0:T(8,128)S(1)}, u32[]{:S(2)}, u32[]{:S(2)}) collective-permute-start(f32[128,128]{1,0:T(8,128)S(1)} %get-tuple-element.14), channel_id=1, source_target_pairs={{0,2},{1,3},{2,0},{3,1},{4,6},{5,7},{6,4},{7,5},{8,10},{9,11},{10,... | collective-permute-start | bytes 196616 | tf_op jit(solution)/shard_map/ppermute | solution.py:295
  4.5 9.6 %collective-permute-start.2 = (f32[128,128]{1,0:T(8,128)S(1)}, f32[128,128]{1,0:T(8,128)S(1)}, u32[]{:S(2)}, u32[]{:S(2)}) collective-permute-start(f32[128,128]{1,0:T(8,128)S(1)} %get-tuple-element.12.near), channel_id=1, source_target_pairs={{0,2},{1,3},{2,0},{3,1},{4,6},{5,7},{6,4},{7,5},{8,10},{9,11},{10,... | collective-permute-start | bytes 196616 | tf_op jit(solution)/shard_map/ppermute | solution.py:295
  4.8 9.3 %collective-permute-start.3 = (f32[128,128]{1,0:T(8,128)S(1)}, f32[128,128]{1,0:T(8,128)S(1)}, u32[]{:S(2)}, u32[]{:S(2)}) collective-permute-start(f32[128,128]{1,0:T(8,128)S(1)} %get-tuple-element.12.near), channel_id=1, source_target_pairs={{4,0},{8,4},{12,8},{16,12},{20,16},{24,20},{28,24},{5,1},{9,5},{13... | collective-permute-start | bytes 196616 | tf_op jit(solution)/shard_map/ppermute | solution.py:295
  6.9 7.2 %collective-permute-start.4 = (f32[128,128]{1,0:T(8,128)S(1)}, f32[128,128]{1,0:T(8,128)S(1)}, u32[]{:S(2)}, u32[]{:S(2)}) collective-permute-start(f32[128,128]{1,0:T(8,128)S(1)} %get-tuple-element.12.near), channel_id=1, source_target_pairs={{4,2},{8,6},{12,10},{16,14},{20,18},{24,22},{28,26},{5,3},{9,7},{1... | collective-permute-start | bytes 196616 | tf_op jit(solution)/shard_map/ppermute | solution.py:295
  10.9 5.2 %collective-permute-start.7 = (f32[128,128]{1,0:T(8,128)S(1)}, f32[128,128]{1,0:T(8,128)S(1)}, u32[]{:S(2)}, u32[]{:S(2)}) collective-permute-start(f32[128,128]{1,0:T(8,128)S(1)} %add.3.refs_0_), channel_id=1, source_target_pairs={{0,4},{4,8},{8,12},{12,16},{16,20},{20,24},{24,28},{1,5},{5,9},{9,... | collective-permute-start | bytes 196616 | tf_op jit(solution)/shard_map/ppermute | solution.py:295
  16.3 7.1 %collective-permute-start.9 = (f32[10,128,512]{2,1,0:T(8,128)S(1)}, f32[10,128,512]{2,1,0:T(8,128)S(1)}, u32[]{:S(2)}, u32[]{:S(2)}) collective-permute-start(f32[10,128,512]{2,1,0:T(8,128)S(1)} %shard_map.85.own.refs_6_), channel_id=1, source_target_pairs={{0,1},{1,0},{2,3},{3,2},{4,5},{5,4},{6,7},{7,6},{8,9},{9,8},{10,11... | collective-permute-start | bytes 7864328 | tf_op jit(solution)/shard_map/ppermute | solution.py:295
  24.4 4.0 %collective-permute-start.13 = (f32[128,128]{1,0:T(8,128)S(1)}, f32[128,128]{1,0:T(8,128)S(1)}, u32[]{:S(2)}, u32[]{:S(2)}) collective-permute-start(f32[128,128]{1,0:T(8,128)S(1)} %get-tuple-element.16.values), channel_id=1, source_target_pairs={{0,4},{1,5},{2,6},{3,7},{4,8},{5,9},{6,10},{7,11},{8,0},{9,1},{10,... | collective-permute-start | bytes 196616 | tf_op jit(solution)/shard_map/ppermute | solution.py:295
  24.8 4.5 %collective-permute-start.14 = (f32[128,128]{1,0:T(8,128)S(1)}, f32[128,128]{1,0:T(8,128)S(1)}, u32[]{:S(2)}, u32[]{:S(2)}) collective-permute-start(f32[128,128]{1,0:T(8,128)S(1)} %get-tuple-element.15.values), channel_id=1, source_target_pairs={{0,12},{1,13},{2,14},{3,15},{4,5},{5,4},{6,7},{7,6},{8,0},{9,1},{1... | collective-permute-start | bytes 196616 | tf_op jit(solution)/shard_map/ppermute | solution.py:295
  25.5 5.3 %collective-permute-start.11 = (f32[128,128]{1,0:T(8,128)S(1)}, f32[128,128]{1,0:T(8,128)S(1)}, u32[]{:S(2)}, u32[]{:S(2)}) collective-permute-start(f32[128,128]{1,0:T(8,128)S(1)} %shard_map.89), channel_id=1, source_target_pairs={{0,1},{1,0},{2,3},{3,2},{4,5},{5,4},{6,7},{7,6},{8,9},{9,8},{10,11... | collective-permute-start | bytes 196616 | tf_op jit(solution)/shard_map/ppermute | solution.py:295
  28.4 4.0 %collective-permute-start.10 = (f32[128,128]{1,0:T(8,128)S(1)}, f32[128,128]{1,0:T(8,128)S(1)}, u32[]{:S(2)}, u32[]{:S(2)}) collective-permute-start(f32[128,128]{1,0:T(8,128)S(1)} %shard_map.88), channel_id=1, source_target_pairs={{0,12},{1,13},{2,14},{3,15},{4,0},{5,1},{6,2},{7,3},{8,9},{9,8},{1... | collective-permute-start | bytes 196616 | tf_op jit(solution)/shard_map/ppermute | solution.py:295
  29.3 5.1 %collective-permute-start.15 = (f32[128,128]{1,0:T(8,128)S(1)}, f32[128,128]{1,0:T(8,128)S(1)}, u32[]{:S(2)}, u32[]{:S(2)}) collective-permute-start(f32[128,128]{1,0:T(8,128)S(1)} %subtract_subtract_fusion.2.near), channel_id=1, source_target_pairs={{0,1},{1,0},{2,3},{3,2},{4,5},{5,4},{6,7},{7,6},{8,10},{9,11},{10,... | collective-permute-start | bytes 196616 | tf_op jit(solution)/shard_map/ppermute | solution.py:295
  32.4 5.2 %collective-permute-start.12 = (f32[128,128]{1,0:T(8,128)S(1)}, f32[128,128]{1,0:T(8,128)S(1)}, u32[]{:S(2)}, u32[]{:S(2)}) collective-permute-start(f32[128,128]{1,0:T(8,128)S(1)} %shard_map.90.refs_0_), channel_id=1, source_target_pairs={{0,2},{1,3},{2,0},{3,1},{4,5},{5,4},{6,7},{7,6},{8,9},{9,8},{10,11... | collective-permute-start | bytes 196616 | tf_op jit(solution)/shard_map/ppermute | solution.py:295
  34.5 4.1 %collective-permute-start.16 = (f32[128,128]{1,0:T(8,128)S(1)}, f32[128,128]{1,0:T(8,128)S(1)}, u32[]{:S(2)}, u32[]{:S(2)}) collective-permute-start(f32[128,128]{1,0:T(8,128)S(1)} %get-tuple-element.17), channel_id=1, source_target_pairs={{0,1},{1,0},{2,3},{3,2},{4,5},{5,4},{6,7},{7,6},{8,16},{9,17},{10,... | collective-permute-start | bytes 196616 | tf_op jit(solution)/shard_map/ppermute | solution.py:295
  37.6 4.1 %collective-permute-start.22 = (f32[128,128]{1,0:T(8,128)S(1)}, f32[128,128]{1,0:T(8,128)S(1)}, u32[]{:S(2)}, u32[]{:S(2)}) collective-permute-start(f32[128,128]{1,0:T(8,128)S(1)} %shard_map.93), channel_id=1, source_target_pairs={{0,12},{1,13},{2,14},{3,15},{4,5},{5,4},{6,7},{7,6},{8,0},{9,1},{1... | collective-permute-start | bytes 196616 | tf_op jit(solution)/shard_map/ppermute | solution.py:295
  41.9 11.0 %collective-permute-start.24 = (f32[128,128]{1,0:T(8,128)S(1)}, f32[128,128]{1,0:T(8,128)S(1)}, u32[]{:S(2)}, u32[]{:S(2)}) collective-permute-start(f32[128,128]{1,0:T(8,128)S(1)} %shard_map.96.part), channel_id=1, source_target_pairs={{0,16},{1,17},{2,18},{3,19},{4,5},{5,4},{6,7},{7,6},{8,9},{9,8},{1... | collective-permute-start | bytes 196616 | tf_op jit(solution)/shard_map/ppermute | solution.py:295
  49.0 4.8 %collective-permute-start.25 = (f32[128,128]{1,0:T(8,128)S(1)}, f32[128,128]{1,0:T(8,128)S(1)}, u32[]{:S(2)}, u32[]{:S(2)}) collective-permute-start(f32[128,128]{1,0:T(8,128)S(1)} %shard_map.96.part), channel_id=1, source_target_pairs={{0,18},{1,19},{2,16},{3,17},{4,0},{5,1},{6,2},{7,3},{8,9},{9,8},{1... | collective-permute-start | bytes 196616 | tf_op jit(solution)/shard_map/ppermute | solution.py:295
  53.8 4.4 %collective-permute-start.26 = (f32[128,128]{1,0:T(8,128)S(1)}, f32[128,128]{1,0:T(8,128)S(1)}, u32[]{:S(2)}, u32[]{:S(2)}) collective-permute-start(f32[128,128]{1,0:T(8,128)S(1)} %shard_map.97.other), channel_id=1, source_target_pairs={{0,8},{1,9},{2,10},{3,11},{4,5},{5,4},{6,7},{7,6},{8,12},{9,13},{1... | collective-permute-start | bytes 196616 | tf_op jit(solution)/shard_map/ppermute | solution.py:295
  53.8 5.2 %collective-permute-start.27 = (f32[128,128]{1,0:T(8,128)S(1)}, f32[128,128]{1,0:T(8,128)S(1)}, u32[]{:S(2)}, u32[]{:S(2)}) collective-permute-start(f32[128,128]{1,0:T(8,128)S(1)} %shard_map.97.other), channel_id=1, source_target_pairs={{0,10},{1,11},{2,8},{3,9},{4,0},{5,1},{6,2},{7,3},{8,6},{9,7},{10,... | collective-permute-start | bytes 196616 | tf_op jit(solution)/shard_map/ppermute | solution.py:295
  61.9 4.9 %collective-permute-start.30 = (f32[128,128]{1,0:T(8,128)S(1)}, f32[128,128]{1,0:T(8,128)S(1)}, u32[]{:S(2)}, u32[]{:S(2)}) collective-permute-start(f32[128,128]{1,0:T(8,128)S(1)} %shard_map.98.other), channel_id=1, source_target_pairs={{0,4},{1,5},{2,6},{3,7},{4,0},{5,1},{6,2},{7,3},{8,12},{9,13},{10,... | collective-permute-start | bytes 196616 | tf_op jit(solution)/shard_map/ppermute | solution.py:295
  65.0 4.0 %collective-permute-start.32 = (f32[128,128]{1,0:T(8,128)S(1)}, f32[128,128]{1,0:T(8,128)S(1)}, u32[]{:S(2)}, u32[]{:S(2)}) collective-permute-start(f32[128,128]{1,0:T(8,128)S(1)} %shard_map.98.other), channel_id=1, source_target_pairs={{0,1},{1,0},{2,3},{3,2},{4,8},{5,9},{6,10},{7,11},{8,4},{9,5},{10,... | collective-permute-start | bytes 196616 | tf_op jit(solution)/shard_map/ppermute | solution.py:295
  65.0 5.0 %collective-permute-start.33 = (f32[128,128]{1,0:T(8,128)S(1)}, f32[128,128]{1,0:T(8,128)S(1)}, u32[]{:S(2)}, u32[]{:S(2)}) collective-permute-start(f32[128,128]{1,0:T(8,128)S(1)} %shard_map.98.other), channel_id=1, source_target_pairs={{0,1},{1,0},{2,3},{3,2},{4,10},{5,11},{6,8},{7,9},{8,6},{9,7},{10,... | collective-permute-start | bytes 196616 | tf_op jit(solution)/shard_map/ppermute | solution.py:295
  66.8 4.4 %collective-permute-start.31 = (f32[128,128]{1,0:T(8,128)S(1)}, f32[128,128]{1,0:T(8,128)S(1)}, u32[]{:S(2)}, u32[]{:S(2)}) collective-permute-start(f32[128,128]{1,0:T(8,128)S(1)} %collective-permute-done.30.low_near), channel_id=1, source_target_pairs={{0,1},{1,0},{2,3},{3,2},{4,6},{5,7},{6,4},{7,5},{8,9},{9,8},{10,11... | collective-permute-start | bytes 196616 | tf_op jit(solution)/shard_map/ppermute | solution.py:295
  72.6 4.0 %collective-permute-start.34 = (f32[128,128]{1,0:T(8,128)S(1)}, f32[128,128]{1,0:T(8,128)S(1)}, u32[]{:S(2)}, u32[]{:S(2)}) collective-permute-start(f32[128,128]{1,0:T(8,128)S(1)} %shard_map.99.mine), channel_id=1, source_target_pairs={{0,1},{1,0},{2,3},{3,2},{4,5},{5,4},{6,7},{7,6},{8,9},{9,8},{10,11... | collective-permute-start | bytes 196616 | tf_op jit(solution)/shard_map/ppermute | solution.py:295
  (19 other events, 112.9 us)

commit v6 on v5

--- a/solution.py
+++ b/solution.py
@@ -213,20 +213,28 @@
         out[...] = part[...]
 
 
-def both_kernel(slabs, spacing, part, other, low_near, low_far, up_near, up_far, own, mate, *refs):
-    out, lower, upper = refs
+def both_kernel(slabs, spacing, count, part, other, *refs):
+    vectors = refs[:4]
+    early = refs[4:count]
+    own, mate, out, lower, upper = refs[count:]
     s = lax.axis_index("slab")
     active = s % (2 * spacing) == spacing
+    first = s % (4 * spacing) == spacing
     linked = s + spacing < slabs
 
+    def pick(n, wanted):
+        values = vectors[n][...]
+        return jnp.where(wanted, early[n][...], values) if n < len(early) else values
+
     @pl.when(active)
     def _():
-        load_vector(lower, low_near[...], low_far[...])
+        load_vector(lower, pick(0, first), pick(1, first))
         out[...] = part[...] - complex_product(own[6:8], mate[6:8], lower)
 
     @pl.when(active & linked)
     def _():
-        load_vector(upper, up_near[...], up_far[...])
+        second = jnp.logical_not(first)
+        load_vector(upper, pick(2, second), pick(3, second))
         out[...] -= complex_product(own[8:10], mate[8:10], upper)
 
     @pl.when(jnp.logical_not(active))
@@ -263,8 +271,8 @@
     target = dict(route)
     taken = set(target.values())
     for a in [a for a in range(count) if a not in target and a not in taken]:
-        target[a] = a ^ 1
-        taken.add(a ^ 1)
+        target[a] = a
+        taken.add(a)
     for a in range(count):
         if a not in target:
             target[a] = next(b for b in range(count) if b not in taken and b % cols == a % cols)
@@ -282,7 +290,7 @@
     every = range(slabs)
     s = lax.axis_index("slab")
 
-    def send(values, moves, flip=0, whole=True):
+    def send(values, moves, flip=0):
         route = []
         for c in everyone:
             for a, b, *h in moves:
@@ -290,9 +298,7 @@
                 for h in h:
                     route.append((b * cols + (c ^ flip), h * cols + c))
                     route.append((h * cols + c, a * cols + c))
-        if whole:
-            route = completed(route, slabs * cols, cols)
-        return lax.ppermute(values, ("slab", "col"), route)
+        return lax.ppermute(values, ("slab", "col"), completed(route, slabs * cols, cols))
 
     def both(values, near_moves, far_moves):
         return send(values, near_moves), send(values, far_moves, 2)
@@ -319,10 +325,10 @@
         open_kernel, waves, mate_waves, side, *t_pair, outs=3, scratch=[pltpu.VMEM((64, width), wide)]
     )
     up = up_near + exchange(up_far)
-    prev = send(up, [(a, a + 1) for a in every[:-1]], whole=False)
+    prev = send(up, [(a, a + 1) for a in every[:-1]])
     down = [(a + 1, a) for a in every[:-1]]
-    next_near = send(psi, down, whole=False)
-    next_far = send(psi, down, 2, whole=False)
+    next_near = send(psi, down)
+    next_far = send(psi, down, 2)
     rest = call(
         kernel(ham_kernel, slabs),
         psi,
@@ -334,7 +340,7 @@
         scratch=[store, store],
         unused=(up,),
     )
-    base = near = rest - prev
+    base = near = rest - jnp.where(s > 0, prev, 0.0)
     front = stack(below[0], above[0], pivots[0], back_lower[0], back_upper[0], after=near)
     front = front, swap(front)
     back = front
@@ -345,7 +351,7 @@
         d = 2**level
         if level == levels - 1:
             beneath = call(kernel(top_kernel, d), near, far, *front, scratch=[store])
-            shares = both(beneath, [(d, 0, d + 1)], [(d, 0, d + 3)])
+            shares = both(beneath, [(d, 0, d - 1)], [(d, 0, d - 3)])
             if level > 1:
                 shares = shares + late
             pivot = call(kernel(pivot_kernel, d), near, far, *back, pivot, scratch=[store])
@@ -416,37 +422,44 @@
         d = 2**level
         sources = [a for a in every if a % (2 * d) == 0]
         upper = [a for a in sources if a > 0]
-        if d > 1:
-            if upper:
-                up_near = send(solved, [(a, a - d, a - 1) for a in upper])
-            low_near = send(solved, [(a, a + d, a + 3) for a in sources])
-            if upper:
-                up_far = send(solved, [(a, a - d, a + 3) for a in upper], 2)
-            low_far = send(solved, [(a, a + d, a + 1) for a in sources], 2)
-        else:
+        if d == 1:
             low_near = send(solved, [(a, a ^ 1) for a in every])
             ways = [(a, a - 1) for a in upper] + [(a - 1, a) for a in upper]
             up_near = send(solved, ways)
             up_far = send(solved, ways, 2)
             low_far = exchange(low_near, [a + 1 for a in sources])
-        if not upper:
-            solved = call(
-                kernel(settle_kernel, d),
-                pivot,
-                low_near,
-                low_far,
-                *back,
-                scratch=[store],
+            vectors = low_near, low_far, up_near, up_far
+        elif level == levels - 1:
+            vectors = both(solved, [(0, d, 1)], [(0, d, 3)])
+        else:
+            sources = [a for a in every if a % (4 * d) == 2 * d]
+            up_near = send(solved, [(a, a - d, a + 1) for a in sources])
+            low_near = send(solved, [(a, a + d, a - 1) for a in sources])
+            up_far = send(solved, [(a, a - d, a + 3) for a in sources], 2)
+            low_far = send(solved, [(a, a + d, a - 3) for a in sources], 2)
+            vectors = (low_near, low_far, up_near, up_far) + early
+        if level > 1:
+            half = d // 2
+            sources = [a for a in every if a % (2 * d) == 0]
+            early = both(
+                solved,
+                [(a, a + half, a + 2 * half + 1) for a in sources],
+                [(a, a + half, a + 2 * half + 3) for a in sources],
             )
+            if len(sources) > 1:
+                early += both(
+                    solved,
+                    [(a, a - half, a - 2 * half + 1) for a in sources if a > 0],
+                    [(a, a - half, a - 2 * half + 3) for a in sources if a > 0],
+                )
+        if level == levels - 1 and levels > 1:
+            solved = call(kernel(settle_kernel, d), pivot, *vectors, *back, scratch=[store])
         else:
             solved = call(
-                kernel(both_kernel, slabs, d),
+                kernel(both_kernel, slabs, d, len(vectors)),
                 pivot,
                 solved,
-                low_near,
-                low_far,
-                up_near,
-                up_far,
+                *vectors,
                 *back,
                 scratch=[store, store],
             )

time: 77.5 us -> 112 us (1.45); the launches traced: 77.3 us -> 111 us
  starting transfers between devices: 51.8 us -> 86 us
  waiting for transfers between devices: 19.8 us -> 16 us
  Pallas kernels: 5.32 us -> 7.11 us
    ppermute x35 -> x37, starting transfers between devices: 51.8 us -> 86 us  [send(): lax.ppermute(values, ('slab', 'col'), completed(route, slabs * cols, cols))]
    ppermute x35 -> x37, waiting for transfers between devices: 19.8 us -> 16 us  [send(): lax.ppermute(values, ('slab', 'col'), completed(route, slabs * cols, cols))]
    pallas_call x19, Pallas kernels: 5.32 us -> 7.11 us  [call(): pl.pallas_call(kernel, out_shape=shape if outs == 1 else (shape,) * outs,...]
  transfers between devices with their start and end apart: 35 -> 37, of which waited for: 18 -> 8; matrix products, arithmetic and copies ran while one was open for 0% -> 1% of each run, Pallas kernels for 3% -> 4%
where the time goes in v6:
time: 112 us; the launch traced here: 111 us
  starting transfers between devices  86 us (77%)
  waiting for transfers between devices  16 us (14%)
  Pallas kernels  7.11 us (6%)
    ppermute x37, starting transfers between devices, send(): lax.ppermute(values, ('slab', 'col'), completed(route, slabs * cols, cols))  86 us
    ppermute x37, waiting for transfers between devices, send(): lax.ppermute(values, ('slab', 'col'), completed(route, slabs * cols, cols))  16 us
    pallas_call x19, Pallas kernels, call(): pl.pallas_call(kernel, out_shape=shape if outs == 1 else (shape,) * outs,...  7.11 us
  transfers between devices with their start and end apart: 37, of which 8 were waited for; matrix products, arithmetic and copies ran while one was open for 1% of the time, Pallas kernels for 4%

profile of v6, /device:TPU:13, one launch (start us, length us, event | category | flops | bytes accessed | tf_op | source)
XLA Modules:
  0.0 110.7 jit_solution(13909911702519411785)
XLA Ops:
  1.2 1.3 %collective-permute-done.other = f32[1,128,128]{2,1,0:T(8,128)S(1)} collective-permute-done((f32[1,128,128]{2,1,0:T(8,128)}, f32[1,128,128]{2,1,0:T(8,128)S(1)}, u32[]{:S(2)}, u32[]{:S(2)}) %collective-permute-start) | collective-permute-done | bytes 65568 | tf_op jit(solution)/shard_map/ppermute | solution.py:301
  5.6 2.0 %collective-permute-start.4 = (f32[128,128]{1,0:T(8,128)S(1)}, f32[128,128]{1,0:T(8,128)}, u32[]{:S(2)}, u32[]{:S(2)}) collective-permute-start(f32[128,128]{1,0:T(8,128)S(1)} %get-tuple-element.12.near), channel_id=1, source_target_pairs={{0,28},{1,29},{2,30},{3,31},{4,2},{5,3},{6,0},{7,1},{8,6},{9,7},{1... | collective-permute-start | bytes 196616 | tf_op jit(solution)/shard_map/ppermute | solution.py:301
  9.8 1.7 %collective-permute-done.4.next_far = f32[128,128]{1,0:T(8,128)} collective-permute-done((f32[128,128]{1,0:T(8,128)S(1)}, f32[128,128]{1,0:T(8,128)}, u32[]{:S(2)}, u32[]{:S(2)}) %collective-permute-start.4) | collective-permute-done | bytes 65568 | tf_op jit(solution)/shard_map/ppermute | solution.py:301
  11.5 1.7 %shard_map.84 = f32[128,128]{1,0:T(8,128)S(1)} custom-call(f32[128,128]{1,0:T(8,128)S(1)} %get-tuple-element.12.near, f32[128,128]{1,0:T(8,128)} %collective-permute-done.2.far, f32[128,128]{1,0:T(8,128)} %collective-permute-done.3.next_near, f32[128,128]{1,0:T(8,128)} %collective-permute-done.4.next_far, f32[1,128,512]{2,1,0:T(8,128)S(1)} %copy-done.6, ...), custom_call_target="tpu_custom_call" | custom-call | flops 1000000000 | bytes 1 | tf_op jit(solution)/shard_map/pallas_call | solution.py:259
  13.5 1.8 %collective-permute-start.9 = (f32[10,128,512]{2,1,0:T(8,128)S(1)}, f32[10,128,512]{2,1,0:T(8,128)S(1)}, u32[]{:S(2)}, u32[]{:S(2)}) collective-permute-start(f32[10,128,512]{2,1,0:T(8,128)S(1)} %shard_map.85.own.refs_6_.refs_4_), channel_id=1, source_target_pairs={{0,1},{1,0},{2,3},{3,2},{4,5},{5,4},{6,7},{7,6},{8,9},{9,8},{10,11... | collective-permute-start | bytes 7864328 | tf_op jit(solution)/shard_map/ppermute | solution.py:301
  15.4 2.8 %collective-permute-start.8 = (f32[128,128]{1,0:T(8,128)S(1)}, f32[128,128]{1,0:T(8,128)S(1)}, u32[]{:S(2)}, u32[]{:S(2)}) collective-permute-start(f32[128,128]{1,0:T(8,128)S(1)} %select_subtract_fusion.refs_5_.near.before.base), channel_id=1, source_target_pairs={{0,0},{1,1},{2,2},{3,3},{4,6},{5,7},{6,4},{7,5},{8,8},{9,9},{10,10... | collective-permute-start | bytes 196616 | tf_op jit(solution)/shard_map/ppermute | solution.py:301
  18.2 2.7 %collective-permute-done.8.far = f32[128,128]{1,0:T(8,128)S(1)} collective-permute-done((f32[128,128]{1,0:T(8,128)S(1)}, f32[128,128]{1,0:T(8,128)S(1)}, u32[]{:S(2)}, u32[]{:S(2)}) %collective-permute-start.8) | collective-permute-done | bytes 65568 | tf_op jit(solution)/shard_map/ppermute | solution.py:301
  22.6 5.7 %collective-permute-start.14 = (f32[128,128]{1,0:T(8,128)S(1)}, f32[128,128]{1,0:T(8,128)S(1)}, u32[]{:S(2)}, u32[]{:S(2)}) collective-permute-start(f32[128,128]{1,0:T(8,128)S(1)} %get-tuple-element.15.values), channel_id=1, source_target_pairs={{0,12},{1,13},{2,14},{3,15},{4,4},{5,5},{6,6},{7,7},{8,0},{9,1},{1... | collective-permute-start | bytes 196616 | tf_op jit(solution)/shard_map/ppermute | solution.py:301
  29.0 1.9 %collective-permute-start.11 = (f32[128,128]{1,0:T(8,128)S(1)}, f32[128,128]{1,0:T(8,128)S(1)}, u32[]{:S(2)}, u32[]{:S(2)}) collective-permute-start(f32[128,128]{1,0:T(8,128)S(1)} %shard_map.89), channel_id=1, source_target_pairs={{0,0},{1,1},{2,2},{3,3},{4,4},{5,5},{6,6},{7,7},{8,8},{9,9},{10,10... | collective-permute-start | bytes 196616 | tf_op jit(solution)/shard_map/ppermute | solution.py:301
  31.0 1.9 %collective-permute-start.10 = (f32[128,128]{1,0:T(8,128)S(1)}, f32[128,128]{1,0:T(8,128)S(1)}, u32[]{:S(2)}, u32[]{:S(2)}) collective-permute-start(f32[128,128]{1,0:T(8,128)S(1)} %shard_map.88), channel_id=1, source_target_pairs={{0,12},{1,13},{2,14},{3,15},{4,0},{5,1},{6,2},{7,3},{8,8},{9,9},{1... | collective-permute-start | bytes 196616 | tf_op jit(solution)/shard_map/ppermute | solution.py:301
  34.0 2.8 %collective-permute-done.10.refs_0_ = f32[128,128]{1,0:T(8,128)S(1)} collective-permute-done((f32[128,128]{1,0:T(8,128)S(1)}, f32[128,128]{1,0:T(8,128)S(1)}, u32[]{:S(2)}, u32[]{:S(2)}) %collective-permute-start.10) | collective-permute-done | bytes 65568 | tf_op jit(solution)/shard_map/ppermute | solution.py:301
  38.3 6.1 %collective-permute-start.16 = (f32[128,128]{1,0:T(8,128)S(1)}, f32[128,128]{1,0:T(8,128)S(1)}, u32[]{:S(2)}, u32[]{:S(2)}) collective-permute-start(f32[128,128]{1,0:T(8,128)S(1)} %get-tuple-element.17), channel_id=1, source_target_pairs={{0,0},{1,1},{2,2},{3,3},{4,4},{5,5},{6,6},{7,7},{8,16},{9,17},{10,... | collective-permute-start | bytes 196616 | tf_op jit(solution)/shard_map/ppermute | solution.py:301
  45.8 1.9 %collective-permute-start.22 = (f32[128,128]{1,0:T(8,128)S(1)}, f32[128,128]{1,0:T(8,128)S(1)}, u32[]{:S(2)}, u32[]{:S(2)}) collective-permute-start(f32[128,128]{1,0:T(8,128)S(1)} %shard_map.93), channel_id=1, source_target_pairs={{0,12},{1,13},{2,14},{3,15},{4,4},{5,5},{6,6},{7,7},{8,0},{9,1},{1... | collective-permute-start | bytes 196616 | tf_op jit(solution)/shard_map/ppermute | solution.py:301
  48.6 5.2 %collective-permute-start.20 = (f32[128,128]{1,0:T(8,128)S(1)}, f32[128,128]{1,0:T(8,128)S(1)}, u32[]{:S(2)}, u32[]{:S(2)}) collective-permute-start(f32[128,128]{1,0:T(8,128)S(1)} %shard_map.92), channel_id=1, source_target_pairs={{0,12},{1,13},{2,14},{3,15},{4,4},{5,5},{6,6},{7,7},{8,8},{9,9},{1... | collective-permute-start | bytes 196616 | tf_op jit(solution)/shard_map/ppermute | solution.py:301
  54.5 4.3 %collective-permute-done.20.refs_2_ = f32[128,128]{1,0:T(8,128)S(1)} collective-permute-done((f32[128,128]{1,0:T(8,128)S(1)}, f32[128,128]{1,0:T(8,128)S(1)}, u32[]{:S(2)}, u32[]{:S(2)}) %collective-permute-start.20) | collective-permute-done | bytes 65568 | tf_op jit(solution)/shard_map/ppermute | solution.py:301
  59.5 10.7 %collective-permute-start.25 = (f32[128,128]{1,0:T(8,128)S(1)}, f32[128,128]{1,0:T(8,128)S(1)}, u32[]{:S(2)}, u32[]{:S(2)}) collective-permute-start(f32[128,128]{1,0:T(8,128)S(1)} %shard_map.96.part), channel_id=1, source_target_pairs={{0,18},{1,19},{2,16},{3,17},{4,4},{5,5},{6,6},{7,7},{8,8},{9,9},{1... | collective-permute-start | bytes 196616 | tf_op jit(solution)/shard_map/ppermute | solution.py:301
  71.6 4.9 %collective-permute-start.26 = (f32[128,128]{1,0:T(8,128)S(1)}, f32[128,128]{1,0:T(8,128)S(1)}, u32[]{:S(2)}, u32[]{:S(2)}) collective-permute-start(f32[128,128]{1,0:T(8,128)S(1)} %shard_map.97.other), channel_id=1, source_target_pairs={{0,0},{1,1},{2,2},{3,3},{4,4},{5,5},{6,6},{7,7},{8,8},{9,9},{10,10... | collective-permute-start | bytes 196616 | tf_op jit(solution)/shard_map/ppermute | solution.py:301
  78.6 8.6 %collective-permute-start.32 = (f32[128,128]{1,0:T(8,128)S(1)}, f32[128,128]{1,0:T(8,128)S(1)}, u32[]{:S(2)}, u32[]{:S(2)}) collective-permute-start(f32[128,128]{1,0:T(8,128)S(1)} %shard_map.98.other), channel_id=1, source_target_pairs={{0,4},{1,5},{2,6},{3,7},{4,0},{5,1},{6,2},{7,3},{8,12},{9,13},{10,... | collective-permute-start | bytes 196616 | tf_op jit(solution)/shard_map/ppermute | solution.py:301
  87.2 2.2 %collective-permute-start.34 = (f32[128,128]{1,0:T(8,128)S(1)}, f32[128,128]{1,0:T(8,128)S(1)}, u32[]{:S(2)}, u32[]{:S(2)}) collective-permute-start(f32[128,128]{1,0:T(8,128)S(1)} %shard_map.98.other), channel_id=1, source_target_pairs={{0,0},{1,1},{2,2},{3,3},{4,8},{5,9},{6,10},{7,11},{8,4},{9,5},{10,... | collective-permute-start | bytes 196616 | tf_op jit(solution)/shard_map/ppermute | solution.py:301
  89.3 3.8 %collective-permute-start.35 = (f32[128,128]{1,0:T(8,128)S(1)}, f32[128,128]{1,0:T(8,128)S(1)}, u32[]{:S(2)}, u32[]{:S(2)}) collective-permute-start(f32[128,128]{1,0:T(8,128)S(1)} %shard_map.98.other), channel_id=1, source_target_pairs={{0,0},{1,1},{2,2},{3,3},{4,10},{5,11},{6,8},{7,9},{8,6},{9,7},{10,... | collective-permute-start | bytes 196616 | tf_op jit(solution)/shard_map/ppermute | solution.py:301
  93.2 3.3 %collective-permute-start.33 = (f32[128,128]{1,0:T(8,128)S(1)}, f32[128,128]{1,0:T(8,128)S(1)}, u32[]{:S(2)}, u32[]{:S(2)}) collective-permute-start(f32[128,128]{1,0:T(8,128)S(1)} %collective-permute-done.32.refs_0_), channel_id=1, source_target_pairs={{0,0},{1,1},{2,2},{3,3},{4,6},{5,7},{6,4},{7,5},{8,8},{9,9},{10,10... | collective-permute-start | bytes 196616 | tf_op jit(solution)/shard_map/ppermute | solution.py:301
  96.5 1.7 %collective-permute-done.33.refs_1_ = f32[128,128]{1,0:T(8,128)S(1)} collective-permute-done((f32[128,128]{1,0:T(8,128)S(1)}, f32[128,128]{1,0:T(8,128)S(1)}, u32[]{:S(2)}, u32[]{:S(2)}) %collective-permute-start.33) | collective-permute-done | bytes 65568 | tf_op jit(solution)/shard_map/ppermute | solution.py:301
  98.2 1.4 %shard_map.99.mine = f32[128,128]{1,0:T(8,128)S(1)} custom-call(f32[128,128]{1,0:T(8,128)S(1)} %shard_map.96.part, f32[128,128]{1,0:T(8,128)S(1)} %shard_map.98.other, f32[128,128]{1,0:T(8,128)S(1)} %collective-permute-done.32.refs_0_, f32[128,128]{1,0:T(8,128)S(1)} %collective-permute-done.33.refs_1_, f32[128,128]{1,0:T(8,128)S(1)} %collective-permute-done.34.refs_2_, ...), custom_call_target="tpu_custom_call" | custom-call | flops 1000000000 | bytes 1 | tf_op jit(solution)/shard_map/pallas_call | solution.py:259
  99.6 9.5 %collective-permute-start.36 = (f32[128,128]{1,0:T(8,128)S(1)}, f32[128,128]{1,0:T(8,128)S(1)}, u32[]{:S(2)}, u32[]{:S(2)}) collective-permute-start(f32[128,128]{1,0:T(8,128)S(1)} %shard_map.99.mine), channel_id=1, source_target_pairs={{0,1},{1,0},{2,3},{3,2},{4,5},{5,4},{6,7},{7,6},{8,9},{9,8},{10,11... | collective-permute-start | bytes 196616 | tf_op jit(solution)/shard_map/ppermute | solution.py:301
  (90 shorter events, 19.9 us)
Async XLA Ops:
  0.7 9.1 %collective-permute-start.5 = (f32[1,128,512]{2,1,0:T(8,128)}, f32[1,128,512]{2,1,0:T(8,128)}, u32[]{:S(2)}, u32[]{:S(2)}) collective-permute-start(f32[1,128,512]{2,1,0:T(8,128)} %own_e.1), channel_id=1, source_target_pairs={{0,1},{1,0},{2,3},{3,2},{4,5},{5,4},{6,7},{7,6},{8,9},{9,8},{10,11... | collective-permute-start | bytes 786440 | tf_op jit(solution)/shard_map/ppermute | solution.py:301
  5.6 5.9 %collective-permute-start.4 = (f32[128,128]{1,0:T(8,128)S(1)}, f32[128,128]{1,0:T(8,128)}, u32[]{:S(2)}, u32[]{:S(2)}) collective-permute-start(f32[128,128]{1,0:T(8,128)S(1)} %get-tuple-element.12.near), channel_id=1, source_target_pairs={{0,28},{1,29},{2,30},{3,31},{4,2},{5,3},{6,0},{7,1},{8,6},{9,7},{1... | collective-permute-start | bytes 196616 | tf_op jit(solution)/shard_map/ppermute | solution.py:301
  13.5 7.4 %collective-permute-start.9 = (f32[10,128,512]{2,1,0:T(8,128)S(1)}, f32[10,128,512]{2,1,0:T(8,128)S(1)}, u32[]{:S(2)}, u32[]{:S(2)}) collective-permute-start(f32[10,128,512]{2,1,0:T(8,128)S(1)} %shard_map.85.own.refs_6_.refs_4_), channel_id=1, source_target_pairs={{0,1},{1,0},{2,3},{3,2},{4,5},{5,4},{6,7},{7,6},{8,9},{9,8},{10,11... | collective-permute-start | bytes 7864328 | tf_op jit(solution)/shard_map/ppermute | solution.py:301
  15.4 5.6 %collective-permute-start.8 = (f32[128,128]{1,0:T(8,128)S(1)}, f32[128,128]{1,0:T(8,128)S(1)}, u32[]{:S(2)}, u32[]{:S(2)}) collective-permute-start(f32[128,128]{1,0:T(8,128)S(1)} %select_subtract_fusion.refs_5_.near.before.base), channel_id=1, source_target_pairs={{0,0},{1,1},{2,2},{3,3},{4,6},{5,7},{6,4},{7,5},{8,8},{9,9},{10,10... | collective-permute-start | bytes 196616 | tf_op jit(solution)/shard_map/ppermute | solution.py:301
  21.9 11.0 %collective-permute-start.13 = (f32[128,128]{1,0:T(8,128)S(1)}, f32[128,128]{1,0:T(8,128)S(1)}, u32[]{:S(2)}, u32[]{:S(2)}) collective-permute-start(f32[128,128]{1,0:T(8,128)S(1)} %get-tuple-element.16.values), channel_id=1, source_target_pairs={{0,4},{1,5},{2,6},{3,7},{4,8},{5,9},{6,10},{7,11},{8,0},{9,1},{10,... | collective-permute-start | bytes 196616 | tf_op jit(solution)/shard_map/ppermute | solution.py:301
  22.6 10.3 %collective-permute-start.14 = (f32[128,128]{1,0:T(8,128)S(1)}, f32[128,128]{1,0:T(8,128)S(1)}, u32[]{:S(2)}, u32[]{:S(2)}) collective-permute-start(f32[128,128]{1,0:T(8,128)S(1)} %get-tuple-element.15.values), channel_id=1, source_target_pairs={{0,12},{1,13},{2,14},{3,15},{4,4},{5,5},{6,6},{7,7},{8,0},{9,1},{1... | collective-permute-start | bytes 196616 | tf_op jit(solution)/shard_map/ppermute | solution.py:301
  29.0 5.0 %collective-permute-start.11 = (f32[128,128]{1,0:T(8,128)S(1)}, f32[128,128]{1,0:T(8,128)S(1)}, u32[]{:S(2)}, u32[]{:S(2)}) collective-permute-start(f32[128,128]{1,0:T(8,128)S(1)} %shard_map.89), channel_id=1, source_target_pairs={{0,0},{1,1},{2,2},{3,3},{4,4},{5,5},{6,6},{7,7},{8,8},{9,9},{10,10... | collective-permute-start | bytes 196616 | tf_op jit(solution)/shard_map/ppermute | solution.py:301
  31.0 5.9 %collective-permute-start.10 = (f32[128,128]{1,0:T(8,128)S(1)}, f32[128,128]{1,0:T(8,128)S(1)}, u32[]{:S(2)}, u32[]{:S(2)}) collective-permute-start(f32[128,128]{1,0:T(8,128)S(1)} %shard_map.88), channel_id=1, source_target_pairs={{0,12},{1,13},{2,14},{3,15},{4,0},{5,1},{6,2},{7,3},{8,8},{9,9},{1... | collective-permute-start | bytes 196616 | tf_op jit(solution)/shard_map/ppermute | solution.py:301
  36.9 8.9 %collective-permute-start.12 = (f32[128,128]{1,0:T(8,128)S(1)}, f32[128,128]{1,0:T(8,128)S(1)}, u32[]{:S(2)}, u32[]{:S(2)}) collective-permute-start(f32[128,128]{1,0:T(8,128)S(1)} %shard_map.90.refs_0_), channel_id=1, source_target_pairs={{0,2},{1,3},{2,0},{3,1},{4,4},{5,5},{6,6},{7,7},{8,8},{9,9},{10,10... | collective-permute-start | bytes 196616 | tf_op jit(solution)/shard_map/ppermute | solution.py:301
  37.6 10.2 %collective-permute-start.18 = (f32[128,128]{1,0:T(8,128)S(1)}, f32[128,128]{1,0:T(8,128)S(1)}, u32[]{:S(2)}, u32[]{:S(2)}) collective-permute-start(f32[128,128]{1,0:T(8,128)S(1)} %get-tuple-element.17), channel_id=1, source_target_pairs={{0,0},{1,1},{2,2},{3,3},{4,8},{5,9},{6,10},{7,11},{8,18},{9,19},{1... | collective-permute-start | bytes 196616 | tf_op jit(solution)/shard_map/ppermute | solution.py:301
  38.3 10.2 %collective-permute-start.16 = (f32[128,128]{1,0:T(8,128)S(1)}, f32[128,128]{1,0:T(8,128)S(1)}, u32[]{:S(2)}, u32[]{:S(2)}) collective-permute-start(f32[128,128]{1,0:T(8,128)S(1)} %get-tuple-element.17), channel_id=1, source_target_pairs={{0,0},{1,1},{2,2},{3,3},{4,4},{5,5},{6,6},{7,7},{8,16},{9,17},{10,... | collective-permute-start | bytes 196616 | tf_op jit(solution)/shard_map/ppermute | solution.py:301
  45.8 8.7 %collective-permute-start.22 = (f32[128,128]{1,0:T(8,128)S(1)}, f32[128,128]{1,0:T(8,128)S(1)}, u32[]{:S(2)}, u32[]{:S(2)}) collective-permute-start(f32[128,128]{1,0:T(8,128)S(1)} %shard_map.93), channel_id=1, source_target_pairs={{0,12},{1,13},{2,14},{3,15},{4,4},{5,5},{6,6},{7,7},{8,0},{9,1},{1... | collective-permute-start | bytes 196616 | tf_op jit(solution)/shard_map/ppermute | solution.py:301
  47.8 6.7 %collective-permute-start.23 = (f32[128,128]{1,0:T(8,128)S(1)}, f32[128,128]{1,0:T(8,128)S(1)}, u32[]{:S(2)}, u32[]{:S(2)}) collective-permute-start(f32[128,128]{1,0:T(8,128)S(1)} %shard_map.93), channel_id=1, source_target_pairs={{0,22},{1,23},{2,20},{3,21},{4,4},{5,5},{6,6},{7,7},{8,2},{9,3},{1... | collective-permute-start | bytes 196616 | tf_op jit(solution)/shard_map/ppermute | solution.py:301
  48.6 10.2 %collective-permute-start.20 = (f32[128,128]{1,0:T(8,128)S(1)}, f32[128,128]{1,0:T(8,128)S(1)}, u32[]{:S(2)}, u32[]{:S(2)}) collective-permute-start(f32[128,128]{1,0:T(8,128)S(1)} %shard_map.92), channel_id=1, source_target_pairs={{0,12},{1,13},{2,14},{3,15},{4,4},{5,5},{6,6},{7,7},{8,8},{9,9},{1... | collective-permute-start | bytes 196616 | tf_op jit(solution)/shard_map/ppermute | solution.py:301
  53.8 5.0 %collective-permute-start.21 = (f32[128,128]{1,0:T(8,128)S(1)}, f32[128,128]{1,0:T(8,128)S(1)}, u32[]{:S(2)}, u32[]{:S(2)}) collective-permute-start(f32[128,128]{1,0:T(8,128)S(1)} %shard_map.92), channel_id=1, source_target_pairs={{0,6},{1,7},{2,4},{3,5},{4,16},{5,17},{6,18},{7,19},{8,8},{9,9},{1... | collective-permute-start | bytes 196616 | tf_op jit(solution)/shard_map/ppermute | solution.py:301
  58.8 12.7 %collective-permute-start.24 = (f32[128,128]{1,0:T(8,128)S(1)}, f32[128,128]{1,0:T(8,128)S(1)}, u32[]{:S(2)}, u32[]{:S(2)}) collective-permute-start(f32[128,128]{1,0:T(8,128)S(1)} %shard_map.96.part), channel_id=1, source_target_pairs={{0,16},{1,17},{2,18},{3,19},{4,0},{5,1},{6,2},{7,3},{8,8},{9,9},{1... | collective-permute-start | bytes 196616 | tf_op jit(solution)/shard_map/ppermute | solution.py:301
  59.5 12.0 %collective-permute-start.25 = (f32[128,128]{1,0:T(8,128)S(1)}, f32[128,128]{1,0:T(8,128)S(1)}, u32[]{:S(2)}, u32[]{:S(2)}) collective-permute-start(f32[128,128]{1,0:T(8,128)S(1)} %shard_map.96.part), channel_id=1, source_target_pairs={{0,18},{1,19},{2,16},{3,17},{4,4},{5,5},{6,6},{7,7},{8,8},{9,9},{1... | collective-permute-start | bytes 196616 | tf_op jit(solution)/shard_map/ppermute | solution.py:301
  70.2 7.7 %collective-permute-start.30 = (f32[128,128]{1,0:T(8,128)S(1)}, f32[128,128]{1,0:T(8,128)S(1)}, u32[]{:S(2)}, u32[]{:S(2)}) collective-permute-start(f32[128,128]{1,0:T(8,128)S(1)} %shard_map.96.part), channel_id=1, source_target_pairs={{0,8},{1,9},{2,10},{3,11},{4,4},{5,5},{6,6},{7,7},{8,20},{9,21},{1... | collective-permute-start | bytes 196616 | tf_op jit(solution)/shard_map/ppermute | solution.py:301
  70.8 7.7 %collective-permute-start.31 = (f32[128,128]{1,0:T(8,128)S(1)}, f32[128,128]{1,0:T(8,128)S(1)}, u32[]{:S(2)}, u32[]{:S(2)}) collective-permute-start(f32[128,128]{1,0:T(8,128)S(1)} %shard_map.96.part), channel_id=1, source_target_pairs={{0,10},{1,11},{2,8},{3,9},{4,4},{5,5},{6,6},{7,7},{8,30},{9,31},{1... | collective-permute-start | bytes 196616 | tf_op jit(solution)/shard_map/ppermute | solution.py:301
  71.6 7.0 %collective-permute-start.26 = (f32[128,128]{1,0:T(8,128)S(1)}, f32[128,128]{1,0:T(8,128)S(1)}, u32[]{:S(2)}, u32[]{:S(2)}) collective-permute-start(f32[128,128]{1,0:T(8,128)S(1)} %shard_map.97.other), channel_id=1, source_target_pairs={{0,0},{1,1},{2,2},{3,3},{4,4},{5,5},{6,6},{7,7},{8,8},{9,9},{10,10... | collective-permute-start | bytes 196616 | tf_op jit(solution)/shard_map/ppermute | solution.py:301
  78.6 14.6 %collective-permute-start.32 = (f32[128,128]{1,0:T(8,128)S(1)}, f32[128,128]{1,0:T(8,128)S(1)}, u32[]{:S(2)}, u32[]{:S(2)}) collective-permute-start(f32[128,128]{1,0:T(8,128)S(1)} %shard_map.98.other), channel_id=1, source_target_pairs={{0,4},{1,5},{2,6},{3,7},{4,0},{5,1},{6,2},{7,3},{8,12},{9,13},{10,... | collective-permute-start | bytes 196616 | tf_op jit(solution)/shard_map/ppermute | solution.py:301
  87.2 9.3 %collective-permute-start.34 = (f32[128,128]{1,0:T(8,128)S(1)}, f32[128,128]{1,0:T(8,128)S(1)}, u32[]{:S(2)}, u32[]{:S(2)}) collective-permute-start(f32[128,128]{1,0:T(8,128)S(1)} %shard_map.98.other), channel_id=1, source_target_pairs={{0,0},{1,1},{2,2},{3,3},{4,8},{5,9},{6,10},{7,11},{8,4},{9,5},{10,... | collective-permute-start | bytes 196616 | tf_op jit(solution)/shard_map/ppermute | solution.py:301
  89.3 7.1 %collective-permute-start.35 = (f32[128,128]{1,0:T(8,128)S(1)}, f32[128,128]{1,0:T(8,128)S(1)}, u32[]{:S(2)}, u32[]{:S(2)}) collective-permute-start(f32[128,128]{1,0:T(8,128)S(1)} %shard_map.98.other), channel_id=1, source_target_pairs={{0,0},{1,1},{2,2},{3,3},{4,10},{5,11},{6,8},{7,9},{8,6},{9,7},{10,... | collective-permute-start | bytes 196616 | tf_op jit(solution)/shard_map/ppermute | solution.py:301
  99.6 10.4 %collective-permute-start.36 = (f32[128,128]{1,0:T(8,128)S(1)}, f32[128,128]{1,0:T(8,128)S(1)}, u32[]{:S(2)}, u32[]{:S(2)}) collective-permute-start(f32[128,128]{1,0:T(8,128)S(1)} %shard_map.99.mine), channel_id=1, source_target_pairs={{0,1},{1,0},{2,3},{3,2},{4,5},{5,4},{6,7},{7,6},{8,9},{9,8},{10,11... | collective-permute-start | bytes 196616 | tf_op jit(solution)/shard_map/ppermute | solution.py:301
  (21 other events, 106.1 us)

commit v7 on v6

--- a/solution.py
+++ b/solution.py
@@ -149,13 +149,13 @@
     out[...] = near[...] - half_step * rotate(ham)
 
 
-def level_kernel(spacing, near, far, own, mate, *refs):
+def level_kernel(spacing, near, far, own, mate, tail, *refs):
     beneath, above, store = refs[-3:]
 
     @pl.when(lax.axis_index("slab") % (2 * spacing) == spacing)
     def _():
         load_vector(store, near[...], far[...])
-        above[...] = complex_product(own[2:4], mate[2:4], store)
+        above[...] = complex_product(own[2:4], mate[2:4], store) + tail[...]
         beneath[...] = complex_product(own[0:2], mate[0:2], store)
 
 
@@ -271,8 +271,8 @@
     target = dict(route)
     taken = set(target.values())
     for a in [a for a in range(count) if a not in target and a not in taken]:
-        target[a] = a
-        taken.add(a)
+        target[a] = a ^ 1
+        taken.add(a ^ 1)
     for a in range(count):
         if a not in target:
             target[a] = next(b for b in range(count) if b not in taken and b % cols == a % cols)
@@ -325,7 +325,7 @@
         open_kernel, waves, mate_waves, side, *t_pair, outs=3, scratch=[pltpu.VMEM((64, width), wide)]
     )
     up = up_near + exchange(up_far)
-    prev = send(up, [(a, a + 1) for a in every[:-1]])
+    prev_odd = send(up, [(a, a ^ 1) for a in every])
     down = [(a + 1, a) for a in every[:-1]]
     next_near = send(psi, down)
     next_far = send(psi, down, 2)
@@ -340,13 +340,15 @@
         scratch=[store, store],
         unused=(up,),
     )
-    base = near = rest - jnp.where(s > 0, prev, 0.0)
-    front = stack(below[0], above[0], pivots[0], back_lower[0], back_upper[0], after=near)
+    near = rest - prev_odd
+    far = exchange(near)
+    blocks = (below[0], above[0], pivots[0], back_lower[0], back_upper[0])
+    front = stack(*blocks, after=near)
     front = front, swap(front)
     back = front
-
-    pivot = base
-    far = exchange(near, [a for a in every if a % 2 == 1])
+    base = rest
+
+    pivot = near
     for level in range(levels):
         d = 2**level
         if level == levels - 1:
@@ -372,6 +374,7 @@
             near,
             far,
             *front,
+            up if level == 0 else jnp.zeros_like(up),
             outs=2,
             scratch=[store],
             unused=() if level == 0 else (base,),

time: 112 us -> 73 us (0.65); the launches traced: 111 us -> 72.9 us
  starting transfers between devices: 86 us -> 47 us
  waiting for transfers between devices: 16 us -> 20.2 us
  Pallas kernels: 7.11 us -> 5.35 us
    ppermute x37, starting transfers between devices: 86 us -> 47 us  [send(): lax.ppermute(values, ('slab', 'col'), completed(route, slabs * cols, cols))]
    ppermute x37, waiting for transfers between devices: 16 us -> 20.2 us  [send(): lax.ppermute(values, ('slab', 'col'), completed(route, slabs * cols, cols))]
    pallas_call x19, Pallas kernels: 7.11 us -> 5.35 us  [call(): pl.pallas_call(kernel, out_shape=shape if outs == 1 else (shape,) * outs,...]
  transfers between devices with their start and end apart: 37 -> 37, of which waited for: 8 -> 19; matrix products, arithmetic and copies ran while one was open for 1% -> 0% of each run, Pallas kernels for 4% -> 3%
where the time goes in v7:
time: 73 us; the launch traced here: 72.9 us
  starting transfers between devices  47 us (64%)
  waiting for transfers between devices  20.2 us (28%)
  Pallas kernels  5.35 us (7%)
    ppermute x37, starting transfers between devices, send(): lax.ppermute(values, ('slab', 'col'), completed(route, slabs * cols, cols))  47 us
    ppermute x37, waiting for transfers between devices, send(): lax.ppermute(values, ('slab', 'col'), completed(route, slabs * cols, cols))  20.2 us
    pallas_call x19, Pallas kernels, call(): pl.pallas_call(kernel, out_shape=shape if outs == 1 else (shape,) * outs,...  5.35 us
  transfers between devices with their start and end apart: 37, of which 19 were waited for; matrix products, arithmetic and copies ran while one was open for 0% of the time, Pallas kernels for 3%

profile of v7, /device:TPU:13, one launch (start us, length us, event | category | flops | bytes accessed | tf_op | source)
XLA Modules:
  0.0 72.9 jit_solution(6878516499394433673)
XLA Ops:
  1.2 1.3 %collective-permute-done.other = f32[1,128,128]{2,1,0:T(8,128)S(1)} collective-permute-done((f32[1,128,128]{2,1,0:T(8,128)}, f32[1,128,128]{2,1,0:T(8,128)S(1)}, u32[]{:S(2)}, u32[]{:S(2)}) %collective-permute-start) | collective-permute-done | bytes 65568 | tf_op jit(solution)/shard_map/ppermute | solution.py:301
  3.3 1.3 %collective-permute-start.6 = (f32[128,128]{1,0:T(8,128)S(1)}, f32[128,128]{1,0:T(8,128)S(1)}, u32[]{:S(2)}, u32[]{:S(2)}) collective-permute-start(f32[128,128]{1,0:T(8,128)S(1)} %get-tuple-element.14), channel_id=1, source_target_pairs={{0,2},{1,3},{2,0},{3,1},{4,6},{5,7},{6,4},{7,5},{8,10},{9,11},{10,... | collective-permute-start | bytes 196616 | tf_op jit(solution)/shard_map/ppermute | solution.py:301
  5.0 2.0 %collective-permute-start.4 = (f32[128,128]{1,0:T(8,128)S(1)}, f32[128,128]{1,0:T(8,128)S(1)}, u32[]{:S(2)}, u32[]{:S(2)}) collective-permute-start(f32[128,128]{1,0:T(8,128)S(1)} %get-tuple-element.12.near), channel_id=1, source_target_pairs={{0,28},{1,29},{2,30},{3,31},{4,2},{5,3},{6,0},{7,1},{8,6},{9,7},{1... | collective-permute-start | bytes 196616 | tf_op jit(solution)/shard_map/ppermute | solution.py:301
  8.8 2.0 %collective-permute-done.4.next_far = f32[128,128]{1,0:T(8,128)S(1)} collective-permute-done((f32[128,128]{1,0:T(8,128)S(1)}, f32[128,128]{1,0:T(8,128)S(1)}, u32[]{:S(2)}, u32[]{:S(2)}) %collective-permute-start.4) | collective-permute-done | bytes 65568 | tf_op jit(solution)/shard_map/ppermute | solution.py:301
  11.6 1.5 %collective-permute-done.7 = f32[128,128]{1,0:T(8,128)S(1)} collective-permute-done((f32[128,128]{1,0:T(8,128)S(1)}, f32[128,128]{1,0:T(8,128)S(1)}, u32[]{:S(2)}, u32[]{:S(2)}) %collective-permute-start.7) | collective-permute-done | bytes 65568 | tf_op jit(solution)/shard_map/ppermute | solution.py:301
  14.7 3.0 %collective-permute-done.8.far = f32[128,128]{1,0:T(8,128)S(1)} collective-permute-done((f32[128,128]{1,0:T(8,128)S(1)}, f32[128,128]{1,0:T(8,128)S(1)}, u32[]{:S(2)}, u32[]{:S(2)}) %collective-permute-start.8) | collective-permute-done | bytes 65568 | tf_op jit(solution)/shard_map/ppermute | solution.py:301
  20.0 1.5 %collective-permute-start.14 = (f32[128,128]{1,0:T(8,128)S(1)}, f32[128,128]{1,0:T(8,128)S(1)}, u32[]{:S(2)}, u32[]{:S(2)}) collective-permute-start(f32[128,128]{1,0:T(8,128)S(1)} %get-tuple-element.15.values), channel_id=1, source_target_pairs={{0,12},{1,13},{2,14},{3,15},{4,5},{5,4},{6,7},{7,6},{8,0},{9,1},{1... | collective-permute-start | bytes 196616 | tf_op jit(solution)/shard_map/ppermute | solution.py:301
  22.2 2.1 %collective-permute-start.11 = (f32[128,128]{1,0:T(8,128)S(1)}, f32[128,128]{1,0:T(8,128)S(1)}, u32[]{:S(2)}, u32[]{:S(2)}) collective-permute-start(f32[128,128]{1,0:T(8,128)S(1)} %shard_map.89), channel_id=1, source_target_pairs={{0,1},{1,0},{2,3},{3,2},{4,5},{5,4},{6,7},{7,6},{8,9},{9,8},{10,11... | collective-permute-start | bytes 196616 | tf_op jit(solution)/shard_map/ppermute | solution.py:301
  24.9 1.6 %collective-permute-start.15 = (f32[128,128]{1,0:T(8,128)S(1)}, f32[128,128]{1,0:T(8,128)S(1)}, u32[]{:S(2)}, u32[]{:S(2)}) collective-permute-start(f32[128,128]{1,0:T(8,128)S(1)} %subtract_subtract_fusion.2.near), channel_id=1, source_target_pairs={{0,1},{1,0},{2,3},{3,2},{4,5},{5,4},{6,7},{7,6},{8,10},{9,11},{10,... | collective-permute-start | bytes 196616 | tf_op jit(solution)/shard_map/ppermute | solution.py:301
  26.5 1.7 %collective-permute-done.10.refs_0_ = f32[128,128]{1,0:T(8,128)S(1)} collective-permute-done((f32[128,128]{1,0:T(8,128)S(1)}, f32[128,128]{1,0:T(8,128)S(1)}, u32[]{:S(2)}, u32[]{:S(2)}) %collective-permute-start.10) | collective-permute-done | bytes 65568 | tf_op jit(solution)/shard_map/ppermute | solution.py:301
  28.3 1.9 %collective-permute-start.12 = (f32[128,128]{1,0:T(8,128)S(1)}, f32[128,128]{1,0:T(8,128)S(1)}, u32[]{:S(2)}, u32[]{:S(2)}) collective-permute-start(f32[128,128]{1,0:T(8,128)S(1)} %shard_map.90.refs_0_), channel_id=1, source_target_pairs={{0,2},{1,3},{2,0},{3,1},{4,5},{5,4},{6,7},{7,6},{8,9},{9,8},{10,11... | collective-permute-start | bytes 196616 | tf_op jit(solution)/shard_map/ppermute | solution.py:301
  30.8 2.3 %collective-permute-start.19 = (f32[128,128]{1,0:T(8,128)S(1)}, f32[128,128]{1,0:T(8,128)S(1)}, u32[]{:S(2)}, u32[]{:S(2)}) collective-permute-start(f32[128,128]{1,0:T(8,128)S(1)} %get-tuple-element.18.values), channel_id=1, source_target_pairs={{0,1},{1,0},{2,3},{3,2},{4,5},{5,4},{6,7},{7,6},{8,9},{9,8},{10,11... | collective-permute-start | bytes 196616 | tf_op jit(solution)/shard_map/ppermute | solution.py:301
  34.0 1.5 %collective-permute-done.16 = f32[128,128]{1,0:T(8,128)S(1)} collective-permute-done((f32[128,128]{1,0:T(8,128)S(1)}, f32[128,128]{1,0:T(8,128)S(1)}, u32[]{:S(2)}, u32[]{:S(2)}) %collective-permute-start.16) | collective-permute-done | bytes 65568 | tf_op jit(solution)/shard_map/ppermute | solution.py:301
  35.6 2.9 %collective-permute-start.20 = (f32[128,128]{1,0:T(8,128)S(1)}, f32[128,128]{1,0:T(8,128)S(1)}, u32[]{:S(2)}, u32[]{:S(2)}) collective-permute-start(f32[128,128]{1,0:T(8,128)S(1)} %shard_map.92), channel_id=1, source_target_pairs={{0,12},{1,13},{2,14},{3,15},{4,5},{5,4},{6,7},{7,6},{8,9},{9,8},{1... | collective-permute-start | bytes 196616 | tf_op jit(solution)/shard_map/ppermute | solution.py:301
  38.5 1.9 %collective-permute-start.21 = (f32[128,128]{1,0:T(8,128)S(1)}, f32[128,128]{1,0:T(8,128)S(1)}, u32[]{:S(2)}, u32[]{:S(2)}) collective-permute-start(f32[128,128]{1,0:T(8,128)S(1)} %shard_map.92), channel_id=1, source_target_pairs={{0,6},{1,7},{2,4},{3,5},{4,16},{5,17},{6,18},{7,19},{8,9},{9,8},{1... | collective-permute-start | bytes 196616 | tf_op jit(solution)/shard_map/ppermute | solution.py:301
  40.4 1.8 %collective-permute-done.20.refs_2_ = f32[128,128]{1,0:T(8,128)S(1)} collective-permute-done((f32[128,128]{1,0:T(8,128)S(1)}, f32[128,128]{1,0:T(8,128)S(1)}, u32[]{:S(2)}, u32[]{:S(2)}) %collective-permute-start.20) | collective-permute-done | bytes 65568 | tf_op jit(solution)/shard_map/ppermute | solution.py:301
  43.1 3.0 %collective-permute-start.25 = (f32[128,128]{1,0:T(8,128)S(1)}, f32[128,128]{1,0:T(8,128)S(1)}, u32[]{:S(2)}, u32[]{:S(2)}) collective-permute-start(f32[128,128]{1,0:T(8,128)S(1)} %shard_map.96.part), channel_id=1, source_target_pairs={{0,18},{1,19},{2,16},{3,17},{4,5},{5,4},{6,7},{7,6},{8,9},{9,8},{1... | collective-permute-start | bytes 196616 | tf_op jit(solution)/shard_map/ppermute | solution.py:301
  46.1 2.3 %collective-permute-start.30 = (f32[128,128]{1,0:T(8,128)S(1)}, f32[128,128]{1,0:T(8,128)S(1)}, u32[]{:S(2)}, u32[]{:S(2)}) collective-permute-start(f32[128,128]{1,0:T(8,128)S(1)} %shard_map.96.part), channel_id=1, source_target_pairs={{0,8},{1,9},{2,10},{3,11},{4,5},{5,4},{6,7},{7,6},{8,20},{9,21},{1... | collective-permute-start | bytes 196616 | tf_op jit(solution)/shard_map/ppermute | solution.py:301
  48.5 2.6 %collective-permute-start.26 = (f32[128,128]{1,0:T(8,128)S(1)}, f32[128,128]{1,0:T(8,128)S(1)}, u32[]{:S(2)}, u32[]{:S(2)}) collective-permute-start(f32[128,128]{1,0:T(8,128)S(1)} %shard_map.97.other), channel_id=1, source_target_pairs={{0,1},{1,0},{2,3},{3,2},{4,5},{5,4},{6,7},{7,6},{8,9},{9,8},{10,11... | collective-permute-start | bytes 196616 | tf_op jit(solution)/shard_map/ppermute | solution.py:301
  51.1 3.8 %collective-permute-start.27 = (f32[128,128]{1,0:T(8,128)S(1)}, f32[128,128]{1,0:T(8,128)S(1)}, u32[]{:S(2)}, u32[]{:S(2)}) collective-permute-start(f32[128,128]{1,0:T(8,128)S(1)} %shard_map.97.other), channel_id=1, source_target_pairs={{0,1},{1,0},{2,3},{3,2},{4,16},{5,17},{6,18},{7,19},{8,9},{9,8},{1... | collective-permute-start | bytes 196616 | tf_op jit(solution)/shard_map/ppermute | solution.py:301
  56.3 3.5 %collective-permute-start.32 = (f32[128,128]{1,0:T(8,128)S(1)}, f32[128,128]{1,0:T(8,128)S(1)}, u32[]{:S(2)}, u32[]{:S(2)}) collective-permute-start(f32[128,128]{1,0:T(8,128)S(1)} %shard_map.98.other), channel_id=1, source_target_pairs={{0,4},{1,5},{2,6},{3,7},{4,0},{5,1},{6,2},{7,3},{8,12},{9,13},{10,... | collective-permute-start | bytes 196616 | tf_op jit(solution)/shard_map/ppermute | solution.py:301
  59.8 2.5 %collective-permute-start.35 = (f32[128,128]{1,0:T(8,128)S(1)}, f32[128,128]{1,0:T(8,128)S(1)}, u32[]{:S(2)}, u32[]{:S(2)}) collective-permute-start(f32[128,128]{1,0:T(8,128)S(1)} %shard_map.98.other), channel_id=1, source_target_pairs={{0,1},{1,0},{2,3},{3,2},{4,10},{5,11},{6,8},{7,9},{8,6},{9,7},{10,... | collective-permute-start | bytes 196616 | tf_op jit(solution)/shard_map/ppermute | solution.py:301
  65.5 1.4 %shard_map.99.mine = f32[128,128]{1,0:T(8,128)S(1)} custom-call(f32[128,128]{1,0:T(8,128)S(1)} %shard_map.96.part, f32[128,128]{1,0:T(8,128)S(1)} %shard_map.98.other, f32[128,128]{1,0:T(8,128)S(1)} %collective-permute-done.32.refs_0_, f32[128,128]{1,0:T(8,128)S(1)} %collective-permute-done.33.refs_1_, f32[128,128]{1,0:T(8,128)S(1)} %collective-permute-done.34.refs_2_, ...), custom_call_target="tpu_custom_call" | custom-call | flops 1000000000 | bytes 1 | tf_op jit(solution)/shard_map/pallas_call | solution.py:259
  66.8 4.4 %collective-permute-start.36 = (f32[128,128]{1,0:T(8,128)S(1)}, f32[128,128]{1,0:T(8,128)S(1)}, u32[]{:S(2)}, u32[]{:S(2)}) collective-permute-start(f32[128,128]{1,0:T(8,128)S(1)} %shard_map.99.mine), channel_id=1, source_target_pairs={{0,1},{1,0},{2,3},{3,2},{4,5},{5,4},{6,7},{7,6},{8,9},{9,8},{10,11... | collective-permute-start | bytes 196616 | tf_op jit(solution)/shard_map/ppermute | solution.py:301
  (91 shorter events, 18.5 us)
Async XLA Ops:
  0.7 6.7 %collective-permute-start.5 = (f32[1,128,512]{2,1,0:T(8,128)}, f32[1,128,512]{2,1,0:T(8,128)S(1)}, u32[]{:S(2)}, u32[]{:S(2)}) collective-permute-start(f32[1,128,512]{2,1,0:T(8,128)} %own_e.1), channel_id=1, source_target_pairs={{0,1},{1,0},{2,3},{3,2},{4,5},{5,4},{6,7},{7,6},{8,9},{9,8},{10,11... | collective-permute-start | bytes 786440 | tf_op jit(solution)/shard_map/ppermute | solution.py:301
  5.0 5.9 %collective-permute-start.4 = (f32[128,128]{1,0:T(8,128)S(1)}, f32[128,128]{1,0:T(8,128)S(1)}, u32[]{:S(2)}, u32[]{:S(2)}) collective-permute-start(f32[128,128]{1,0:T(8,128)S(1)} %get-tuple-element.12.near), channel_id=1, source_target_pairs={{0,28},{1,29},{2,30},{3,31},{4,2},{5,3},{6,0},{7,1},{8,6},{9,7},{1... | collective-permute-start | bytes 196616 | tf_op jit(solution)/shard_map/ppermute | solution.py:301
  7.1 6.0 %collective-permute-start.7 = (f32[128,128]{1,0:T(8,128)S(1)}, f32[128,128]{1,0:T(8,128)S(1)}, u32[]{:S(2)}, u32[]{:S(2)}) collective-permute-start(f32[128,128]{1,0:T(8,128)S(1)} %add.3.refs_0_.tail), channel_id=1, source_target_pairs={{0,4},{1,5},{2,6},{3,7},{4,0},{5,1},{6,2},{7,3},{8,12},{9,13},{10,... | collective-permute-start | bytes 196616 | tf_op jit(solution)/shard_map/ppermute | solution.py:301
  13.3 5.2 %collective-permute-start.9 = (f32[10,128,512]{2,1,0:T(8,128)S(1)}, f32[10,128,512]{2,1,0:T(8,128)S(1)}, u32[]{:S(2)}, u32[]{:S(2)}) collective-permute-start(f32[10,128,512]{2,1,0:T(8,128)S(1)} %shard_map.85.own.refs_6_.refs_4_), channel_id=1, source_target_pairs={{0,1},{1,0},{2,3},{3,2},{4,5},{5,4},{6,7},{7,6},{8,9},{9,8},{10,11... | collective-permute-start | bytes 7864328 | tf_op jit(solution)/shard_map/ppermute | solution.py:301
  19.5 4.7 %collective-permute-start.13 = (f32[128,128]{1,0:T(8,128)S(1)}, f32[128,128]{1,0:T(8,128)S(1)}, u32[]{:S(2)}, u32[]{:S(2)}) collective-permute-start(f32[128,128]{1,0:T(8,128)S(1)} %get-tuple-element.16.values), channel_id=1, source_target_pairs={{0,4},{1,5},{2,6},{3,7},{4,8},{5,9},{6,10},{7,11},{8,0},{9,1},{10,... | collective-permute-start | bytes 196616 | tf_op jit(solution)/shard_map/ppermute | solution.py:301
  20.0 5.0 %collective-permute-start.14 = (f32[128,128]{1,0:T(8,128)S(1)}, f32[128,128]{1,0:T(8,128)S(1)}, u32[]{:S(2)}, u32[]{:S(2)}) collective-permute-start(f32[128,128]{1,0:T(8,128)S(1)} %get-tuple-element.15.values), channel_id=1, source_target_pairs={{0,12},{1,13},{2,14},{3,15},{4,5},{5,4},{6,7},{7,6},{8,0},{9,1},{1... | collective-permute-start | bytes 196616 | tf_op jit(solution)/shard_map/ppermute | solution.py:301
  22.2 4.4 %collective-permute-start.11 = (f32[128,128]{1,0:T(8,128)S(1)}, f32[128,128]{1,0:T(8,128)S(1)}, u32[]{:S(2)}, u32[]{:S(2)}) collective-permute-start(f32[128,128]{1,0:T(8,128)S(1)} %shard_map.89), channel_id=1, source_target_pairs={{0,1},{1,0},{2,3},{3,2},{4,5},{5,4},{6,7},{7,6},{8,9},{9,8},{10,11... | collective-permute-start | bytes 196616 | tf_op jit(solution)/shard_map/ppermute | solution.py:301
  24.3 4.0 %collective-permute-start.10 = (f32[128,128]{1,0:T(8,128)S(1)}, f32[128,128]{1,0:T(8,128)S(1)}, u32[]{:S(2)}, u32[]{:S(2)}) collective-permute-start(f32[128,128]{1,0:T(8,128)S(1)} %shard_map.88), channel_id=1, source_target_pairs={{0,12},{1,13},{2,14},{3,15},{4,0},{5,1},{6,2},{7,3},{8,9},{9,8},{1... | collective-permute-start | bytes 196616 | tf_op jit(solution)/shard_map/ppermute | solution.py:301
  24.9 5.3 %collective-permute-start.15 = (f32[128,128]{1,0:T(8,128)S(1)}, f32[128,128]{1,0:T(8,128)S(1)}, u32[]{:S(2)}, u32[]{:S(2)}) collective-permute-start(f32[128,128]{1,0:T(8,128)S(1)} %subtract_subtract_fusion.2.near), channel_id=1, source_target_pairs={{0,1},{1,0},{2,3},{3,2},{4,5},{5,4},{6,7},{7,6},{8,10},{9,11},{10,... | collective-permute-start | bytes 196616 | tf_op jit(solution)/shard_map/ppermute | solution.py:301
  28.3 4.8 %collective-permute-start.12 = (f32[128,128]{1,0:T(8,128)S(1)}, f32[128,128]{1,0:T(8,128)S(1)}, u32[]{:S(2)}, u32[]{:S(2)}) collective-permute-start(f32[128,128]{1,0:T(8,128)S(1)} %shard_map.90.refs_0_), channel_id=1, source_target_pairs={{0,2},{1,3},{2,0},{3,1},{4,5},{5,4},{6,7},{7,6},{8,9},{9,8},{10,11... | collective-permute-start | bytes 196616 | tf_op jit(solution)/shard_map/ppermute | solution.py:301
  30.3 5.2 %collective-permute-start.16 = (f32[128,128]{1,0:T(8,128)S(1)}, f32[128,128]{1,0:T(8,128)S(1)}, u32[]{:S(2)}, u32[]{:S(2)}) collective-permute-start(f32[128,128]{1,0:T(8,128)S(1)} %get-tuple-element.17), channel_id=1, source_target_pairs={{0,1},{1,0},{2,3},{3,2},{4,5},{5,4},{6,7},{7,6},{8,16},{9,17},{10,... | collective-permute-start | bytes 196616 | tf_op jit(solution)/shard_map/ppermute | solution.py:301
  33.1 7.3 %collective-permute-start.22 = (f32[128,128]{1,0:T(8,128)S(1)}, f32[128,128]{1,0:T(8,128)S(1)}, u32[]{:S(2)}, u32[]{:S(2)}) collective-permute-start(f32[128,128]{1,0:T(8,128)S(1)} %shard_map.93), channel_id=1, source_target_pairs={{0,12},{1,13},{2,14},{3,15},{4,5},{5,4},{6,7},{7,6},{8,0},{9,1},{1... | collective-permute-start | bytes 196616 | tf_op jit(solution)/shard_map/ppermute | solution.py:301
  33.2 7.2 %collective-permute-start.23 = (f32[128,128]{1,0:T(8,128)S(1)}, f32[128,128]{1,0:T(8,128)S(1)}, u32[]{:S(2)}, u32[]{:S(2)}) collective-permute-start(f32[128,128]{1,0:T(8,128)S(1)} %shard_map.93), channel_id=1, source_target_pairs={{0,22},{1,23},{2,20},{3,21},{4,5},{5,4},{6,7},{7,6},{8,2},{9,3},{1... | collective-permute-start | bytes 196616 | tf_op jit(solution)/shard_map/ppermute | solution.py:301
  35.6 6.6 %collective-permute-start.20 = (f32[128,128]{1,0:T(8,128)S(1)}, f32[128,128]{1,0:T(8,128)S(1)}, u32[]{:S(2)}, u32[]{:S(2)}) collective-permute-start(f32[128,128]{1,0:T(8,128)S(1)} %shard_map.92), channel_id=1, source_target_pairs={{0,12},{1,13},{2,14},{3,15},{4,5},{5,4},{6,7},{7,6},{8,9},{9,8},{1... | collective-permute-start | bytes 196616 | tf_op jit(solution)/shard_map/ppermute | solution.py:301
  42.2 6.2 %collective-permute-start.24 = (f32[128,128]{1,0:T(8,128)S(1)}, f32[128,128]{1,0:T(8,128)S(1)}, u32[]{:S(2)}, u32[]{:S(2)}) collective-permute-start(f32[128,128]{1,0:T(8,128)S(1)} %shard_map.96.part), channel_id=1, source_target_pairs={{0,16},{1,17},{2,18},{3,19},{4,0},{5,1},{6,2},{7,3},{8,9},{9,8},{1... | collective-permute-start | bytes 196616 | tf_op jit(solution)/shard_map/ppermute | solution.py:301
  43.1 5.4 %collective-permute-start.25 = (f32[128,128]{1,0:T(8,128)S(1)}, f32[128,128]{1,0:T(8,128)S(1)}, u32[]{:S(2)}, u32[]{:S(2)}) collective-permute-start(f32[128,128]{1,0:T(8,128)S(1)} %shard_map.96.part), channel_id=1, source_target_pairs={{0,18},{1,19},{2,16},{3,17},{4,5},{5,4},{6,7},{7,6},{8,9},{9,8},{1... | collective-permute-start | bytes 196616 | tf_op jit(solution)/shard_map/ppermute | solution.py:301
  46.1 8.8 %collective-permute-start.30 = (f32[128,128]{1,0:T(8,128)S(1)}, f32[128,128]{1,0:T(8,128)S(1)}, u32[]{:S(2)}, u32[]{:S(2)}) collective-permute-start(f32[128,128]{1,0:T(8,128)S(1)} %shard_map.96.part), channel_id=1, source_target_pairs={{0,8},{1,9},{2,10},{3,11},{4,5},{5,4},{6,7},{7,6},{8,20},{9,21},{1... | collective-permute-start | bytes 196616 | tf_op jit(solution)/shard_map/ppermute | solution.py:301
  48.5 6.9 %collective-permute-start.31 = (f32[128,128]{1,0:T(8,128)S(1)}, f32[128,128]{1,0:T(8,128)S(1)}, u32[]{:S(2)}, u32[]{:S(2)}) collective-permute-start(f32[128,128]{1,0:T(8,128)S(1)} %shard_map.96.part), channel_id=1, source_target_pairs={{0,10},{1,11},{2,8},{3,9},{4,5},{5,4},{6,7},{7,6},{8,30},{9,31},{1... | collective-permute-start | bytes 196616 | tf_op jit(solution)/shard_map/ppermute | solution.py:301
  48.5 6.9 %collective-permute-start.26 = (f32[128,128]{1,0:T(8,128)S(1)}, f32[128,128]{1,0:T(8,128)S(1)}, u32[]{:S(2)}, u32[]{:S(2)}) collective-permute-start(f32[128,128]{1,0:T(8,128)S(1)} %shard_map.97.other), channel_id=1, source_target_pairs={{0,1},{1,0},{2,3},{3,2},{4,5},{5,4},{6,7},{7,6},{8,9},{9,8},{10,11... | collective-permute-start | bytes 196616 | tf_op jit(solution)/shard_map/ppermute | solution.py:301
  51.1 4.7 %collective-permute-start.27 = (f32[128,128]{1,0:T(8,128)S(1)}, f32[128,128]{1,0:T(8,128)S(1)}, u32[]{:S(2)}, u32[]{:S(2)}) collective-permute-start(f32[128,128]{1,0:T(8,128)S(1)} %shard_map.97.other), channel_id=1, source_target_pairs={{0,1},{1,0},{2,3},{3,2},{4,16},{5,17},{6,18},{7,19},{8,9},{9,8},{1... | collective-permute-start | bytes 196616 | tf_op jit(solution)/shard_map/ppermute | solution.py:301
  56.3 6.1 %collective-permute-start.32 = (f32[128,128]{1,0:T(8,128)S(1)}, f32[128,128]{1,0:T(8,128)S(1)}, u32[]{:S(2)}, u32[]{:S(2)}) collective-permute-start(f32[128,128]{1,0:T(8,128)S(1)} %shard_map.98.other), channel_id=1, source_target_pairs={{0,4},{1,5},{2,6},{3,7},{4,0},{5,1},{6,2},{7,3},{8,12},{9,13},{10,... | collective-permute-start | bytes 196616 | tf_op jit(solution)/shard_map/ppermute | solution.py:301
  59.8 4.1 %collective-permute-start.34 = (f32[128,128]{1,0:T(8,128)S(1)}, f32[128,128]{1,0:T(8,128)S(1)}, u32[]{:S(2)}, u32[]{:S(2)}) collective-permute-start(f32[128,128]{1,0:T(8,128)S(1)} %shard_map.98.other), channel_id=1, source_target_pairs={{0,1},{1,0},{2,3},{3,2},{4,8},{5,9},{6,10},{7,11},{8,4},{9,5},{10,... | collective-permute-start | bytes 196616 | tf_op jit(solution)/shard_map/ppermute | solution.py:301
  59.8 5.0 %collective-permute-start.35 = (f32[128,128]{1,0:T(8,128)S(1)}, f32[128,128]{1,0:T(8,128)S(1)}, u32[]{:S(2)}, u32[]{:S(2)}) collective-permute-start(f32[128,128]{1,0:T(8,128)S(1)} %shard_map.98.other), channel_id=1, source_target_pairs={{0,1},{1,0},{2,3},{3,2},{4,10},{5,11},{6,8},{7,9},{8,6},{9,7},{10,... | collective-permute-start | bytes 196616 | tf_op jit(solution)/shard_map/ppermute | solution.py:301
  66.8 5.3 %collective-permute-start.36 = (f32[128,128]{1,0:T(8,128)S(1)}, f32[128,128]{1,0:T(8,128)S(1)}, u32[]{:S(2)}, u32[]{:S(2)}) collective-permute-start(f32[128,128]{1,0:T(8,128)S(1)} %shard_map.99.mine), channel_id=1, source_target_pairs={{0,1},{1,0},{2,3},{3,2},{4,5},{5,4},{6,7},{7,6},{8,9},{9,8},{10,11... | collective-permute-start | bytes 196616 | tf_op jit(solution)/shard_map/ppermute | solution.py:301
  (21 other events, 101.6 us)

commit v8 on v7

--- a/solution.py
+++ b/solution.py
@@ -142,11 +142,21 @@
 
 def ham_kernel(slabs, near, far, next_near, next_far, own_e, mate_e, own_t, mate_t, *refs):
     out, here, there = refs[-3:]
-    linked = lax.axis_index("slab") < slabs - 1
+    s = lax.axis_index("slab")
     load_vector(here, near[...], far[...])
-    load_vector(there, keep(linked, next_near), keep(linked, next_far))
-    ham = real_product(own_e[0], mate_e[0], here) + real_product(own_t[0], mate_t[0], there)
-    out[...] = near[...] - half_step * rotate(ham)
+    out[...] = near[...] - half_step * rotate(real_product(own_e[0], mate_e[0], here))
+
+    @pl.when((s % 2 == 1) & (s < slabs - 1))
+    def _():
+        load_vector(there, next_near[...], next_far[...])
+        out[...] -= half_step * rotate(real_product(own_t[0], mate_t[0], there))
+
+
+def even_kernel(rest, next_near, next_far, own, mate, out, store):
+    @pl.when(lax.axis_index("slab") % 2 == 0)
+    def _():
+        load_vector(store, next_near[...], next_far[...])
+        out[...] = rest[...] - half_step * rotate(real_product(own[0], mate[0], store))
 
 
 def level_kernel(spacing, near, far, own, mate, tail, *refs):
@@ -289,15 +299,19 @@
     levels = slabs.bit_length() - 1
     every = range(slabs)
     s = lax.axis_index("slab")
+    odd = s % 2 == 1
 
     def send(values, moves, flip=0):
         route = []
         for c in everyone:
             for a, b, *h in moves:
                 route.append((a * cols + c, b * cols + (c ^ flip)))
+                here = b * cols + (c ^ flip)
                 for h in h:
-                    route.append((b * cols + (c ^ flip), h * cols + c))
-                    route.append((h * cols + c, a * cols + c))
+                    route.append((here, h * cols + c))
+                    here = h * cols + c
+                if here != b * cols + (c ^ flip):
+                    route.append((here, a * cols + c))
         return lax.ppermute(values, ("slab", "col"), completed(route, slabs * cols, cols))
 
     def both(values, near_moves, far_moves):
@@ -325,35 +339,33 @@
         open_kernel, waves, mate_waves, side, *t_pair, outs=3, scratch=[pltpu.VMEM((64, width), wide)]
     )
     up = up_near + exchange(up_far)
-    prev_odd = send(up, [(a, a ^ 1) for a in every])
-    down = [(a + 1, a) for a in every[:-1]]
-    next_near = send(psi, down)
-    next_far = send(psi, down, 2)
+    psi_far = exchange(psi)
+    between = [(a, b) for k in every[1:-1:2] for a, b in ((k, k + 1), (k + 1, k))]
+    stepped = send(jnp.where(odd, psi, up), [(a, a ^ 1) for a in every])
     rest = call(
         kernel(ham_kernel, slabs),
         psi,
-        exchange(psi),
-        next_near,
-        next_far,
+        psi_far,
+        *both(psi, between, between),
         *e_pair,
         *t_pair,
         scratch=[store, store],
         unused=(up,),
     )
-    near = rest - prev_odd
-    far = exchange(near)
-    blocks = (below[0], above[0], pivots[0], back_lower[0], back_upper[0])
+    near = rest - stepped
+    far = exchange(jnp.where(odd, near, stepped))
+    blocks = below[0], above[0], pivots[0], back_lower[0], back_upper[0]
     front = stack(*blocks, after=near)
     front = front, swap(front)
     back = front
-    base = rest
+    base = call(even_kernel, rest, stepped, far, *t_pair, scratch=[store])
 
     pivot = near
     for level in range(levels):
         d = 2**level
         if level == levels - 1:
             beneath = call(kernel(top_kernel, d), near, far, *front, scratch=[store])
-            shares = both(beneath, [(d, 0, d - 1)], [(d, 0, d - 3)])
+            shares = both(beneath, [(d, 0, 1, d + 1)], [(d, 0, 1, d - 1)])
             if level > 1:
                 shares = shares + late
             pivot = call(kernel(pivot_kernel, d), near, far, *back, pivot, scratch=[store])
@@ -377,7 +389,6 @@
             up if level == 0 else jnp.zeros_like(up),
             outs=2,
             scratch=[store],
-            unused=() if level == 0 else (base,),
         )
         if level == 0:
             more = send(over, [(b - 1, b, b - 2) for b in urgent])
@@ -390,15 +401,16 @@
                 late.append(send(held, [(b - 1, b, b + 1) for b in patient if b > 0]))
             near = base - more - less
             far = exchange(near, urgent)
-            base = call(kernel(reduce_kernel, d, len(late)), base, *late)
-            base_far = exchange(base, patient)
             continue
         more = both(over, [(b - d, b, b - 1) for b in urgent], [(b - d, b, b - 3) for b in urgent])
         less = both(
             beneath, [(b + d, b, b + 1) for b in urgent], [(b + d, b, b + 3) for b in urgent]
         )
         pivot = call(kernel(pivot_kernel, d), near, far, *back, pivot, scratch=[store])
-        if level > 1:
+        if level == 1:
+            base = call(kernel(reduce_kernel, 1, len(late)), base, *late, unused=(beneath,))
+            base_far = exchange(base, [a for a in every if a % 4 == 0])
+        else:
             is_late = s % (2 * d) == 0
             for n, share in enumerate(late):
                 share = jnp.where(is_late & ((s > 0) | (n < 2)), share, 0.0)
@@ -433,7 +445,7 @@
             low_far = exchange(low_near, [a + 1 for a in sources])
             vectors = low_near, low_far, up_near, up_far
         elif level == levels - 1:
-            vectors = both(solved, [(0, d, 1)], [(0, d, 3)])
+            vectors = both(solved, [(0, d, d + 1, 1)], [(0, d, d + 1, 3)])
         else:
             sources = [a for a in every if a % (4 * d) == 2 * d]
             up_near = send(solved, [(a, a - d, a + 1) for a in sources])

time: 73 us -> 74.7 us (1.023)
  starting transfers between devices: 47 us -> 42.7 us
  waiting for transfers between devices: 20.2 us -> 23.3 us
  Pallas kernels: 5.35 us -> 7.28 us
  other arithmetic: 0.06 us -> 0.91 us
    ppermute x37, starting transfers between devices: 47 us -> 42.7 us  [send(): lax.ppermute(values, ('slab', 'col'), completed(route, slabs * cols, cols))]
    ppermute x37, waiting for transfers between devices: 20.2 us -> 23.3 us  [send(): lax.ppermute(values, ('slab', 'col'), completed(route, slabs * cols, cols))]
    pallas_call x19 -> x20, Pallas kernels: 5.35 us -> 7.28 us  [call(): pl.pallas_call(kernel, out_shape=shape if outs == 1 else (shape,) * outs,...]
    select_n x0 -> x2, other arithmetic: none -> 0.87 us  [the longest x1 0.85 us: per_device(): stepped = send(jnp.where(odd, psi, up), [(a, a ^ 1) for a in every])]
  transfers between devices with their start and end apart: 37 -> 37, of which waited for: 19 -> 15; matrix products, arithmetic and copies ran while one was open for 0% -> 1% of each run, Pallas kernels for 3% -> 4%
where the time goes in v8:
time: 74.7 us; the launch traced here: 74.5 us
  starting transfers between devices  42.7 us (57%)
  waiting for transfers between devices  23.3 us (31%)
  Pallas kernels  7.28 us (10%)
  other arithmetic  0.91 us (1%)
    ppermute x37, starting transfers between devices, send(): lax.ppermute(values, ('slab', 'col'), completed(route, slabs * cols, cols))  42.7 us
    ppermute x37, waiting for transfers between devices, send(): lax.ppermute(values, ('slab', 'col'), completed(route, slabs * cols, cols))  23.3 us
    pallas_call x20, Pallas kernels, call(): pl.pallas_call(kernel, out_shape=shape if outs == 1 else (shape,) * outs,...  7.28 us
  transfers between devices with their start and end apart: 37, of which 15 were waited for; matrix products, arithmetic and copies ran while one was open for 1% of the time, Pallas kernels for 4%

profile of v8, /device:TPU:13, one launch (start us, length us, event | category | flops | bytes accessed | tf_op | source)
XLA Modules:
  0.0 74.5 jit_solution(12763500807202461805)
XLA Ops:
  0.8 1.4 %collective-permute-done.other = f32[1,128,128]{2,1,0:T(8,128)S(1)} collective-permute-done((f32[1,128,128]{2,1,0:T(8,128)}, f32[1,128,128]{2,1,0:T(8,128)S(1)}, u32[]{:S(2)}, u32[]{:S(2)}) %collective-permute-start) | collective-permute-done | bytes 65568 | tf_op jit(solution)/shard_map/ppermute | solution.py:315
  2.2 1.3 %shard_map.83 = (f32[128,128]{1,0:T(8,128)S(1)}, f32[128,128]{1,0:T(8,128)S(1)}, f32[128,128]{1,0:T(8,128)}) custom-call(f32[1,128,128]{2,1,0:T(8,128)S(1)} %copy-done.7, f32[1,128,128]{2,1,0:T(8,128)S(1)} %collective-permute-done.other, s32[8,128]{1,0:T(8,128)S(1)} %shard_map.82.side, f32[1,128,512]{2,1,0:T(8,128)S(1)} %copy-done.6, ...), custom_call_target="tpu_custom_call" | custom-call | flops 1000000000 | bytes 1 | tf_op jit(solution)/shard_map/pallas_call | solution.py:269
  3.5 1.3 %collective-permute-start.6 = (f32[128,128]{1,0:T(8,128)}, f32[128,128]{1,0:T(8,128)}, u32[]{:S(2)}, u32[]{:S(2)}) collective-permute-start(f32[128,128]{1,0:T(8,128)} %get-tuple-element.14), channel_id=1, source_target_pairs={{0,2},{1,3},{2,0},{3,1},{4,6},{5,7},{6,4},{7,5},{8,10},{9,11},{10,... | collective-permute-start | bytes 196616 | tf_op jit(solution)/shard_map/ppermute | solution.py:315
  5.4 1.2 %collective-permute-start.4 = (f32[128,128]{1,0:T(8,128)S(1)}, f32[128,128]{1,0:T(8,128)S(1)}, u32[]{:S(2)}, u32[]{:S(2)}) collective-permute-start(f32[128,128]{1,0:T(8,128)S(1)} %get-tuple-element.12.near), channel_id=1, source_target_pairs={{0,1},{1,0},{2,3},{3,2},{4,10},{5,11},{6,8},{7,9},{8,6},{9,7},{10,... | collective-permute-start | bytes 196616 | tf_op jit(solution)/shard_map/ppermute | solution.py:315
  11.8 2.0 %shard_map.84.rest = f32[128,128]{1,0:T(8,128)S(1)} custom-call(f32[128,128]{1,0:T(8,128)S(1)} %get-tuple-element.12.near, f32[128,128]{1,0:T(8,128)S(1)} %collective-permute-done.2.far, f32[128,128]{1,0:T(8,128)S(1)} %collective-permute-done.3.next_near, f32[128,128]{1,0:T(8,128)S(1)} %collective-permute-done.4.next_far, f32[1,128,512]{2,1,0:T(8,128)S(1)} %copy-done.5, ...), custom_call_target="tpu_custom_call" | custom-call | flops 1000000000 | bytes 1 | tf_op jit(solution)/shard_map/pallas_call | solution.py:269
  14.1 1.4 %collective-permute-start.9 = (f32[10,128,512]{2,1,0:T(8,128)S(1)}, f32[10,128,512]{2,1,0:T(8,128)S(1)}, u32[]{:S(2)}, u32[]{:S(2)}) collective-permute-start(f32[10,128,512]{2,1,0:T(8,128)S(1)} %shard_map.86.own.refs_6_.refs_4_), channel_id=1, source_target_pairs={{0,1},{1,0},{2,3},{3,2},{4,5},{5,4},{6,7},{7,6},{8,9},{9,8},{10,11... | collective-permute-start | bytes 7864328 | tf_op jit(solution)/shard_map/ppermute | solution.py:315
  16.2 3.0 %collective-permute-done.8.next_far.far = f32[128,128]{1,0:T(8,128)S(1)} collective-permute-done((f32[128,128]{1,0:T(8,128)S(1)}, f32[128,128]{1,0:T(8,128)S(1)}, u32[]{:S(2)}, u32[]{:S(2)}) %collective-permute-start.8) | collective-permute-done | bytes 65568 | tf_op jit(solution)/shard_map/ppermute | solution.py:315
  22.2 1.8 %collective-permute-start.11 = (f32[128,128]{1,0:T(8,128)S(1)}, f32[128,128]{1,0:T(8,128)S(1)}, u32[]{:S(2)}, u32[]{:S(2)}) collective-permute-start(f32[128,128]{1,0:T(8,128)S(1)} %shard_map.90), channel_id=1, source_target_pairs={{0,1},{1,0},{2,3},{3,2},{4,5},{5,4},{6,7},{7,6},{8,9},{9,8},{10,11... | collective-permute-start | bytes 196616 | tf_op jit(solution)/shard_map/ppermute | solution.py:315
  25.1 1.6 %collective-permute-start.14 = (f32[128,128]{1,0:T(8,128)S(1)}, f32[128,128]{1,0:T(8,128)S(1)}, u32[]{:S(2)}, u32[]{:S(2)}) collective-permute-start(f32[128,128]{1,0:T(8,128)S(1)} %subtract_subtract_fusion.2.near), channel_id=1, source_target_pairs={{0,1},{1,0},{2,3},{3,2},{4,5},{5,4},{6,7},{7,6},{8,10},{9,11},{10,... | collective-permute-start | bytes 196616 | tf_op jit(solution)/shard_map/ppermute | solution.py:315
  27.9 4.0 %collective-permute-start.16 = (f32[128,128]{1,0:T(8,128)S(1)}, f32[128,128]{1,0:T(8,128)S(1)}, u32[]{:S(2)}, u32[]{:S(2)}) collective-permute-start(f32[128,128]{1,0:T(8,128)S(1)} %get-tuple-element.18), channel_id=1, source_target_pairs={{0,1},{1,0},{2,3},{3,2},{4,5},{5,4},{6,7},{7,6},{8,16},{9,17},{10,... | collective-permute-start | bytes 196616 | tf_op jit(solution)/shard_map/ppermute | solution.py:315
  34.7 1.8 %collective-permute-start.22 = (f32[128,128]{1,0:T(8,128)S(1)}, f32[128,128]{1,0:T(8,128)S(1)}, u32[]{:S(2)}, u32[]{:S(2)}) collective-permute-start(f32[128,128]{1,0:T(8,128)S(1)} %shard_map.94), channel_id=1, source_target_pairs={{0,12},{1,13},{2,14},{3,15},{4,5},{5,4},{6,7},{7,6},{8,0},{9,1},{1... | collective-permute-start | bytes 196616 | tf_op jit(solution)/shard_map/ppermute | solution.py:315
  36.7 3.5 %collective-permute-start.21 = (f32[128,128]{1,0:T(8,128)S(1)}, f32[128,128]{1,0:T(8,128)S(1)}, u32[]{:S(2)}, u32[]{:S(2)}) collective-permute-start(f32[128,128]{1,0:T(8,128)S(1)} %shard_map.93), channel_id=1, source_target_pairs={{0,6},{1,7},{2,4},{3,5},{4,12},{5,13},{6,14},{7,15},{8,9},{9,8},{1... | collective-permute-start | bytes 196616 | tf_op jit(solution)/shard_map/ppermute | solution.py:315
  40.9 1.4 %collective-permute-done.22.refs_4_ = f32[128,128]{1,0:T(8,128)S(1)} collective-permute-done((f32[128,128]{1,0:T(8,128)S(1)}, f32[128,128]{1,0:T(8,128)S(1)}, u32[]{:S(2)}, u32[]{:S(2)}) %collective-permute-start.22) | collective-permute-done | bytes 65568 | tf_op jit(solution)/shard_map/ppermute | solution.py:315
  42.3 2.8 %collective-permute-start.25 = (f32[128,128]{1,0:T(8,128)S(1)}, f32[128,128]{1,0:T(8,128)S(1)}, u32[]{:S(2)}, u32[]{:S(2)}) collective-permute-start(f32[128,128]{1,0:T(8,128)S(1)} %shard_map.97.part), channel_id=1, source_target_pairs={{0,18},{1,19},{2,16},{3,17},{4,5},{5,4},{6,7},{7,6},{8,9},{9,8},{1... | collective-permute-start | bytes 196616 | tf_op jit(solution)/shard_map/ppermute | solution.py:315
  45.2 2.5 %collective-permute-start.24 = (f32[128,128]{1,0:T(8,128)S(1)}, f32[128,128]{1,0:T(8,128)S(1)}, u32[]{:S(2)}, u32[]{:S(2)}) collective-permute-start(f32[128,128]{1,0:T(8,128)S(1)} %shard_map.97.part), channel_id=1, source_target_pairs={{0,16},{1,17},{2,18},{3,19},{4,0},{5,1},{6,2},{7,3},{8,9},{9,8},{1... | collective-permute-start | bytes 196616 | tf_op jit(solution)/shard_map/ppermute | solution.py:315
  48.6 2.3 %collective-permute-start.29 = (f32[128,128]{1,0:T(8,128)S(1)}, f32[128,128]{1,0:T(8,128)S(1)}, u32[]{:S(2)}, u32[]{:S(2)}) collective-permute-start(f32[128,128]{1,0:T(8,128)S(1)} %shard_map.98.other), channel_id=1, source_target_pairs={{0,1},{1,0},{2,3},{3,2},{4,5},{5,4},{6,7},{7,6},{8,30},{9,31},{10,... | collective-permute-start | bytes 196616 | tf_op jit(solution)/shard_map/ppermute | solution.py:315
  51.4 2.4 %collective-permute-start.26 = (f32[128,128]{1,0:T(8,128)S(1)}, f32[128,128]{1,0:T(8,128)S(1)}, u32[]{:S(2)}, u32[]{:S(2)}) collective-permute-start(f32[128,128]{1,0:T(8,128)S(1)} %shard_map.98.other), channel_id=1, source_target_pairs={{0,1},{1,0},{2,3},{3,2},{4,5},{5,4},{6,7},{7,6},{8,9},{9,8},{10,11... | collective-permute-start | bytes 196616 | tf_op jit(solution)/shard_map/ppermute | solution.py:315
  53.9 6.9 %collective-permute-done.26.refs_0_ = f32[128,128]{1,0:T(8,128)S(1)} collective-permute-done((f32[128,128]{1,0:T(8,128)S(1)}, f32[128,128]{1,0:T(8,128)S(1)}, u32[]{:S(2)}, u32[]{:S(2)}) %collective-permute-start.26) | collective-permute-done | bytes 65568 | tf_op jit(solution)/shard_map/ppermute | solution.py:315
  60.9 1.8 %collective-permute-start.34 = (f32[128,128]{1,0:T(8,128)S(1)}, f32[128,128]{1,0:T(8,128)S(1)}, u32[]{:S(2)}, u32[]{:S(2)}) collective-permute-start(f32[128,128]{1,0:T(8,128)S(1)} %shard_map.99.other), channel_id=1, source_target_pairs={{0,1},{1,0},{2,3},{3,2},{4,8},{5,9},{6,10},{7,11},{8,4},{9,5},{10,... | collective-permute-start | bytes 196616 | tf_op jit(solution)/shard_map/ppermute | solution.py:315
  62.7 1.2 %collective-permute-done.32.refs_0_ = f32[128,128]{1,0:T(8,128)S(1)} collective-permute-done((f32[128,128]{1,0:T(8,128)S(1)}, f32[128,128]{1,0:T(8,128)S(1)}, u32[]{:S(2)}, u32[]{:S(2)}) %collective-permute-start.32) | collective-permute-done | bytes 65568 | tf_op jit(solution)/shard_map/ppermute | solution.py:315
  64.4 1.4 %collective-permute-done.35.refs_3_ = f32[128,128]{1,0:T(8,128)S(1)} collective-permute-done((f32[128,128]{1,0:T(8,128)S(1)}, f32[128,128]{1,0:T(8,128)S(1)}, u32[]{:S(2)}, u32[]{:S(2)}) %collective-permute-start.35) | collective-permute-done | bytes 65568 | tf_op jit(solution)/shard_map/ppermute | solution.py:315
  65.8 1.5 %collective-permute-done.33.refs_1_ = f32[128,128]{1,0:T(8,128)S(1)} collective-permute-done((f32[128,128]{1,0:T(8,128)S(1)}, f32[128,128]{1,0:T(8,128)S(1)}, u32[]{:S(2)}, u32[]{:S(2)}) %collective-permute-start.33) | collective-permute-done | bytes 65568 | tf_op jit(solution)/shard_map/ppermute | solution.py:315
  67.3 1.4 %shard_map.100.mine = f32[128,128]{1,0:T(8,128)S(1)} custom-call(f32[128,128]{1,0:T(8,128)S(1)} %shard_map.97.part, f32[128,128]{1,0:T(8,128)S(1)} %shard_map.99.other, f32[128,128]{1,0:T(8,128)S(1)} %collective-permute-done.32.refs_0_, f32[128,128]{1,0:T(8,128)S(1)} %collective-permute-done.33.refs_1_, f32[128,128]{1,0:T(8,128)S(1)} %collective-permute-done.34.refs_2_, ...), custom_call_target="tpu_custom_call" | custom-call | flops 1000000000 | bytes 1 | tf_op jit(solution)/shard_map/pallas_call | solution.py:269
  68.7 4.2 %collective-permute-start.36 = (f32[128,128]{1,0:T(8,128)S(1)}, f32[128,128]{1,0:T(8,128)S(1)}, u32[]{:S(2)}, u32[]{:S(2)}) collective-permute-start(f32[128,128]{1,0:T(8,128)S(1)} %shard_map.100.mine), channel_id=1, source_target_pairs={{0,1},{1,0},{2,3},{3,2},{4,5},{5,4},{6,7},{7,6},{8,9},{9,8},{10,11... | collective-permute-start | bytes 196616 | tf_op jit(solution)/shard_map/ppermute | solution.py:315
  (92 shorter events, 19.9 us)
Async XLA Ops:
  3.5 5.5 %collective-permute-start.6 = (f32[128,128]{1,0:T(8,128)}, f32[128,128]{1,0:T(8,128)}, u32[]{:S(2)}, u32[]{:S(2)}) collective-permute-start(f32[128,128]{1,0:T(8,128)} %get-tuple-element.14), channel_id=1, source_target_pairs={{0,2},{1,3},{2,0},{3,1},{4,6},{5,7},{6,4},{7,5},{8,10},{9,11},{10,... | collective-permute-start | bytes 196616 | tf_op jit(solution)/shard_map/ppermute | solution.py:315
  4.8 5.4 %collective-permute-start.5 = (f32[1,128,512]{2,1,0:T(8,128)S(1)}, f32[1,128,512]{2,1,0:T(8,128)}, u32[]{:S(2)}, u32[]{:S(2)}) collective-permute-start(f32[1,128,512]{2,1,0:T(8,128)S(1)} %copy-done.5), channel_id=1, source_target_pairs={{0,1},{1,0},{2,3},{3,2},{4,5},{5,4},{6,7},{7,6},{8,9},{9,8},{10,11... | collective-permute-start | bytes 786440 | tf_op jit(solution)/shard_map/ppermute | solution.py:315
  5.4 5.8 %collective-permute-start.4 = (f32[128,128]{1,0:T(8,128)S(1)}, f32[128,128]{1,0:T(8,128)S(1)}, u32[]{:S(2)}, u32[]{:S(2)}) collective-permute-start(f32[128,128]{1,0:T(8,128)S(1)} %get-tuple-element.12.near), channel_id=1, source_target_pairs={{0,1},{1,0},{2,3},{3,2},{4,10},{5,11},{6,8},{7,9},{8,6},{9,7},{10,... | collective-permute-start | bytes 196616 | tf_op jit(solution)/shard_map/ppermute | solution.py:315
  6.6 5.1 %collective-permute-start.3 = (f32[128,128]{1,0:T(8,128)S(1)}, f32[128,128]{1,0:T(8,128)S(1)}, u32[]{:S(2)}, u32[]{:S(2)}) collective-permute-start(f32[128,128]{1,0:T(8,128)S(1)} %get-tuple-element.12.near), channel_id=1, source_target_pairs={{0,1},{1,0},{2,3},{3,2},{4,8},{5,9},{6,10},{7,11},{8,4},{9,5},{10,... | collective-permute-start | bytes 196616 | tf_op jit(solution)/shard_map/ppermute | solution.py:315
  7.7 4.0 %collective-permute-start.2 = (f32[128,128]{1,0:T(8,128)S(1)}, f32[128,128]{1,0:T(8,128)S(1)}, u32[]{:S(2)}, u32[]{:S(2)}) collective-permute-start(f32[128,128]{1,0:T(8,128)S(1)} %get-tuple-element.12.near), channel_id=1, source_target_pairs={{0,2},{1,3},{2,0},{3,1},{4,6},{5,7},{6,4},{7,5},{8,10},{9,11},{10,... | collective-permute-start | bytes 196616 | tf_op jit(solution)/shard_map/ppermute | solution.py:315
  9.8 4.0 %collective-permute-start.7 = (f32[128,128]{1,0:T(8,128)S(1)}, f32[128,128]{1,0:T(8,128)S(1)}, u32[]{:S(2)}, u32[]{:S(2)}) collective-permute-start(f32[128,128]{1,0:T(8,128)S(1)} %get-tuple-element.21), channel_id=1, source_target_pairs={{0,4},{1,5},{2,6},{3,7},{4,0},{5,1},{6,2},{7,3},{8,12},{9,13},{10,... | collective-permute-start | bytes 196616 | tf_op jit(solution)/shard_map/ppermute | solution.py:315
  14.1 6.0 %collective-permute-start.9 = (f32[10,128,512]{2,1,0:T(8,128)S(1)}, f32[10,128,512]{2,1,0:T(8,128)S(1)}, u32[]{:S(2)}, u32[]{:S(2)}) collective-permute-start(f32[10,128,512]{2,1,0:T(8,128)S(1)} %shard_map.86.own.refs_6_.refs_4_), channel_id=1, source_target_pairs={{0,1},{1,0},{2,3},{3,2},{4,5},{5,4},{6,7},{7,6},{8,9},{9,8},{10,11... | collective-permute-start | bytes 7864328 | tf_op jit(solution)/shard_map/ppermute | solution.py:315
  21.0 4.1 %collective-permute-start.13 = (f32[128,128]{1,0:T(8,128)S(1)}, f32[128,128]{1,0:T(8,128)S(1)}, u32[]{:S(2)}, u32[]{:S(2)}) collective-permute-start(f32[128,128]{1,0:T(8,128)S(1)} %get-tuple-element.15.values), channel_id=1, source_target_pairs={{0,12},{1,13},{2,14},{3,15},{4,5},{5,4},{6,7},{7,6},{8,0},{9,1},{1... | collective-permute-start | bytes 196616 | tf_op jit(solution)/shard_map/ppermute | solution.py:315
  21.1 4.0 %collective-permute-start.12 = (f32[128,128]{1,0:T(8,128)S(1)}, f32[128,128]{1,0:T(8,128)S(1)}, u32[]{:S(2)}, u32[]{:S(2)}) collective-permute-start(f32[128,128]{1,0:T(8,128)S(1)} %get-tuple-element.16.values), channel_id=1, source_target_pairs={{0,4},{1,5},{2,6},{3,7},{4,8},{5,9},{6,10},{7,11},{8,0},{9,1},{10,... | collective-permute-start | bytes 196616 | tf_op jit(solution)/shard_map/ppermute | solution.py:315
  22.2 10.7 %collective-permute-start.11 = (f32[128,128]{1,0:T(8,128)S(1)}, f32[128,128]{1,0:T(8,128)S(1)}, u32[]{:S(2)}, u32[]{:S(2)}) collective-permute-start(f32[128,128]{1,0:T(8,128)S(1)} %shard_map.90), channel_id=1, source_target_pairs={{0,1},{1,0},{2,3},{3,2},{4,5},{5,4},{6,7},{7,6},{8,9},{9,8},{10,11... | collective-permute-start | bytes 196616 | tf_op jit(solution)/shard_map/ppermute | solution.py:315
  26.7 6.2 %collective-permute-start.10 = (f32[128,128]{1,0:T(8,128)S(1)}, f32[128,128]{1,0:T(8,128)S(1)}, u32[]{:S(2)}, u32[]{:S(2)}) collective-permute-start(f32[128,128]{1,0:T(8,128)S(1)} %shard_map.89), channel_id=1, source_target_pairs={{0,12},{1,13},{2,14},{3,15},{4,0},{5,1},{6,2},{7,3},{8,9},{9,8},{1... | collective-permute-start | bytes 196616 | tf_op jit(solution)/shard_map/ppermute | solution.py:315
  27.6 7.2 %collective-permute-start.18 = (f32[128,128]{1,0:T(8,128)S(1)}, f32[128,128]{1,0:T(8,128)S(1)}, u32[]{:S(2)}, u32[]{:S(2)}) collective-permute-start(f32[128,128]{1,0:T(8,128)S(1)} %get-tuple-element.18), channel_id=1, source_target_pairs={{0,1},{1,0},{2,3},{3,2},{4,8},{5,9},{6,10},{7,11},{8,18},{9,19},{1... | collective-permute-start | bytes 196616 | tf_op jit(solution)/shard_map/ppermute | solution.py:315
  27.9 8.7 %collective-permute-start.16 = (f32[128,128]{1,0:T(8,128)S(1)}, f32[128,128]{1,0:T(8,128)S(1)}, u32[]{:S(2)}, u32[]{:S(2)}) collective-permute-start(f32[128,128]{1,0:T(8,128)S(1)} %get-tuple-element.18), channel_id=1, source_target_pairs={{0,1},{1,0},{2,3},{3,2},{4,5},{5,4},{6,7},{7,6},{8,16},{9,17},{10,... | collective-permute-start | bytes 196616 | tf_op jit(solution)/shard_map/ppermute | solution.py:315
  32.0 4.6 %collective-permute-start.19 = (f32[128,128]{1,0:T(8,128)S(1)}, f32[128,128]{1,0:T(8,128)S(1)}, u32[]{:S(2)}, u32[]{:S(2)}) collective-permute-start(f32[128,128]{1,0:T(8,128)S(1)} %get-tuple-element.17.refs_2_.values), channel_id=1, source_target_pairs={{0,1},{1,0},{2,3},{3,2},{4,5},{5,4},{6,7},{7,6},{8,9},{9,8},{10,11... | collective-permute-start | bytes 196616 | tf_op jit(solution)/shard_map/ppermute | solution.py:315
  34.4 6.5 %collective-permute-start.23 = (f32[128,128]{1,0:T(8,128)S(1)}, f32[128,128]{1,0:T(8,128)S(1)}, u32[]{:S(2)}, u32[]{:S(2)}) collective-permute-start(f32[128,128]{1,0:T(8,128)S(1)} %shard_map.94), channel_id=1, source_target_pairs={{0,22},{1,23},{2,20},{3,21},{4,5},{5,4},{6,7},{7,6},{8,2},{9,3},{1... | collective-permute-start | bytes 196616 | tf_op jit(solution)/shard_map/ppermute | solution.py:315
  34.7 7.6 %collective-permute-start.22 = (f32[128,128]{1,0:T(8,128)S(1)}, f32[128,128]{1,0:T(8,128)S(1)}, u32[]{:S(2)}, u32[]{:S(2)}) collective-permute-start(f32[128,128]{1,0:T(8,128)S(1)} %shard_map.94), channel_id=1, source_target_pairs={{0,12},{1,13},{2,14},{3,15},{4,5},{5,4},{6,7},{7,6},{8,0},{9,1},{1... | collective-permute-start | bytes 196616 | tf_op jit(solution)/shard_map/ppermute | solution.py:315
  36.7 5.7 %collective-permute-start.21 = (f32[128,128]{1,0:T(8,128)S(1)}, f32[128,128]{1,0:T(8,128)S(1)}, u32[]{:S(2)}, u32[]{:S(2)}) collective-permute-start(f32[128,128]{1,0:T(8,128)S(1)} %shard_map.93), channel_id=1, source_target_pairs={{0,6},{1,7},{2,4},{3,5},{4,12},{5,13},{6,14},{7,15},{8,9},{9,8},{1... | collective-permute-start | bytes 196616 | tf_op jit(solution)/shard_map/ppermute | solution.py:315
  42.3 5.9 %collective-permute-start.25 = (f32[128,128]{1,0:T(8,128)S(1)}, f32[128,128]{1,0:T(8,128)S(1)}, u32[]{:S(2)}, u32[]{:S(2)}) collective-permute-start(f32[128,128]{1,0:T(8,128)S(1)} %shard_map.97.part), channel_id=1, source_target_pairs={{0,18},{1,19},{2,16},{3,17},{4,5},{5,4},{6,7},{7,6},{8,9},{9,8},{1... | collective-permute-start | bytes 196616 | tf_op jit(solution)/shard_map/ppermute | solution.py:315
  47.7 6.1 %collective-permute-start.30 = (f32[128,128]{1,0:T(8,128)S(1)}, f32[128,128]{1,0:T(8,128)S(1)}, u32[]{:S(2)}, u32[]{:S(2)}) collective-permute-start(f32[128,128]{1,0:T(8,128)S(1)} %shard_map.97.part), channel_id=1, source_target_pairs={{0,8},{1,9},{2,10},{3,11},{4,5},{5,4},{6,7},{7,6},{8,20},{9,21},{1... | collective-permute-start | bytes 196616 | tf_op jit(solution)/shard_map/ppermute | solution.py:315
  48.6 5.2 %collective-permute-start.29 = (f32[128,128]{1,0:T(8,128)S(1)}, f32[128,128]{1,0:T(8,128)S(1)}, u32[]{:S(2)}, u32[]{:S(2)}) collective-permute-start(f32[128,128]{1,0:T(8,128)S(1)} %shard_map.98.other), channel_id=1, source_target_pairs={{0,1},{1,0},{2,3},{3,2},{4,5},{5,4},{6,7},{7,6},{8,30},{9,31},{10,... | collective-permute-start | bytes 196616 | tf_op jit(solution)/shard_map/ppermute | solution.py:315
  51.4 9.3 %collective-permute-start.26 = (f32[128,128]{1,0:T(8,128)S(1)}, f32[128,128]{1,0:T(8,128)S(1)}, u32[]{:S(2)}, u32[]{:S(2)}) collective-permute-start(f32[128,128]{1,0:T(8,128)S(1)} %shard_map.98.other), channel_id=1, source_target_pairs={{0,1},{1,0},{2,3},{3,2},{4,5},{5,4},{6,7},{7,6},{8,9},{9,8},{10,11... | collective-permute-start | bytes 196616 | tf_op jit(solution)/shard_map/ppermute | solution.py:315
  60.8 5.0 %collective-permute-start.35 = (f32[128,128]{1,0:T(8,128)S(1)}, f32[128,128]{1,0:T(8,128)S(1)}, u32[]{:S(2)}, u32[]{:S(2)}) collective-permute-start(f32[128,128]{1,0:T(8,128)S(1)} %shard_map.99.other), channel_id=1, source_target_pairs={{0,1},{1,0},{2,3},{3,2},{4,10},{5,11},{6,8},{7,9},{8,6},{9,7},{10,... | collective-permute-start | bytes 196616 | tf_op jit(solution)/shard_map/ppermute | solution.py:315
  60.9 5.0 %collective-permute-start.34 = (f32[128,128]{1,0:T(8,128)S(1)}, f32[128,128]{1,0:T(8,128)S(1)}, u32[]{:S(2)}, u32[]{:S(2)}) collective-permute-start(f32[128,128]{1,0:T(8,128)S(1)} %shard_map.99.other), channel_id=1, source_target_pairs={{0,1},{1,0},{2,3},{3,2},{4,8},{5,9},{6,10},{7,11},{8,4},{9,5},{10,... | collective-permute-start | bytes 196616 | tf_op jit(solution)/shard_map/ppermute | solution.py:315
  68.7 5.1 %collective-permute-start.36 = (f32[128,128]{1,0:T(8,128)S(1)}, f32[128,128]{1,0:T(8,128)S(1)}, u32[]{:S(2)}, u32[]{:S(2)}) collective-permute-start(f32[128,128]{1,0:T(8,128)S(1)} %shard_map.100.mine), channel_id=1, source_target_pairs={{0,1},{1,0},{2,3},{3,2},{4,5},{5,4},{6,7},{7,6},{8,9},{9,8},{10,11... | collective-permute-start | bytes 196616 | tf_op jit(solution)/shard_map/ppermute | solution.py:315
  (21 other events, 96.8 us)

commit v9 on v8

--- a/solution.py
+++ b/solution.py
@@ -104,17 +104,6 @@
         depth = source.shape[0]
         out[place : place + depth] = source[...]
         place += depth
-
-
-def reduce_kernel(spacing, count, base, *refs):
-    out = refs[-1]
-    less, *more = refs[:count]
-    s = lax.axis_index("slab")
-    kept = s % (4 * spacing) == 0
-    values = base[...] - keep(kept, less)
-    for late in more:
-        values = values - keep(kept & (s > 0), late)
-    out[...] = values
 
 
 def open_kernel(mine, other, side, own, mate, psi, near, far, store):
@@ -140,6 +129,34 @@
         out[...] = half_step * rotate(pair.T)
 
 
+def cross_kernel(packed, near, other, up, crossing):
+    whole = near[...] + other[...]
+    up[...] = whole
+    crossing[...] = jnp.where(lax.axis_index("slab") % 2 == 1, packed[...], whole)
+
+
+def near_kernel(rest, stepped, near, crossing):
+    whole = rest[...] - stepped[...]
+    near[...] = whole
+    crossing[...] = jnp.where(lax.axis_index("slab") % 2 == 1, whole, stepped[...])
+
+
+def urgent_kernel(base, more, less, out):
+    kept = lax.axis_index("slab") % 4 == 2
+    out[...] = base[...] - keep(kept, more) - keep(kept, less)
+
+
+def reduce_kernel(spacing, count, base, *refs):
+    out = refs[-1]
+    less, *more = refs[:count]
+    s = lax.axis_index("slab")
+    kept = s % (4 * spacing) == 0
+    values = base[...] - keep(kept, less)
+    for late in more:
+        values = values - keep(kept & (s > 0), late)
+    out[...] = values
+
+
 def ham_kernel(slabs, near, far, next_near, next_far, own_e, mate_e, own_t, mate_t, *refs):
     out, here, there = refs[-3:]
     s = lax.axis_index("slab")
@@ -178,7 +195,8 @@
         beneath[...] = complex_product(own[0:2], mate[0:2], store)
 
 
-def pivot_kernel(spacing, near, far, own, mate, before, out, store):
+def pivot_kernel(spacing, near, far, own, mate, before, *refs):
+    out, store = refs[-2:]
     active = lax.axis_index("slab") % (2 * spacing) == spacing
 
     @pl.when(active)
@@ -298,8 +316,6 @@
     store = pltpu.VMEM((width, LANES), short)
     levels = slabs.bit_length() - 1
     every = range(slabs)
-    s = lax.axis_index("slab")
-    odd = s % 2 == 1
 
     def send(values, moves, flip=0):
         route = []
@@ -338,10 +354,10 @@
     psi, up_near, up_far = call(
         open_kernel, waves, mate_waves, side, *t_pair, outs=3, scratch=[pltpu.VMEM((64, width), wide)]
     )
-    up = up_near + exchange(up_far)
+    up, crossing = call(cross_kernel, psi, up_near, exchange(up_far), outs=2)
     psi_far = exchange(psi)
     between = [(a, b) for k in every[1:-1:2] for a, b in ((k, k + 1), (k + 1, k))]
-    stepped = send(jnp.where(odd, psi, up), [(a, a ^ 1) for a in every])
+    stepped = send(crossing, [(a, a ^ 1) for a in every])
     rest = call(
         kernel(ham_kernel, slabs),
         psi,
@@ -352,8 +368,8 @@
         scratch=[store, store],
         unused=(up,),
     )
-    near = rest - stepped
-    far = exchange(jnp.where(odd, near, stepped))
+    near, crossing = call(near_kernel, rest, stepped, outs=2)
+    far = exchange(crossing)
     blocks = below[0], above[0], pivots[0], back_lower[0], back_upper[0]
     front = stack(*blocks, after=near)
     front = front, swap(front)
@@ -365,7 +381,7 @@
         d = 2**level
         if level == levels - 1:
             beneath = call(kernel(top_kernel, d), near, far, *front, scratch=[store])
-            shares = both(beneath, [(d, 0, 1, d + 1)], [(d, 0, 1, d - 1)])
+            shares = both(beneath, [(d, 0, 1, d + 1)], [(d, 0, 1, d + 1)])
             if level > 1:
                 shares = shares + late
             pivot = call(kernel(pivot_kernel, d), near, far, *back, pivot, scratch=[store])
@@ -389,43 +405,51 @@
             up if level == 0 else jnp.zeros_like(up),
             outs=2,
             scratch=[store],
+            unused=(base,) if level == 1 else (),
         )
         if level == 0:
             more = send(over, [(b - 1, b, b - 2) for b in urgent])
             less = send(beneath, [(b + 1, b, b - 2) for b in urgent])
-            pivot = call(kernel(pivot_kernel, d), near, far, *back, pivot, scratch=[store])
-            held = call(copy_kernel, beneath, unused=(pivot,))
+            pivot = call(
+                kernel(pivot_kernel, d),
+                near,
+                far,
+                *back,
+                pivot,
+                scratch=[store],
+                unused=(over,),
+                flops=1,
+            )
+            held = call(copy_kernel, beneath, unused=(pivot,), flops=1)
             late = [send(held, [(b + 1, b, b + 3) for b in patient])]
             if len(patient) > 1:
-                held = call(copy_kernel, over, unused=(pivot,))
-                late.append(send(held, [(b - 1, b, b + 1) for b in patient if b > 0]))
-            near = base - more - less
+                held = call(copy_kernel, over, unused=(pivot,), flops=1)
+                ways = [(b - 1, b, b + 1 if b + 4 < slabs else b + 3) for b in patient if b > 0]
+                late.append(send(held, ways))
+            near = call(urgent_kernel, base, more, less)
             far = exchange(near, urgent)
+            base = call(kernel(reduce_kernel, d, len(late)), base, *late, unused=(near,))
+            base_far = exchange(base, patient)
             continue
         more = both(over, [(b - d, b, b - 1) for b in urgent], [(b - d, b, b - 3) for b in urgent])
         less = both(
             beneath, [(b + d, b, b + 1) for b in urgent], [(b + d, b, b + 3) for b in urgent]
         )
         pivot = call(kernel(pivot_kernel, d), near, far, *back, pivot, scratch=[store])
-        if level == 1:
-            base = call(kernel(reduce_kernel, 1, len(late)), base, *late, unused=(beneath,))
-            base_far = exchange(base, [a for a in every if a % 4 == 0])
-        else:
-            is_late = s % (2 * d) == 0
-            for n, share in enumerate(late):
-                share = jnp.where(is_late & ((s > 0) | (n < 2)), share, 0.0)
-                if n % 2 == 0:
-                    base = base - share
-                else:
-                    base_far = base_far - share
+        if level > 1:
+            count = len(late) // 2
+            base = call(kernel(reduce_kernel, d // 2, count), base, *late[::2], unused=(beneath,))
+            base_far = call(
+                kernel(reduce_kernel, d // 2, count), base_far, *late[1::2], unused=(beneath,)
+            )
         near = base - more[0] - less[0]
         far = base_far - more[1] - less[1]
-        held = call(copy_kernel, beneath, unused=(base_far,))
+        held = call(copy_kernel, beneath, unused=(more[0],))
         late = both(
             held, [(b + d, b, b + d + 1) for b in patient], [(b + d, b, b + d + 3) for b in patient]
         )
         if len(patient) > 1:
-            held = call(copy_kernel, over, unused=(base_far,))
+            held = call(copy_kernel, over, unused=(more[0],))
             late = late + both(
                 held,
                 [(b - d, b, b - d + 1) for b in patient if b > 0],
@@ -445,28 +469,22 @@
             low_far = exchange(low_near, [a + 1 for a in sources])
             vectors = low_near, low_far, up_near, up_far
         elif level == levels - 1:
-            vectors = both(solved, [(0, d, d + 1, 1)], [(0, d, d + 1, 3)])
+            vectors = both(solved, [(0, d, d + 1, 1)], [(0, d, d + 1, 1)])
         else:
             sources = [a for a in every if a % (4 * d) == 2 * d]
-            up_near = send(solved, [(a, a - d, a + 1) for a in sources])
-            low_near = send(solved, [(a, a + d, a - 1) for a in sources])
-            up_far = send(solved, [(a, a - d, a + 3) for a in sources], 2)
-            low_far = send(solved, [(a, a + d, a - 3) for a in sources], 2)
+            ways = [(a, a - d, a - d + 1, a + 1) for a in sources]
+            up_near, up_far = both(solved, ways, ways)
+            ways = [(a, a + d, a + d + 1, a + 1) for a in sources]
+            low_near, low_far = both(solved, ways, ways)
             vectors = (low_near, low_far, up_near, up_far) + early
         if level > 1:
             half = d // 2
             sources = [a for a in every if a % (2 * d) == 0]
-            early = both(
-                solved,
-                [(a, a + half, a + 2 * half + 1) for a in sources],
-                [(a, a + half, a + 2 * half + 3) for a in sources],
-            )
+            ways = [(a, a + half, a + half + 1, a + 1) for a in sources]
+            early = both(solved, ways, ways)
             if len(sources) > 1:
-                early += both(
-                    solved,
-                    [(a, a - half, a - 2 * half + 1) for a in sources if a > 0],
-                    [(a, a - half, a - 2 * half + 3) for a in sources if a > 0],
-                )
+                ways = [(a, a - half, a - half + 1, a + 1) for a in sources if a > 0]
+                early += both(solved, ways, ways)
         if level == levels - 1 and levels > 1:
             solved = call(kernel(settle_kernel, d), pivot, *vectors, *back, scratch=[store])
         else:

time: 74.7 us -> 72.1 us (0.965)
  waiting for transfers between devices: 23.3 us -> 21 us
  Pallas kernels: 7.28 us -> 5.77 us
  local copies, waits for them, and re-layouts: 0.04 us -> 1.3 us
  starting transfers between devices: 42.7 us -> 43.6 us
  other arithmetic: 0.91 us -> 0.03 us
    ppermute x37, waiting for transfers between devices: 23.3 us -> 21 us  [send(): lax.ppermute(values, ('slab', 'col'), completed(route, slabs * cols, cols))]
    pallas_call x20 -> x23, Pallas kernels: 7.28 us -> 5.77 us  [call(): pl.pallas_call(kernel, out_shape=shape if outs == 1 else (shape,) * outs,...]
    unnamed x16, local copies, waits for them, and re-layouts: 0.03 us -> 1.3 us
    select_n x2 -> x0, other arithmetic: 0.87 us -> none  [the longest x1 0.85 us: per_device(): stepped = send(jnp.where(odd, psi, up), [(a, a ^ 1) for a in every])]
    ppermute x37, starting transfers between devices: 42.7 us -> 43.6 us  [send(): lax.ppermute(values, ('slab', 'col'), completed(route, slabs * cols, cols))]
  transfers between devices with their start and end apart: 37 -> 37, of which waited for: 15 -> 19; matrix products, arithmetic and copies ran while one was open for 1% -> 0% of each run, Pallas kernels for 4% -> 4%
where the time goes in v9:
time: 72.1 us; the launch traced here: 72 us
  starting transfers between devices  43.6 us (60%)
  waiting for transfers between devices  21 us (29%)
  Pallas kernels  5.77 us (8%)
  local copies, waits for them, and re-layouts  1.3 us (2%)
    ppermute x37, starting transfers between devices, send(): lax.ppermute(values, ('slab', 'col'), completed(route, slabs * cols, cols))  43.6 us
    ppermute x37, waiting for transfers between devices, send(): lax.ppermute(values, ('slab', 'col'), completed(route, slabs * cols, cols))  21 us
    pallas_call x23, Pallas kernels, call(): pl.pallas_call(kernel, out_shape=shape if outs == 1 else (shape,) * outs,...  5.77 us
  transfers between devices with their start and end apart: 37, of which 19 were waited for; matrix products, arithmetic and copies ran while one was open for 0% of the time, Pallas kernels for 4%

profile of v9, /device:TPU:13, one launch (start us, length us, event | category | flops | bytes accessed | tf_op | source)
XLA Modules:
  0.0 72.0 jit_solution(1618551481102405951)
XLA Ops:
  2.8 1.3 %collective-permute-start.6 = (f32[128,128]{1,0:T(8,128)S(1)}, f32[128,128]{1,0:T(8,128)S(1)}, u32[]{:S(2)}, u32[]{:S(2)}) collective-permute-start(f32[128,128]{1,0:T(8,128)S(1)} %get-tuple-element.18), channel_id=1, source_target_pairs={{0,2},{1,3},{2,0},{3,1},{4,6},{5,7},{6,4},{7,5},{8,10},{9,11},{10,... | collective-permute-start | bytes 196616 | tf_op jit(solution)/shard_map/ppermute | solution.py:331
  4.1 1.2 %collective-permute-start.4 = (f32[128,128]{1,0:T(8,128)S(1)}, f32[128,128]{1,0:T(8,128)S(1)}, u32[]{:S(2)}, u32[]{:S(2)}) collective-permute-start(f32[128,128]{1,0:T(8,128)S(1)} %get-tuple-element.16.packed.near), channel_id=1, source_target_pairs={{0,1},{1,0},{2,3},{3,2},{4,10},{5,11},{6,8},{7,9},{8,6},{9,7},{10,... | collective-permute-start | bytes 196616 | tf_op jit(solution)/shard_map/ppermute | solution.py:331
  5.3 1.1 %collective-permute-start.3 = (f32[128,128]{1,0:T(8,128)S(1)}, f32[128,128]{1,0:T(8,128)S(1)}, u32[]{:S(2)}, u32[]{:S(2)}) collective-permute-start(f32[128,128]{1,0:T(8,128)S(1)} %get-tuple-element.16.packed.near), channel_id=1, source_target_pairs={{0,1},{1,0},{2,3},{3,2},{4,8},{5,9},{6,10},{7,11},{8,4},{9,5},{10,... | collective-permute-start | bytes 196616 | tf_op jit(solution)/shard_map/ppermute | solution.py:331
  6.5 1.2 %collective-permute-start.2 = (f32[128,128]{1,0:T(8,128)S(1)}, f32[128,128]{1,0:T(8,128)S(1)}, u32[]{:S(2)}, u32[]{:S(2)}) collective-permute-start(f32[128,128]{1,0:T(8,128)S(1)} %get-tuple-element.16.packed.near), channel_id=1, source_target_pairs={{0,2},{1,3},{2,0},{3,1},{4,6},{5,7},{6,4},{7,5},{8,10},{9,11},{10,... | collective-permute-start | bytes 196616 | tf_op jit(solution)/shard_map/ppermute | solution.py:331
  8.0 1.2 %collective-permute-done.4.next_far = f32[128,128]{1,0:T(8,128)S(1)} collective-permute-done((f32[128,128]{1,0:T(8,128)S(1)}, f32[128,128]{1,0:T(8,128)S(1)}, u32[]{:S(2)}, u32[]{:S(2)}) %collective-permute-start.4) | collective-permute-done | bytes 65568 | tf_op jit(solution)/shard_map/ppermute | solution.py:331
  13.3 1.6 %collective-permute-start.9 = (f32[10,128,512]{2,1,0:T(8,128)S(1)}, f32[10,128,512]{2,1,0:T(8,128)S(1)}, u32[]{:S(2)}, u32[]{:S(2)}) collective-permute-start(f32[10,128,512]{2,1,0:T(8,128)S(1)} %shard_map.88.own.refs_6_.refs_4_), channel_id=1, source_target_pairs={{0,1},{1,0},{2,3},{3,2},{4,5},{5,4},{6,7},{7,6},{8,9},{9,8},{10,11... | collective-permute-start | bytes 7864328 | tf_op jit(solution)/shard_map/ppermute | solution.py:331
  15.0 1.2 %collective-permute-start.8 = (f32[128,128]{1,0:T(8,128)S(1)}, f32[128,128]{1,0:T(8,128)S(1)}, u32[]{:S(2)}, u32[]{:S(2)}) collective-permute-start(f32[128,128]{1,0:T(8,128)S(1)} %get-tuple-element.21), channel_id=1, source_target_pairs={{0,2},{1,3},{2,0},{3,1},{4,6},{5,7},{6,4},{7,5},{8,10},{9,11},{10,... | collective-permute-start | bytes 196616 | tf_op jit(solution)/shard_map/ppermute | solution.py:331
  16.2 2.5 %collective-permute-done.8.next_far.far = f32[128,128]{1,0:T(8,128)S(1)} collective-permute-done((f32[128,128]{1,0:T(8,128)S(1)}, f32[128,128]{1,0:T(8,128)S(1)}, u32[]{:S(2)}, u32[]{:S(2)}) %collective-permute-start.8) | collective-permute-done | bytes 65568 | tf_op jit(solution)/shard_map/ppermute | solution.py:331
  21.7 2.3 %collective-permute-start.11 = (f32[128,128]{1,0:T(8,128)S(1)}, f32[128,128]{1,0:T(8,128)S(1)}, u32[]{:S(2)}, u32[]{:S(2)}) collective-permute-start(f32[128,128]{1,0:T(8,128)S(1)} %shard_map.92), channel_id=1, source_target_pairs={{0,1},{1,0},{2,3},{3,2},{4,5},{5,4},{6,7},{7,6},{8,9},{9,8},{10,11... | collective-permute-start | bytes 196616 | tf_op jit(solution)/shard_map/ppermute | solution.py:331
  24.5 1.6 %collective-permute-start.15 = (f32[128,128]{1,0:T(8,128)S(1)}, f32[128,128]{1,0:T(8,128)S(1)}, u32[]{:S(2)}, u32[]{:S(2)}) collective-permute-start(f32[128,128]{1,0:T(8,128)S(1)} %shard_map.93.refs_2_.near), channel_id=1, source_target_pairs={{0,1},{1,0},{2,3},{3,2},{4,5},{5,4},{6,7},{7,6},{8,10},{9,11},{10,... | collective-permute-start | bytes 196616 | tf_op jit(solution)/shard_map/ppermute | solution.py:331
  26.2 1.8 %collective-permute-done.10.refs_0_ = f32[128,128]{1,0:T(8,128)S(1)} collective-permute-done((f32[128,128]{1,0:T(8,128)S(1)}, f32[128,128]{1,0:T(8,128)S(1)}, u32[]{:S(2)}, u32[]{:S(2)}) %collective-permute-start.10) | collective-permute-done | bytes 65568 | tf_op jit(solution)/shard_map/ppermute | solution.py:331
  28.0 1.9 %collective-permute-start.14 = (f32[128,128]{1,0:T(8,128)S(1)}, f32[128,128]{1,0:T(8,128)S(1)}, u32[]{:S(2)}, u32[]{:S(2)}) collective-permute-start(f32[128,128]{1,0:T(8,128)S(1)} %shard_map.94.refs_0_), channel_id=1, source_target_pairs={{0,2},{1,3},{2,0},{3,1},{4,5},{5,4},{6,7},{7,6},{8,9},{9,8},{10,11... | collective-permute-start | bytes 196616 | tf_op jit(solution)/shard_map/ppermute | solution.py:331
  30.9 1.7 %collective-permute-start.19 = (f32[128,128]{1,0:T(8,128)S(1)}, f32[128,128]{1,0:T(8,128)S(1)}, u32[]{:S(2)}, u32[]{:S(2)}) collective-permute-start(f32[128,128]{1,0:T(8,128)S(1)} %get-tuple-element.26.values), channel_id=1, source_target_pairs={{0,1},{1,0},{2,3},{3,2},{4,5},{5,4},{6,7},{7,6},{8,9},{9,8},{10,11... | collective-permute-start | bytes 196616 | tf_op jit(solution)/shard_map/ppermute | solution.py:331
  32.6 3.0 %collective-permute-done.16.refs_0_ = f32[128,128]{1,0:T(8,128)S(1)} collective-permute-done((f32[128,128]{1,0:T(8,128)S(1)}, f32[128,128]{1,0:T(8,128)S(1)}, u32[]{:S(2)}, u32[]{:S(2)}) %collective-permute-start.16) | collective-permute-done | bytes 65568 | tf_op jit(solution)/shard_map/ppermute | solution.py:331
  36.6 1.3 %collective-permute-start.21 = (f32[128,128]{1,0:T(8,128)S(1)}, f32[128,128]{1,0:T(8,128)S(1)}, u32[]{:S(2)}, u32[]{:S(2)}) collective-permute-start(f32[128,128]{1,0:T(8,128)S(1)} %shard_map.96), channel_id=1, source_target_pairs={{0,6},{1,7},{2,4},{3,5},{4,20},{5,21},{6,22},{7,23},{8,9},{9,8},{1... | collective-permute-start | bytes 196616 | tf_op jit(solution)/shard_map/ppermute | solution.py:331
  37.9 3.6 %collective-permute-done.22.refs_4_ = f32[128,128]{1,0:T(8,128)S(1)} collective-permute-done((f32[128,128]{1,0:T(8,128)S(1)}, f32[128,128]{1,0:T(8,128)S(1)}, u32[]{:S(2)}, u32[]{:S(2)}) %collective-permute-start.22) | collective-permute-done | bytes 65568 | tf_op jit(solution)/shard_map/ppermute | solution.py:331
  42.6 3.9 %collective-permute-start.31 = (f32[128,128]{1,0:T(8,128)S(1)}, f32[128,128]{1,0:T(8,128)S(1)}, u32[]{:S(2)}, u32[]{:S(2)}) collective-permute-start(f32[128,128]{1,0:T(8,128)S(1)} %shard_map.100.part), channel_id=1, source_target_pairs={{0,10},{1,11},{2,8},{3,9},{4,0},{5,1},{6,2},{7,3},{8,14},{9,15},{1... | collective-permute-start | bytes 196616 | tf_op jit(solution)/shard_map/ppermute | solution.py:331
  46.5 2.3 %collective-permute-start.30 = (f32[128,128]{1,0:T(8,128)S(1)}, f32[128,128]{1,0:T(8,128)S(1)}, u32[]{:S(2)}, u32[]{:S(2)}) collective-permute-start(f32[128,128]{1,0:T(8,128)S(1)} %shard_map.100.part), channel_id=1, source_target_pairs={{0,8},{1,9},{2,10},{3,11},{4,0},{5,1},{6,2},{7,3},{8,12},{9,13},{1... | collective-permute-start | bytes 196616 | tf_op jit(solution)/shard_map/ppermute | solution.py:331
  49.3 3.4 %collective-permute-start.28 = (f32[128,128]{1,0:T(8,128)S(1)}, f32[128,128]{1,0:T(8,128)S(1)}, u32[]{:S(2)}, u32[]{:S(2)}) collective-permute-start(f32[128,128]{1,0:T(8,128)S(1)} %shard_map.101.other), channel_id=1, source_target_pairs={{0,1},{1,0},{2,3},{3,2},{4,5},{5,4},{6,7},{7,6},{8,12},{9,13},{10,... | collective-permute-start | bytes 196616 | tf_op jit(solution)/shard_map/ppermute | solution.py:331
  52.6 3.1 %collective-permute-start.27 = (f32[128,128]{1,0:T(8,128)S(1)}, f32[128,128]{1,0:T(8,128)S(1)}, u32[]{:S(2)}, u32[]{:S(2)}) collective-permute-start(f32[128,128]{1,0:T(8,128)S(1)} %shard_map.101.other), channel_id=1, source_target_pairs={{0,1},{1,0},{2,3},{3,2},{4,5},{5,4},{6,7},{7,6},{8,9},{9,8},{10,11... | collective-permute-start | bytes 196616 | tf_op jit(solution)/shard_map/ppermute | solution.py:331
  57.8 2.1 %collective-permute-start.34 = (f32[128,128]{1,0:T(8,128)S(1)}, f32[128,128]{1,0:T(8,128)S(1)}, u32[]{:S(2)}, u32[]{:S(2)}) collective-permute-start(f32[128,128]{1,0:T(8,128)S(1)} %shard_map.102.other), channel_id=1, source_target_pairs={{0,1},{1,0},{2,3},{3,2},{4,8},{5,9},{6,10},{7,11},{8,4},{9,5},{10,... | collective-permute-start | bytes 196616 | tf_op jit(solution)/shard_map/ppermute | solution.py:331
  60.6 1.8 %collective-permute-done.35.refs_3_ = f32[128,128]{1,0:T(8,128)S(1)} collective-permute-done((f32[128,128]{1,0:T(8,128)S(1)}, f32[128,128]{1,0:T(8,128)S(1)}, u32[]{:S(2)}, u32[]{:S(2)}) %collective-permute-start.35) | collective-permute-done | bytes 65568 | tf_op jit(solution)/shard_map/ppermute | solution.py:331
  63.3 1.4 %shard_map.103.mine = f32[128,128]{1,0:T(8,128)S(1)} custom-call(f32[128,128]{1,0:T(8,128)S(1)} %shard_map.100.part, f32[128,128]{1,0:T(8,128)S(1)} %shard_map.102.other, f32[128,128]{1,0:T(8,128)S(1)} %collective-permute-done.32.refs_0_, f32[128,128]{1,0:T(8,128)S(1)} %collective-permute-done.33.refs_1_, f32[128,128]{1,0:T(8,128)S(1)} %collective-permute-done.34.refs_2_, ...), custom_call_target="tpu_custom_call" | custom-call | flops 1000000000 | bytes 1 | tf_op jit(solution)/shard_map/pallas_call | solution.py:287
  64.7 5.7 %collective-permute-start.36 = (f32[128,128]{1,0:T(8,128)S(1)}, f32[128,128]{1,0:T(8,128)S(1)}, u32[]{:S(2)}, u32[]{:S(2)}) collective-permute-start(f32[128,128]{1,0:T(8,128)S(1)} %shard_map.103.mine), channel_id=1, source_target_pairs={{0,1},{1,0},{2,3},{3,2},{4,5},{5,4},{6,7},{7,6},{8,9},{9,8},{10,11... | collective-permute-start | bytes 196616 | tf_op jit(solution)/shard_map/ppermute | solution.py:331
  (92 shorter events, 19.6 us)
Async XLA Ops:
  0.8 7.2 %collective-permute-start.5 = (f32[1,128,512]{2,1,0:T(8,128)}, f32[1,128,512]{2,1,0:T(8,128)S(1)}, u32[]{:S(2)}, u32[]{:S(2)}) collective-permute-start(f32[1,128,512]{2,1,0:T(8,128)} %own_e.1), channel_id=1, source_target_pairs={{0,1},{1,0},{2,3},{3,2},{4,5},{5,4},{6,7},{7,6},{8,9},{9,8},{10,11... | collective-permute-start | bytes 786440 | tf_op jit(solution)/shard_map/ppermute | solution.py:331
  2.8 4.8 %collective-permute-start.6 = (f32[128,128]{1,0:T(8,128)S(1)}, f32[128,128]{1,0:T(8,128)S(1)}, u32[]{:S(2)}, u32[]{:S(2)}) collective-permute-start(f32[128,128]{1,0:T(8,128)S(1)} %get-tuple-element.18), channel_id=1, source_target_pairs={{0,2},{1,3},{2,0},{3,1},{4,6},{5,7},{6,4},{7,5},{8,10},{9,11},{10,... | collective-permute-start | bytes 196616 | tf_op jit(solution)/shard_map/ppermute | solution.py:331
  4.1 5.1 %collective-permute-start.4 = (f32[128,128]{1,0:T(8,128)S(1)}, f32[128,128]{1,0:T(8,128)S(1)}, u32[]{:S(2)}, u32[]{:S(2)}) collective-permute-start(f32[128,128]{1,0:T(8,128)S(1)} %get-tuple-element.16.packed.near), channel_id=1, source_target_pairs={{0,1},{1,0},{2,3},{3,2},{4,10},{5,11},{6,8},{7,9},{8,6},{9,7},{10,... | collective-permute-start | bytes 196616 | tf_op jit(solution)/shard_map/ppermute | solution.py:331
  5.3 4.9 %collective-permute-start.3 = (f32[128,128]{1,0:T(8,128)S(1)}, f32[128,128]{1,0:T(8,128)S(1)}, u32[]{:S(2)}, u32[]{:S(2)}) collective-permute-start(f32[128,128]{1,0:T(8,128)S(1)} %get-tuple-element.16.packed.near), channel_id=1, source_target_pairs={{0,1},{1,0},{2,3},{3,2},{4,8},{5,9},{6,10},{7,11},{8,4},{9,5},{10,... | collective-permute-start | bytes 196616 | tf_op jit(solution)/shard_map/ppermute | solution.py:331
  7.7 4.2 %collective-permute-start.7 = (f32[128,128]{1,0:T(8,128)S(1)}, f32[128,128]{1,0:T(8,128)S(1)}, u32[]{:S(2)}, u32[]{:S(2)}) collective-permute-start(f32[128,128]{1,0:T(8,128)S(1)} %get-tuple-element.20), channel_id=1, source_target_pairs={{0,4},{1,5},{2,6},{3,7},{4,0},{5,1},{6,2},{7,3},{8,12},{9,13},{10,... | collective-permute-start | bytes 196616 | tf_op jit(solution)/shard_map/ppermute | solution.py:331
  13.3 6.2 %collective-permute-start.9 = (f32[10,128,512]{2,1,0:T(8,128)S(1)}, f32[10,128,512]{2,1,0:T(8,128)S(1)}, u32[]{:S(2)}, u32[]{:S(2)}) collective-permute-start(f32[10,128,512]{2,1,0:T(8,128)S(1)} %shard_map.88.own.refs_6_.refs_4_), channel_id=1, source_target_pairs={{0,1},{1,0},{2,3},{3,2},{4,5},{5,4},{6,7},{7,6},{8,9},{9,8},{10,11... | collective-permute-start | bytes 7864328 | tf_op jit(solution)/shard_map/ppermute | solution.py:331
  20.4 4.1 %collective-permute-start.13 = (f32[128,128]{1,0:T(8,128)S(1)}, f32[128,128]{1,0:T(8,128)S(1)}, u32[]{:S(2)}, u32[]{:S(2)}) collective-permute-start(f32[128,128]{1,0:T(8,128)S(1)} %get-tuple-element.23.values), channel_id=1, source_target_pairs={{0,12},{1,13},{2,14},{3,15},{4,5},{5,4},{6,7},{7,6},{8,0},{9,1},{1... | collective-permute-start | bytes 196616 | tf_op jit(solution)/shard_map/ppermute | solution.py:331
  21.7 4.5 %collective-permute-start.11 = (f32[128,128]{1,0:T(8,128)S(1)}, f32[128,128]{1,0:T(8,128)S(1)}, u32[]{:S(2)}, u32[]{:S(2)}) collective-permute-start(f32[128,128]{1,0:T(8,128)S(1)} %shard_map.92), channel_id=1, source_target_pairs={{0,1},{1,0},{2,3},{3,2},{4,5},{5,4},{6,7},{7,6},{8,9},{9,8},{10,11... | collective-permute-start | bytes 196616 | tf_op jit(solution)/shard_map/ppermute | solution.py:331
  24.5 5.4 %collective-permute-start.15 = (f32[128,128]{1,0:T(8,128)S(1)}, f32[128,128]{1,0:T(8,128)S(1)}, u32[]{:S(2)}, u32[]{:S(2)}) collective-permute-start(f32[128,128]{1,0:T(8,128)S(1)} %shard_map.93.refs_2_.near), channel_id=1, source_target_pairs={{0,1},{1,0},{2,3},{3,2},{4,5},{5,4},{6,7},{7,6},{8,10},{9,11},{10,... | collective-permute-start | bytes 196616 | tf_op jit(solution)/shard_map/ppermute | solution.py:331
  28.0 8.5 %collective-permute-start.14 = (f32[128,128]{1,0:T(8,128)S(1)}, f32[128,128]{1,0:T(8,128)S(1)}, u32[]{:S(2)}, u32[]{:S(2)}) collective-permute-start(f32[128,128]{1,0:T(8,128)S(1)} %shard_map.94.refs_0_), channel_id=1, source_target_pairs={{0,2},{1,3},{2,0},{3,1},{4,5},{5,4},{6,7},{7,6},{8,9},{9,8},{10,11... | collective-permute-start | bytes 196616 | tf_op jit(solution)/shard_map/ppermute | solution.py:331
  30.0 6.5 %collective-permute-start.18 = (f32[128,128]{1,0:T(8,128)S(1)}, f32[128,128]{1,0:T(8,128)S(1)}, u32[]{:S(2)}, u32[]{:S(2)}) collective-permute-start(f32[128,128]{1,0:T(8,128)S(1)} %get-tuple-element.25), channel_id=1, source_target_pairs={{0,1},{1,0},{2,3},{3,2},{4,8},{5,9},{6,10},{7,11},{8,18},{9,19},{1... | collective-permute-start | bytes 196616 | tf_op jit(solution)/shard_map/ppermute | solution.py:331
  30.1 5.6 %collective-permute-start.16 = (f32[128,128]{1,0:T(8,128)S(1)}, f32[128,128]{1,0:T(8,128)S(1)}, u32[]{:S(2)}, u32[]{:S(2)}) collective-permute-start(f32[128,128]{1,0:T(8,128)S(1)} %get-tuple-element.25), channel_id=1, source_target_pairs={{0,1},{1,0},{2,3},{3,2},{4,5},{5,4},{6,7},{7,6},{8,16},{9,17},{10,... | collective-permute-start | bytes 196616 | tf_op jit(solution)/shard_map/ppermute | solution.py:331
  30.9 5.6 %collective-permute-start.19 = (f32[128,128]{1,0:T(8,128)S(1)}, f32[128,128]{1,0:T(8,128)S(1)}, u32[]{:S(2)}, u32[]{:S(2)}) collective-permute-start(f32[128,128]{1,0:T(8,128)S(1)} %get-tuple-element.26.values), channel_id=1, source_target_pairs={{0,1},{1,0},{2,3},{3,2},{4,5},{5,4},{6,7},{7,6},{8,9},{9,8},{10,11... | collective-permute-start | bytes 196616 | tf_op jit(solution)/shard_map/ppermute | solution.py:331
  36.5 5.0 %collective-permute-start.22 = (f32[128,128]{1,0:T(8,128)S(1)}, f32[128,128]{1,0:T(8,128)S(1)}, u32[]{:S(2)}, u32[]{:S(2)}) collective-permute-start(f32[128,128]{1,0:T(8,128)S(1)} %shard_map.97), channel_id=1, source_target_pairs={{0,12},{1,13},{2,14},{3,15},{4,5},{5,4},{6,7},{7,6},{8,0},{9,1},{1... | collective-permute-start | bytes 196616 | tf_op jit(solution)/shard_map/ppermute | solution.py:331
  36.6 4.9 %collective-permute-start.21 = (f32[128,128]{1,0:T(8,128)S(1)}, f32[128,128]{1,0:T(8,128)S(1)}, u32[]{:S(2)}, u32[]{:S(2)}) collective-permute-start(f32[128,128]{1,0:T(8,128)S(1)} %shard_map.96), channel_id=1, source_target_pairs={{0,6},{1,7},{2,4},{3,5},{4,20},{5,21},{6,22},{7,23},{8,9},{9,8},{1... | collective-permute-start | bytes 196616 | tf_op jit(solution)/shard_map/ppermute | solution.py:331
  41.5 7.3 %collective-permute-start.25 = (f32[128,128]{1,0:T(8,128)S(1)}, f32[128,128]{1,0:T(8,128)S(1)}, u32[]{:S(2)}, u32[]{:S(2)}) collective-permute-start(f32[128,128]{1,0:T(8,128)S(1)} %shard_map.100.part), channel_id=1, source_target_pairs={{0,18},{1,19},{2,16},{3,17},{4,0},{5,1},{6,2},{7,3},{8,9},{9,8},{1... | collective-permute-start | bytes 196616 | tf_op jit(solution)/shard_map/ppermute | solution.py:331
  42.5 6.2 %collective-permute-start.24 = (f32[128,128]{1,0:T(8,128)S(1)}, f32[128,128]{1,0:T(8,128)S(1)}, u32[]{:S(2)}, u32[]{:S(2)}) collective-permute-start(f32[128,128]{1,0:T(8,128)S(1)} %shard_map.100.part), channel_id=1, source_target_pairs={{0,16},{1,17},{2,18},{3,19},{4,0},{5,1},{6,2},{7,3},{8,9},{9,8},{1... | collective-permute-start | bytes 196616 | tf_op jit(solution)/shard_map/ppermute | solution.py:331
  42.6 13.1 %collective-permute-start.31 = (f32[128,128]{1,0:T(8,128)S(1)}, f32[128,128]{1,0:T(8,128)S(1)}, u32[]{:S(2)}, u32[]{:S(2)}) collective-permute-start(f32[128,128]{1,0:T(8,128)S(1)} %shard_map.100.part), channel_id=1, source_target_pairs={{0,10},{1,11},{2,8},{3,9},{4,0},{5,1},{6,2},{7,3},{8,14},{9,15},{1... | collective-permute-start | bytes 196616 | tf_op jit(solution)/shard_map/ppermute | solution.py:331
  46.5 9.2 %collective-permute-start.30 = (f32[128,128]{1,0:T(8,128)S(1)}, f32[128,128]{1,0:T(8,128)S(1)}, u32[]{:S(2)}, u32[]{:S(2)}) collective-permute-start(f32[128,128]{1,0:T(8,128)S(1)} %shard_map.100.part), channel_id=1, source_target_pairs={{0,8},{1,9},{2,10},{3,11},{4,0},{5,1},{6,2},{7,3},{8,12},{9,13},{1... | collective-permute-start | bytes 196616 | tf_op jit(solution)/shard_map/ppermute | solution.py:331
  48.8 6.9 %collective-permute-start.29 = (f32[128,128]{1,0:T(8,128)S(1)}, f32[128,128]{1,0:T(8,128)S(1)}, u32[]{:S(2)}, u32[]{:S(2)}) collective-permute-start(f32[128,128]{1,0:T(8,128)S(1)} %shard_map.101.other), channel_id=1, source_target_pairs={{0,1},{1,0},{2,3},{3,2},{4,5},{5,4},{6,7},{7,6},{8,14},{9,15},{10,... | collective-permute-start | bytes 196616 | tf_op jit(solution)/shard_map/ppermute | solution.py:331
  49.3 6.4 %collective-permute-start.28 = (f32[128,128]{1,0:T(8,128)S(1)}, f32[128,128]{1,0:T(8,128)S(1)}, u32[]{:S(2)}, u32[]{:S(2)}) collective-permute-start(f32[128,128]{1,0:T(8,128)S(1)} %shard_map.101.other), channel_id=1, source_target_pairs={{0,1},{1,0},{2,3},{3,2},{4,5},{5,4},{6,7},{7,6},{8,12},{9,13},{10,... | collective-permute-start | bytes 196616 | tf_op jit(solution)/shard_map/ppermute | solution.py:331
  57.0 5.5 %collective-permute-start.35 = (f32[128,128]{1,0:T(8,128)S(1)}, f32[128,128]{1,0:T(8,128)S(1)}, u32[]{:S(2)}, u32[]{:S(2)}) collective-permute-start(f32[128,128]{1,0:T(8,128)S(1)} %shard_map.102.other), channel_id=1, source_target_pairs={{0,1},{1,0},{2,3},{3,2},{4,10},{5,11},{6,8},{7,9},{8,6},{9,7},{10,... | collective-permute-start | bytes 196616 | tf_op jit(solution)/shard_map/ppermute | solution.py:331
  57.8 4.9 %collective-permute-start.34 = (f32[128,128]{1,0:T(8,128)S(1)}, f32[128,128]{1,0:T(8,128)S(1)}, u32[]{:S(2)}, u32[]{:S(2)}) collective-permute-start(f32[128,128]{1,0:T(8,128)S(1)} %shard_map.102.other), channel_id=1, source_target_pairs={{0,1},{1,0},{2,3},{3,2},{4,8},{5,9},{6,10},{7,11},{8,4},{9,5},{10,... | collective-permute-start | bytes 196616 | tf_op jit(solution)/shard_map/ppermute | solution.py:331
  64.7 6.6 %collective-permute-start.36 = (f32[128,128]{1,0:T(8,128)S(1)}, f32[128,128]{1,0:T(8,128)S(1)}, u32[]{:S(2)}, u32[]{:S(2)}) collective-permute-start(f32[128,128]{1,0:T(8,128)S(1)} %shard_map.103.mine), channel_id=1, source_target_pairs={{0,1},{1,0},{2,3},{3,2},{4,5},{5,4},{6,7},{7,6},{8,9},{9,8},{10,11... | collective-permute-start | bytes 196616 | tf_op jit(solution)/shard_map/ppermute | solution.py:331
  (21 other events, 59.1 us)

commit v10 on v9

--- a/solution.py
+++ b/solution.py
@@ -354,7 +354,7 @@
     psi, up_near, up_far = call(
         open_kernel, waves, mate_waves, side, *t_pair, outs=3, scratch=[pltpu.VMEM((64, width), wide)]
     )
-    up, crossing = call(cross_kernel, psi, up_near, exchange(up_far), outs=2)
+    up, crossing = call(cross_kernel, psi, up_near, exchange(up_far), outs=2, flops=1)
     psi_far = exchange(psi)
     between = [(a, b) for k in every[1:-1:2] for a, b in ((k, k + 1), (k + 1, k))]
     stepped = send(crossing, [(a, a ^ 1) for a in every])
@@ -368,7 +368,7 @@
         scratch=[store, store],
         unused=(up,),
     )
-    near, crossing = call(near_kernel, rest, stepped, outs=2)
+    near, crossing = call(near_kernel, rest, stepped, outs=2, flops=1)
     far = exchange(crossing)
     blocks = below[0], above[0], pivots[0], back_lower[0], back_upper[0]
     front = stack(*blocks, after=near)
@@ -381,7 +381,7 @@
         d = 2**level
         if level == levels - 1:
             beneath = call(kernel(top_kernel, d), near, far, *front, scratch=[store])
-            shares = both(beneath, [(d, 0, 1, d + 1)], [(d, 0, 1, d + 1)])
+            shares = both(beneath, [(d, 0, 1, d - 1)], [(d, 0, 1, d + 3)])
             if level > 1:
                 shares = shares + late
             pivot = call(kernel(pivot_kernel, d), near, far, *back, pivot, scratch=[store])
@@ -408,7 +408,7 @@
             unused=(base,) if level == 1 else (),
         )
         if level == 0:
-            more = send(over, [(b - 1, b, b - 2) for b in urgent])
+            more = send(over, [(a, b) for k in urgent for a, b in ((k - 1, k), (k, k - 1))])
             less = send(beneath, [(b + 1, b, b - 2) for b in urgent])
             pivot = call(
                 kernel(pivot_kernel, d),
@@ -445,9 +445,8 @@
         near = base - more[0] - less[0]
         far = base_far - more[1] - less[1]
         held = call(copy_kernel, beneath, unused=(more[0],))
-        late = both(
-            held, [(b + d, b, b + d + 1) for b in patient], [(b + d, b, b + d + 3) for b in patient]
-        )
+        ways = [(b + d, b, b + 1, b + d + 1) for b in patient]
+        late = both(held, ways, ways)
         if len(patient) > 1:
             held = call(copy_kernel, over, unused=(more[0],))
             late = late + both(
@@ -472,10 +471,11 @@
             vectors = both(solved, [(0, d, d + 1, 1)], [(0, d, d + 1, 1)])
         else:
             sources = [a for a in every if a % (4 * d) == 2 * d]
-            ways = [(a, a - d, a - d + 1, a + 1) for a in sources]
-            up_near, up_far = both(solved, ways, ways)
-            ways = [(a, a + d, a + d + 1, a + 1) for a in sources]
-            low_near, low_far = both(solved, ways, ways)
+            up_near = send(solved, [(a, a - d, a - d + 1, a + 1) for a in sources])
+            last = -3 if d == 2 else 3
+            up_far = send(solved, [(a, a - d, a - d + 1, a + last) for a in sources], 2)
+            low_far = send(solved, [(a, a + d, a + d + 1, a - 1) for a in sources], 2)
+            low_near = send(solved, [(a, a + d, a + d + 1) for a in sources])
             vectors = (low_near, low_far, up_near, up_far) + early
         if level > 1:
             half = d // 2

time: 72.1 us -> 72.4 us (level)
  starting transfers between devices: 43.6 us -> 45.6 us
  local copies, waits for them, and re-layouts: 1.3 us -> 0.05 us
    ppermute x37, starting transfers between devices: 43.6 us -> 45.6 us  [send(): lax.ppermute(values, ('slab', 'col'), completed(route, slabs * cols, cols))]
    unnamed x16, local copies, waits for them, and re-layouts: 1.3 us -> 0.04 us
  transfers between devices with their start and end apart: 37 -> 37, of which waited for: 19 -> 16; matrix products, arithmetic and copies ran while one was open for 0% -> 0% of each run, Pallas kernels for 4% -> 4%
where the time goes in v10:
time: 72.4 us; the launch traced here: 72.2 us
  starting transfers between devices  45.6 us (63%)
  waiting for transfers between devices  20.5 us (28%)
  Pallas kernels  5.8 us (8%)
    ppermute x37, starting transfers between devices, send(): lax.ppermute(values, ('slab', 'col'), completed(route, slabs * cols, cols))  45.6 us
    ppermute x37, waiting for transfers between devices, send(): lax.ppermute(values, ('slab', 'col'), completed(route, slabs * cols, cols))  20.5 us
    pallas_call x23, Pallas kernels, call(): pl.pallas_call(kernel, out_shape=shape if outs == 1 else (shape,) * outs,...  5.8 us
  transfers between devices with their start and end apart: 37, of which 16 were waited for; matrix products, arithmetic and copies ran while one was open for 0% of the time, Pallas kernels for 4%

profile of v10, /device:TPU:13, one launch (start us, length us, event | category | flops | bytes accessed | tf_op | source)
XLA Modules:
  0.0 72.2 jit_solution(3739652279978283642)
XLA Ops:
  1.2 1.3 %collective-permute-done.other = f32[1,128,128]{2,1,0:T(8,128)S(1)} collective-permute-done((f32[1,128,128]{2,1,0:T(8,128)}, f32[1,128,128]{2,1,0:T(8,128)S(1)}, u32[]{:S(2)}, u32[]{:S(2)}) %collective-permute-start) | collective-permute-done | bytes 65568 | tf_op jit(solution)/shard_map/ppermute | solution.py:331
  3.3 1.3 %collective-permute-start.6 = (f32[128,128]{1,0:T(8,128)S(1)}, f32[128,128]{1,0:T(8,128)S(1)}, u32[]{:S(2)}, u32[]{:S(2)}) collective-permute-start(f32[128,128]{1,0:T(8,128)S(1)} %get-tuple-element.18), channel_id=1, source_target_pairs={{0,2},{1,3},{2,0},{3,1},{4,6},{5,7},{6,4},{7,5},{8,10},{9,11},{10,... | collective-permute-start | bytes 196616 | tf_op jit(solution)/shard_map/ppermute | solution.py:331
  4.5 1.2 %collective-permute-start.4 = (f32[128,128]{1,0:T(8,128)S(1)}, f32[128,128]{1,0:T(8,128)S(1)}, u32[]{:S(2)}, u32[]{:S(2)}) collective-permute-start(f32[128,128]{1,0:T(8,128)S(1)} %get-tuple-element.16.packed.near), channel_id=1, source_target_pairs={{0,1},{1,0},{2,3},{3,2},{4,10},{5,11},{6,8},{7,9},{8,6},{9,7},{10,... | collective-permute-start | bytes 196616 | tf_op jit(solution)/shard_map/ppermute | solution.py:331
  6.9 1.2 %collective-permute-start.2 = (f32[128,128]{1,0:T(8,128)S(1)}, f32[128,128]{1,0:T(8,128)S(1)}, u32[]{:S(2)}, u32[]{:S(2)}) collective-permute-start(f32[128,128]{1,0:T(8,128)S(1)} %get-tuple-element.16.packed.near), channel_id=1, source_target_pairs={{0,2},{1,3},{2,0},{3,1},{4,6},{5,7},{6,4},{7,5},{8,10},{9,11},{10,... | collective-permute-start | bytes 196616 | tf_op jit(solution)/shard_map/ppermute | solution.py:331
  8.4 1.2 %collective-permute-done.4.next_far = f32[128,128]{1,0:T(8,128)S(1)} collective-permute-done((f32[128,128]{1,0:T(8,128)S(1)}, f32[128,128]{1,0:T(8,128)S(1)}, u32[]{:S(2)}, u32[]{:S(2)}) %collective-permute-start.4) | collective-permute-done | bytes 65568 | tf_op jit(solution)/shard_map/ppermute | solution.py:331
  12.5 1.7 %collective-permute-start.9 = (f32[10,128,512]{2,1,0:T(8,128)S(1)}, f32[10,128,512]{2,1,0:T(8,128)S(1)}, u32[]{:S(2)}, u32[]{:S(2)}) collective-permute-start(f32[10,128,512]{2,1,0:T(8,128)S(1)} %shard_map.88.own.refs_6_.refs_4_), channel_id=1, source_target_pairs={{0,1},{1,0},{2,3},{3,2},{4,5},{5,4},{6,7},{7,6},{8,9},{9,8},{10,11... | collective-permute-start | bytes 7864328 | tf_op jit(solution)/shard_map/ppermute | solution.py:331
  15.0 2.9 %collective-permute-done.8.next_far.far = f32[128,128]{1,0:T(8,128)S(1)} collective-permute-done((f32[128,128]{1,0:T(8,128)S(1)}, f32[128,128]{1,0:T(8,128)S(1)}, u32[]{:S(2)}, u32[]{:S(2)}) %collective-permute-start.8) | collective-permute-done | bytes 65568 | tf_op jit(solution)/shard_map/ppermute | solution.py:331
  21.0 3.3 %collective-permute-start.11 = (f32[128,128]{1,0:T(8,128)S(1)}, f32[128,128]{1,0:T(8,128)S(1)}, u32[]{:S(2)}, u32[]{:S(2)}) collective-permute-start(f32[128,128]{1,0:T(8,128)S(1)} %shard_map.92), channel_id=1, source_target_pairs={{0,1},{1,0},{2,3},{3,2},{4,5},{5,4},{6,7},{7,6},{8,9},{9,8},{10,11... | collective-permute-start | bytes 196616 | tf_op jit(solution)/shard_map/ppermute | solution.py:331
  25.8 2.5 %collective-permute-done.10.refs_0_ = f32[128,128]{1,0:T(8,128)S(1)} collective-permute-done((f32[128,128]{1,0:T(8,128)S(1)}, f32[128,128]{1,0:T(8,128)S(1)}, u32[]{:S(2)}, u32[]{:S(2)}) %collective-permute-start.10) | collective-permute-done | bytes 65568 | tf_op jit(solution)/shard_map/ppermute | solution.py:331
  28.3 1.5 %collective-permute-start.14 = (f32[128,128]{1,0:T(8,128)S(1)}, f32[128,128]{1,0:T(8,128)S(1)}, u32[]{:S(2)}, u32[]{:S(2)}) collective-permute-start(f32[128,128]{1,0:T(8,128)S(1)} %shard_map.94.refs_0_), channel_id=1, source_target_pairs={{0,2},{1,3},{2,0},{3,1},{4,5},{5,4},{6,7},{7,6},{8,9},{9,8},{10,11... | collective-permute-start | bytes 196616 | tf_op jit(solution)/shard_map/ppermute | solution.py:331
  31.0 2.0 %collective-permute-start.19 = (f32[128,128]{1,0:T(8,128)S(1)}, f32[128,128]{1,0:T(8,128)S(1)}, u32[]{:S(2)}, u32[]{:S(2)}) collective-permute-start(f32[128,128]{1,0:T(8,128)S(1)} %get-tuple-element.26.values), channel_id=1, source_target_pairs={{0,1},{1,0},{2,3},{3,2},{4,5},{5,4},{6,7},{7,6},{8,9},{9,8},{10,11... | collective-permute-start | bytes 196616 | tf_op jit(solution)/shard_map/ppermute | solution.py:331
  33.0 3.3 %collective-permute-done.16.refs_0_ = f32[128,128]{1,0:T(8,128)S(1)} collective-permute-done((f32[128,128]{1,0:T(8,128)S(1)}, f32[128,128]{1,0:T(8,128)S(1)}, u32[]{:S(2)}, u32[]{:S(2)}) %collective-permute-start.16) | collective-permute-done | bytes 65568 | tf_op jit(solution)/shard_map/ppermute | solution.py:331
  37.5 3.2 %collective-permute-start.20 = (f32[128,128]{1,0:T(8,128)S(1)}, f32[128,128]{1,0:T(8,128)S(1)}, u32[]{:S(2)}, u32[]{:S(2)}) collective-permute-start(f32[128,128]{1,0:T(8,128)S(1)} %shard_map.96), channel_id=1, source_target_pairs={{0,4},{1,5},{2,6},{3,7},{4,12},{5,13},{6,14},{7,15},{8,9},{9,8},{1... | collective-permute-start | bytes 196616 | tf_op jit(solution)/shard_map/ppermute | solution.py:331
  40.8 2.3 %collective-permute-done.20.refs_2_ = f32[128,128]{1,0:T(8,128)S(1)} collective-permute-done((f32[128,128]{1,0:T(8,128)S(1)}, f32[128,128]{1,0:T(8,128)S(1)}, u32[]{:S(2)}, u32[]{:S(2)}) %collective-permute-start.20) | collective-permute-done | bytes 65568 | tf_op jit(solution)/shard_map/ppermute | solution.py:331
  43.1 1.9 %collective-permute-start.25 = (f32[128,128]{1,0:T(8,128)S(1)}, f32[128,128]{1,0:T(8,128)S(1)}, u32[]{:S(2)}, u32[]{:S(2)}) collective-permute-start(f32[128,128]{1,0:T(8,128)S(1)} %shard_map.100.part), channel_id=1, source_target_pairs={{0,18},{1,19},{2,16},{3,17},{4,0},{5,1},{6,2},{7,3},{8,9},{9,8},{1... | collective-permute-start | bytes 196616 | tf_op jit(solution)/shard_map/ppermute | solution.py:331
  45.1 2.3 %collective-permute-start.31 = (f32[128,128]{1,0:T(8,128)S(1)}, f32[128,128]{1,0:T(8,128)S(1)}, u32[]{:S(2)}, u32[]{:S(2)}) collective-permute-start(f32[128,128]{1,0:T(8,128)S(1)} %shard_map.100.part), channel_id=1, source_target_pairs={{0,10},{1,11},{2,8},{3,9},{4,0},{5,1},{6,2},{7,3},{8,14},{9,15},{1... | collective-permute-start | bytes 196616 | tf_op jit(solution)/shard_map/ppermute | solution.py:331
  47.4 2.6 %collective-permute-start.29 = (f32[128,128]{1,0:T(8,128)S(1)}, f32[128,128]{1,0:T(8,128)S(1)}, u32[]{:S(2)}, u32[]{:S(2)}) collective-permute-start(f32[128,128]{1,0:T(8,128)S(1)} %shard_map.101.other), channel_id=1, source_target_pairs={{0,1},{1,0},{2,3},{3,2},{4,16},{5,17},{6,18},{7,19},{8,14},{9,15},... | collective-permute-start | bytes 196616 | tf_op jit(solution)/shard_map/ppermute | solution.py:331
  50.0 1.9 %collective-permute-start.28 = (f32[128,128]{1,0:T(8,128)S(1)}, f32[128,128]{1,0:T(8,128)S(1)}, u32[]{:S(2)}, u32[]{:S(2)}) collective-permute-start(f32[128,128]{1,0:T(8,128)S(1)} %shard_map.101.other), channel_id=1, source_target_pairs={{0,1},{1,0},{2,3},{3,2},{4,5},{5,4},{6,7},{7,6},{8,12},{9,13},{10,... | collective-permute-start | bytes 196616 | tf_op jit(solution)/shard_map/ppermute | solution.py:331
  51.9 3.4 %collective-permute-start.26 = (f32[128,128]{1,0:T(8,128)S(1)}, f32[128,128]{1,0:T(8,128)S(1)}, u32[]{:S(2)}, u32[]{:S(2)}) collective-permute-start(f32[128,128]{1,0:T(8,128)S(1)} %shard_map.101.other), channel_id=1, source_target_pairs={{0,1},{1,0},{2,3},{3,2},{4,5},{5,4},{6,7},{7,6},{8,9},{9,8},{10,11... | collective-permute-start | bytes 196616 | tf_op jit(solution)/shard_map/ppermute | solution.py:331
  56.2 2.2 %collective-permute-start.32 = (f32[128,128]{1,0:T(8,128)S(1)}, f32[128,128]{1,0:T(8,128)S(1)}, u32[]{:S(2)}, u32[]{:S(2)}) collective-permute-start(f32[128,128]{1,0:T(8,128)S(1)} %shard_map.102.other), channel_id=1, source_target_pairs={{0,4},{1,5},{2,6},{3,7},{4,0},{5,1},{6,2},{7,3},{8,12},{9,13},{10,... | collective-permute-start | bytes 196616 | tf_op jit(solution)/shard_map/ppermute | solution.py:331
  58.7 2.1 %collective-permute-start.34 = (f32[128,128]{1,0:T(8,128)S(1)}, f32[128,128]{1,0:T(8,128)S(1)}, u32[]{:S(2)}, u32[]{:S(2)}) collective-permute-start(f32[128,128]{1,0:T(8,128)S(1)} %shard_map.102.other), channel_id=1, source_target_pairs={{0,1},{1,0},{2,3},{3,2},{4,8},{5,9},{6,10},{7,11},{8,4},{9,5},{10,... | collective-permute-start | bytes 196616 | tf_op jit(solution)/shard_map/ppermute | solution.py:331
  62.0 2.0 %collective-permute-done.35.refs_3_ = f32[128,128]{1,0:T(8,128)S(1)} collective-permute-done((f32[128,128]{1,0:T(8,128)S(1)}, f32[128,128]{1,0:T(8,128)S(1)}, u32[]{:S(2)}, u32[]{:S(2)}) %collective-permute-start.35) | collective-permute-done | bytes 65568 | tf_op jit(solution)/shard_map/ppermute | solution.py:331
  64.2 1.4 %shard_map.103.mine = f32[128,128]{1,0:T(8,128)S(1)} custom-call(f32[128,128]{1,0:T(8,128)S(1)} %shard_map.100.part, f32[128,128]{1,0:T(8,128)S(1)} %shard_map.102.other, f32[128,128]{1,0:T(8,128)S(1)} %collective-permute-done.32.refs_0_, f32[128,128]{1,0:T(8,128)S(1)} %collective-permute-done.33.refs_1_, f32[128,128]{1,0:T(8,128)S(1)} %collective-permute-done.34.refs_2_, ...), custom_call_target="tpu_custom_call" | custom-call | flops 1000000000 | bytes 1 | tf_op jit(solution)/shard_map/pallas_call | solution.py:287
  65.6 5.0 %collective-permute-start.36 = (f32[128,128]{1,0:T(8,128)S(1)}, f32[128,128]{1,0:T(8,128)S(1)}, u32[]{:S(2)}, u32[]{:S(2)}) collective-permute-start(f32[128,128]{1,0:T(8,128)S(1)} %shard_map.103.mine), channel_id=1, source_target_pairs={{0,1},{1,0},{2,3},{3,2},{4,5},{5,4},{6,7},{7,6},{8,9},{9,8},{10,11... | collective-permute-start | bytes 196616 | tf_op jit(solution)/shard_map/ppermute | solution.py:331
  (92 shorter events, 18.0 us)
Async XLA Ops:
  0.7 7.7 %collective-permute-start.5 = (f32[1,128,512]{2,1,0:T(8,128)}, f32[1,128,512]{2,1,0:T(8,128)S(1)}, u32[]{:S(2)}, u32[]{:S(2)}) collective-permute-start(f32[1,128,512]{2,1,0:T(8,128)} %own_e.1), channel_id=1, source_target_pairs={{0,1},{1,0},{2,3},{3,2},{4,5},{5,4},{6,7},{7,6},{8,9},{9,8},{10,11... | collective-permute-start | bytes 786440 | tf_op jit(solution)/shard_map/ppermute | solution.py:331
  3.3 4.8 %collective-permute-start.6 = (f32[128,128]{1,0:T(8,128)S(1)}, f32[128,128]{1,0:T(8,128)S(1)}, u32[]{:S(2)}, u32[]{:S(2)}) collective-permute-start(f32[128,128]{1,0:T(8,128)S(1)} %get-tuple-element.18), channel_id=1, source_target_pairs={{0,2},{1,3},{2,0},{3,1},{4,6},{5,7},{6,4},{7,5},{8,10},{9,11},{10,... | collective-permute-start | bytes 196616 | tf_op jit(solution)/shard_map/ppermute | solution.py:331
  4.5 5.1 %collective-permute-start.4 = (f32[128,128]{1,0:T(8,128)S(1)}, f32[128,128]{1,0:T(8,128)S(1)}, u32[]{:S(2)}, u32[]{:S(2)}) collective-permute-start(f32[128,128]{1,0:T(8,128)S(1)} %get-tuple-element.16.packed.near), channel_id=1, source_target_pairs={{0,1},{1,0},{2,3},{3,2},{4,10},{5,11},{6,8},{7,9},{8,6},{9,7},{10,... | collective-permute-start | bytes 196616 | tf_op jit(solution)/shard_map/ppermute | solution.py:331
  5.8 4.9 %collective-permute-start.3 = (f32[128,128]{1,0:T(8,128)S(1)}, f32[128,128]{1,0:T(8,128)S(1)}, u32[]{:S(2)}, u32[]{:S(2)}) collective-permute-start(f32[128,128]{1,0:T(8,128)S(1)} %get-tuple-element.16.packed.near), channel_id=1, source_target_pairs={{0,1},{1,0},{2,3},{3,2},{4,8},{5,9},{6,10},{7,11},{8,4},{9,5},{10,... | collective-permute-start | bytes 196616 | tf_op jit(solution)/shard_map/ppermute | solution.py:331
  12.5 6.3 %collective-permute-start.9 = (f32[10,128,512]{2,1,0:T(8,128)S(1)}, f32[10,128,512]{2,1,0:T(8,128)S(1)}, u32[]{:S(2)}, u32[]{:S(2)}) collective-permute-start(f32[10,128,512]{2,1,0:T(8,128)S(1)} %shard_map.88.own.refs_6_.refs_4_), channel_id=1, source_target_pairs={{0,1},{1,0},{2,3},{3,2},{4,5},{5,4},{6,7},{7,6},{8,9},{9,8},{10,11... | collective-permute-start | bytes 7864328 | tf_op jit(solution)/shard_map/ppermute | solution.py:331
  19.8 4.5 %collective-permute-start.13 = (f32[128,128]{1,0:T(8,128)S(1)}, f32[128,128]{1,0:T(8,128)S(1)}, u32[]{:S(2)}, u32[]{:S(2)}) collective-permute-start(f32[128,128]{1,0:T(8,128)S(1)} %get-tuple-element.23.values), channel_id=1, source_target_pairs={{0,12},{1,13},{2,14},{3,15},{4,5},{5,4},{6,7},{7,6},{8,0},{9,1},{1... | collective-permute-start | bytes 196616 | tf_op jit(solution)/shard_map/ppermute | solution.py:331
  19.8 4.5 %collective-permute-start.12 = (f32[128,128]{1,0:T(8,128)S(1)}, f32[128,128]{1,0:T(8,128)S(1)}, u32[]{:S(2)}, u32[]{:S(2)}) collective-permute-start(f32[128,128]{1,0:T(8,128)S(1)} %get-tuple-element.24.refs_0_.values), channel_id=1, source_target_pairs={{0,1},{1,0},{2,3},{3,2},{4,8},{5,9},{6,10},{7,11},{8,4},{9,5},{10,... | collective-permute-start | bytes 196616 | tf_op jit(solution)/shard_map/ppermute | solution.py:331
  21.0 4.8 %collective-permute-start.11 = (f32[128,128]{1,0:T(8,128)S(1)}, f32[128,128]{1,0:T(8,128)S(1)}, u32[]{:S(2)}, u32[]{:S(2)}) collective-permute-start(f32[128,128]{1,0:T(8,128)S(1)} %shard_map.92), channel_id=1, source_target_pairs={{0,1},{1,0},{2,3},{3,2},{4,5},{5,4},{6,7},{7,6},{8,9},{9,8},{10,11... | collective-permute-start | bytes 196616 | tf_op jit(solution)/shard_map/ppermute | solution.py:331
  24.3 5.5 %collective-permute-start.15 = (f32[128,128]{1,0:T(8,128)S(1)}, f32[128,128]{1,0:T(8,128)S(1)}, u32[]{:S(2)}, u32[]{:S(2)}) collective-permute-start(f32[128,128]{1,0:T(8,128)S(1)} %shard_map.93.refs_2_.near), channel_id=1, source_target_pairs={{0,1},{1,0},{2,3},{3,2},{4,5},{5,4},{6,7},{7,6},{8,10},{9,11},{10,... | collective-permute-start | bytes 196616 | tf_op jit(solution)/shard_map/ppermute | solution.py:331
  28.3 8.1 %collective-permute-start.14 = (f32[128,128]{1,0:T(8,128)S(1)}, f32[128,128]{1,0:T(8,128)S(1)}, u32[]{:S(2)}, u32[]{:S(2)}) collective-permute-start(f32[128,128]{1,0:T(8,128)S(1)} %shard_map.94.refs_0_), channel_id=1, source_target_pairs={{0,2},{1,3},{2,0},{3,1},{4,5},{5,4},{6,7},{7,6},{8,9},{9,8},{10,11... | collective-permute-start | bytes 196616 | tf_op jit(solution)/shard_map/ppermute | solution.py:331
  29.9 6.5 %collective-permute-start.18 = (f32[128,128]{1,0:T(8,128)S(1)}, f32[128,128]{1,0:T(8,128)S(1)}, u32[]{:S(2)}, u32[]{:S(2)}) collective-permute-start(f32[128,128]{1,0:T(8,128)S(1)} %get-tuple-element.25), channel_id=1, source_target_pairs={{0,1},{1,0},{2,3},{3,2},{4,8},{5,9},{6,10},{7,11},{8,18},{9,19},{1... | collective-permute-start | bytes 196616 | tf_op jit(solution)/shard_map/ppermute | solution.py:331
  30.0 6.3 %collective-permute-start.16 = (f32[128,128]{1,0:T(8,128)S(1)}, f32[128,128]{1,0:T(8,128)S(1)}, u32[]{:S(2)}, u32[]{:S(2)}) collective-permute-start(f32[128,128]{1,0:T(8,128)S(1)} %get-tuple-element.25), channel_id=1, source_target_pairs={{0,1},{1,0},{2,3},{3,2},{4,5},{5,4},{6,7},{7,6},{8,16},{9,17},{10,... | collective-permute-start | bytes 196616 | tf_op jit(solution)/shard_map/ppermute | solution.py:331
  31.0 5.4 %collective-permute-start.19 = (f32[128,128]{1,0:T(8,128)S(1)}, f32[128,128]{1,0:T(8,128)S(1)}, u32[]{:S(2)}, u32[]{:S(2)}) collective-permute-start(f32[128,128]{1,0:T(8,128)S(1)} %get-tuple-element.26.values), channel_id=1, source_target_pairs={{0,1},{1,0},{2,3},{3,2},{4,5},{5,4},{6,7},{7,6},{8,9},{9,8},{10,11... | collective-permute-start | bytes 196616 | tf_op jit(solution)/shard_map/ppermute | solution.py:331
  36.3 4.5 %collective-permute-start.23 = (f32[128,128]{1,0:T(8,128)S(1)}, f32[128,128]{1,0:T(8,128)S(1)}, u32[]{:S(2)}, u32[]{:S(2)}) collective-permute-start(f32[128,128]{1,0:T(8,128)S(1)} %shard_map.97), channel_id=1, source_target_pairs={{0,6},{1,7},{2,4},{3,5},{4,12},{5,13},{6,14},{7,15},{8,2},{9,3},{1... | collective-permute-start | bytes 196616 | tf_op jit(solution)/shard_map/ppermute | solution.py:331
  36.3 4.4 %collective-permute-start.22 = (f32[128,128]{1,0:T(8,128)S(1)}, f32[128,128]{1,0:T(8,128)S(1)}, u32[]{:S(2)}, u32[]{:S(2)}) collective-permute-start(f32[128,128]{1,0:T(8,128)S(1)} %shard_map.97), channel_id=1, source_target_pairs={{0,4},{1,5},{2,6},{3,7},{4,12},{5,13},{6,14},{7,15},{8,0},{9,1},{1... | collective-permute-start | bytes 196616 | tf_op jit(solution)/shard_map/ppermute | solution.py:331
  37.5 5.6 %collective-permute-start.20 = (f32[128,128]{1,0:T(8,128)S(1)}, f32[128,128]{1,0:T(8,128)S(1)}, u32[]{:S(2)}, u32[]{:S(2)}) collective-permute-start(f32[128,128]{1,0:T(8,128)S(1)} %shard_map.96), channel_id=1, source_target_pairs={{0,4},{1,5},{2,6},{3,7},{4,12},{5,13},{6,14},{7,15},{8,9},{9,8},{1... | collective-permute-start | bytes 196616 | tf_op jit(solution)/shard_map/ppermute | solution.py:331
  45.1 6.8 %collective-permute-start.31 = (f32[128,128]{1,0:T(8,128)S(1)}, f32[128,128]{1,0:T(8,128)S(1)}, u32[]{:S(2)}, u32[]{:S(2)}) collective-permute-start(f32[128,128]{1,0:T(8,128)S(1)} %shard_map.100.part), channel_id=1, source_target_pairs={{0,10},{1,11},{2,8},{3,9},{4,0},{5,1},{6,2},{7,3},{8,14},{9,15},{1... | collective-permute-start | bytes 196616 | tf_op jit(solution)/shard_map/ppermute | solution.py:331
  47.4 8.0 %collective-permute-start.30 = (f32[128,128]{1,0:T(8,128)S(1)}, f32[128,128]{1,0:T(8,128)S(1)}, u32[]{:S(2)}, u32[]{:S(2)}) collective-permute-start(f32[128,128]{1,0:T(8,128)S(1)} %shard_map.100.part), channel_id=1, source_target_pairs={{0,8},{1,9},{2,10},{3,11},{4,0},{5,1},{6,2},{7,3},{8,12},{9,13},{1... | collective-permute-start | bytes 196616 | tf_op jit(solution)/shard_map/ppermute | solution.py:331
  47.4 7.9 %collective-permute-start.29 = (f32[128,128]{1,0:T(8,128)S(1)}, f32[128,128]{1,0:T(8,128)S(1)}, u32[]{:S(2)}, u32[]{:S(2)}) collective-permute-start(f32[128,128]{1,0:T(8,128)S(1)} %shard_map.101.other), channel_id=1, source_target_pairs={{0,1},{1,0},{2,3},{3,2},{4,16},{5,17},{6,18},{7,19},{8,14},{9,15},... | collective-permute-start | bytes 196616 | tf_op jit(solution)/shard_map/ppermute | solution.py:331
  50.0 5.4 %collective-permute-start.28 = (f32[128,128]{1,0:T(8,128)S(1)}, f32[128,128]{1,0:T(8,128)S(1)}, u32[]{:S(2)}, u32[]{:S(2)}) collective-permute-start(f32[128,128]{1,0:T(8,128)S(1)} %shard_map.101.other), channel_id=1, source_target_pairs={{0,1},{1,0},{2,3},{3,2},{4,5},{5,4},{6,7},{7,6},{8,12},{9,13},{10,... | collective-permute-start | bytes 196616 | tf_op jit(solution)/shard_map/ppermute | solution.py:331
  56.2 4.6 %collective-permute-start.32 = (f32[128,128]{1,0:T(8,128)S(1)}, f32[128,128]{1,0:T(8,128)S(1)}, u32[]{:S(2)}, u32[]{:S(2)}) collective-permute-start(f32[128,128]{1,0:T(8,128)S(1)} %shard_map.102.other), channel_id=1, source_target_pairs={{0,4},{1,5},{2,6},{3,7},{4,0},{5,1},{6,2},{7,3},{8,12},{9,13},{10,... | collective-permute-start | bytes 196616 | tf_op jit(solution)/shard_map/ppermute | solution.py:331
  58.4 5.5 %collective-permute-start.35 = (f32[128,128]{1,0:T(8,128)S(1)}, f32[128,128]{1,0:T(8,128)S(1)}, u32[]{:S(2)}, u32[]{:S(2)}) collective-permute-start(f32[128,128]{1,0:T(8,128)S(1)} %shard_map.102.other), channel_id=1, source_target_pairs={{0,1},{1,0},{2,3},{3,2},{4,10},{5,11},{6,8},{7,9},{8,6},{9,7},{10,... | collective-permute-start | bytes 196616 | tf_op jit(solution)/shard_map/ppermute | solution.py:331
  58.7 5.3 %collective-permute-start.34 = (f32[128,128]{1,0:T(8,128)S(1)}, f32[128,128]{1,0:T(8,128)S(1)}, u32[]{:S(2)}, u32[]{:S(2)}) collective-permute-start(f32[128,128]{1,0:T(8,128)S(1)} %shard_map.102.other), channel_id=1, source_target_pairs={{0,1},{1,0},{2,3},{3,2},{4,8},{5,9},{6,10},{7,11},{8,4},{9,5},{10,... | collective-permute-start | bytes 196616 | tf_op jit(solution)/shard_map/ppermute | solution.py:331
  65.6 5.9 %collective-permute-start.36 = (f32[128,128]{1,0:T(8,128)S(1)}, f32[128,128]{1,0:T(8,128)S(1)}, u32[]{:S(2)}, u32[]{:S(2)}) collective-permute-start(f32[128,128]{1,0:T(8,128)S(1)} %shard_map.103.mine), channel_id=1, source_target_pairs={{0,1},{1,0},{2,3},{3,2},{4,5},{5,4},{6,7},{7,6},{8,9},{9,8},{10,11... | collective-permute-start | bytes 196616 | tf_op jit(solution)/shard_map/ppermute | solution.py:331
  (21 other events, 106.2 us)

commit v11 on v10

--- a/solution.py
+++ b/solution.py
@@ -141,9 +141,10 @@
     crossing[...] = jnp.where(lax.axis_index("slab") % 2 == 1, whole, stepped[...])
 
 
-def urgent_kernel(base, more, less, out):
-    kept = lax.axis_index("slab") % 4 == 2
-    out[...] = base[...] - keep(kept, more) - keep(kept, less)
+def even_slabs_kernel(base, more, less, out):
+    s = lax.axis_index("slab")
+    even = s % 2 == 0
+    out[...] = base[...] - keep(even & (s > 0), more) - keep(even, less)
 
 
 def reduce_kernel(spacing, count, base, *refs):
@@ -381,7 +382,7 @@
         d = 2**level
         if level == levels - 1:
             beneath = call(kernel(top_kernel, d), near, far, *front, scratch=[store])
-            shares = both(beneath, [(d, 0, 1, d - 1)], [(d, 0, 1, d + 3)])
+            shares = both(beneath, [(d, 0, 1, d + 1)], [(d, 0, 1, d - 1)])
             if level > 1:
                 shares = shares + late
             pivot = call(kernel(pivot_kernel, d), near, far, *back, pivot, scratch=[store])
@@ -405,11 +406,10 @@
             up if level == 0 else jnp.zeros_like(up),
             outs=2,
             scratch=[store],
-            unused=(base,) if level == 1 else (),
         )
         if level == 0:
-            more = send(over, [(a, b) for k in urgent for a, b in ((k - 1, k), (k, k - 1))])
-            less = send(beneath, [(b + 1, b, b - 2) for b in urgent])
+            more = send(over, between)
+            less = send(beneath, [(a, a ^ 1) for a in every])
             pivot = call(
                 kernel(pivot_kernel, d),
                 near,
@@ -420,23 +420,16 @@
                 unused=(over,),
                 flops=1,
             )
-            held = call(copy_kernel, beneath, unused=(pivot,), flops=1)
-            late = [send(held, [(b + 1, b, b + 3) for b in patient])]
-            if len(patient) > 1:
-                held = call(copy_kernel, over, unused=(pivot,), flops=1)
-                ways = [(b - 1, b, b + 1 if b + 4 < slabs else b + 3) for b in patient if b > 0]
-                late.append(send(held, ways))
-            near = call(urgent_kernel, base, more, less)
-            far = exchange(near, urgent)
-            base = call(kernel(reduce_kernel, d, len(late)), base, *late, unused=(near,))
-            base_far = exchange(base, patient)
+            base = near = call(even_slabs_kernel, base, more, less)
+            base_far = far = exchange(near, every[::2])
+            late = ()
             continue
         more = both(over, [(b - d, b, b - 1) for b in urgent], [(b - d, b, b - 3) for b in urgent])
         less = both(
             beneath, [(b + d, b, b + 1) for b in urgent], [(b + d, b, b + 3) for b in urgent]
         )
         pivot = call(kernel(pivot_kernel, d), near, far, *back, pivot, scratch=[store])
-        if level > 1:
+        if late:
             count = len(late) // 2
             base = call(kernel(reduce_kernel, d // 2, count), base, *late[::2], unused=(beneath,))
             base_far = call(
@@ -445,7 +438,7 @@
         near = base - more[0] - less[0]
         far = base_far - more[1] - less[1]
         held = call(copy_kernel, beneath, unused=(more[0],))
-        ways = [(b + d, b, b + 1, b + d + 1) for b in patient]
+        ways = [(b + d, b, b + 1) for b in patient]
         late = both(held, ways, ways)
         if len(patient) > 1:
             held = call(copy_kernel, over, unused=(more[0],))
@@ -472,8 +465,7 @@
         else:
             sources = [a for a in every if a % (4 * d) == 2 * d]
             up_near = send(solved, [(a, a - d, a - d + 1, a + 1) for a in sources])
-            last = -3 if d == 2 else 3
-            up_far = send(solved, [(a, a - d, a - d + 1, a + last) for a in sources], 2)
+            up_far = send(solved, [(a, a - d, a - d + 1, a + 1) for a in sources], 2)
             low_far = send(solved, [(a, a + d, a + d + 1, a - 1) for a in sources], 2)
             low_near = send(solved, [(a, a + d, a + d + 1) for a in sources])
             vectors = (low_near, low_far, up_near, up_far) + early

time: 72.4 us -> 72.8 us (level)
  starting transfers between devices: 45.6 us -> 51.5 us
  waiting for transfers between devices: 20.5 us -> 15 us
    ppermute x37 -> x34, starting transfers between devices: 45.6 us -> 51.5 us  [send(): lax.ppermute(values, ('slab', 'col'), completed(route, slabs * cols, cols))]
    ppermute x37 -> x34, waiting for transfers between devices: 20.5 us -> 15 us  [send(): lax.ppermute(values, ('slab', 'col'), completed(route, slabs * cols, cols))]
    pallas_call x23 -> x20, Pallas kernels: 5.8 us -> 5.71 us  [call(): pl.pallas_call(kernel, out_shape=shape if outs == 1 else (shape,) * outs,...]
  transfers between devices with their start and end apart: 37 -> 34, of which waited for: 16 -> 16; matrix products, arithmetic and copies ran while one was open for 0% -> 0% of each run, Pallas kernels for 4% -> 3%
where the time goes in v11:
time: 72.8 us; the launch traced here: 72.5 us
  starting transfers between devices  51.5 us (71%)
  waiting for transfers between devices  15 us (21%)
  Pallas kernels  5.71 us (8%)
    ppermute x34, starting transfers between devices, send(): lax.ppermute(values, ('slab', 'col'), completed(route, slabs * cols, cols))  51.5 us
    ppermute x34, waiting for transfers between devices, send(): lax.ppermute(values, ('slab', 'col'), completed(route, slabs * cols, cols))  15 us
    pallas_call x20, Pallas kernels, call(): pl.pallas_call(kernel, out_shape=shape if outs == 1 else (shape,) * outs,...  5.71 us
  transfers between devices with their start and end apart: 34, of which 16 were waited for; matrix products, arithmetic and copies ran while one was open for 0% of the time, Pallas kernels for 3%

profile of v11, /device:TPU:13, one launch (start us, length us, event | category | flops | bytes accessed | tf_op | source)
XLA Modules:
  0.0 72.5 jit_solution(14689062036793914026)
XLA Ops:
  1.2 1.3 %collective-permute-done.other = f32[1,128,128]{2,1,0:T(8,128)S(1)} collective-permute-done((f32[1,128,128]{2,1,0:T(8,128)}, f32[1,128,128]{2,1,0:T(8,128)S(1)}, u32[]{:S(2)}, u32[]{:S(2)}) %collective-permute-start) | collective-permute-done | bytes 65568 | tf_op jit(solution)/shard_map/ppermute | solution.py:332
  3.3 1.3 %collective-permute-start.6 = (f32[128,128]{1,0:T(8,128)S(1)}, f32[128,128]{1,0:T(8,128)S(1)}, u32[]{:S(2)}, u32[]{:S(2)}) collective-permute-start(f32[128,128]{1,0:T(8,128)S(1)} %get-tuple-element.18), channel_id=1, source_target_pairs={{0,2},{1,3},{2,0},{3,1},{4,6},{5,7},{6,4},{7,5},{8,10},{9,11},{10,... | collective-permute-start | bytes 196616 | tf_op jit(solution)/shard_map/ppermute | solution.py:332
  4.5 1.2 %collective-permute-start.4 = (f32[128,128]{1,0:T(8,128)S(1)}, f32[128,128]{1,0:T(8,128)S(1)}, u32[]{:S(2)}, u32[]{:S(2)}) collective-permute-start(f32[128,128]{1,0:T(8,128)S(1)} %get-tuple-element.16.packed.near), channel_id=1, source_target_pairs={{0,1},{1,0},{2,3},{3,2},{4,10},{5,11},{6,8},{7,9},{8,6},{9,7},{10,... | collective-permute-start | bytes 196616 | tf_op jit(solution)/shard_map/ppermute | solution.py:332
  6.9 1.2 %collective-permute-start.2 = (f32[128,128]{1,0:T(8,128)S(1)}, f32[128,128]{1,0:T(8,128)S(1)}, u32[]{:S(2)}, u32[]{:S(2)}) collective-permute-start(f32[128,128]{1,0:T(8,128)S(1)} %get-tuple-element.16.packed.near), channel_id=1, source_target_pairs={{0,2},{1,3},{2,0},{3,1},{4,6},{5,7},{6,4},{7,5},{8,10},{9,11},{10,... | collective-permute-start | bytes 196616 | tf_op jit(solution)/shard_map/ppermute | solution.py:332
  8.4 1.2 %collective-permute-done.4.next_far = f32[128,128]{1,0:T(8,128)S(1)} collective-permute-done((f32[128,128]{1,0:T(8,128)S(1)}, f32[128,128]{1,0:T(8,128)S(1)}, u32[]{:S(2)}, u32[]{:S(2)}) %collective-permute-start.4) | collective-permute-done | bytes 65568 | tf_op jit(solution)/shard_map/ppermute | solution.py:332
  12.5 1.7 %collective-permute-start.9 = (f32[10,128,512]{2,1,0:T(8,128)S(1)}, f32[10,128,512]{2,1,0:T(8,128)S(1)}, u32[]{:S(2)}, u32[]{:S(2)}) collective-permute-start(f32[10,128,512]{2,1,0:T(8,128)S(1)} %shard_map.88.own.refs_6_.refs_4_), channel_id=1, source_target_pairs={{0,1},{1,0},{2,3},{3,2},{4,5},{5,4},{6,7},{7,6},{8,9},{9,8},{10,11... | collective-permute-start | bytes 7864328 | tf_op jit(solution)/shard_map/ppermute | solution.py:332
  15.0 2.9 %collective-permute-done.8.next_far.far = f32[128,128]{1,0:T(8,128)S(1)} collective-permute-done((f32[128,128]{1,0:T(8,128)S(1)}, f32[128,128]{1,0:T(8,128)S(1)}, u32[]{:S(2)}, u32[]{:S(2)}) %collective-permute-start.8) | collective-permute-done | bytes 65568 | tf_op jit(solution)/shard_map/ppermute | solution.py:332
  19.8 2.5 %collective-permute-start.10 = (f32[128,128]{1,0:T(8,128)S(1)}, f32[128,128]{1,0:T(8,128)S(1)}, u32[]{:S(2)}, u32[]{:S(2)}) collective-permute-start(f32[128,128]{1,0:T(8,128)S(1)} %get-tuple-element.23.refs_0_), channel_id=1, source_target_pairs={{0,1},{1,0},{2,3},{3,2},{4,8},{5,9},{6,10},{7,11},{8,4},{9,5},{10,... | collective-permute-start | bytes 196616 | tf_op jit(solution)/shard_map/ppermute | solution.py:332
  22.9 1.1 %collective-permute-done.10.more = f32[128,128]{1,0:T(8,128)S(1)} collective-permute-done((f32[128,128]{1,0:T(8,128)S(1)}, f32[128,128]{1,0:T(8,128)S(1)}, u32[]{:S(2)}, u32[]{:S(2)}) %collective-permute-start.10) | collective-permute-done | bytes 65568 | tf_op jit(solution)/shard_map/ppermute | solution.py:332
  24.1 1.9 %collective-permute-start.12 = (f32[128,128]{1,0:T(8,128)S(1)}, f32[128,128]{1,0:T(8,128)S(1)}, u32[]{:S(2)}, u32[]{:S(2)}) collective-permute-start(f32[128,128]{1,0:T(8,128)S(1)} %shard_map.90.near.refs_0_), channel_id=1, source_target_pairs={{0,2},{1,3},{2,0},{3,1},{4,5},{5,4},{6,7},{7,6},{8,10},{9,11},{10,... | collective-permute-start | bytes 196616 | tf_op jit(solution)/shard_map/ppermute | solution.py:332
  27.2 3.0 %collective-permute-start.13 = (f32[128,128]{1,0:T(8,128)S(1)}, f32[128,128]{1,0:T(8,128)S(1)}, u32[]{:S(2)}, u32[]{:S(2)}) collective-permute-start(f32[128,128]{1,0:T(8,128)S(1)} %get-tuple-element.25), channel_id=1, source_target_pairs={{0,1},{1,0},{2,3},{3,2},{4,5},{5,4},{6,7},{7,6},{8,16},{9,17},{10,... | collective-permute-start | bytes 196616 | tf_op jit(solution)/shard_map/ppermute | solution.py:332
  30.3 3.5 %collective-permute-start.16 = (f32[128,128]{1,0:T(8,128)S(1)}, f32[128,128]{1,0:T(8,128)S(1)}, u32[]{:S(2)}, u32[]{:S(2)}) collective-permute-start(f32[128,128]{1,0:T(8,128)S(1)} %get-tuple-element.26.values), channel_id=1, source_target_pairs={{0,1},{1,0},{2,3},{3,2},{4,5},{5,4},{6,7},{7,6},{8,9},{9,8},{10,11... | collective-permute-start | bytes 196616 | tf_op jit(solution)/shard_map/ppermute | solution.py:332
  33.8 2.3 %collective-permute-start.20 = (f32[128,128]{1,0:T(8,128)S(1)}, f32[128,128]{1,0:T(8,128)S(1)}, u32[]{:S(2)}, u32[]{:S(2)}) collective-permute-start(f32[128,128]{1,0:T(8,128)S(1)} %shard_map.93), channel_id=1, source_target_pairs={{0,6},{1,7},{2,4},{3,5},{4,8},{5,9},{6,10},{7,11},{8,2},{9,3},{10,... | collective-permute-start | bytes 196616 | tf_op jit(solution)/shard_map/ppermute | solution.py:332
  36.3 3.3 %collective-permute-start.18 = (f32[128,128]{1,0:T(8,128)S(1)}, f32[128,128]{1,0:T(8,128)S(1)}, u32[]{:S(2)}, u32[]{:S(2)}) collective-permute-start(f32[128,128]{1,0:T(8,128)S(1)} %shard_map.92), channel_id=1, source_target_pairs={{0,6},{1,7},{2,4},{3,5},{4,12},{5,13},{6,14},{7,15},{8,9},{9,8},{1... | collective-permute-start | bytes 196616 | tf_op jit(solution)/shard_map/ppermute | solution.py:332
  39.7 1.8 %collective-permute-start.17 = (f32[128,128]{1,0:T(8,128)S(1)}, f32[128,128]{1,0:T(8,128)S(1)}, u32[]{:S(2)}, u32[]{:S(2)}) collective-permute-start(f32[128,128]{1,0:T(8,128)S(1)} %shard_map.92), channel_id=1, source_target_pairs={{0,4},{1,5},{2,6},{3,7},{4,20},{5,21},{6,22},{7,23},{8,9},{9,8},{1... | collective-permute-start | bytes 196616 | tf_op jit(solution)/shard_map/ppermute | solution.py:332
  42.4 1.7 %collective-permute-start.22 = (f32[128,128]{1,0:T(8,128)S(1)}, f32[128,128]{1,0:T(8,128)S(1)}, u32[]{:S(2)}, u32[]{:S(2)}) collective-permute-start(f32[128,128]{1,0:T(8,128)S(1)} %shard_map.97.part), channel_id=1, source_target_pairs={{0,18},{1,19},{2,16},{3,17},{4,0},{5,1},{6,2},{7,3},{8,9},{9,8},{1... | collective-permute-start | bytes 196616 | tf_op jit(solution)/shard_map/ppermute | solution.py:332
  44.1 2.9 %collective-permute-start.28 = (f32[128,128]{1,0:T(8,128)S(1)}, f32[128,128]{1,0:T(8,128)S(1)}, u32[]{:S(2)}, u32[]{:S(2)}) collective-permute-start(f32[128,128]{1,0:T(8,128)S(1)} %shard_map.97.part), channel_id=1, source_target_pairs={{0,10},{1,11},{2,8},{3,9},{4,0},{5,1},{6,2},{7,3},{8,14},{9,15},{1... | collective-permute-start | bytes 196616 | tf_op jit(solution)/shard_map/ppermute | solution.py:332
  47.1 3.5 %collective-permute-start.26 = (f32[128,128]{1,0:T(8,128)S(1)}, f32[128,128]{1,0:T(8,128)S(1)}, u32[]{:S(2)}, u32[]{:S(2)}) collective-permute-start(f32[128,128]{1,0:T(8,128)S(1)} %shard_map.98.other), channel_id=1, source_target_pairs={{0,1},{1,0},{2,3},{3,2},{4,5},{5,4},{6,7},{7,6},{8,14},{9,15},{10,... | collective-permute-start | bytes 196616 | tf_op jit(solution)/shard_map/ppermute | solution.py:332
  51.3 4.4 %collective-permute-start.23 = (f32[128,128]{1,0:T(8,128)S(1)}, f32[128,128]{1,0:T(8,128)S(1)}, u32[]{:S(2)}, u32[]{:S(2)}) collective-permute-start(f32[128,128]{1,0:T(8,128)S(1)} %shard_map.98.other), channel_id=1, source_target_pairs={{0,1},{1,0},{2,3},{3,2},{4,5},{5,4},{6,7},{7,6},{8,9},{9,8},{10,11... | collective-permute-start | bytes 196616 | tf_op jit(solution)/shard_map/ppermute | solution.py:332
  57.1 1.2 %collective-permute-start.32 = (f32[128,128]{1,0:T(8,128)S(1)}, f32[128,128]{1,0:T(8,128)S(1)}, u32[]{:S(2)}, u32[]{:S(2)}) collective-permute-start(f32[128,128]{1,0:T(8,128)S(1)} %shard_map.99.other), channel_id=1, source_target_pairs={{0,1},{1,0},{2,3},{3,2},{4,10},{5,11},{6,8},{7,9},{8,6},{9,7},{10,... | collective-permute-start | bytes 196616 | tf_op jit(solution)/shard_map/ppermute | solution.py:332
  58.4 1.6 %collective-permute-start.31 = (f32[128,128]{1,0:T(8,128)S(1)}, f32[128,128]{1,0:T(8,128)S(1)}, u32[]{:S(2)}, u32[]{:S(2)}) collective-permute-start(f32[128,128]{1,0:T(8,128)S(1)} %shard_map.99.other), channel_id=1, source_target_pairs={{0,1},{1,0},{2,3},{3,2},{4,8},{5,9},{6,10},{7,11},{8,4},{9,5},{10,... | collective-permute-start | bytes 196616 | tf_op jit(solution)/shard_map/ppermute | solution.py:332
  60.7 1.7 %collective-permute-done.32.refs_3_ = f32[128,128]{1,0:T(8,128)S(1)} collective-permute-done((f32[128,128]{1,0:T(8,128)S(1)}, f32[128,128]{1,0:T(8,128)S(1)}, u32[]{:S(2)}, u32[]{:S(2)}) %collective-permute-start.32) | collective-permute-done | bytes 65568 | tf_op jit(solution)/shard_map/ppermute | solution.py:332
  63.1 1.4 %shard_map.100.mine = f32[128,128]{1,0:T(8,128)S(1)} custom-call(f32[128,128]{1,0:T(8,128)S(1)} %shard_map.97.part, f32[128,128]{1,0:T(8,128)S(1)} %shard_map.99.other, f32[128,128]{1,0:T(8,128)S(1)} %collective-permute-done.29.refs_0_, f32[128,128]{1,0:T(8,128)S(1)} %collective-permute-done.30.refs_1_, f32[128,128]{1,0:T(8,128)S(1)} %collective-permute-done.31.refs_2_, ...), custom_call_target="tpu_custom_call" | custom-call | flops 1000000000 | bytes 1 | tf_op jit(solution)/shard_map/pallas_call | solution.py:288
  64.5 6.4 %collective-permute-start.33 = (f32[128,128]{1,0:T(8,128)S(1)}, f32[128,128]{1,0:T(8,128)S(1)}, u32[]{:S(2)}, u32[]{:S(2)}) collective-permute-start(f32[128,128]{1,0:T(8,128)S(1)} %shard_map.100.mine), channel_id=1, source_target_pairs={{0,1},{1,0},{2,3},{3,2},{4,5},{5,4},{6,7},{7,6},{8,9},{9,8},{10,11... | collective-permute-start | bytes 196616 | tf_op jit(solution)/shard_map/ppermute | solution.py:332
  (83 shorter events, 17.1 us)
Async XLA Ops:
  0.7 7.7 %collective-permute-start.5 = (f32[1,128,512]{2,1,0:T(8,128)}, f32[1,128,512]{2,1,0:T(8,128)S(1)}, u32[]{:S(2)}, u32[]{:S(2)}) collective-permute-start(f32[1,128,512]{2,1,0:T(8,128)} %own_e.1), channel_id=1, source_target_pairs={{0,1},{1,0},{2,3},{3,2},{4,5},{5,4},{6,7},{7,6},{8,9},{9,8},{10,11... | collective-permute-start | bytes 786440 | tf_op jit(solution)/shard_map/ppermute | solution.py:332
  3.3 4.8 %collective-permute-start.6 = (f32[128,128]{1,0:T(8,128)S(1)}, f32[128,128]{1,0:T(8,128)S(1)}, u32[]{:S(2)}, u32[]{:S(2)}) collective-permute-start(f32[128,128]{1,0:T(8,128)S(1)} %get-tuple-element.18), channel_id=1, source_target_pairs={{0,2},{1,3},{2,0},{3,1},{4,6},{5,7},{6,4},{7,5},{8,10},{9,11},{10,... | collective-permute-start | bytes 196616 | tf_op jit(solution)/shard_map/ppermute | solution.py:332
  4.5 5.1 %collective-permute-start.4 = (f32[128,128]{1,0:T(8,128)S(1)}, f32[128,128]{1,0:T(8,128)S(1)}, u32[]{:S(2)}, u32[]{:S(2)}) collective-permute-start(f32[128,128]{1,0:T(8,128)S(1)} %get-tuple-element.16.packed.near), channel_id=1, source_target_pairs={{0,1},{1,0},{2,3},{3,2},{4,10},{5,11},{6,8},{7,9},{8,6},{9,7},{10,... | collective-permute-start | bytes 196616 | tf_op jit(solution)/shard_map/ppermute | solution.py:332
  5.8 4.9 %collective-permute-start.3 = (f32[128,128]{1,0:T(8,128)S(1)}, f32[128,128]{1,0:T(8,128)S(1)}, u32[]{:S(2)}, u32[]{:S(2)}) collective-permute-start(f32[128,128]{1,0:T(8,128)S(1)} %get-tuple-element.16.packed.near), channel_id=1, source_target_pairs={{0,1},{1,0},{2,3},{3,2},{4,8},{5,9},{6,10},{7,11},{8,4},{9,5},{10,... | collective-permute-start | bytes 196616 | tf_op jit(solution)/shard_map/ppermute | solution.py:332
  6.9 3.9 %collective-permute-start.2 = (f32[128,128]{1,0:T(8,128)S(1)}, f32[128,128]{1,0:T(8,128)S(1)}, u32[]{:S(2)}, u32[]{:S(2)}) collective-permute-start(f32[128,128]{1,0:T(8,128)S(1)} %get-tuple-element.16.packed.near), channel_id=1, source_target_pairs={{0,2},{1,3},{2,0},{3,1},{4,6},{5,7},{6,4},{7,5},{8,10},{9,11},{10,... | collective-permute-start | bytes 196616 | tf_op jit(solution)/shard_map/ppermute | solution.py:332
  8.1 4.2 %collective-permute-start.7 = (f32[128,128]{1,0:T(8,128)S(1)}, f32[128,128]{1,0:T(8,128)S(1)}, u32[]{:S(2)}, u32[]{:S(2)}) collective-permute-start(f32[128,128]{1,0:T(8,128)S(1)} %get-tuple-element.20), channel_id=1, source_target_pairs={{0,4},{1,5},{2,6},{3,7},{4,0},{5,1},{6,2},{7,3},{8,12},{9,13},{10,... | collective-permute-start | bytes 196616 | tf_op jit(solution)/shard_map/ppermute | solution.py:332
  12.5 6.3 %collective-permute-start.9 = (f32[10,128,512]{2,1,0:T(8,128)S(1)}, f32[10,128,512]{2,1,0:T(8,128)S(1)}, u32[]{:S(2)}, u32[]{:S(2)}) collective-permute-start(f32[10,128,512]{2,1,0:T(8,128)S(1)} %shard_map.88.own.refs_6_.refs_4_), channel_id=1, source_target_pairs={{0,1},{1,0},{2,3},{3,2},{4,5},{5,4},{6,7},{7,6},{8,9},{9,8},{10,11... | collective-permute-start | bytes 7864328 | tf_op jit(solution)/shard_map/ppermute | solution.py:332
  19.8 4.2 %collective-permute-start.10 = (f32[128,128]{1,0:T(8,128)S(1)}, f32[128,128]{1,0:T(8,128)S(1)}, u32[]{:S(2)}, u32[]{:S(2)}) collective-permute-start(f32[128,128]{1,0:T(8,128)S(1)} %get-tuple-element.23.refs_0_), channel_id=1, source_target_pairs={{0,1},{1,0},{2,3},{3,2},{4,8},{5,9},{6,10},{7,11},{8,4},{9,5},{10,... | collective-permute-start | bytes 196616 | tf_op jit(solution)/shard_map/ppermute | solution.py:332
  26.9 9.4 %collective-permute-start.15 = (f32[128,128]{1,0:T(8,128)S(1)}, f32[128,128]{1,0:T(8,128)S(1)}, u32[]{:S(2)}, u32[]{:S(2)}) collective-permute-start(f32[128,128]{1,0:T(8,128)S(1)} %get-tuple-element.25), channel_id=1, source_target_pairs={{0,1},{1,0},{2,3},{3,2},{4,8},{5,9},{6,10},{7,11},{8,18},{9,19},{1... | collective-permute-start | bytes 196616 | tf_op jit(solution)/shard_map/ppermute | solution.py:332
  27.2 6.6 %collective-permute-start.13 = (f32[128,128]{1,0:T(8,128)S(1)}, f32[128,128]{1,0:T(8,128)S(1)}, u32[]{:S(2)}, u32[]{:S(2)}) collective-permute-start(f32[128,128]{1,0:T(8,128)S(1)} %get-tuple-element.25), channel_id=1, source_target_pairs={{0,1},{1,0},{2,3},{3,2},{4,5},{5,4},{6,7},{7,6},{8,16},{9,17},{10,... | collective-permute-start | bytes 196616 | tf_op jit(solution)/shard_map/ppermute | solution.py:332
  30.3 6.0 %collective-permute-start.16 = (f32[128,128]{1,0:T(8,128)S(1)}, f32[128,128]{1,0:T(8,128)S(1)}, u32[]{:S(2)}, u32[]{:S(2)}) collective-permute-start(f32[128,128]{1,0:T(8,128)S(1)} %get-tuple-element.26.values), channel_id=1, source_target_pairs={{0,1},{1,0},{2,3},{3,2},{4,5},{5,4},{6,7},{7,6},{8,9},{9,8},{10,11... | collective-permute-start | bytes 196616 | tf_op jit(solution)/shard_map/ppermute | solution.py:332
  33.8 7.7 %collective-permute-start.20 = (f32[128,128]{1,0:T(8,128)S(1)}, f32[128,128]{1,0:T(8,128)S(1)}, u32[]{:S(2)}, u32[]{:S(2)}) collective-permute-start(f32[128,128]{1,0:T(8,128)S(1)} %shard_map.93), channel_id=1, source_target_pairs={{0,6},{1,7},{2,4},{3,5},{4,8},{5,9},{6,10},{7,11},{8,2},{9,3},{10,... | collective-permute-start | bytes 196616 | tf_op jit(solution)/shard_map/ppermute | solution.py:332
  36.1 5.4 %collective-permute-start.19 = (f32[128,128]{1,0:T(8,128)S(1)}, f32[128,128]{1,0:T(8,128)S(1)}, u32[]{:S(2)}, u32[]{:S(2)}) collective-permute-start(f32[128,128]{1,0:T(8,128)S(1)} %shard_map.93), channel_id=1, source_target_pairs={{0,4},{1,5},{2,6},{3,7},{4,8},{5,9},{6,10},{7,11},{8,0},{9,1},{10,... | collective-permute-start | bytes 196616 | tf_op jit(solution)/shard_map/ppermute | solution.py:332
  36.3 5.2 %collective-permute-start.18 = (f32[128,128]{1,0:T(8,128)S(1)}, f32[128,128]{1,0:T(8,128)S(1)}, u32[]{:S(2)}, u32[]{:S(2)}) collective-permute-start(f32[128,128]{1,0:T(8,128)S(1)} %shard_map.92), channel_id=1, source_target_pairs={{0,6},{1,7},{2,4},{3,5},{4,12},{5,13},{6,14},{7,15},{8,9},{9,8},{1... | collective-permute-start | bytes 196616 | tf_op jit(solution)/shard_map/ppermute | solution.py:332
  42.4 4.7 %collective-permute-start.22 = (f32[128,128]{1,0:T(8,128)S(1)}, f32[128,128]{1,0:T(8,128)S(1)}, u32[]{:S(2)}, u32[]{:S(2)}) collective-permute-start(f32[128,128]{1,0:T(8,128)S(1)} %shard_map.97.part), channel_id=1, source_target_pairs={{0,18},{1,19},{2,16},{3,17},{4,0},{5,1},{6,2},{7,3},{8,9},{9,8},{1... | collective-permute-start | bytes 196616 | tf_op jit(solution)/shard_map/ppermute | solution.py:332
  44.1 7.2 %collective-permute-start.28 = (f32[128,128]{1,0:T(8,128)S(1)}, f32[128,128]{1,0:T(8,128)S(1)}, u32[]{:S(2)}, u32[]{:S(2)}) collective-permute-start(f32[128,128]{1,0:T(8,128)S(1)} %shard_map.97.part), channel_id=1, source_target_pairs={{0,10},{1,11},{2,8},{3,9},{4,0},{5,1},{6,2},{7,3},{8,14},{9,15},{1... | collective-permute-start | bytes 196616 | tf_op jit(solution)/shard_map/ppermute | solution.py:332
  47.1 8.6 %collective-permute-start.27 = (f32[128,128]{1,0:T(8,128)S(1)}, f32[128,128]{1,0:T(8,128)S(1)}, u32[]{:S(2)}, u32[]{:S(2)}) collective-permute-start(f32[128,128]{1,0:T(8,128)S(1)} %shard_map.97.part), channel_id=1, source_target_pairs={{0,8},{1,9},{2,10},{3,11},{4,0},{5,1},{6,2},{7,3},{8,12},{9,13},{1... | collective-permute-start | bytes 196616 | tf_op jit(solution)/shard_map/ppermute | solution.py:332
  47.1 8.6 %collective-permute-start.26 = (f32[128,128]{1,0:T(8,128)S(1)}, f32[128,128]{1,0:T(8,128)S(1)}, u32[]{:S(2)}, u32[]{:S(2)}) collective-permute-start(f32[128,128]{1,0:T(8,128)S(1)} %shard_map.98.other), channel_id=1, source_target_pairs={{0,1},{1,0},{2,3},{3,2},{4,5},{5,4},{6,7},{7,6},{8,14},{9,15},{10,... | collective-permute-start | bytes 196616 | tf_op jit(solution)/shard_map/ppermute | solution.py:332
  50.6 5.1 %collective-permute-start.25 = (f32[128,128]{1,0:T(8,128)S(1)}, f32[128,128]{1,0:T(8,128)S(1)}, u32[]{:S(2)}, u32[]{:S(2)}) collective-permute-start(f32[128,128]{1,0:T(8,128)S(1)} %shard_map.98.other), channel_id=1, source_target_pairs={{0,1},{1,0},{2,3},{3,2},{4,5},{5,4},{6,7},{7,6},{8,12},{9,13},{10,... | collective-permute-start | bytes 196616 | tf_op jit(solution)/shard_map/ppermute | solution.py:332
  51.3 4.4 %collective-permute-start.24 = (f32[128,128]{1,0:T(8,128)S(1)}, f32[128,128]{1,0:T(8,128)S(1)}, u32[]{:S(2)}, u32[]{:S(2)}) collective-permute-start(f32[128,128]{1,0:T(8,128)S(1)} %shard_map.98.other), channel_id=1, source_target_pairs={{0,1},{1,0},{2,3},{3,2},{4,5},{5,4},{6,7},{7,6},{8,9},{9,8},{10,11... | collective-permute-start | bytes 196616 | tf_op jit(solution)/shard_map/ppermute | solution.py:332
  51.3 5.3 %collective-permute-start.23 = (f32[128,128]{1,0:T(8,128)S(1)}, f32[128,128]{1,0:T(8,128)S(1)}, u32[]{:S(2)}, u32[]{:S(2)}) collective-permute-start(f32[128,128]{1,0:T(8,128)S(1)} %shard_map.98.other), channel_id=1, source_target_pairs={{0,1},{1,0},{2,3},{3,2},{4,5},{5,4},{6,7},{7,6},{8,9},{9,8},{10,11... | collective-permute-start | bytes 196616 | tf_op jit(solution)/shard_map/ppermute | solution.py:332
  57.1 5.3 %collective-permute-start.32 = (f32[128,128]{1,0:T(8,128)S(1)}, f32[128,128]{1,0:T(8,128)S(1)}, u32[]{:S(2)}, u32[]{:S(2)}) collective-permute-start(f32[128,128]{1,0:T(8,128)S(1)} %shard_map.99.other), channel_id=1, source_target_pairs={{0,1},{1,0},{2,3},{3,2},{4,10},{5,11},{6,8},{7,9},{8,6},{9,7},{10,... | collective-permute-start | bytes 196616 | tf_op jit(solution)/shard_map/ppermute | solution.py:332
  58.4 4.4 %collective-permute-start.31 = (f32[128,128]{1,0:T(8,128)S(1)}, f32[128,128]{1,0:T(8,128)S(1)}, u32[]{:S(2)}, u32[]{:S(2)}) collective-permute-start(f32[128,128]{1,0:T(8,128)S(1)} %shard_map.99.other), channel_id=1, source_target_pairs={{0,1},{1,0},{2,3},{3,2},{4,8},{5,9},{6,10},{7,11},{8,4},{9,5},{10,... | collective-permute-start | bytes 196616 | tf_op jit(solution)/shard_map/ppermute | solution.py:332
  64.5 7.3 %collective-permute-start.33 = (f32[128,128]{1,0:T(8,128)S(1)}, f32[128,128]{1,0:T(8,128)S(1)}, u32[]{:S(2)}, u32[]{:S(2)}) collective-permute-start(f32[128,128]{1,0:T(8,128)S(1)} %shard_map.100.mine), channel_id=1, source_target_pairs={{0,1},{1,0},{2,3},{3,2},{4,5},{5,4},{6,7},{7,6},{8,9},{9,8},{10,11... | collective-permute-start | bytes 196616 | tf_op jit(solution)/shard_map/ppermute | solution.py:332
  (18 other events, 88.8 us)

commit v12 on v11

--- a/solution.py
+++ b/solution.py
@@ -177,14 +177,23 @@
         out[...] = rest[...] - half_step * rotate(real_product(own[0], mate[0], store))
 
 
-def level_kernel(spacing, near, far, own, mate, tail, *refs):
+def level_kernel(spacing, near, far, own, mate, *refs):
     beneath, above, store = refs[-3:]
 
     @pl.when(lax.axis_index("slab") % (2 * spacing) == spacing)
     def _():
         load_vector(store, near[...], far[...])
-        above[...] = complex_product(own[2:4], mate[2:4], store) + tail[...]
+        above[...] = complex_product(own[2:4], mate[2:4], store)
         beneath[...] = complex_product(own[0:2], mate[0:2], store)
+
+
+def over_kernel(spacing, near, far, own, mate, *refs):
+    tail, _, out, store = refs
+
+    @pl.when(lax.axis_index("slab") % (2 * spacing) == spacing)
+    def _():
+        load_vector(store, near[...], far[...])
+        out[...] = complex_product(own[2:4], mate[2:4], store) + tail[...]
 
 
 def top_kernel(spacing, near, far, own, mate, *refs):
@@ -378,13 +387,31 @@
     base = call(even_kernel, rest, stepped, far, *t_pair, scratch=[store])
 
     pivot = near
+    waiting = None
+
+    def late_shares(after):
+        if waiting is None:
+            return ()
+        beneath, over, d = waiting
+        patient = [b for b in every if b % (4 * d) == 0]
+        held = call(copy_kernel, beneath, unused=(after,))
+        ways = [(b + d, b, b + 1) for b in patient]
+        shares = both(held, ways, ways)
+        if len(patient) > 1:
+            held = call(copy_kernel, over, unused=(after,))
+            shares += both(
+                held,
+                [(b - d, b, b - d + 1) for b in patient if b > 0],
+                [(b - d, b, b - d + 3) for b in patient if b > 0],
+            )
+        return shares
+
     for level in range(levels):
         d = 2**level
         if level == levels - 1:
             beneath = call(kernel(top_kernel, d), near, far, *front, scratch=[store])
-            shares = both(beneath, [(d, 0, 1, d + 1)], [(d, 0, 1, d - 1)])
-            if level > 1:
-                shares = shares + late
+            shares = late_shares(beneath)
+            shares += both(beneath, [(d, 0, 1, d + 1)], [(d, 0, 1, d - 1)])
             pivot = call(kernel(pivot_kernel, d), near, far, *back, pivot, scratch=[store])
             pivot = call(
                 kernel(root_kernel, len(shares) // 2),
@@ -396,17 +423,15 @@
                 scratch=[store],
             )
             break
-        urgent = [b for b in every if b % (4 * d) == 2 * d]
-        patient = [b for b in every if b % (4 * d) == 0]
-        beneath, over = call(
-            kernel(level_kernel, d),
-            near,
-            far,
-            *front,
-            up if level == 0 else jnp.zeros_like(up),
-            outs=2,
-            scratch=[store],
-        )
+        if level > 0:
+            beneath, over = call(
+                kernel(level_kernel, d), near, far, *front, outs=2, scratch=[store]
+            )
+        else:
+            beneath = call(kernel(top_kernel, d), near, far, *front, scratch=[store])
+            over = call(
+                kernel(over_kernel, d), near, far, *front, up, scratch=[store], unused=(beneath,)
+            )
         if level == 0:
             more = send(over, between)
             less = send(beneath, [(a, a ^ 1) for a in every])
@@ -422,31 +447,21 @@
             )
             base = near = call(even_slabs_kernel, base, more, less)
             base_far = far = exchange(near, every[::2])
-            late = ()
             continue
+        urgent = [b for b in every if b % (4 * d) == 2 * d]
         more = both(over, [(b - d, b, b - 1) for b in urgent], [(b - d, b, b - 3) for b in urgent])
         less = both(
             beneath, [(b + d, b, b + 1) for b in urgent], [(b + d, b, b + 3) for b in urgent]
         )
         pivot = call(kernel(pivot_kernel, d), near, far, *back, pivot, scratch=[store])
+        late = late_shares(beneath)
         if late:
             count = len(late) // 2
-            base = call(kernel(reduce_kernel, d // 2, count), base, *late[::2], unused=(beneath,))
-            base_far = call(
-                kernel(reduce_kernel, d // 2, count), base_far, *late[1::2], unused=(beneath,)
-            )
+            base = call(kernel(reduce_kernel, d // 2, count), base, *late[::2])
+            base_far = call(kernel(reduce_kernel, d // 2, count), base_far, *late[1::2])
         near = base - more[0] - less[0]
         far = base_far - more[1] - less[1]
-        held = call(copy_kernel, beneath, unused=(more[0],))
-        ways = [(b + d, b, b + 1) for b in patient]
-        late = both(held, ways, ways)
-        if len(patient) > 1:
-            held = call(copy_kernel, over, unused=(more[0],))
-            late = late + both(
-                held,
-                [(b - d, b, b - d + 1) for b in patient if b > 0],
-                [(b - d, b, b - d + 3) for b in patient if b > 0],
-            )
+        waiting = beneath, over, d
 
     solved = pivot
     for level in reversed(range(levels)):
@@ -466,8 +481,8 @@
             sources = [a for a in every if a % (4 * d) == 2 * d]
             up_near = send(solved, [(a, a - d, a - d + 1, a + 1) for a in sources])
             up_far = send(solved, [(a, a - d, a - d + 1, a + 1) for a in sources], 2)
-            low_far = send(solved, [(a, a + d, a + d + 1, a - 1) for a in sources], 2)
-            low_near = send(solved, [(a, a + d, a + d + 1) for a in sources])
+            low_far = send(solved, [(a, a + d, a + d + 1, a + 1) for a in sources], 2)
+            low_near = send(solved, [(a, a + d, a + d + 1, a + 1) for a in sources])
             vectors = (low_near, low_far, up_near, up_far) + early
         if level > 1:
             half = d // 2

time: 72.8 us -> 72.2 us (level)
  starting transfers between devices: 51.5 us -> 48.4 us
  waiting for transfers between devices: 15 us -> 17.2 us
    ppermute x34, starting transfers between devices: 51.5 us -> 48.4 us  [send(): lax.ppermute(values, ('slab', 'col'), completed(route, slabs * cols, cols))]
    ppermute x34, waiting for transfers between devices: 15 us -> 17.2 us  [send(): lax.ppermute(values, ('slab', 'col'), completed(route, slabs * cols, cols))]
    pallas_call x20 -> x21, Pallas kernels: 5.71 us -> 6.12 us  [call(): pl.pallas_call(kernel, out_shape=shape if outs == 1 else (shape,) * outs,...]
  transfers between devices with their start and end apart: 34 -> 34, of which waited for: 16 -> 19; matrix products, arithmetic and copies ran while one was open for 0% -> 0% of each run, Pallas kernels for 3% -> 4%
where the time goes in v12:
time: 72.2 us; the launch traced here: 72.1 us
  starting transfers between devices  48.4 us (67%)
  waiting for transfers between devices  17.2 us (24%)
  Pallas kernels  6.12 us (8%)
    ppermute x34, starting transfers between devices, send(): lax.ppermute(values, ('slab', 'col'), completed(route, slabs * cols, cols))  48.4 us
    ppermute x34, waiting for transfers between devices, send(): lax.ppermute(values, ('slab', 'col'), completed(route, slabs * cols, cols))  17.2 us
    pallas_call x21, Pallas kernels, call(): pl.pallas_call(kernel, out_shape=shape if outs == 1 else (shape,) * outs,...  6.12 us
  transfers between devices with their start and end apart: 34, of which 19 were waited for; matrix products, arithmetic and copies ran while one was open for 0% of the time, Pallas kernels for 4%

profile of v12, /device:TPU:13, one launch (start us, length us, event | category | flops | bytes accessed | tf_op | source)
XLA Modules:
  0.0 72.1 jit_solution(10860448962183105735)
XLA Ops:
  1.2 1.3 %collective-permute-done.other = f32[1,128,128]{2,1,0:T(8,128)S(1)} collective-permute-done((f32[1,128,128]{2,1,0:T(8,128)}, f32[1,128,128]{2,1,0:T(8,128)S(1)}, u32[]{:S(2)}, u32[]{:S(2)}) %collective-permute-start) | collective-permute-done | bytes 65568 | tf_op jit(solution)/shard_map/ppermute | solution.py:341
  3.3 1.3 %collective-permute-start.6 = (f32[128,128]{1,0:T(8,128)S(1)}, f32[128,128]{1,0:T(8,128)S(1)}, u32[]{:S(2)}, u32[]{:S(2)}) collective-permute-start(f32[128,128]{1,0:T(8,128)S(1)} %get-tuple-element.16), channel_id=1, source_target_pairs={{0,2},{1,3},{2,0},{3,1},{4,6},{5,7},{6,4},{7,5},{8,10},{9,11},{10,... | collective-permute-start | bytes 196616 | tf_op jit(solution)/shard_map/ppermute | solution.py:341
  4.5 1.2 %collective-permute-start.4 = (f32[128,128]{1,0:T(8,128)S(1)}, f32[128,128]{1,0:T(8,128)S(1)}, u32[]{:S(2)}, u32[]{:S(2)}) collective-permute-start(f32[128,128]{1,0:T(8,128)S(1)} %get-tuple-element.14.packed.near), channel_id=1, source_target_pairs={{0,1},{1,0},{2,3},{3,2},{4,10},{5,11},{6,8},{7,9},{8,6},{9,7},{10,... | collective-permute-start | bytes 196616 | tf_op jit(solution)/shard_map/ppermute | solution.py:341
  5.8 1.1 %collective-permute-start.3 = (f32[128,128]{1,0:T(8,128)S(1)}, f32[128,128]{1,0:T(8,128)S(1)}, u32[]{:S(2)}, u32[]{:S(2)}) collective-permute-start(f32[128,128]{1,0:T(8,128)S(1)} %get-tuple-element.14.packed.near), channel_id=1, source_target_pairs={{0,1},{1,0},{2,3},{3,2},{4,8},{5,9},{6,10},{7,11},{8,4},{9,5},{10,... | collective-permute-start | bytes 196616 | tf_op jit(solution)/shard_map/ppermute | solution.py:341
  6.9 1.2 %collective-permute-start.2 = (f32[128,128]{1,0:T(8,128)S(1)}, f32[128,128]{1,0:T(8,128)S(1)}, u32[]{:S(2)}, u32[]{:S(2)}) collective-permute-start(f32[128,128]{1,0:T(8,128)S(1)} %get-tuple-element.14.packed.near), channel_id=1, source_target_pairs={{0,2},{1,3},{2,0},{3,1},{4,6},{5,7},{6,4},{7,5},{8,10},{9,11},{10,... | collective-permute-start | bytes 196616 | tf_op jit(solution)/shard_map/ppermute | solution.py:341
  8.4 1.2 %collective-permute-done.4.next_far = f32[128,128]{1,0:T(8,128)S(1)} collective-permute-done((f32[128,128]{1,0:T(8,128)S(1)}, f32[128,128]{1,0:T(8,128)S(1)}, u32[]{:S(2)}, u32[]{:S(2)}) %collective-permute-start.4) | collective-permute-done | bytes 65568 | tf_op jit(solution)/shard_map/ppermute | solution.py:341
  12.5 1.7 %collective-permute-start.9 = (f32[10,128,512]{2,1,0:T(8,128)S(1)}, f32[10,128,512]{2,1,0:T(8,128)S(1)}, u32[]{:S(2)}, u32[]{:S(2)}) collective-permute-start(f32[10,128,512]{2,1,0:T(8,128)S(1)} %shard_map.88.own.refs_6_.refs_4_), channel_id=1, source_target_pairs={{0,1},{1,0},{2,3},{3,2},{4,5},{5,4},{6,7},{7,6},{8,9},{9,8},{10,11... | collective-permute-start | bytes 7864328 | tf_op jit(solution)/shard_map/ppermute | solution.py:341
  15.0 2.9 %collective-permute-done.8.next_far.far = f32[128,128]{1,0:T(8,128)S(1)} collective-permute-done((f32[128,128]{1,0:T(8,128)S(1)}, f32[128,128]{1,0:T(8,128)S(1)}, u32[]{:S(2)}, u32[]{:S(2)}) %collective-permute-start.8) | collective-permute-done | bytes 65568 | tf_op jit(solution)/shard_map/ppermute | solution.py:341
  20.2 1.8 %collective-permute-start.10 = (f32[128,128]{1,0:T(8,128)S(1)}, f32[128,128]{1,0:T(8,128)S(1)}, u32[]{:S(2)}, u32[]{:S(2)}) collective-permute-start(f32[128,128]{1,0:T(8,128)S(1)} %shard_map.90.refs_0_), channel_id=1, source_target_pairs={{0,1},{1,0},{2,3},{3,2},{4,8},{5,9},{6,10},{7,11},{8,4},{9,5},{10,... | collective-permute-start | bytes 196616 | tf_op jit(solution)/shard_map/ppermute | solution.py:341
  22.0 2.3 %collective-permute-done.10.more = f32[128,128]{1,0:T(8,128)S(1)} collective-permute-done((f32[128,128]{1,0:T(8,128)S(1)}, f32[128,128]{1,0:T(8,128)S(1)}, u32[]{:S(2)}, u32[]{:S(2)}) %collective-permute-start.10) | collective-permute-done | bytes 65568 | tf_op jit(solution)/shard_map/ppermute | solution.py:341
  24.4 1.6 %collective-permute-start.12 = (f32[128,128]{1,0:T(8,128)S(1)}, f32[128,128]{1,0:T(8,128)S(1)}, u32[]{:S(2)}, u32[]{:S(2)}) collective-permute-start(f32[128,128]{1,0:T(8,128)S(1)} %shard_map.91.near.refs_0_), channel_id=1, source_target_pairs={{0,2},{1,3},{2,0},{3,1},{4,5},{5,4},{6,7},{7,6},{8,10},{9,11},{10,... | collective-permute-start | bytes 196616 | tf_op jit(solution)/shard_map/ppermute | solution.py:341
  27.2 2.8 %collective-permute-start.13 = (f32[128,128]{1,0:T(8,128)S(1)}, f32[128,128]{1,0:T(8,128)S(1)}, u32[]{:S(2)}, u32[]{:S(2)}) collective-permute-start(f32[128,128]{1,0:T(8,128)S(1)} %get-tuple-element.22), channel_id=1, source_target_pairs={{0,1},{1,0},{2,3},{3,2},{4,5},{5,4},{6,7},{7,6},{8,16},{9,17},{10,... | collective-permute-start | bytes 196616 | tf_op jit(solution)/shard_map/ppermute | solution.py:341
  30.0 3.5 %collective-permute-start.16 = (f32[128,128]{1,0:T(8,128)S(1)}, f32[128,128]{1,0:T(8,128)S(1)}, u32[]{:S(2)}, u32[]{:S(2)}) collective-permute-start(f32[128,128]{1,0:T(8,128)S(1)} %get-tuple-element.21.values), channel_id=1, source_target_pairs={{0,1},{1,0},{2,3},{3,2},{4,5},{5,4},{6,7},{7,6},{8,9},{9,8},{10,11... | collective-permute-start | bytes 196616 | tf_op jit(solution)/shard_map/ppermute | solution.py:341
  34.8 1.2 %collective-permute-start.18 = (f32[128,128]{1,0:T(8,128)S(1)}, f32[128,128]{1,0:T(8,128)S(1)}, u32[]{:S(2)}, u32[]{:S(2)}) collective-permute-start(f32[128,128]{1,0:T(8,128)S(1)} %shard_map.94), channel_id=1, source_target_pairs={{0,6},{1,7},{2,4},{3,5},{4,8},{5,9},{6,10},{7,11},{8,2},{9,3},{10,... | collective-permute-start | bytes 196616 | tf_op jit(solution)/shard_map/ppermute | solution.py:341
  36.1 4.9 %collective-permute-start.20 = (f32[128,128]{1,0:T(8,128)S(1)}, f32[128,128]{1,0:T(8,128)S(1)}, u32[]{:S(2)}, u32[]{:S(2)}) collective-permute-start(f32[128,128]{1,0:T(8,128)S(1)} %shard_map.93.refs_0_), channel_id=1, source_target_pairs={{0,6},{1,7},{2,4},{3,5},{4,12},{5,13},{6,14},{7,15},{8,9},{9,8},{1... | collective-permute-start | bytes 196616 | tf_op jit(solution)/shard_map/ppermute | solution.py:341
  42.7 1.7 %collective-permute-start.22 = (f32[128,128]{1,0:T(8,128)S(1)}, f32[128,128]{1,0:T(8,128)S(1)}, u32[]{:S(2)}, u32[]{:S(2)}) collective-permute-start(f32[128,128]{1,0:T(8,128)S(1)} %shard_map.98.part), channel_id=1, source_target_pairs={{0,18},{1,19},{2,16},{3,17},{4,0},{5,1},{6,2},{7,3},{8,9},{9,8},{1... | collective-permute-start | bytes 196616 | tf_op jit(solution)/shard_map/ppermute | solution.py:341
  44.4 3.1 %collective-permute-start.28 = (f32[128,128]{1,0:T(8,128)S(1)}, f32[128,128]{1,0:T(8,128)S(1)}, u32[]{:S(2)}, u32[]{:S(2)}) collective-permute-start(f32[128,128]{1,0:T(8,128)S(1)} %shard_map.98.part), channel_id=1, source_target_pairs={{0,10},{1,11},{2,8},{3,9},{4,0},{5,1},{6,2},{7,3},{8,14},{9,15},{1... | collective-permute-start | bytes 196616 | tf_op jit(solution)/shard_map/ppermute | solution.py:341
  47.5 2.7 %collective-permute-start.26 = (f32[128,128]{1,0:T(8,128)S(1)}, f32[128,128]{1,0:T(8,128)S(1)}, u32[]{:S(2)}, u32[]{:S(2)}) collective-permute-start(f32[128,128]{1,0:T(8,128)S(1)} %shard_map.99.other), channel_id=1, source_target_pairs={{0,1},{1,0},{2,3},{3,2},{4,5},{5,4},{6,7},{7,6},{8,14},{9,15},{10,... | collective-permute-start | bytes 196616 | tf_op jit(solution)/shard_map/ppermute | solution.py:341
  50.3 1.5 %collective-permute-start.25 = (f32[128,128]{1,0:T(8,128)S(1)}, f32[128,128]{1,0:T(8,128)S(1)}, u32[]{:S(2)}, u32[]{:S(2)}) collective-permute-start(f32[128,128]{1,0:T(8,128)S(1)} %shard_map.99.other), channel_id=1, source_target_pairs={{0,1},{1,0},{2,3},{3,2},{4,5},{5,4},{6,7},{7,6},{8,12},{9,13},{10,... | collective-permute-start | bytes 196616 | tf_op jit(solution)/shard_map/ppermute | solution.py:341
  51.8 4.1 %collective-permute-start.24 = (f32[128,128]{1,0:T(8,128)S(1)}, f32[128,128]{1,0:T(8,128)S(1)}, u32[]{:S(2)}, u32[]{:S(2)}) collective-permute-start(f32[128,128]{1,0:T(8,128)S(1)} %shard_map.99.other), channel_id=1, source_target_pairs={{0,1},{1,0},{2,3},{3,2},{4,5},{5,4},{6,7},{7,6},{8,9},{9,8},{10,11... | collective-permute-start | bytes 196616 | tf_op jit(solution)/shard_map/ppermute | solution.py:341
  57.4 2.9 %collective-permute-start.31 = (f32[128,128]{1,0:T(8,128)S(1)}, f32[128,128]{1,0:T(8,128)S(1)}, u32[]{:S(2)}, u32[]{:S(2)}) collective-permute-start(f32[128,128]{1,0:T(8,128)S(1)} %shard_map.100.other), channel_id=1, source_target_pairs={{0,1},{1,0},{2,3},{3,2},{4,8},{5,9},{6,10},{7,11},{8,4},{9,5},{10,... | collective-permute-start | bytes 196616 | tf_op jit(solution)/shard_map/ppermute | solution.py:341
  60.9 1.8 %collective-permute-done.32.refs_3_ = f32[128,128]{1,0:T(8,128)S(1)} collective-permute-done((f32[128,128]{1,0:T(8,128)S(1)}, f32[128,128]{1,0:T(8,128)S(1)}, u32[]{:S(2)}, u32[]{:S(2)}) %collective-permute-start.32) | collective-permute-done | bytes 65568 | tf_op jit(solution)/shard_map/ppermute | solution.py:341
  63.4 1.4 %shard_map.101.mine = f32[128,128]{1,0:T(8,128)S(1)} custom-call(f32[128,128]{1,0:T(8,128)S(1)} %shard_map.98.part, f32[128,128]{1,0:T(8,128)S(1)} %shard_map.100.other, f32[128,128]{1,0:T(8,128)S(1)} %collective-permute-done.29.refs_0_, f32[128,128]{1,0:T(8,128)S(1)} %collective-permute-done.30.refs_1_, f32[128,128]{1,0:T(8,128)S(1)} %collective-permute-done.31.refs_2_, ...), custom_call_target="tpu_custom_call" | custom-call | flops 1000000000 | bytes 1 | tf_op jit(solution)/shard_map/pallas_call | solution.py:297
  64.8 5.7 %collective-permute-start.33 = (f32[128,128]{1,0:T(8,128)S(1)}, f32[128,128]{1,0:T(8,128)S(1)}, u32[]{:S(2)}, u32[]{:S(2)}) collective-permute-start(f32[128,128]{1,0:T(8,128)S(1)} %shard_map.101.mine), channel_id=1, source_target_pairs={{0,1},{1,0},{2,3},{3,2},{4,5},{5,4},{6,7},{7,6},{8,9},{9,8},{10,11... | collective-permute-start | bytes 196616 | tf_op jit(solution)/shard_map/ppermute | solution.py:341
  (83 shorter events, 16.9 us)
Async XLA Ops:
  0.7 7.7 %collective-permute-start.5 = (f32[1,128,512]{2,1,0:T(8,128)}, f32[1,128,512]{2,1,0:T(8,128)S(1)}, u32[]{:S(2)}, u32[]{:S(2)}) collective-permute-start(f32[1,128,512]{2,1,0:T(8,128)} %own_e.1), channel_id=1, source_target_pairs={{0,1},{1,0},{2,3},{3,2},{4,5},{5,4},{6,7},{7,6},{8,9},{9,8},{10,11... | collective-permute-start | bytes 786440 | tf_op jit(solution)/shard_map/ppermute | solution.py:341
  3.3 4.8 %collective-permute-start.6 = (f32[128,128]{1,0:T(8,128)S(1)}, f32[128,128]{1,0:T(8,128)S(1)}, u32[]{:S(2)}, u32[]{:S(2)}) collective-permute-start(f32[128,128]{1,0:T(8,128)S(1)} %get-tuple-element.16), channel_id=1, source_target_pairs={{0,2},{1,3},{2,0},{3,1},{4,6},{5,7},{6,4},{7,5},{8,10},{9,11},{10,... | collective-permute-start | bytes 196616 | tf_op jit(solution)/shard_map/ppermute | solution.py:341
  4.5 5.1 %collective-permute-start.4 = (f32[128,128]{1,0:T(8,128)S(1)}, f32[128,128]{1,0:T(8,128)S(1)}, u32[]{:S(2)}, u32[]{:S(2)}) collective-permute-start(f32[128,128]{1,0:T(8,128)S(1)} %get-tuple-element.14.packed.near), channel_id=1, source_target_pairs={{0,1},{1,0},{2,3},{3,2},{4,10},{5,11},{6,8},{7,9},{8,6},{9,7},{10,... | collective-permute-start | bytes 196616 | tf_op jit(solution)/shard_map/ppermute | solution.py:341
  5.8 4.9 %collective-permute-start.3 = (f32[128,128]{1,0:T(8,128)S(1)}, f32[128,128]{1,0:T(8,128)S(1)}, u32[]{:S(2)}, u32[]{:S(2)}) collective-permute-start(f32[128,128]{1,0:T(8,128)S(1)} %get-tuple-element.14.packed.near), channel_id=1, source_target_pairs={{0,1},{1,0},{2,3},{3,2},{4,8},{5,9},{6,10},{7,11},{8,4},{9,5},{10,... | collective-permute-start | bytes 196616 | tf_op jit(solution)/shard_map/ppermute | solution.py:341
  6.9 3.9 %collective-permute-start.2 = (f32[128,128]{1,0:T(8,128)S(1)}, f32[128,128]{1,0:T(8,128)S(1)}, u32[]{:S(2)}, u32[]{:S(2)}) collective-permute-start(f32[128,128]{1,0:T(8,128)S(1)} %get-tuple-element.14.packed.near), channel_id=1, source_target_pairs={{0,2},{1,3},{2,0},{3,1},{4,6},{5,7},{6,4},{7,5},{8,10},{9,11},{10,... | collective-permute-start | bytes 196616 | tf_op jit(solution)/shard_map/ppermute | solution.py:341
  8.1 4.2 %collective-permute-start.7 = (f32[128,128]{1,0:T(8,128)S(1)}, f32[128,128]{1,0:T(8,128)S(1)}, u32[]{:S(2)}, u32[]{:S(2)}) collective-permute-start(f32[128,128]{1,0:T(8,128)S(1)} %get-tuple-element.18), channel_id=1, source_target_pairs={{0,4},{1,5},{2,6},{3,7},{4,0},{5,1},{6,2},{7,3},{8,12},{9,13},{10,... | collective-permute-start | bytes 196616 | tf_op jit(solution)/shard_map/ppermute | solution.py:341
  12.5 6.3 %collective-permute-start.9 = (f32[10,128,512]{2,1,0:T(8,128)S(1)}, f32[10,128,512]{2,1,0:T(8,128)S(1)}, u32[]{:S(2)}, u32[]{:S(2)}) collective-permute-start(f32[10,128,512]{2,1,0:T(8,128)S(1)} %shard_map.88.own.refs_6_.refs_4_), channel_id=1, source_target_pairs={{0,1},{1,0},{2,3},{3,2},{4,5},{5,4},{6,7},{7,6},{8,9},{9,8},{10,11... | collective-permute-start | bytes 7864328 | tf_op jit(solution)/shard_map/ppermute | solution.py:341
  19.5 4.9 %collective-permute-start.11 = (f32[128,128]{1,0:T(8,128)S(1)}, f32[128,128]{1,0:T(8,128)S(1)}, u32[]{:S(2)}, u32[]{:S(2)}) collective-permute-start(f32[128,128]{1,0:T(8,128)S(1)} %shard_map.89.refs_1_), channel_id=1, source_target_pairs={{0,4},{1,5},{2,6},{3,7},{4,0},{5,1},{6,2},{7,3},{8,12},{9,13},{10,... | collective-permute-start | bytes 196616 | tf_op jit(solution)/shard_map/ppermute | solution.py:341
  20.2 4.1 %collective-permute-start.10 = (f32[128,128]{1,0:T(8,128)S(1)}, f32[128,128]{1,0:T(8,128)S(1)}, u32[]{:S(2)}, u32[]{:S(2)}) collective-permute-start(f32[128,128]{1,0:T(8,128)S(1)} %shard_map.90.refs_0_), channel_id=1, source_target_pairs={{0,1},{1,0},{2,3},{3,2},{4,8},{5,9},{6,10},{7,11},{8,4},{9,5},{10,... | collective-permute-start | bytes 196616 | tf_op jit(solution)/shard_map/ppermute | solution.py:341
  26.8 6.7 %collective-permute-start.15 = (f32[128,128]{1,0:T(8,128)S(1)}, f32[128,128]{1,0:T(8,128)S(1)}, u32[]{:S(2)}, u32[]{:S(2)}) collective-permute-start(f32[128,128]{1,0:T(8,128)S(1)} %get-tuple-element.22), channel_id=1, source_target_pairs={{0,1},{1,0},{2,3},{3,2},{4,8},{5,9},{6,10},{7,11},{8,18},{9,19},{1... | collective-permute-start | bytes 196616 | tf_op jit(solution)/shard_map/ppermute | solution.py:341
  27.2 7.2 %collective-permute-start.13 = (f32[128,128]{1,0:T(8,128)S(1)}, f32[128,128]{1,0:T(8,128)S(1)}, u32[]{:S(2)}, u32[]{:S(2)}) collective-permute-start(f32[128,128]{1,0:T(8,128)S(1)} %get-tuple-element.22), channel_id=1, source_target_pairs={{0,1},{1,0},{2,3},{3,2},{4,5},{5,4},{6,7},{7,6},{8,16},{9,17},{10,... | collective-permute-start | bytes 196616 | tf_op jit(solution)/shard_map/ppermute | solution.py:341
  30.0 4.4 %collective-permute-start.16 = (f32[128,128]{1,0:T(8,128)S(1)}, f32[128,128]{1,0:T(8,128)S(1)}, u32[]{:S(2)}, u32[]{:S(2)}) collective-permute-start(f32[128,128]{1,0:T(8,128)S(1)} %get-tuple-element.21.values), channel_id=1, source_target_pairs={{0,1},{1,0},{2,3},{3,2},{4,5},{5,4},{6,7},{7,6},{8,9},{9,8},{10,11... | collective-permute-start | bytes 196616 | tf_op jit(solution)/shard_map/ppermute | solution.py:341
  34.8 7.0 %collective-permute-start.18 = (f32[128,128]{1,0:T(8,128)S(1)}, f32[128,128]{1,0:T(8,128)S(1)}, u32[]{:S(2)}, u32[]{:S(2)}) collective-permute-start(f32[128,128]{1,0:T(8,128)S(1)} %shard_map.94), channel_id=1, source_target_pairs={{0,6},{1,7},{2,4},{3,5},{4,8},{5,9},{6,10},{7,11},{8,2},{9,3},{10,... | collective-permute-start | bytes 196616 | tf_op jit(solution)/shard_map/ppermute | solution.py:341
  36.0 5.8 %collective-permute-start.17 = (f32[128,128]{1,0:T(8,128)S(1)}, f32[128,128]{1,0:T(8,128)S(1)}, u32[]{:S(2)}, u32[]{:S(2)}) collective-permute-start(f32[128,128]{1,0:T(8,128)S(1)} %shard_map.94), channel_id=1, source_target_pairs={{0,4},{1,5},{2,6},{3,7},{4,8},{5,9},{6,10},{7,11},{8,0},{9,1},{10,... | collective-permute-start | bytes 196616 | tf_op jit(solution)/shard_map/ppermute | solution.py:341
  36.1 6.3 %collective-permute-start.20 = (f32[128,128]{1,0:T(8,128)S(1)}, f32[128,128]{1,0:T(8,128)S(1)}, u32[]{:S(2)}, u32[]{:S(2)}) collective-permute-start(f32[128,128]{1,0:T(8,128)S(1)} %shard_map.93.refs_0_), channel_id=1, source_target_pairs={{0,6},{1,7},{2,4},{3,5},{4,12},{5,13},{6,14},{7,15},{8,9},{9,8},{1... | collective-permute-start | bytes 196616 | tf_op jit(solution)/shard_map/ppermute | solution.py:341
  42.7 4.9 %collective-permute-start.22 = (f32[128,128]{1,0:T(8,128)S(1)}, f32[128,128]{1,0:T(8,128)S(1)}, u32[]{:S(2)}, u32[]{:S(2)}) collective-permute-start(f32[128,128]{1,0:T(8,128)S(1)} %shard_map.98.part), channel_id=1, source_target_pairs={{0,18},{1,19},{2,16},{3,17},{4,0},{5,1},{6,2},{7,3},{8,9},{9,8},{1... | collective-permute-start | bytes 196616 | tf_op jit(solution)/shard_map/ppermute | solution.py:341
  44.4 11.4 %collective-permute-start.28 = (f32[128,128]{1,0:T(8,128)S(1)}, f32[128,128]{1,0:T(8,128)S(1)}, u32[]{:S(2)}, u32[]{:S(2)}) collective-permute-start(f32[128,128]{1,0:T(8,128)S(1)} %shard_map.98.part), channel_id=1, source_target_pairs={{0,10},{1,11},{2,8},{3,9},{4,0},{5,1},{6,2},{7,3},{8,14},{9,15},{1... | collective-permute-start | bytes 196616 | tf_op jit(solution)/shard_map/ppermute | solution.py:341
  47.5 8.3 %collective-permute-start.27 = (f32[128,128]{1,0:T(8,128)S(1)}, f32[128,128]{1,0:T(8,128)S(1)}, u32[]{:S(2)}, u32[]{:S(2)}) collective-permute-start(f32[128,128]{1,0:T(8,128)S(1)} %shard_map.98.part), channel_id=1, source_target_pairs={{0,8},{1,9},{2,10},{3,11},{4,0},{5,1},{6,2},{7,3},{8,12},{9,13},{1... | collective-permute-start | bytes 196616 | tf_op jit(solution)/shard_map/ppermute | solution.py:341
  47.5 8.3 %collective-permute-start.26 = (f32[128,128]{1,0:T(8,128)S(1)}, f32[128,128]{1,0:T(8,128)S(1)}, u32[]{:S(2)}, u32[]{:S(2)}) collective-permute-start(f32[128,128]{1,0:T(8,128)S(1)} %shard_map.99.other), channel_id=1, source_target_pairs={{0,1},{1,0},{2,3},{3,2},{4,5},{5,4},{6,7},{7,6},{8,14},{9,15},{10,... | collective-permute-start | bytes 196616 | tf_op jit(solution)/shard_map/ppermute | solution.py:341
  50.3 5.5 %collective-permute-start.25 = (f32[128,128]{1,0:T(8,128)S(1)}, f32[128,128]{1,0:T(8,128)S(1)}, u32[]{:S(2)}, u32[]{:S(2)}) collective-permute-start(f32[128,128]{1,0:T(8,128)S(1)} %shard_map.99.other), channel_id=1, source_target_pairs={{0,1},{1,0},{2,3},{3,2},{4,5},{5,4},{6,7},{7,6},{8,12},{9,13},{10,... | collective-permute-start | bytes 196616 | tf_op jit(solution)/shard_map/ppermute | solution.py:341
  51.8 5.0 %collective-permute-start.24 = (f32[128,128]{1,0:T(8,128)S(1)}, f32[128,128]{1,0:T(8,128)S(1)}, u32[]{:S(2)}, u32[]{:S(2)}) collective-permute-start(f32[128,128]{1,0:T(8,128)S(1)} %shard_map.99.other), channel_id=1, source_target_pairs={{0,1},{1,0},{2,3},{3,2},{4,5},{5,4},{6,7},{7,6},{8,9},{9,8},{10,11... | collective-permute-start | bytes 196616 | tf_op jit(solution)/shard_map/ppermute | solution.py:341
  57.4 5.4 %collective-permute-start.32 = (f32[128,128]{1,0:T(8,128)S(1)}, f32[128,128]{1,0:T(8,128)S(1)}, u32[]{:S(2)}, u32[]{:S(2)}) collective-permute-start(f32[128,128]{1,0:T(8,128)S(1)} %shard_map.100.other), channel_id=1, source_target_pairs={{0,1},{1,0},{2,3},{3,2},{4,10},{5,11},{6,8},{7,9},{8,6},{9,7},{10,... | collective-permute-start | bytes 196616 | tf_op jit(solution)/shard_map/ppermute | solution.py:341
  57.4 5.7 %collective-permute-start.31 = (f32[128,128]{1,0:T(8,128)S(1)}, f32[128,128]{1,0:T(8,128)S(1)}, u32[]{:S(2)}, u32[]{:S(2)}) collective-permute-start(f32[128,128]{1,0:T(8,128)S(1)} %shard_map.100.other), channel_id=1, source_target_pairs={{0,1},{1,0},{2,3},{3,2},{4,8},{5,9},{6,10},{7,11},{8,4},{9,5},{10,... | collective-permute-start | bytes 196616 | tf_op jit(solution)/shard_map/ppermute | solution.py:341
  64.8 6.6 %collective-permute-start.33 = (f32[128,128]{1,0:T(8,128)S(1)}, f32[128,128]{1,0:T(8,128)S(1)}, u32[]{:S(2)}, u32[]{:S(2)}) collective-permute-start(f32[128,128]{1,0:T(8,128)S(1)} %shard_map.101.mine), channel_id=1, source_target_pairs={{0,1},{1,0},{2,3},{3,2},{4,5},{5,4},{6,7},{7,6},{8,9},{9,8},{10,11... | collective-permute-start | bytes 196616 | tf_op jit(solution)/shard_map/ppermute | solution.py:341
  (18 other events, 84.3 us)

commit v13 on v12

--- a/solution.py
+++ b/solution.py
@@ -449,7 +449,9 @@
             base_far = far = exchange(near, every[::2])
             continue
         urgent = [b for b in every if b % (4 * d) == 2 * d]
-        more = both(over, [(b - d, b, b - 1) for b in urgent], [(b - d, b, b - 3) for b in urgent])
+        more = both(
+            over, [(b - d, b, b - 1) for b in urgent], [(b - d, b, b - 2 * d) for b in urgent]
+        )
         less = both(
             beneath, [(b + d, b, b + 1) for b in urgent], [(b + d, b, b + 3) for b in urgent]
         )
@@ -487,11 +489,12 @@
         if level > 1:
             half = d // 2
             sources = [a for a in every if a % (2 * d) == 0]
+            held = call(copy_kernel, solved, unused=(vectors[0],))
             ways = [(a, a + half, a + half + 1, a + 1) for a in sources]
-            early = both(solved, ways, ways)
+            early = both(held, ways, ways)
             if len(sources) > 1:
                 ways = [(a, a - half, a - half + 1, a + 1) for a in sources if a > 0]
-                early += both(solved, ways, ways)
+                early += both(held, ways, ways)
         if level == levels - 1 and levels > 1:
             solved = call(kernel(settle_kernel, d), pivot, *vectors, *back, scratch=[store])
         else:

time: 72.2 us -> 73.3 us (1.015); the launches traced: 72.1 us -> 72.2 us
  waiting for transfers between devices: 17.2 us -> 19 us
  starting transfers between devices: 48.4 us -> 46.8 us
    ppermute x34, waiting for transfers between devices: 17.2 us -> 19 us  [send(): lax.ppermute(values, ('slab', 'col'), completed(route, slabs * cols, cols))]
    ppermute x34, starting transfers between devices: 48.4 us -> 46.8 us  [send(): lax.ppermute(values, ('slab', 'col'), completed(route, slabs * cols, cols))]
    pallas_call x21 -> x22, Pallas kernels: 6.12 us -> 6.13 us  [call(): pl.pallas_call(kernel, out_shape=shape if outs == 1 else (shape,) * outs,...]
where the time goes in v13:
time: 73.3 us; the launch traced here: 72.2 us
  starting transfers between devices  46.8 us (64%)
  waiting for transfers between devices  19 us (26%)
  Pallas kernels  6.13 us (8%)
    ppermute x34, starting transfers between devices, send(): lax.ppermute(values, ('slab', 'col'), completed(route, slabs * cols, cols))  46.8 us
    ppermute x34, waiting for transfers between devices, send(): lax.ppermute(values, ('slab', 'col'), completed(route, slabs * cols, cols))  19 us
    pallas_call x22, Pallas kernels, call(): pl.pallas_call(kernel, out_shape=shape if outs == 1 else (shape,) * outs,...  6.13 us
  transfers between devices with their start and end apart: 34, of which 19 were waited for; matrix products, arithmetic and copies ran while one was open for 0% of the time, Pallas kernels for 4%

profile of v13, /device:TPU:13, one launch (start us, length us, event | category | flops | bytes accessed | tf_op | source)
XLA Modules:
  0.0 72.2 jit_solution(12075042150464146560)
XLA Ops:
  1.2 1.3 %collective-permute-done.other = f32[1,128,128]{2,1,0:T(8,128)S(1)} collective-permute-done((f32[1,128,128]{2,1,0:T(8,128)}, f32[1,128,128]{2,1,0:T(8,128)S(1)}, u32[]{:S(2)}, u32[]{:S(2)}) %collective-permute-start) | collective-permute-done | bytes 65568 | tf_op jit(solution)/shard_map/ppermute | solution.py:341
  3.3 1.3 %collective-permute-start.6 = (f32[128,128]{1,0:T(8,128)S(1)}, f32[128,128]{1,0:T(8,128)S(1)}, u32[]{:S(2)}, u32[]{:S(2)}) collective-permute-start(f32[128,128]{1,0:T(8,128)S(1)} %get-tuple-element.16), channel_id=1, source_target_pairs={{0,2},{1,3},{2,0},{3,1},{4,6},{5,7},{6,4},{7,5},{8,10},{9,11},{10,... | collective-permute-start | bytes 196616 | tf_op jit(solution)/shard_map/ppermute | solution.py:341
  4.5 1.2 %collective-permute-start.4 = (f32[128,128]{1,0:T(8,128)S(1)}, f32[128,128]{1,0:T(8,128)S(1)}, u32[]{:S(2)}, u32[]{:S(2)}) collective-permute-start(f32[128,128]{1,0:T(8,128)S(1)} %get-tuple-element.14.packed.near), channel_id=1, source_target_pairs={{0,1},{1,0},{2,3},{3,2},{4,10},{5,11},{6,8},{7,9},{8,6},{9,7},{10,... | collective-permute-start | bytes 196616 | tf_op jit(solution)/shard_map/ppermute | solution.py:341
  6.9 1.2 %collective-permute-start.2 = (f32[128,128]{1,0:T(8,128)S(1)}, f32[128,128]{1,0:T(8,128)S(1)}, u32[]{:S(2)}, u32[]{:S(2)}) collective-permute-start(f32[128,128]{1,0:T(8,128)S(1)} %get-tuple-element.14.packed.near), channel_id=1, source_target_pairs={{0,2},{1,3},{2,0},{3,1},{4,6},{5,7},{6,4},{7,5},{8,10},{9,11},{10,... | collective-permute-start | bytes 196616 | tf_op jit(solution)/shard_map/ppermute | solution.py:341
  8.4 1.2 %collective-permute-done.4.next_far = f32[128,128]{1,0:T(8,128)S(1)} collective-permute-done((f32[128,128]{1,0:T(8,128)S(1)}, f32[128,128]{1,0:T(8,128)S(1)}, u32[]{:S(2)}, u32[]{:S(2)}) %collective-permute-start.4) | collective-permute-done | bytes 65568 | tf_op jit(solution)/shard_map/ppermute | solution.py:341
  12.5 1.7 %collective-permute-start.9 = (f32[10,128,512]{2,1,0:T(8,128)S(1)}, f32[10,128,512]{2,1,0:T(8,128)S(1)}, u32[]{:S(2)}, u32[]{:S(2)}) collective-permute-start(f32[10,128,512]{2,1,0:T(8,128)S(1)} %shard_map.88.own.refs_6_.refs_4_), channel_id=1, source_target_pairs={{0,1},{1,0},{2,3},{3,2},{4,5},{5,4},{6,7},{7,6},{8,9},{9,8},{10,11... | collective-permute-start | bytes 7864328 | tf_op jit(solution)/shard_map/ppermute | solution.py:341
  15.0 2.9 %collective-permute-done.8.next_far.far = f32[128,128]{1,0:T(8,128)S(1)} collective-permute-done((f32[128,128]{1,0:T(8,128)S(1)}, f32[128,128]{1,0:T(8,128)S(1)}, u32[]{:S(2)}, u32[]{:S(2)}) %collective-permute-start.8) | collective-permute-done | bytes 65568 | tf_op jit(solution)/shard_map/ppermute | solution.py:341
  20.2 1.8 %collective-permute-start.10 = (f32[128,128]{1,0:T(8,128)S(1)}, f32[128,128]{1,0:T(8,128)S(1)}, u32[]{:S(2)}, u32[]{:S(2)}) collective-permute-start(f32[128,128]{1,0:T(8,128)S(1)} %shard_map.90.refs_0_), channel_id=1, source_target_pairs={{0,1},{1,0},{2,3},{3,2},{4,8},{5,9},{6,10},{7,11},{8,4},{9,5},{10,... | collective-permute-start | bytes 196616 | tf_op jit(solution)/shard_map/ppermute | solution.py:341
  22.0 2.3 %collective-permute-done.10.more = f32[128,128]{1,0:T(8,128)S(1)} collective-permute-done((f32[128,128]{1,0:T(8,128)S(1)}, f32[128,128]{1,0:T(8,128)S(1)}, u32[]{:S(2)}, u32[]{:S(2)}) %collective-permute-start.10) | collective-permute-done | bytes 65568 | tf_op jit(solution)/shard_map/ppermute | solution.py:341
  24.4 1.6 %collective-permute-start.12 = (f32[128,128]{1,0:T(8,128)S(1)}, f32[128,128]{1,0:T(8,128)S(1)}, u32[]{:S(2)}, u32[]{:S(2)}) collective-permute-start(f32[128,128]{1,0:T(8,128)S(1)} %shard_map.91.near.refs_0_), channel_id=1, source_target_pairs={{0,2},{1,3},{2,0},{3,1},{4,5},{5,4},{6,7},{7,6},{8,10},{9,11},{10,... | collective-permute-start | bytes 196616 | tf_op jit(solution)/shard_map/ppermute | solution.py:341
  27.2 2.8 %collective-permute-start.13 = (f32[128,128]{1,0:T(8,128)S(1)}, f32[128,128]{1,0:T(8,128)S(1)}, u32[]{:S(2)}, u32[]{:S(2)}) collective-permute-start(f32[128,128]{1,0:T(8,128)S(1)} %get-tuple-element.22), channel_id=1, source_target_pairs={{0,1},{1,0},{2,3},{3,2},{4,5},{5,4},{6,7},{7,6},{8,16},{9,17},{10,... | collective-permute-start | bytes 196616 | tf_op jit(solution)/shard_map/ppermute | solution.py:341
  30.0 3.5 %collective-permute-start.16 = (f32[128,128]{1,0:T(8,128)S(1)}, f32[128,128]{1,0:T(8,128)S(1)}, u32[]{:S(2)}, u32[]{:S(2)}) collective-permute-start(f32[128,128]{1,0:T(8,128)S(1)} %get-tuple-element.21.values), channel_id=1, source_target_pairs={{0,1},{1,0},{2,3},{3,2},{4,5},{5,4},{6,7},{7,6},{8,9},{9,8},{10,11... | collective-permute-start | bytes 196616 | tf_op jit(solution)/shard_map/ppermute | solution.py:341
  35.7 5.4 %collective-permute-start.20 = (f32[128,128]{1,0:T(8,128)S(1)}, f32[128,128]{1,0:T(8,128)S(1)}, u32[]{:S(2)}, u32[]{:S(2)}) collective-permute-start(f32[128,128]{1,0:T(8,128)S(1)} %shard_map.93.refs_0_), channel_id=1, source_target_pairs={{0,6},{1,7},{2,4},{3,5},{4,12},{5,13},{6,14},{7,15},{8,9},{9,8},{1... | collective-permute-start | bytes 196616 | tf_op jit(solution)/shard_map/ppermute | solution.py:341
  42.7 1.5 %collective-permute-start.21 = (f32[128,128]{1,0:T(8,128)S(1)}, f32[128,128]{1,0:T(8,128)S(1)}, u32[]{:S(2)}, u32[]{:S(2)}) collective-permute-start(f32[128,128]{1,0:T(8,128)S(1)} %shard_map.98.part.values), channel_id=1, source_target_pairs={{0,16},{1,17},{2,18},{3,19},{4,0},{5,1},{6,2},{7,3},{8,9},{9,8},{1... | collective-permute-start | bytes 196616 | tf_op jit(solution)/shard_map/ppermute | solution.py:341
  45.1 2.0 %collective-permute-start.28 = (f32[128,128]{1,0:T(8,128)S(1)}, f32[128,128]{1,0:T(8,128)S(1)}, u32[]{:S(2)}, u32[]{:S(2)}) collective-permute-start(f32[128,128]{1,0:T(8,128)S(1)} %shard_map.100), channel_id=1, source_target_pairs={{0,10},{1,11},{2,8},{3,9},{4,0},{5,1},{6,2},{7,3},{8,14},{9,15},{1... | collective-permute-start | bytes 196616 | tf_op jit(solution)/shard_map/ppermute | solution.py:341
  47.0 2.0 %collective-permute-start.27 = (f32[128,128]{1,0:T(8,128)S(1)}, f32[128,128]{1,0:T(8,128)S(1)}, u32[]{:S(2)}, u32[]{:S(2)}) collective-permute-start(f32[128,128]{1,0:T(8,128)S(1)} %shard_map.100), channel_id=1, source_target_pairs={{0,8},{1,9},{2,10},{3,11},{4,0},{5,1},{6,2},{7,3},{8,12},{9,13},{1... | collective-permute-start | bytes 196616 | tf_op jit(solution)/shard_map/ppermute | solution.py:341
  49.0 2.6 %collective-permute-start.26 = (f32[128,128]{1,0:T(8,128)S(1)}, f32[128,128]{1,0:T(8,128)S(1)}, u32[]{:S(2)}, u32[]{:S(2)}) collective-permute-start(f32[128,128]{1,0:T(8,128)S(1)} %shard_map.99.other), channel_id=1, source_target_pairs={{0,1},{1,0},{2,3},{3,2},{4,5},{5,4},{6,7},{7,6},{8,14},{9,15},{10,... | collective-permute-start | bytes 196616 | tf_op jit(solution)/shard_map/ppermute | solution.py:341
  51.6 2.6 %collective-permute-start.25 = (f32[128,128]{1,0:T(8,128)S(1)}, f32[128,128]{1,0:T(8,128)S(1)}, u32[]{:S(2)}, u32[]{:S(2)}) collective-permute-start(f32[128,128]{1,0:T(8,128)S(1)} %shard_map.99.other), channel_id=1, source_target_pairs={{0,1},{1,0},{2,3},{3,2},{4,5},{5,4},{6,7},{7,6},{8,12},{9,13},{10,... | collective-permute-start | bytes 196616 | tf_op jit(solution)/shard_map/ppermute | solution.py:341
  54.3 2.9 %collective-permute-start.24 = (f32[128,128]{1,0:T(8,128)S(1)}, f32[128,128]{1,0:T(8,128)S(1)}, u32[]{:S(2)}, u32[]{:S(2)}) collective-permute-start(f32[128,128]{1,0:T(8,128)S(1)} %shard_map.99.other), channel_id=1, source_target_pairs={{0,1},{1,0},{2,3},{3,2},{4,5},{5,4},{6,7},{7,6},{8,9},{9,8},{10,11... | collective-permute-start | bytes 196616 | tf_op jit(solution)/shard_map/ppermute | solution.py:341
  58.5 3.0 %collective-permute-start.32 = (f32[128,128]{1,0:T(8,128)S(1)}, f32[128,128]{1,0:T(8,128)S(1)}, u32[]{:S(2)}, u32[]{:S(2)}) collective-permute-start(f32[128,128]{1,0:T(8,128)S(1)} %shard_map.101.other), channel_id=1, source_target_pairs={{0,1},{1,0},{2,3},{3,2},{4,10},{5,11},{6,8},{7,9},{8,6},{9,7},{10,... | collective-permute-start | bytes 196616 | tf_op jit(solution)/shard_map/ppermute | solution.py:341
  62.1 1.5 %collective-permute-done.32.refs_3_ = f32[128,128]{1,0:T(8,128)S(1)} collective-permute-done((f32[128,128]{1,0:T(8,128)S(1)}, f32[128,128]{1,0:T(8,128)S(1)}, u32[]{:S(2)}, u32[]{:S(2)}) %collective-permute-start.32) | collective-permute-done | bytes 65568 | tf_op jit(solution)/shard_map/ppermute | solution.py:341
  63.5 2.0 %collective-permute-done.31.refs_2_ = f32[128,128]{1,0:T(8,128)S(1)} collective-permute-done((f32[128,128]{1,0:T(8,128)S(1)}, f32[128,128]{1,0:T(8,128)S(1)}, u32[]{:S(2)}, u32[]{:S(2)}) %collective-permute-start.31) | collective-permute-done | bytes 65568 | tf_op jit(solution)/shard_map/ppermute | solution.py:341
  65.6 1.4 %shard_map.102.mine = f32[128,128]{1,0:T(8,128)S(1)} custom-call(f32[128,128]{1,0:T(8,128)S(1)} %shard_map.98.part.values, f32[128,128]{1,0:T(8,128)S(1)} %shard_map.101.other, f32[128,128]{1,0:T(8,128)S(1)} %collective-permute-done.29.refs_0_, f32[128,128]{1,0:T(8,128)S(1)} %collective-permute-done.30.refs_1_, ...), custom_call_target="tpu_custom_call" | custom-call | flops 1000000000 | bytes 1 | tf_op jit(solution)/shard_map/pallas_call | solution.py:297
  66.9 3.7 %collective-permute-start.33 = (f32[128,128]{1,0:T(8,128)S(1)}, f32[128,128]{1,0:T(8,128)S(1)}, u32[]{:S(2)}, u32[]{:S(2)}) collective-permute-start(f32[128,128]{1,0:T(8,128)S(1)} %shard_map.102.mine), channel_id=1, source_target_pairs={{0,1},{1,0},{2,3},{3,2},{4,5},{5,4},{6,7},{7,6},{8,9},{9,8},{10,11... | collective-permute-start | bytes 196616 | tf_op jit(solution)/shard_map/ppermute | solution.py:341
  (84 shorter events, 18.6 us)
Async XLA Ops:
  0.7 7.7 %collective-permute-start.5 = (f32[1,128,512]{2,1,0:T(8,128)}, f32[1,128,512]{2,1,0:T(8,128)S(1)}, u32[]{:S(2)}, u32[]{:S(2)}) collective-permute-start(f32[1,128,512]{2,1,0:T(8,128)} %own_e.1), channel_id=1, source_target_pairs={{0,1},{1,0},{2,3},{3,2},{4,5},{5,4},{6,7},{7,6},{8,9},{9,8},{10,11... | collective-permute-start | bytes 786440 | tf_op jit(solution)/shard_map/ppermute | solution.py:341
  3.3 4.8 %collective-permute-start.6 = (f32[128,128]{1,0:T(8,128)S(1)}, f32[128,128]{1,0:T(8,128)S(1)}, u32[]{:S(2)}, u32[]{:S(2)}) collective-permute-start(f32[128,128]{1,0:T(8,128)S(1)} %get-tuple-element.16), channel_id=1, source_target_pairs={{0,2},{1,3},{2,0},{3,1},{4,6},{5,7},{6,4},{7,5},{8,10},{9,11},{10,... | collective-permute-start | bytes 196616 | tf_op jit(solution)/shard_map/ppermute | solution.py:341
  4.5 5.1 %collective-permute-start.4 = (f32[128,128]{1,0:T(8,128)S(1)}, f32[128,128]{1,0:T(8,128)S(1)}, u32[]{:S(2)}, u32[]{:S(2)}) collective-permute-start(f32[128,128]{1,0:T(8,128)S(1)} %get-tuple-element.14.packed.near), channel_id=1, source_target_pairs={{0,1},{1,0},{2,3},{3,2},{4,10},{5,11},{6,8},{7,9},{8,6},{9,7},{10,... | collective-permute-start | bytes 196616 | tf_op jit(solution)/shard_map/ppermute | solution.py:341
  5.8 4.9 %collective-permute-start.3 = (f32[128,128]{1,0:T(8,128)S(1)}, f32[128,128]{1,0:T(8,128)S(1)}, u32[]{:S(2)}, u32[]{:S(2)}) collective-permute-start(f32[128,128]{1,0:T(8,128)S(1)} %get-tuple-element.14.packed.near), channel_id=1, source_target_pairs={{0,1},{1,0},{2,3},{3,2},{4,8},{5,9},{6,10},{7,11},{8,4},{9,5},{10,... | collective-permute-start | bytes 196616 | tf_op jit(solution)/shard_map/ppermute | solution.py:341
  6.9 3.9 %collective-permute-start.2 = (f32[128,128]{1,0:T(8,128)S(1)}, f32[128,128]{1,0:T(8,128)S(1)}, u32[]{:S(2)}, u32[]{:S(2)}) collective-permute-start(f32[128,128]{1,0:T(8,128)S(1)} %get-tuple-element.14.packed.near), channel_id=1, source_target_pairs={{0,2},{1,3},{2,0},{3,1},{4,6},{5,7},{6,4},{7,5},{8,10},{9,11},{10,... | collective-permute-start | bytes 196616 | tf_op jit(solution)/shard_map/ppermute | solution.py:341
  8.1 4.2 %collective-permute-start.7 = (f32[128,128]{1,0:T(8,128)S(1)}, f32[128,128]{1,0:T(8,128)S(1)}, u32[]{:S(2)}, u32[]{:S(2)}) collective-permute-start(f32[128,128]{1,0:T(8,128)S(1)} %get-tuple-element.18), channel_id=1, source_target_pairs={{0,4},{1,5},{2,6},{3,7},{4,0},{5,1},{6,2},{7,3},{8,12},{9,13},{10,... | collective-permute-start | bytes 196616 | tf_op jit(solution)/shard_map/ppermute | solution.py:341
  12.5 6.3 %collective-permute-start.9 = (f32[10,128,512]{2,1,0:T(8,128)S(1)}, f32[10,128,512]{2,1,0:T(8,128)S(1)}, u32[]{:S(2)}, u32[]{:S(2)}) collective-permute-start(f32[10,128,512]{2,1,0:T(8,128)S(1)} %shard_map.88.own.refs_6_.refs_4_), channel_id=1, source_target_pairs={{0,1},{1,0},{2,3},{3,2},{4,5},{5,4},{6,7},{7,6},{8,9},{9,8},{10,11... | collective-permute-start | bytes 7864328 | tf_op jit(solution)/shard_map/ppermute | solution.py:341
  19.5 4.9 %collective-permute-start.11 = (f32[128,128]{1,0:T(8,128)S(1)}, f32[128,128]{1,0:T(8,128)S(1)}, u32[]{:S(2)}, u32[]{:S(2)}) collective-permute-start(f32[128,128]{1,0:T(8,128)S(1)} %shard_map.89.refs_1_), channel_id=1, source_target_pairs={{0,4},{1,5},{2,6},{3,7},{4,0},{5,1},{6,2},{7,3},{8,12},{9,13},{10,... | collective-permute-start | bytes 196616 | tf_op jit(solution)/shard_map/ppermute | solution.py:341
  20.2 4.1 %collective-permute-start.10 = (f32[128,128]{1,0:T(8,128)S(1)}, f32[128,128]{1,0:T(8,128)S(1)}, u32[]{:S(2)}, u32[]{:S(2)}) collective-permute-start(f32[128,128]{1,0:T(8,128)S(1)} %shard_map.90.refs_0_), channel_id=1, source_target_pairs={{0,1},{1,0},{2,3},{3,2},{4,8},{5,9},{6,10},{7,11},{8,4},{9,5},{10,... | collective-permute-start | bytes 196616 | tf_op jit(solution)/shard_map/ppermute | solution.py:341
  26.8 6.7 %collective-permute-start.15 = (f32[128,128]{1,0:T(8,128)S(1)}, f32[128,128]{1,0:T(8,128)S(1)}, u32[]{:S(2)}, u32[]{:S(2)}) collective-permute-start(f32[128,128]{1,0:T(8,128)S(1)} %get-tuple-element.22), channel_id=1, source_target_pairs={{0,8},{1,9},{2,10},{3,11},{4,5},{5,4},{6,7},{7,6},{8,18},{9,19},{1... | collective-permute-start | bytes 196616 | tf_op jit(solution)/shard_map/ppermute | solution.py:341
  27.2 7.2 %collective-permute-start.13 = (f32[128,128]{1,0:T(8,128)S(1)}, f32[128,128]{1,0:T(8,128)S(1)}, u32[]{:S(2)}, u32[]{:S(2)}) collective-permute-start(f32[128,128]{1,0:T(8,128)S(1)} %get-tuple-element.22), channel_id=1, source_target_pairs={{0,1},{1,0},{2,3},{3,2},{4,5},{5,4},{6,7},{7,6},{8,16},{9,17},{10,... | collective-permute-start | bytes 196616 | tf_op jit(solution)/shard_map/ppermute | solution.py:341
  30.0 4.4 %collective-permute-start.16 = (f32[128,128]{1,0:T(8,128)S(1)}, f32[128,128]{1,0:T(8,128)S(1)}, u32[]{:S(2)}, u32[]{:S(2)}) collective-permute-start(f32[128,128]{1,0:T(8,128)S(1)} %get-tuple-element.21.values), channel_id=1, source_target_pairs={{0,1},{1,0},{2,3},{3,2},{4,5},{5,4},{6,7},{7,6},{8,9},{9,8},{10,11... | collective-permute-start | bytes 196616 | tf_op jit(solution)/shard_map/ppermute | solution.py:341
  34.8 7.0 %collective-permute-start.18 = (f32[128,128]{1,0:T(8,128)S(1)}, f32[128,128]{1,0:T(8,128)S(1)}, u32[]{:S(2)}, u32[]{:S(2)}) collective-permute-start(f32[128,128]{1,0:T(8,128)S(1)} %shard_map.94), channel_id=1, source_target_pairs={{0,6},{1,7},{2,4},{3,5},{4,8},{5,9},{6,10},{7,11},{8,2},{9,3},{10,... | collective-permute-start | bytes 196616 | tf_op jit(solution)/shard_map/ppermute | solution.py:341
  35.6 6.2 %collective-permute-start.17 = (f32[128,128]{1,0:T(8,128)S(1)}, f32[128,128]{1,0:T(8,128)S(1)}, u32[]{:S(2)}, u32[]{:S(2)}) collective-permute-start(f32[128,128]{1,0:T(8,128)S(1)} %shard_map.94), channel_id=1, source_target_pairs={{0,4},{1,5},{2,6},{3,7},{4,8},{5,9},{6,10},{7,11},{8,0},{9,1},{10,... | collective-permute-start | bytes 196616 | tf_op jit(solution)/shard_map/ppermute | solution.py:341
  35.7 6.7 %collective-permute-start.20 = (f32[128,128]{1,0:T(8,128)S(1)}, f32[128,128]{1,0:T(8,128)S(1)}, u32[]{:S(2)}, u32[]{:S(2)}) collective-permute-start(f32[128,128]{1,0:T(8,128)S(1)} %shard_map.93.refs_0_), channel_id=1, source_target_pairs={{0,6},{1,7},{2,4},{3,5},{4,12},{5,13},{6,14},{7,15},{8,9},{9,8},{1... | collective-permute-start | bytes 196616 | tf_op jit(solution)/shard_map/ppermute | solution.py:341
  44.1 4.9 %collective-permute-start.22 = (f32[128,128]{1,0:T(8,128)S(1)}, f32[128,128]{1,0:T(8,128)S(1)}, u32[]{:S(2)}, u32[]{:S(2)}) collective-permute-start(f32[128,128]{1,0:T(8,128)S(1)} %shard_map.98.part.values), channel_id=1, source_target_pairs={{0,18},{1,19},{2,16},{3,17},{4,0},{5,1},{6,2},{7,3},{8,9},{9,8},{1... | collective-permute-start | bytes 196616 | tf_op jit(solution)/shard_map/ppermute | solution.py:341
  45.1 12.1 %collective-permute-start.28 = (f32[128,128]{1,0:T(8,128)S(1)}, f32[128,128]{1,0:T(8,128)S(1)}, u32[]{:S(2)}, u32[]{:S(2)}) collective-permute-start(f32[128,128]{1,0:T(8,128)S(1)} %shard_map.100), channel_id=1, source_target_pairs={{0,10},{1,11},{2,8},{3,9},{4,0},{5,1},{6,2},{7,3},{8,14},{9,15},{1... | collective-permute-start | bytes 196616 | tf_op jit(solution)/shard_map/ppermute | solution.py:341
  47.0 10.1 %collective-permute-start.27 = (f32[128,128]{1,0:T(8,128)S(1)}, f32[128,128]{1,0:T(8,128)S(1)}, u32[]{:S(2)}, u32[]{:S(2)}) collective-permute-start(f32[128,128]{1,0:T(8,128)S(1)} %shard_map.100), channel_id=1, source_target_pairs={{0,8},{1,9},{2,10},{3,11},{4,0},{5,1},{6,2},{7,3},{8,12},{9,13},{1... | collective-permute-start | bytes 196616 | tf_op jit(solution)/shard_map/ppermute | solution.py:341
  49.0 8.1 %collective-permute-start.26 = (f32[128,128]{1,0:T(8,128)S(1)}, f32[128,128]{1,0:T(8,128)S(1)}, u32[]{:S(2)}, u32[]{:S(2)}) collective-permute-start(f32[128,128]{1,0:T(8,128)S(1)} %shard_map.99.other), channel_id=1, source_target_pairs={{0,1},{1,0},{2,3},{3,2},{4,5},{5,4},{6,7},{7,6},{8,14},{9,15},{10,... | collective-permute-start | bytes 196616 | tf_op jit(solution)/shard_map/ppermute | solution.py:341
  51.6 5.5 %collective-permute-start.25 = (f32[128,128]{1,0:T(8,128)S(1)}, f32[128,128]{1,0:T(8,128)S(1)}, u32[]{:S(2)}, u32[]{:S(2)}) collective-permute-start(f32[128,128]{1,0:T(8,128)S(1)} %shard_map.99.other), channel_id=1, source_target_pairs={{0,1},{1,0},{2,3},{3,2},{4,5},{5,4},{6,7},{7,6},{8,12},{9,13},{10,... | collective-permute-start | bytes 196616 | tf_op jit(solution)/shard_map/ppermute | solution.py:341
  58.5 5.0 %collective-permute-start.32 = (f32[128,128]{1,0:T(8,128)S(1)}, f32[128,128]{1,0:T(8,128)S(1)}, u32[]{:S(2)}, u32[]{:S(2)}) collective-permute-start(f32[128,128]{1,0:T(8,128)S(1)} %shard_map.101.other), channel_id=1, source_target_pairs={{0,1},{1,0},{2,3},{3,2},{4,10},{5,11},{6,8},{7,9},{8,6},{9,7},{10,... | collective-permute-start | bytes 196616 | tf_op jit(solution)/shard_map/ppermute | solution.py:341
  61.5 4.0 %collective-permute-start.31 = (f32[128,128]{1,0:T(8,128)S(1)}, f32[128,128]{1,0:T(8,128)S(1)}, u32[]{:S(2)}, u32[]{:S(2)}) collective-permute-start(f32[128,128]{1,0:T(8,128)S(1)} %shard_map.101.other), channel_id=1, source_target_pairs={{0,1},{1,0},{2,3},{3,2},{4,8},{5,9},{6,10},{7,11},{8,4},{9,5},{10,... | collective-permute-start | bytes 196616 | tf_op jit(solution)/shard_map/ppermute | solution.py:341
  61.6 4.0 %collective-permute-start.30 = (f32[128,128]{1,0:T(8,128)S(1)}, f32[128,128]{1,0:T(8,128)S(1)}, u32[]{:S(2)}, u32[]{:S(2)}) collective-permute-start(f32[128,128]{1,0:T(8,128)S(1)} %collective-permute-done.29.refs_0_), channel_id=1, source_target_pairs={{0,1},{1,0},{2,3},{3,2},{4,6},{5,7},{6,4},{7,5},{8,9},{9,8},{10,11... | collective-permute-start | bytes 196616 | tf_op jit(solution)/shard_map/ppermute | solution.py:341
  66.9 4.6 %collective-permute-start.33 = (f32[128,128]{1,0:T(8,128)S(1)}, f32[128,128]{1,0:T(8,128)S(1)}, u32[]{:S(2)}, u32[]{:S(2)}) collective-permute-start(f32[128,128]{1,0:T(8,128)S(1)} %shard_map.102.mine), channel_id=1, source_target_pairs={{0,1},{1,0},{2,3},{3,2},{4,5},{5,4},{6,7},{7,6},{8,9},{9,8},{10,11... | collective-permute-start | bytes 196616 | tf_op jit(solution)/shard_map/ppermute | solution.py:341
  (18 other events, 84.0 us)

commit v14 on v12

--- a/solution.py
+++ b/solution.py
@@ -141,21 +141,10 @@
     crossing[...] = jnp.where(lax.axis_index("slab") % 2 == 1, whole, stepped[...])
 
 
-def even_slabs_kernel(base, more, less, out):
+def join_kernel(spacing, base, more, less, out):
     s = lax.axis_index("slab")
-    even = s % 2 == 0
-    out[...] = base[...] - keep(even & (s > 0), more) - keep(even, less)
-
-
-def reduce_kernel(spacing, count, base, *refs):
-    out = refs[-1]
-    less, *more = refs[:count]
-    s = lax.axis_index("slab")
-    kept = s % (4 * spacing) == 0
-    values = base[...] - keep(kept, less)
-    for late in more:
-        values = values - keep(kept & (s > 0), late)
-    out[...] = values
+    left = s % (2 * spacing) == 0
+    out[...] = base[...] - keep(left & (s > 0), more) - keep(left, less)
 
 
 def ham_kernel(slabs, near, far, next_near, next_far, own_e, mate_e, own_t, mate_t, *refs):
@@ -278,10 +267,6 @@
     @pl.when(jnp.logical_not(active))
     def _():
         out[...] = other[...]
-
-
-def copy_kernel(values, *refs):
-    refs[-1][...] = values[...]
 
 
 def call(
@@ -387,31 +372,11 @@
     base = call(even_kernel, rest, stepped, far, *t_pair, scratch=[store])
 
     pivot = near
-    waiting = None
-
-    def late_shares(after):
-        if waiting is None:
-            return ()
-        beneath, over, d = waiting
-        patient = [b for b in every if b % (4 * d) == 0]
-        held = call(copy_kernel, beneath, unused=(after,))
-        ways = [(b + d, b, b + 1) for b in patient]
-        shares = both(held, ways, ways)
-        if len(patient) > 1:
-            held = call(copy_kernel, over, unused=(after,))
-            shares += both(
-                held,
-                [(b - d, b, b - d + 1) for b in patient if b > 0],
-                [(b - d, b, b - d + 3) for b in patient if b > 0],
-            )
-        return shares
-
     for level in range(levels):
         d = 2**level
         if level == levels - 1:
             beneath = call(kernel(top_kernel, d), near, far, *front, scratch=[store])
-            shares = late_shares(beneath)
-            shares += both(beneath, [(d, 0, 1, d + 1)], [(d, 0, 1, d - 1)])
+            shares = both(beneath, [(d, 0, 1, d + 1)], [(d, 0, 1, d - 1)])
             pivot = call(kernel(pivot_kernel, d), near, far, *back, pivot, scratch=[store])
             pivot = call(
                 kernel(root_kernel, len(shares) // 2),
@@ -445,23 +410,20 @@
                 unused=(over,),
                 flops=1,
             )
-            base = near = call(even_slabs_kernel, base, more, less)
+            base = near = call(kernel(join_kernel, d), base, more, less)
             base_far = far = exchange(near, every[::2])
             continue
-        urgent = [b for b in every if b % (4 * d) == 2 * d]
-        more = both(over, [(b - d, b, b - 1) for b in urgent], [(b - d, b, b - 3) for b in urgent])
+        active = [a for a in every if a % (2 * d) == d]
+        rising = [a for a in active if a + d < slabs]
+        more = both(
+            over, [(a, a + d, a + 1) for a in rising], [(a, a + d, a - 1) for a in rising]
+        )
         less = both(
-            beneath, [(b + d, b, b + 1) for b in urgent], [(b + d, b, b + 3) for b in urgent]
+            beneath, [(a, a - d, a - 1) for a in active], [(a, a - d, a + 1) for a in active]
         )
         pivot = call(kernel(pivot_kernel, d), near, far, *back, pivot, scratch=[store])
-        late = late_shares(beneath)
-        if late:
-            count = len(late) // 2
-            base = call(kernel(reduce_kernel, d // 2, count), base, *late[::2])
-            base_far = call(kernel(reduce_kernel, d // 2, count), base_far, *late[1::2])
-        near = base - more[0] - less[0]
-        far = base_far - more[1] - less[1]
-        waiting = beneath, over, d
+        near = base = call(kernel(join_kernel, d), base, more[0], less[0])
+        far = base_far = call(kernel(join_kernel, d), base_far, more[1], less[1])
 
     solved = pivot
     for level in reversed(range(levels)):

time: 72.2 us -> 72.1 us (level)
  starting transfers between devices: 48.4 us -> 46.8 us
  waiting for transfers between devices: 17.2 us -> 18.4 us
    ppermute x34 -> x32, starting transfers between devices: 48.4 us -> 46.8 us  [send(): lax.ppermute(values, ('slab', 'col'), completed(route, slabs * cols, cols))]
    ppermute x34 -> x32, waiting for transfers between devices: 17.2 us -> 18.4 us  [send(): lax.ppermute(values, ('slab', 'col'), completed(route, slabs * cols, cols))]
    pallas_call x21 -> x22, Pallas kernels: 6.12 us -> 6.16 us  [call(): pl.pallas_call(kernel, out_shape=shape if outs == 1 else (shape,) * outs,...]
  transfers between devices with their start and end apart: 34 -> 32, of which waited for: 19 -> 18; matrix products, arithmetic and copies ran while one was open for 0% -> 0% of each run, Pallas kernels for 4% -> 4%
where the time goes in v14:
time: 72.1 us; the launch traced here: 71.6 us
  starting transfers between devices  46.8 us (65%)
  waiting for transfers between devices  18.4 us (26%)
  Pallas kernels  6.16 us (9%)
    ppermute x32, starting transfers between devices, send(): lax.ppermute(values, ('slab', 'col'), completed(route, slabs * cols, cols))  46.8 us
    ppermute x32, waiting for transfers between devices, send(): lax.ppermute(values, ('slab', 'col'), completed(route, slabs * cols, cols))  18.4 us
    pallas_call x22, Pallas kernels, call(): pl.pallas_call(kernel, out_shape=shape if outs == 1 else (shape,) * outs,...  6.16 us
  transfers between devices with their start and end apart: 32, of which 18 were waited for; matrix products, arithmetic and copies ran while one was open for 0% of the time, Pallas kernels for 4%

profile of v14, /device:TPU:13, one launch (start us, length us, event | category | flops | bytes accessed | tf_op | source)
XLA Modules:
  0.0 71.6 jit_solution(2307640732205722907)
XLA Ops:
  1.2 1.3 %collective-permute-done.other = f32[1,128,128]{2,1,0:T(8,128)S(1)} collective-permute-done((f32[1,128,128]{2,1,0:T(8,128)}, f32[1,128,128]{2,1,0:T(8,128)S(1)}, u32[]{:S(2)}, u32[]{:S(2)}) %collective-permute-start) | collective-permute-done | bytes 65568 | tf_op jit(solution)/shard_map/ppermute | solution.py:326
  3.3 1.3 %collective-permute-start.6 = (f32[128,128]{1,0:T(8,128)S(1)}, f32[128,128]{1,0:T(8,128)S(1)}, u32[]{:S(2)}, u32[]{:S(2)}) collective-permute-start(f32[128,128]{1,0:T(8,128)S(1)} %get-tuple-element.16), channel_id=1, source_target_pairs={{0,2},{1,3},{2,0},{3,1},{4,6},{5,7},{6,4},{7,5},{8,10},{9,11},{10,... | collective-permute-start | bytes 196616 | tf_op jit(solution)/shard_map/ppermute | solution.py:326
  4.5 1.2 %collective-permute-start.4 = (f32[128,128]{1,0:T(8,128)S(1)}, f32[128,128]{1,0:T(8,128)S(1)}, u32[]{:S(2)}, u32[]{:S(2)}) collective-permute-start(f32[128,128]{1,0:T(8,128)S(1)} %get-tuple-element.14.packed.near), channel_id=1, source_target_pairs={{0,1},{1,0},{2,3},{3,2},{4,10},{5,11},{6,8},{7,9},{8,6},{9,7},{10,... | collective-permute-start | bytes 196616 | tf_op jit(solution)/shard_map/ppermute | solution.py:326
  5.8 1.1 %collective-permute-start.3 = (f32[128,128]{1,0:T(8,128)S(1)}, f32[128,128]{1,0:T(8,128)S(1)}, u32[]{:S(2)}, u32[]{:S(2)}) collective-permute-start(f32[128,128]{1,0:T(8,128)S(1)} %get-tuple-element.14.packed.near), channel_id=1, source_target_pairs={{0,1},{1,0},{2,3},{3,2},{4,8},{5,9},{6,10},{7,11},{8,4},{9,5},{10,... | collective-permute-start | bytes 196616 | tf_op jit(solution)/shard_map/ppermute | solution.py:326
  6.9 1.2 %collective-permute-start.2 = (f32[128,128]{1,0:T(8,128)S(1)}, f32[128,128]{1,0:T(8,128)S(1)}, u32[]{:S(2)}, u32[]{:S(2)}) collective-permute-start(f32[128,128]{1,0:T(8,128)S(1)} %get-tuple-element.14.packed.near), channel_id=1, source_target_pairs={{0,2},{1,3},{2,0},{3,1},{4,6},{5,7},{6,4},{7,5},{8,10},{9,11},{10,... | collective-permute-start | bytes 196616 | tf_op jit(solution)/shard_map/ppermute | solution.py:326
  8.4 1.2 %collective-permute-done.4.next_far = f32[128,128]{1,0:T(8,128)S(1)} collective-permute-done((f32[128,128]{1,0:T(8,128)S(1)}, f32[128,128]{1,0:T(8,128)S(1)}, u32[]{:S(2)}, u32[]{:S(2)}) %collective-permute-start.4) | collective-permute-done | bytes 65568 | tf_op jit(solution)/shard_map/ppermute | solution.py:326
  12.5 1.7 %collective-permute-start.9 = (f32[10,128,512]{2,1,0:T(8,128)S(1)}, f32[10,128,512]{2,1,0:T(8,128)S(1)}, u32[]{:S(2)}, u32[]{:S(2)}) collective-permute-start(f32[10,128,512]{2,1,0:T(8,128)S(1)} %shard_map.88.own.refs_4_.refs_6_), channel_id=1, source_target_pairs={{0,1},{1,0},{2,3},{3,2},{4,5},{5,4},{6,7},{7,6},{8,9},{9,8},{10,11... | collective-permute-start | bytes 7864328 | tf_op jit(solution)/shard_map/ppermute | solution.py:326
  15.0 2.9 %collective-permute-done.8.next_far.far = f32[128,128]{1,0:T(8,128)S(1)} collective-permute-done((f32[128,128]{1,0:T(8,128)S(1)}, f32[128,128]{1,0:T(8,128)S(1)}, u32[]{:S(2)}, u32[]{:S(2)}) %collective-permute-start.8) | collective-permute-done | bytes 65568 | tf_op jit(solution)/shard_map/ppermute | solution.py:326
  20.2 1.8 %collective-permute-start.10 = (f32[128,128]{1,0:T(8,128)S(1)}, f32[128,128]{1,0:T(8,128)S(1)}, u32[]{:S(2)}, u32[]{:S(2)}) collective-permute-start(f32[128,128]{1,0:T(8,128)S(1)} %shard_map.90.refs_0_), channel_id=1, source_target_pairs={{0,1},{1,0},{2,3},{3,2},{4,8},{5,9},{6,10},{7,11},{8,4},{9,5},{10,... | collective-permute-start | bytes 196616 | tf_op jit(solution)/shard_map/ppermute | solution.py:326
  22.0 2.3 %collective-permute-done.10.more = f32[128,128]{1,0:T(8,128)S(1)} collective-permute-done((f32[128,128]{1,0:T(8,128)S(1)}, f32[128,128]{1,0:T(8,128)S(1)}, u32[]{:S(2)}, u32[]{:S(2)}) %collective-permute-start.10) | collective-permute-done | bytes 65568 | tf_op jit(solution)/shard_map/ppermute | solution.py:326
  24.4 1.6 %collective-permute-start.12 = (f32[128,128]{1,0:T(8,128)S(1)}, f32[128,128]{1,0:T(8,128)S(1)}, u32[]{:S(2)}, u32[]{:S(2)}) collective-permute-start(f32[128,128]{1,0:T(8,128)S(1)} %shard_map.91.near.base), channel_id=1, source_target_pairs={{0,2},{1,3},{2,0},{3,1},{4,5},{5,4},{6,7},{7,6},{8,10},{9,11},{10,... | collective-permute-start | bytes 196616 | tf_op jit(solution)/shard_map/ppermute | solution.py:326
  27.2 2.8 %collective-permute-start.13 = (f32[128,128]{1,0:T(8,128)S(1)}, f32[128,128]{1,0:T(8,128)S(1)}, u32[]{:S(2)}, u32[]{:S(2)}) collective-permute-start(f32[128,128]{1,0:T(8,128)S(1)} %get-tuple-element.21), channel_id=1, source_target_pairs={{0,1},{1,0},{2,3},{3,2},{4,5},{5,4},{6,7},{7,6},{8,16},{9,17},{10,... | collective-permute-start | bytes 196616 | tf_op jit(solution)/shard_map/ppermute | solution.py:326
  30.0 3.5 %collective-permute-start.14 = (f32[128,128]{1,0:T(8,128)S(1)}, f32[128,128]{1,0:T(8,128)S(1)}, u32[]{:S(2)}, u32[]{:S(2)}) collective-permute-start(f32[128,128]{1,0:T(8,128)S(1)} %get-tuple-element.22), channel_id=1, source_target_pairs={{0,4},{1,5},{2,6},{3,7},{4,8},{5,9},{6,10},{7,11},{8,0},{9,1},{10,... | collective-permute-start | bytes 196616 | tf_op jit(solution)/shard_map/ppermute | solution.py:326
  33.5 1.9 %collective-permute-done.16.less = f32[128,128]{1,0:T(8,128)S(1)} collective-permute-done((f32[128,128]{1,0:T(8,128)S(1)}, f32[128,128]{1,0:T(8,128)S(1)}, u32[]{:S(2)}, u32[]{:S(2)}) %collective-permute-start.16) | collective-permute-done | bytes 65568 | tf_op jit(solution)/shard_map/ppermute | solution.py:326
  35.5 3.9 %collective-permute-start.18 = (f32[128,128]{1,0:T(8,128)S(1)}, f32[128,128]{1,0:T(8,128)S(1)}, u32[]{:S(2)}, u32[]{:S(2)}) collective-permute-start(f32[128,128]{1,0:T(8,128)S(1)} %shard_map.95), channel_id=1, source_target_pairs={{0,6},{1,7},{2,4},{3,5},{4,12},{5,13},{6,14},{7,15},{8,9},{9,8},{1... | collective-permute-start | bytes 196616 | tf_op jit(solution)/shard_map/ppermute | solution.py:326
  39.4 1.8 %collective-permute-start.17 = (f32[128,128]{1,0:T(8,128)S(1)}, f32[128,128]{1,0:T(8,128)S(1)}, u32[]{:S(2)}, u32[]{:S(2)}) collective-permute-start(f32[128,128]{1,0:T(8,128)S(1)} %shard_map.95), channel_id=1, source_target_pairs={{0,4},{1,5},{2,6},{3,7},{4,20},{5,21},{6,22},{7,23},{8,9},{9,8},{1... | collective-permute-start | bytes 196616 | tf_op jit(solution)/shard_map/ppermute | solution.py:326
  42.2 1.9 %collective-permute-start.20 = (f32[128,128]{1,0:T(8,128)S(1)}, f32[128,128]{1,0:T(8,128)S(1)}, u32[]{:S(2)}, u32[]{:S(2)}) collective-permute-start(f32[128,128]{1,0:T(8,128)S(1)} %shard_map.99.part), channel_id=1, source_target_pairs={{0,18},{1,19},{2,16},{3,17},{4,0},{5,1},{6,2},{7,3},{8,9},{9,8},{1... | collective-permute-start | bytes 196616 | tf_op jit(solution)/shard_map/ppermute | solution.py:326
  44.1 2.3 %collective-permute-start.26 = (f32[128,128]{1,0:T(8,128)S(1)}, f32[128,128]{1,0:T(8,128)S(1)}, u32[]{:S(2)}, u32[]{:S(2)}) collective-permute-start(f32[128,128]{1,0:T(8,128)S(1)} %shard_map.99.part), channel_id=1, source_target_pairs={{0,10},{1,11},{2,8},{3,9},{4,0},{5,1},{6,2},{7,3},{8,14},{9,15},{1... | collective-permute-start | bytes 196616 | tf_op jit(solution)/shard_map/ppermute | solution.py:326
  46.5 3.6 %collective-permute-start.24 = (f32[128,128]{1,0:T(8,128)S(1)}, f32[128,128]{1,0:T(8,128)S(1)}, u32[]{:S(2)}, u32[]{:S(2)}) collective-permute-start(f32[128,128]{1,0:T(8,128)S(1)} %shard_map.100.other), channel_id=1, source_target_pairs={{0,1},{1,0},{2,3},{3,2},{4,5},{5,4},{6,7},{7,6},{8,14},{9,15},{10,... | collective-permute-start | bytes 196616 | tf_op jit(solution)/shard_map/ppermute | solution.py:326
  50.7 4.6 %collective-permute-start.22 = (f32[128,128]{1,0:T(8,128)S(1)}, f32[128,128]{1,0:T(8,128)S(1)}, u32[]{:S(2)}, u32[]{:S(2)}) collective-permute-start(f32[128,128]{1,0:T(8,128)S(1)} %shard_map.100.other), channel_id=1, source_target_pairs={{0,1},{1,0},{2,3},{3,2},{4,5},{5,4},{6,7},{7,6},{8,9},{9,8},{10,11... | collective-permute-start | bytes 196616 | tf_op jit(solution)/shard_map/ppermute | solution.py:326
  56.7 2.8 %collective-permute-start.29 = (f32[128,128]{1,0:T(8,128)S(1)}, f32[128,128]{1,0:T(8,128)S(1)}, u32[]{:S(2)}, u32[]{:S(2)}) collective-permute-start(f32[128,128]{1,0:T(8,128)S(1)} %shard_map.101.other), channel_id=1, source_target_pairs={{0,1},{1,0},{2,3},{3,2},{4,8},{5,9},{6,10},{7,11},{8,4},{9,5},{10,... | collective-permute-start | bytes 196616 | tf_op jit(solution)/shard_map/ppermute | solution.py:326
  60.2 1.9 %collective-permute-done.30.refs_3_ = f32[128,128]{1,0:T(8,128)S(1)} collective-permute-done((f32[128,128]{1,0:T(8,128)S(1)}, f32[128,128]{1,0:T(8,128)S(1)}, u32[]{:S(2)}, u32[]{:S(2)}) %collective-permute-start.30) | collective-permute-done | bytes 65568 | tf_op jit(solution)/shard_map/ppermute | solution.py:326
  63.0 1.4 %shard_map.102.mine = f32[128,128]{1,0:T(8,128)S(1)} custom-call(f32[128,128]{1,0:T(8,128)S(1)} %shard_map.99.part, f32[128,128]{1,0:T(8,128)S(1)} %shard_map.101.other, f32[128,128]{1,0:T(8,128)S(1)} %collective-permute-done.27.refs_0_, f32[128,128]{1,0:T(8,128)S(1)} %collective-permute-done.28.refs_1_, f32[128,128]{1,0:T(8,128)S(1)} %collective-permute-done.29.refs_2_, ...), custom_call_target="tpu_custom_call" | custom-call | flops 1000000000 | bytes 1 | tf_op jit(solution)/shard_map/pallas_call | solution.py:282
  64.3 5.7 %collective-permute-start.31 = (f32[128,128]{1,0:T(8,128)S(1)}, f32[128,128]{1,0:T(8,128)S(1)}, u32[]{:S(2)}, u32[]{:S(2)}) collective-permute-start(f32[128,128]{1,0:T(8,128)S(1)} %shard_map.102.mine), channel_id=1, source_target_pairs={{0,1},{1,0},{2,3},{3,2},{4,5},{5,4},{6,7},{7,6},{8,9},{9,8},{10,11... | collective-permute-start | bytes 196616 | tf_op jit(solution)/shard_map/ppermute | solution.py:326
  (78 shorter events, 15.5 us)
Async XLA Ops:
  0.7 7.7 %collective-permute-start.5 = (f32[1,128,512]{2,1,0:T(8,128)}, f32[1,128,512]{2,1,0:T(8,128)S(1)}, u32[]{:S(2)}, u32[]{:S(2)}) collective-permute-start(f32[1,128,512]{2,1,0:T(8,128)} %own_e.1), channel_id=1, source_target_pairs={{0,1},{1,0},{2,3},{3,2},{4,5},{5,4},{6,7},{7,6},{8,9},{9,8},{10,11... | collective-permute-start | bytes 786440 | tf_op jit(solution)/shard_map/ppermute | solution.py:326
  3.3 4.8 %collective-permute-start.6 = (f32[128,128]{1,0:T(8,128)S(1)}, f32[128,128]{1,0:T(8,128)S(1)}, u32[]{:S(2)}, u32[]{:S(2)}) collective-permute-start(f32[128,128]{1,0:T(8,128)S(1)} %get-tuple-element.16), channel_id=1, source_target_pairs={{0,2},{1,3},{2,0},{3,1},{4,6},{5,7},{6,4},{7,5},{8,10},{9,11},{10,... | collective-permute-start | bytes 196616 | tf_op jit(solution)/shard_map/ppermute | solution.py:326
  4.5 5.1 %collective-permute-start.4 = (f32[128,128]{1,0:T(8,128)S(1)}, f32[128,128]{1,0:T(8,128)S(1)}, u32[]{:S(2)}, u32[]{:S(2)}) collective-permute-start(f32[128,128]{1,0:T(8,128)S(1)} %get-tuple-element.14.packed.near), channel_id=1, source_target_pairs={{0,1},{1,0},{2,3},{3,2},{4,10},{5,11},{6,8},{7,9},{8,6},{9,7},{10,... | collective-permute-start | bytes 196616 | tf_op jit(solution)/shard_map/ppermute | solution.py:326
  5.8 4.9 %collective-permute-start.3 = (f32[128,128]{1,0:T(8,128)S(1)}, f32[128,128]{1,0:T(8,128)S(1)}, u32[]{:S(2)}, u32[]{:S(2)}) collective-permute-start(f32[128,128]{1,0:T(8,128)S(1)} %get-tuple-element.14.packed.near), channel_id=1, source_target_pairs={{0,1},{1,0},{2,3},{3,2},{4,8},{5,9},{6,10},{7,11},{8,4},{9,5},{10,... | collective-permute-start | bytes 196616 | tf_op jit(solution)/shard_map/ppermute | solution.py:326
  6.9 3.9 %collective-permute-start.2 = (f32[128,128]{1,0:T(8,128)S(1)}, f32[128,128]{1,0:T(8,128)S(1)}, u32[]{:S(2)}, u32[]{:S(2)}) collective-permute-start(f32[128,128]{1,0:T(8,128)S(1)} %get-tuple-element.14.packed.near), channel_id=1, source_target_pairs={{0,2},{1,3},{2,0},{3,1},{4,6},{5,7},{6,4},{7,5},{8,10},{9,11},{10,... | collective-permute-start | bytes 196616 | tf_op jit(solution)/shard_map/ppermute | solution.py:326
  8.1 4.2 %collective-permute-start.7 = (f32[128,128]{1,0:T(8,128)S(1)}, f32[128,128]{1,0:T(8,128)S(1)}, u32[]{:S(2)}, u32[]{:S(2)}) collective-permute-start(f32[128,128]{1,0:T(8,128)S(1)} %get-tuple-element.18), channel_id=1, source_target_pairs={{0,4},{1,5},{2,6},{3,7},{4,0},{5,1},{6,2},{7,3},{8,12},{9,13},{10,... | collective-permute-start | bytes 196616 | tf_op jit(solution)/shard_map/ppermute | solution.py:326
  12.5 6.3 %collective-permute-start.9 = (f32[10,128,512]{2,1,0:T(8,128)S(1)}, f32[10,128,512]{2,1,0:T(8,128)S(1)}, u32[]{:S(2)}, u32[]{:S(2)}) collective-permute-start(f32[10,128,512]{2,1,0:T(8,128)S(1)} %shard_map.88.own.refs_4_.refs_6_), channel_id=1, source_target_pairs={{0,1},{1,0},{2,3},{3,2},{4,5},{5,4},{6,7},{7,6},{8,9},{9,8},{10,11... | collective-permute-start | bytes 7864328 | tf_op jit(solution)/shard_map/ppermute | solution.py:326
  14.3 3.7 %collective-permute-start.8 = (f32[128,128]{1,0:T(8,128)S(1)}, f32[128,128]{1,0:T(8,128)S(1)}, u32[]{:S(2)}, u32[]{:S(2)}) collective-permute-start(f32[128,128]{1,0:T(8,128)S(1)} %get-tuple-element.19), channel_id=1, source_target_pairs={{0,2},{1,3},{2,0},{3,1},{4,6},{5,7},{6,4},{7,5},{8,10},{9,11},{10,... | collective-permute-start | bytes 196616 | tf_op jit(solution)/shard_map/ppermute | solution.py:326
  19.5 4.9 %collective-permute-start.11 = (f32[128,128]{1,0:T(8,128)S(1)}, f32[128,128]{1,0:T(8,128)S(1)}, u32[]{:S(2)}, u32[]{:S(2)}) collective-permute-start(f32[128,128]{1,0:T(8,128)S(1)} %shard_map.89.refs_1_), channel_id=1, source_target_pairs={{0,4},{1,5},{2,6},{3,7},{4,0},{5,1},{6,2},{7,3},{8,12},{9,13},{10,... | collective-permute-start | bytes 196616 | tf_op jit(solution)/shard_map/ppermute | solution.py:326
  20.2 4.1 %collective-permute-start.10 = (f32[128,128]{1,0:T(8,128)S(1)}, f32[128,128]{1,0:T(8,128)S(1)}, u32[]{:S(2)}, u32[]{:S(2)}) collective-permute-start(f32[128,128]{1,0:T(8,128)S(1)} %shard_map.90.refs_0_), channel_id=1, source_target_pairs={{0,1},{1,0},{2,3},{3,2},{4,8},{5,9},{6,10},{7,11},{8,4},{9,5},{10,... | collective-permute-start | bytes 196616 | tf_op jit(solution)/shard_map/ppermute | solution.py:326
  26.8 6.7 %collective-permute-start.15 = (f32[128,128]{1,0:T(8,128)S(1)}, f32[128,128]{1,0:T(8,128)S(1)}, u32[]{:S(2)}, u32[]{:S(2)}) collective-permute-start(f32[128,128]{1,0:T(8,128)S(1)} %get-tuple-element.21), channel_id=1, source_target_pairs={{0,1},{1,0},{2,3},{3,2},{4,8},{5,9},{6,10},{7,11},{8,18},{9,19},{1... | collective-permute-start | bytes 196616 | tf_op jit(solution)/shard_map/ppermute | solution.py:326
  27.2 8.3 %collective-permute-start.13 = (f32[128,128]{1,0:T(8,128)S(1)}, f32[128,128]{1,0:T(8,128)S(1)}, u32[]{:S(2)}, u32[]{:S(2)}) collective-permute-start(f32[128,128]{1,0:T(8,128)S(1)} %get-tuple-element.21), channel_id=1, source_target_pairs={{0,1},{1,0},{2,3},{3,2},{4,5},{5,4},{6,7},{7,6},{8,16},{9,17},{10,... | collective-permute-start | bytes 196616 | tf_op jit(solution)/shard_map/ppermute | solution.py:326
  30.0 5.5 %collective-permute-start.16 = (f32[128,128]{1,0:T(8,128)S(1)}, f32[128,128]{1,0:T(8,128)S(1)}, u32[]{:S(2)}, u32[]{:S(2)}) collective-permute-start(f32[128,128]{1,0:T(8,128)S(1)} %get-tuple-element.22), channel_id=1, source_target_pairs={{0,14},{1,15},{2,12},{3,13},{4,5},{5,4},{6,7},{7,6},{8,2},{9,3},{1... | collective-permute-start | bytes 196616 | tf_op jit(solution)/shard_map/ppermute | solution.py:326
  30.0 5.5 %collective-permute-start.14 = (f32[128,128]{1,0:T(8,128)S(1)}, f32[128,128]{1,0:T(8,128)S(1)}, u32[]{:S(2)}, u32[]{:S(2)}) collective-permute-start(f32[128,128]{1,0:T(8,128)S(1)} %get-tuple-element.22), channel_id=1, source_target_pairs={{0,4},{1,5},{2,6},{3,7},{4,8},{5,9},{6,10},{7,11},{8,0},{9,1},{10,... | collective-permute-start | bytes 196616 | tf_op jit(solution)/shard_map/ppermute | solution.py:326
  35.5 5.7 %collective-permute-start.18 = (f32[128,128]{1,0:T(8,128)S(1)}, f32[128,128]{1,0:T(8,128)S(1)}, u32[]{:S(2)}, u32[]{:S(2)}) collective-permute-start(f32[128,128]{1,0:T(8,128)S(1)} %shard_map.95), channel_id=1, source_target_pairs={{0,6},{1,7},{2,4},{3,5},{4,12},{5,13},{6,14},{7,15},{8,9},{9,8},{1... | collective-permute-start | bytes 196616 | tf_op jit(solution)/shard_map/ppermute | solution.py:326
  42.2 4.3 %collective-permute-start.20 = (f32[128,128]{1,0:T(8,128)S(1)}, f32[128,128]{1,0:T(8,128)S(1)}, u32[]{:S(2)}, u32[]{:S(2)}) collective-permute-start(f32[128,128]{1,0:T(8,128)S(1)} %shard_map.99.part), channel_id=1, source_target_pairs={{0,18},{1,19},{2,16},{3,17},{4,0},{5,1},{6,2},{7,3},{8,9},{9,8},{1... | collective-permute-start | bytes 196616 | tf_op jit(solution)/shard_map/ppermute | solution.py:326
  44.1 11.2 %collective-permute-start.26 = (f32[128,128]{1,0:T(8,128)S(1)}, f32[128,128]{1,0:T(8,128)S(1)}, u32[]{:S(2)}, u32[]{:S(2)}) collective-permute-start(f32[128,128]{1,0:T(8,128)S(1)} %shard_map.99.part), channel_id=1, source_target_pairs={{0,10},{1,11},{2,8},{3,9},{4,0},{5,1},{6,2},{7,3},{8,14},{9,15},{1... | collective-permute-start | bytes 196616 | tf_op jit(solution)/shard_map/ppermute | solution.py:326
  46.4 8.9 %collective-permute-start.25 = (f32[128,128]{1,0:T(8,128)S(1)}, f32[128,128]{1,0:T(8,128)S(1)}, u32[]{:S(2)}, u32[]{:S(2)}) collective-permute-start(f32[128,128]{1,0:T(8,128)S(1)} %shard_map.99.part), channel_id=1, source_target_pairs={{0,8},{1,9},{2,10},{3,11},{4,0},{5,1},{6,2},{7,3},{8,12},{9,13},{1... | collective-permute-start | bytes 196616 | tf_op jit(solution)/shard_map/ppermute | solution.py:326
  46.5 8.9 %collective-permute-start.24 = (f32[128,128]{1,0:T(8,128)S(1)}, f32[128,128]{1,0:T(8,128)S(1)}, u32[]{:S(2)}, u32[]{:S(2)}) collective-permute-start(f32[128,128]{1,0:T(8,128)S(1)} %shard_map.100.other), channel_id=1, source_target_pairs={{0,1},{1,0},{2,3},{3,2},{4,5},{5,4},{6,7},{7,6},{8,14},{9,15},{10,... | collective-permute-start | bytes 196616 | tf_op jit(solution)/shard_map/ppermute | solution.py:326
  50.1 5.2 %collective-permute-start.23 = (f32[128,128]{1,0:T(8,128)S(1)}, f32[128,128]{1,0:T(8,128)S(1)}, u32[]{:S(2)}, u32[]{:S(2)}) collective-permute-start(f32[128,128]{1,0:T(8,128)S(1)} %shard_map.100.other), channel_id=1, source_target_pairs={{0,1},{1,0},{2,3},{3,2},{4,5},{5,4},{6,7},{7,6},{8,12},{9,13},{10,... | collective-permute-start | bytes 196616 | tf_op jit(solution)/shard_map/ppermute | solution.py:326
  50.7 5.6 %collective-permute-start.22 = (f32[128,128]{1,0:T(8,128)S(1)}, f32[128,128]{1,0:T(8,128)S(1)}, u32[]{:S(2)}, u32[]{:S(2)}) collective-permute-start(f32[128,128]{1,0:T(8,128)S(1)} %shard_map.100.other), channel_id=1, source_target_pairs={{0,1},{1,0},{2,3},{3,2},{4,5},{5,4},{6,7},{7,6},{8,9},{9,8},{10,11... | collective-permute-start | bytes 196616 | tf_op jit(solution)/shard_map/ppermute | solution.py:326
  56.7 5.5 %collective-permute-start.30 = (f32[128,128]{1,0:T(8,128)S(1)}, f32[128,128]{1,0:T(8,128)S(1)}, u32[]{:S(2)}, u32[]{:S(2)}) collective-permute-start(f32[128,128]{1,0:T(8,128)S(1)} %shard_map.101.other), channel_id=1, source_target_pairs={{0,1},{1,0},{2,3},{3,2},{4,10},{5,11},{6,8},{7,9},{8,6},{9,7},{10,... | collective-permute-start | bytes 196616 | tf_op jit(solution)/shard_map/ppermute | solution.py:326
  56.7 5.7 %collective-permute-start.29 = (f32[128,128]{1,0:T(8,128)S(1)}, f32[128,128]{1,0:T(8,128)S(1)}, u32[]{:S(2)}, u32[]{:S(2)}) collective-permute-start(f32[128,128]{1,0:T(8,128)S(1)} %shard_map.101.other), channel_id=1, source_target_pairs={{0,1},{1,0},{2,3},{3,2},{4,8},{5,9},{6,10},{7,11},{8,4},{9,5},{10,... | collective-permute-start | bytes 196616 | tf_op jit(solution)/shard_map/ppermute | solution.py:326
  64.3 6.6 %collective-permute-start.31 = (f32[128,128]{1,0:T(8,128)S(1)}, f32[128,128]{1,0:T(8,128)S(1)}, u32[]{:S(2)}, u32[]{:S(2)}) collective-permute-start(f32[128,128]{1,0:T(8,128)S(1)} %shard_map.102.mine), channel_id=1, source_target_pairs={{0,1},{1,0},{2,3},{3,2},{4,5},{5,4},{6,7},{7,6},{8,9},{9,8},{10,11... | collective-permute-start | bytes 196616 | tf_op jit(solution)/shard_map/ppermute | solution.py:326
  (16 other events, 79.7 us)

commit v15 on v14

--- a/solution.py
+++ b/solution.py
@@ -414,13 +414,19 @@
             base_far = far = exchange(near, every[::2])
             continue
         active = [a for a in every if a % (2 * d) == d]
-        rising = [a for a in active if a + d < slabs]
-        more = both(
-            over, [(a, a + d, a + 1) for a in rising], [(a, a + d, a - 1) for a in rising]
-        )
-        less = both(
-            beneath, [(a, a - d, a - 1) for a in active], [(a, a - d, a + 1) for a in active]
-        )
+
+        def ways(step, helper):
+            moves = []
+            for a in active:
+                b = a + step
+                if b % (4 * d) == 2 * d:
+                    moves.append((a, b, a + helper))
+                elif b < slabs:
+                    moves += [(a, b), (b, a)]
+            return moves
+
+        more = both(over, ways(d, 1), ways(d, -1))
+        less = both(beneath, ways(-d, -1), ways(-d, 1))
         pivot = call(kernel(pivot_kernel, d), near, far, *back, pivot, scratch=[store])
         near = base = call(kernel(join_kernel, d), base, more[0], less[0])
         far = base_far = call(kernel(join_kernel, d), base_far, more[1], less[1])

time: 72.1 us -> 72.5 us (level)
  waiting for transfers between devices: 18.4 us -> 17.4 us
    ppermute x32, waiting for transfers between devices: 18.4 us -> 17.4 us  [send(): lax.ppermute(values, ('slab', 'col'), completed(route, slabs * cols, cols))]
  transfers between devices with their start and end apart: 32 -> 32, of which waited for: 18 -> 19; matrix products, arithmetic and copies ran while one was open for 0% -> 0% of each run, Pallas kernels for 4% -> 4%
where the time goes in v15:
time: 72.5 us; the launch traced here: 71.4 us
  starting transfers between devices  47.5 us (66%)
  waiting for transfers between devices  17.4 us (24%)
  Pallas kernels  6.15 us (8%)
    ppermute x32, starting transfers between devices, send(): lax.ppermute(values, ('slab', 'col'), completed(route, slabs * cols, cols))  47.5 us
    ppermute x32, waiting for transfers between devices, send(): lax.ppermute(values, ('slab', 'col'), completed(route, slabs * cols, cols))  17.4 us
    pallas_call x22, Pallas kernels, call(): pl.pallas_call(kernel, out_shape=shape if outs == 1 else (shape,) * outs,...  6.15 us
  transfers between devices with their start and end apart: 32, of which 19 were waited for; matrix products, arithmetic and copies ran while one was open for 0% of the time, Pallas kernels for 4%

profile of v15, /device:TPU:13, one launch (start us, length us, event | category | flops | bytes accessed | tf_op | source)
XLA Modules:
  0.0 71.4 jit_solution(6423333221500385268)
XLA Ops:
  1.2 1.3 %collective-permute-done.other = f32[1,128,128]{2,1,0:T(8,128)S(1)} collective-permute-done((f32[1,128,128]{2,1,0:T(8,128)}, f32[1,128,128]{2,1,0:T(8,128)S(1)}, u32[]{:S(2)}, u32[]{:S(2)}) %collective-permute-start) | collective-permute-done | bytes 65568 | tf_op jit(solution)/shard_map/ppermute | solution.py:326
  3.3 1.3 %collective-permute-start.6 = (f32[128,128]{1,0:T(8,128)S(1)}, f32[128,128]{1,0:T(8,128)S(1)}, u32[]{:S(2)}, u32[]{:S(2)}) collective-permute-start(f32[128,128]{1,0:T(8,128)S(1)} %get-tuple-element.16), channel_id=1, source_target_pairs={{0,2},{1,3},{2,0},{3,1},{4,6},{5,7},{6,4},{7,5},{8,10},{9,11},{10,... | collective-permute-start | bytes 196616 | tf_op jit(solution)/shard_map/ppermute | solution.py:326
  4.5 1.2 %collective-permute-start.4 = (f32[128,128]{1,0:T(8,128)S(1)}, f32[128,128]{1,0:T(8,128)S(1)}, u32[]{:S(2)}, u32[]{:S(2)}) collective-permute-start(f32[128,128]{1,0:T(8,128)S(1)} %get-tuple-element.14.packed.near), channel_id=1, source_target_pairs={{0,1},{1,0},{2,3},{3,2},{4,10},{5,11},{6,8},{7,9},{8,6},{9,7},{10,... | collective-permute-start | bytes 196616 | tf_op jit(solution)/shard_map/ppermute | solution.py:326
  5.8 1.1 %collective-permute-start.3 = (f32[128,128]{1,0:T(8,128)S(1)}, f32[128,128]{1,0:T(8,128)S(1)}, u32[]{:S(2)}, u32[]{:S(2)}) collective-permute-start(f32[128,128]{1,0:T(8,128)S(1)} %get-tuple-element.14.packed.near), channel_id=1, source_target_pairs={{0,1},{1,0},{2,3},{3,2},{4,8},{5,9},{6,10},{7,11},{8,4},{9,5},{10,... | collective-permute-start | bytes 196616 | tf_op jit(solution)/shard_map/ppermute | solution.py:326
  6.9 1.2 %collective-permute-start.2 = (f32[128,128]{1,0:T(8,128)S(1)}, f32[128,128]{1,0:T(8,128)S(1)}, u32[]{:S(2)}, u32[]{:S(2)}) collective-permute-start(f32[128,128]{1,0:T(8,128)S(1)} %get-tuple-element.14.packed.near), channel_id=1, source_target_pairs={{0,2},{1,3},{2,0},{3,1},{4,6},{5,7},{6,4},{7,5},{8,10},{9,11},{10,... | collective-permute-start | bytes 196616 | tf_op jit(solution)/shard_map/ppermute | solution.py:326
  8.4 1.2 %collective-permute-done.4.next_far = f32[128,128]{1,0:T(8,128)S(1)} collective-permute-done((f32[128,128]{1,0:T(8,128)S(1)}, f32[128,128]{1,0:T(8,128)S(1)}, u32[]{:S(2)}, u32[]{:S(2)}) %collective-permute-start.4) | collective-permute-done | bytes 65568 | tf_op jit(solution)/shard_map/ppermute | solution.py:326
  10.8 1.1 %shard_map.85.rest = f32[128,128]{1,0:T(8,128)S(1)} custom-call(f32[128,128]{1,0:T(8,128)S(1)} %get-tuple-element.14.packed.near, f32[128,128]{1,0:T(8,128)S(1)} %collective-permute-done.2.far, f32[128,128]{1,0:T(8,128)S(1)} %collective-permute-done.3.next_near, f32[128,128]{1,0:T(8,128)S(1)} %collective-permute-done.4.next_far, ...), custom_call_target="tpu_custom_call" | custom-call | flops 1000000000 | bytes 1 | tf_op jit(solution)/shard_map/pallas_call | solution.py:282
  12.5 1.7 %collective-permute-start.9 = (f32[10,128,512]{2,1,0:T(8,128)S(1)}, f32[10,128,512]{2,1,0:T(8,128)S(1)}, u32[]{:S(2)}, u32[]{:S(2)}) collective-permute-start(f32[10,128,512]{2,1,0:T(8,128)S(1)} %shard_map.88.own.refs_4_.refs_6_), channel_id=1, source_target_pairs={{0,1},{1,0},{2,3},{3,2},{4,5},{5,4},{6,7},{7,6},{8,9},{9,8},{10,11... | collective-permute-start | bytes 7864328 | tf_op jit(solution)/shard_map/ppermute | solution.py:326
  15.0 2.9 %collective-permute-done.8.next_far.far = f32[128,128]{1,0:T(8,128)S(1)} collective-permute-done((f32[128,128]{1,0:T(8,128)S(1)}, f32[128,128]{1,0:T(8,128)S(1)}, u32[]{:S(2)}, u32[]{:S(2)}) %collective-permute-start.8) | collective-permute-done | bytes 65568 | tf_op jit(solution)/shard_map/ppermute | solution.py:326
  20.2 1.8 %collective-permute-start.10 = (f32[128,128]{1,0:T(8,128)S(1)}, f32[128,128]{1,0:T(8,128)S(1)}, u32[]{:S(2)}, u32[]{:S(2)}) collective-permute-start(f32[128,128]{1,0:T(8,128)S(1)} %shard_map.90.refs_0_), channel_id=1, source_target_pairs={{0,1},{1,0},{2,3},{3,2},{4,8},{5,9},{6,10},{7,11},{8,4},{9,5},{10,... | collective-permute-start | bytes 196616 | tf_op jit(solution)/shard_map/ppermute | solution.py:326
  22.0 2.3 %collective-permute-done.10.more = f32[128,128]{1,0:T(8,128)S(1)} collective-permute-done((f32[128,128]{1,0:T(8,128)S(1)}, f32[128,128]{1,0:T(8,128)S(1)}, u32[]{:S(2)}, u32[]{:S(2)}) %collective-permute-start.10) | collective-permute-done | bytes 65568 | tf_op jit(solution)/shard_map/ppermute | solution.py:326
  24.4 1.6 %collective-permute-start.12 = (f32[128,128]{1,0:T(8,128)S(1)}, f32[128,128]{1,0:T(8,128)S(1)}, u32[]{:S(2)}, u32[]{:S(2)}) collective-permute-start(f32[128,128]{1,0:T(8,128)S(1)} %shard_map.91.near.base), channel_id=1, source_target_pairs={{0,2},{1,3},{2,0},{3,1},{4,5},{5,4},{6,7},{7,6},{8,10},{9,11},{10,... | collective-permute-start | bytes 196616 | tf_op jit(solution)/shard_map/ppermute | solution.py:326
  27.2 2.8 %collective-permute-start.13 = (f32[128,128]{1,0:T(8,128)S(1)}, f32[128,128]{1,0:T(8,128)S(1)}, u32[]{:S(2)}, u32[]{:S(2)}) collective-permute-start(f32[128,128]{1,0:T(8,128)S(1)} %get-tuple-element.21), channel_id=1, source_target_pairs={{0,1},{1,0},{2,3},{3,2},{4,5},{5,4},{6,7},{7,6},{8,16},{9,17},{10,... | collective-permute-start | bytes 196616 | tf_op jit(solution)/shard_map/ppermute | solution.py:326
  30.0 3.5 %collective-permute-start.16 = (f32[128,128]{1,0:T(8,128)S(1)}, f32[128,128]{1,0:T(8,128)S(1)}, u32[]{:S(2)}, u32[]{:S(2)}) collective-permute-start(f32[128,128]{1,0:T(8,128)S(1)} %get-tuple-element.22), channel_id=1, source_target_pairs={{0,10},{1,11},{2,8},{3,9},{4,5},{5,4},{6,7},{7,6},{8,2},{9,3},{10,... | collective-permute-start | bytes 196616 | tf_op jit(solution)/shard_map/ppermute | solution.py:326
  34.8 4.7 %collective-permute-start.18 = (f32[128,128]{1,0:T(8,128)S(1)}, f32[128,128]{1,0:T(8,128)S(1)}, u32[]{:S(2)}, u32[]{:S(2)}) collective-permute-start(f32[128,128]{1,0:T(8,128)S(1)} %shard_map.95), channel_id=1, source_target_pairs={{0,6},{1,7},{2,4},{3,5},{4,12},{5,13},{6,14},{7,15},{8,9},{9,8},{1... | collective-permute-start | bytes 196616 | tf_op jit(solution)/shard_map/ppermute | solution.py:326
  39.4 1.8 %collective-permute-start.17 = (f32[128,128]{1,0:T(8,128)S(1)}, f32[128,128]{1,0:T(8,128)S(1)}, u32[]{:S(2)}, u32[]{:S(2)}) collective-permute-start(f32[128,128]{1,0:T(8,128)S(1)} %shard_map.95), channel_id=1, source_target_pairs={{0,4},{1,5},{2,6},{3,7},{4,20},{5,21},{6,22},{7,23},{8,9},{9,8},{1... | collective-permute-start | bytes 196616 | tf_op jit(solution)/shard_map/ppermute | solution.py:326
  43.3 4.1 %collective-permute-start.26 = (f32[128,128]{1,0:T(8,128)S(1)}, f32[128,128]{1,0:T(8,128)S(1)}, u32[]{:S(2)}, u32[]{:S(2)}) collective-permute-start(f32[128,128]{1,0:T(8,128)S(1)} %shard_map.99.part), channel_id=1, source_target_pairs={{0,10},{1,11},{2,8},{3,9},{4,0},{5,1},{6,2},{7,3},{8,14},{9,15},{1... | collective-permute-start | bytes 196616 | tf_op jit(solution)/shard_map/ppermute | solution.py:326
  47.5 1.2 %collective-permute-start.24 = (f32[128,128]{1,0:T(8,128)S(1)}, f32[128,128]{1,0:T(8,128)S(1)}, u32[]{:S(2)}, u32[]{:S(2)}) collective-permute-start(f32[128,128]{1,0:T(8,128)S(1)} %shard_map.100.other), channel_id=1, source_target_pairs={{0,1},{1,0},{2,3},{3,2},{4,5},{5,4},{6,7},{7,6},{8,14},{9,15},{10,... | collective-permute-start | bytes 196616 | tf_op jit(solution)/shard_map/ppermute | solution.py:326
  48.7 3.0 %collective-permute-start.23 = (f32[128,128]{1,0:T(8,128)S(1)}, f32[128,128]{1,0:T(8,128)S(1)}, u32[]{:S(2)}, u32[]{:S(2)}) collective-permute-start(f32[128,128]{1,0:T(8,128)S(1)} %shard_map.100.other), channel_id=1, source_target_pairs={{0,1},{1,0},{2,3},{3,2},{4,5},{5,4},{6,7},{7,6},{8,12},{9,13},{10,... | collective-permute-start | bytes 196616 | tf_op jit(solution)/shard_map/ppermute | solution.py:326
  51.7 4.1 %collective-permute-start.22 = (f32[128,128]{1,0:T(8,128)S(1)}, f32[128,128]{1,0:T(8,128)S(1)}, u32[]{:S(2)}, u32[]{:S(2)}) collective-permute-start(f32[128,128]{1,0:T(8,128)S(1)} %shard_map.100.other), channel_id=1, source_target_pairs={{0,1},{1,0},{2,3},{3,2},{4,5},{5,4},{6,7},{7,6},{8,9},{9,8},{10,11... | collective-permute-start | bytes 196616 | tf_op jit(solution)/shard_map/ppermute | solution.py:326
  57.1 3.2 %collective-permute-start.29 = (f32[128,128]{1,0:T(8,128)S(1)}, f32[128,128]{1,0:T(8,128)S(1)}, u32[]{:S(2)}, u32[]{:S(2)}) collective-permute-start(f32[128,128]{1,0:T(8,128)S(1)} %shard_map.101.other), channel_id=1, source_target_pairs={{0,1},{1,0},{2,3},{3,2},{4,8},{5,9},{6,10},{7,11},{8,4},{9,5},{10,... | collective-permute-start | bytes 196616 | tf_op jit(solution)/shard_map/ppermute | solution.py:326
  60.6 1.5 %collective-permute-done.30.refs_3_ = f32[128,128]{1,0:T(8,128)S(1)} collective-permute-done((f32[128,128]{1,0:T(8,128)S(1)}, f32[128,128]{1,0:T(8,128)S(1)}, u32[]{:S(2)}, u32[]{:S(2)}) %collective-permute-start.30) | collective-permute-done | bytes 65568 | tf_op jit(solution)/shard_map/ppermute | solution.py:326
  63.4 1.4 %shard_map.102.mine = f32[128,128]{1,0:T(8,128)S(1)} custom-call(f32[128,128]{1,0:T(8,128)S(1)} %shard_map.99.part, f32[128,128]{1,0:T(8,128)S(1)} %shard_map.101.other, f32[128,128]{1,0:T(8,128)S(1)} %collective-permute-done.27.refs_0_, f32[128,128]{1,0:T(8,128)S(1)} %collective-permute-done.28.refs_1_, f32[128,128]{1,0:T(8,128)S(1)} %collective-permute-done.29.refs_2_, ...), custom_call_target="tpu_custom_call" | custom-call | flops 1000000000 | bytes 1 | tf_op jit(solution)/shard_map/pallas_call | solution.py:282
  64.8 5.0 %collective-permute-start.31 = (f32[128,128]{1,0:T(8,128)S(1)}, f32[128,128]{1,0:T(8,128)S(1)}, u32[]{:S(2)}, u32[]{:S(2)}) collective-permute-start(f32[128,128]{1,0:T(8,128)S(1)} %shard_map.102.mine), channel_id=1, source_target_pairs={{0,1},{1,0},{2,3},{3,2},{4,5},{5,4},{6,7},{7,6},{8,9},{9,8},{10,11... | collective-permute-start | bytes 196616 | tf_op jit(solution)/shard_map/ppermute | solution.py:326
  (78 shorter events, 16.1 us)
Async XLA Ops:
  0.7 7.7 %collective-permute-start.5 = (f32[1,128,512]{2,1,0:T(8,128)}, f32[1,128,512]{2,1,0:T(8,128)S(1)}, u32[]{:S(2)}, u32[]{:S(2)}) collective-permute-start(f32[1,128,512]{2,1,0:T(8,128)} %own_e.1), channel_id=1, source_target_pairs={{0,1},{1,0},{2,3},{3,2},{4,5},{5,4},{6,7},{7,6},{8,9},{9,8},{10,11... | collective-permute-start | bytes 786440 | tf_op jit(solution)/shard_map/ppermute | solution.py:326
  3.3 4.8 %collective-permute-start.6 = (f32[128,128]{1,0:T(8,128)S(1)}, f32[128,128]{1,0:T(8,128)S(1)}, u32[]{:S(2)}, u32[]{:S(2)}) collective-permute-start(f32[128,128]{1,0:T(8,128)S(1)} %get-tuple-element.16), channel_id=1, source_target_pairs={{0,2},{1,3},{2,0},{3,1},{4,6},{5,7},{6,4},{7,5},{8,10},{9,11},{10,... | collective-permute-start | bytes 196616 | tf_op jit(solution)/shard_map/ppermute | solution.py:326
  4.5 5.1 %collective-permute-start.4 = (f32[128,128]{1,0:T(8,128)S(1)}, f32[128,128]{1,0:T(8,128)S(1)}, u32[]{:S(2)}, u32[]{:S(2)}) collective-permute-start(f32[128,128]{1,0:T(8,128)S(1)} %get-tuple-element.14.packed.near), channel_id=1, source_target_pairs={{0,1},{1,0},{2,3},{3,2},{4,10},{5,11},{6,8},{7,9},{8,6},{9,7},{10,... | collective-permute-start | bytes 196616 | tf_op jit(solution)/shard_map/ppermute | solution.py:326
  5.8 4.9 %collective-permute-start.3 = (f32[128,128]{1,0:T(8,128)S(1)}, f32[128,128]{1,0:T(8,128)S(1)}, u32[]{:S(2)}, u32[]{:S(2)}) collective-permute-start(f32[128,128]{1,0:T(8,128)S(1)} %get-tuple-element.14.packed.near), channel_id=1, source_target_pairs={{0,1},{1,0},{2,3},{3,2},{4,8},{5,9},{6,10},{7,11},{8,4},{9,5},{10,... | collective-permute-start | bytes 196616 | tf_op jit(solution)/shard_map/ppermute | solution.py:326
  6.9 3.9 %collective-permute-start.2 = (f32[128,128]{1,0:T(8,128)S(1)}, f32[128,128]{1,0:T(8,128)S(1)}, u32[]{:S(2)}, u32[]{:S(2)}) collective-permute-start(f32[128,128]{1,0:T(8,128)S(1)} %get-tuple-element.14.packed.near), channel_id=1, source_target_pairs={{0,2},{1,3},{2,0},{3,1},{4,6},{5,7},{6,4},{7,5},{8,10},{9,11},{10,... | collective-permute-start | bytes 196616 | tf_op jit(solution)/shard_map/ppermute | solution.py:326
  8.1 4.2 %collective-permute-start.7 = (f32[128,128]{1,0:T(8,128)S(1)}, f32[128,128]{1,0:T(8,128)S(1)}, u32[]{:S(2)}, u32[]{:S(2)}) collective-permute-start(f32[128,128]{1,0:T(8,128)S(1)} %get-tuple-element.18), channel_id=1, source_target_pairs={{0,4},{1,5},{2,6},{3,7},{4,0},{5,1},{6,2},{7,3},{8,12},{9,13},{10,... | collective-permute-start | bytes 196616 | tf_op jit(solution)/shard_map/ppermute | solution.py:326
  12.5 6.3 %collective-permute-start.9 = (f32[10,128,512]{2,1,0:T(8,128)S(1)}, f32[10,128,512]{2,1,0:T(8,128)S(1)}, u32[]{:S(2)}, u32[]{:S(2)}) collective-permute-start(f32[10,128,512]{2,1,0:T(8,128)S(1)} %shard_map.88.own.refs_4_.refs_6_), channel_id=1, source_target_pairs={{0,1},{1,0},{2,3},{3,2},{4,5},{5,4},{6,7},{7,6},{8,9},{9,8},{10,11... | collective-permute-start | bytes 7864328 | tf_op jit(solution)/shard_map/ppermute | solution.py:326
  14.3 3.7 %collective-permute-start.8 = (f32[128,128]{1,0:T(8,128)S(1)}, f32[128,128]{1,0:T(8,128)S(1)}, u32[]{:S(2)}, u32[]{:S(2)}) collective-permute-start(f32[128,128]{1,0:T(8,128)S(1)} %get-tuple-element.19), channel_id=1, source_target_pairs={{0,2},{1,3},{2,0},{3,1},{4,6},{5,7},{6,4},{7,5},{8,10},{9,11},{10,... | collective-permute-start | bytes 196616 | tf_op jit(solution)/shard_map/ppermute | solution.py:326
  19.5 4.9 %collective-permute-start.11 = (f32[128,128]{1,0:T(8,128)S(1)}, f32[128,128]{1,0:T(8,128)S(1)}, u32[]{:S(2)}, u32[]{:S(2)}) collective-permute-start(f32[128,128]{1,0:T(8,128)S(1)} %shard_map.89.refs_1_), channel_id=1, source_target_pairs={{0,4},{1,5},{2,6},{3,7},{4,0},{5,1},{6,2},{7,3},{8,12},{9,13},{10,... | collective-permute-start | bytes 196616 | tf_op jit(solution)/shard_map/ppermute | solution.py:326
  20.2 4.1 %collective-permute-start.10 = (f32[128,128]{1,0:T(8,128)S(1)}, f32[128,128]{1,0:T(8,128)S(1)}, u32[]{:S(2)}, u32[]{:S(2)}) collective-permute-start(f32[128,128]{1,0:T(8,128)S(1)} %shard_map.90.refs_0_), channel_id=1, source_target_pairs={{0,1},{1,0},{2,3},{3,2},{4,8},{5,9},{6,10},{7,11},{8,4},{9,5},{10,... | collective-permute-start | bytes 196616 | tf_op jit(solution)/shard_map/ppermute | solution.py:326
  26.8 6.7 %collective-permute-start.15 = (f32[128,128]{1,0:T(8,128)S(1)}, f32[128,128]{1,0:T(8,128)S(1)}, u32[]{:S(2)}, u32[]{:S(2)}) collective-permute-start(f32[128,128]{1,0:T(8,128)S(1)} %get-tuple-element.21), channel_id=1, source_target_pairs={{0,1},{1,0},{2,3},{3,2},{4,8},{5,9},{6,10},{7,11},{8,18},{9,19},{1... | collective-permute-start | bytes 196616 | tf_op jit(solution)/shard_map/ppermute | solution.py:326
  27.2 7.2 %collective-permute-start.13 = (f32[128,128]{1,0:T(8,128)S(1)}, f32[128,128]{1,0:T(8,128)S(1)}, u32[]{:S(2)}, u32[]{:S(2)}) collective-permute-start(f32[128,128]{1,0:T(8,128)S(1)} %get-tuple-element.21), channel_id=1, source_target_pairs={{0,1},{1,0},{2,3},{3,2},{4,5},{5,4},{6,7},{7,6},{8,16},{9,17},{10,... | collective-permute-start | bytes 196616 | tf_op jit(solution)/shard_map/ppermute | solution.py:326
  30.0 4.4 %collective-permute-start.16 = (f32[128,128]{1,0:T(8,128)S(1)}, f32[128,128]{1,0:T(8,128)S(1)}, u32[]{:S(2)}, u32[]{:S(2)}) collective-permute-start(f32[128,128]{1,0:T(8,128)S(1)} %get-tuple-element.22), channel_id=1, source_target_pairs={{0,10},{1,11},{2,8},{3,9},{4,5},{5,4},{6,7},{7,6},{8,2},{9,3},{10,... | collective-permute-start | bytes 196616 | tf_op jit(solution)/shard_map/ppermute | solution.py:326
  34.8 6.5 %collective-permute-start.18 = (f32[128,128]{1,0:T(8,128)S(1)}, f32[128,128]{1,0:T(8,128)S(1)}, u32[]{:S(2)}, u32[]{:S(2)}) collective-permute-start(f32[128,128]{1,0:T(8,128)S(1)} %shard_map.95), channel_id=1, source_target_pairs={{0,6},{1,7},{2,4},{3,5},{4,12},{5,13},{6,14},{7,15},{8,9},{9,8},{1... | collective-permute-start | bytes 196616 | tf_op jit(solution)/shard_map/ppermute | solution.py:326
  42.2 5.3 %collective-permute-start.20 = (f32[128,128]{1,0:T(8,128)S(1)}, f32[128,128]{1,0:T(8,128)S(1)}, u32[]{:S(2)}, u32[]{:S(2)}) collective-permute-start(f32[128,128]{1,0:T(8,128)S(1)} %shard_map.99.part), channel_id=1, source_target_pairs={{0,18},{1,19},{2,16},{3,17},{4,0},{5,1},{6,2},{7,3},{8,9},{9,8},{1... | collective-permute-start | bytes 196616 | tf_op jit(solution)/shard_map/ppermute | solution.py:326
  43.2 4.3 %collective-permute-start.19 = (f32[128,128]{1,0:T(8,128)S(1)}, f32[128,128]{1,0:T(8,128)S(1)}, u32[]{:S(2)}, u32[]{:S(2)}) collective-permute-start(f32[128,128]{1,0:T(8,128)S(1)} %shard_map.99.part), channel_id=1, source_target_pairs={{0,16},{1,17},{2,18},{3,19},{4,0},{5,1},{6,2},{7,3},{8,9},{9,8},{1... | collective-permute-start | bytes 196616 | tf_op jit(solution)/shard_map/ppermute | solution.py:326
  43.3 12.5 %collective-permute-start.26 = (f32[128,128]{1,0:T(8,128)S(1)}, f32[128,128]{1,0:T(8,128)S(1)}, u32[]{:S(2)}, u32[]{:S(2)}) collective-permute-start(f32[128,128]{1,0:T(8,128)S(1)} %shard_map.99.part), channel_id=1, source_target_pairs={{0,10},{1,11},{2,8},{3,9},{4,0},{5,1},{6,2},{7,3},{8,14},{9,15},{1... | collective-permute-start | bytes 196616 | tf_op jit(solution)/shard_map/ppermute | solution.py:326
  47.4 8.3 %collective-permute-start.25 = (f32[128,128]{1,0:T(8,128)S(1)}, f32[128,128]{1,0:T(8,128)S(1)}, u32[]{:S(2)}, u32[]{:S(2)}) collective-permute-start(f32[128,128]{1,0:T(8,128)S(1)} %shard_map.99.part), channel_id=1, source_target_pairs={{0,8},{1,9},{2,10},{3,11},{4,0},{5,1},{6,2},{7,3},{8,12},{9,13},{1... | collective-permute-start | bytes 196616 | tf_op jit(solution)/shard_map/ppermute | solution.py:326
  47.5 8.3 %collective-permute-start.24 = (f32[128,128]{1,0:T(8,128)S(1)}, f32[128,128]{1,0:T(8,128)S(1)}, u32[]{:S(2)}, u32[]{:S(2)}) collective-permute-start(f32[128,128]{1,0:T(8,128)S(1)} %shard_map.100.other), channel_id=1, source_target_pairs={{0,1},{1,0},{2,3},{3,2},{4,5},{5,4},{6,7},{7,6},{8,14},{9,15},{10,... | collective-permute-start | bytes 196616 | tf_op jit(solution)/shard_map/ppermute | solution.py:326
  48.7 7.1 %collective-permute-start.23 = (f32[128,128]{1,0:T(8,128)S(1)}, f32[128,128]{1,0:T(8,128)S(1)}, u32[]{:S(2)}, u32[]{:S(2)}) collective-permute-start(f32[128,128]{1,0:T(8,128)S(1)} %shard_map.100.other), channel_id=1, source_target_pairs={{0,1},{1,0},{2,3},{3,2},{4,5},{5,4},{6,7},{7,6},{8,12},{9,13},{10,... | collective-permute-start | bytes 196616 | tf_op jit(solution)/shard_map/ppermute | solution.py:326
  51.7 5.0 %collective-permute-start.22 = (f32[128,128]{1,0:T(8,128)S(1)}, f32[128,128]{1,0:T(8,128)S(1)}, u32[]{:S(2)}, u32[]{:S(2)}) collective-permute-start(f32[128,128]{1,0:T(8,128)S(1)} %shard_map.100.other), channel_id=1, source_target_pairs={{0,1},{1,0},{2,3},{3,2},{4,5},{5,4},{6,7},{7,6},{8,9},{9,8},{10,11... | collective-permute-start | bytes 196616 | tf_op jit(solution)/shard_map/ppermute | solution.py:326
  57.0 5.1 %collective-permute-start.30 = (f32[128,128]{1,0:T(8,128)S(1)}, f32[128,128]{1,0:T(8,128)S(1)}, u32[]{:S(2)}, u32[]{:S(2)}) collective-permute-start(f32[128,128]{1,0:T(8,128)S(1)} %shard_map.101.other), channel_id=1, source_target_pairs={{0,1},{1,0},{2,3},{3,2},{4,10},{5,11},{6,8},{7,9},{8,6},{9,7},{10,... | collective-permute-start | bytes 196616 | tf_op jit(solution)/shard_map/ppermute | solution.py:326
  57.1 5.7 %collective-permute-start.29 = (f32[128,128]{1,0:T(8,128)S(1)}, f32[128,128]{1,0:T(8,128)S(1)}, u32[]{:S(2)}, u32[]{:S(2)}) collective-permute-start(f32[128,128]{1,0:T(8,128)S(1)} %shard_map.101.other), channel_id=1, source_target_pairs={{0,1},{1,0},{2,3},{3,2},{4,8},{5,9},{6,10},{7,11},{8,4},{9,5},{10,... | collective-permute-start | bytes 196616 | tf_op jit(solution)/shard_map/ppermute | solution.py:326
  64.8 5.9 %collective-permute-start.31 = (f32[128,128]{1,0:T(8,128)S(1)}, f32[128,128]{1,0:T(8,128)S(1)}, u32[]{:S(2)}, u32[]{:S(2)}) collective-permute-start(f32[128,128]{1,0:T(8,128)S(1)} %shard_map.102.mine), channel_id=1, source_target_pairs={{0,1},{1,0},{2,3},{3,2},{4,5},{5,4},{6,7},{7,6},{8,9},{9,8},{10,11... | collective-permute-start | bytes 196616 | tf_op jit(solution)/shard_map/ppermute | solution.py:326
  (16 other events, 78.5 us)

commit v16 on v14

--- a/solution.py
+++ b/solution.py
@@ -238,6 +238,26 @@
     @pl.when(jnp.logical_not(active))
     def _():
         out[...] = part[...]
+
+
+def side_term_kernel(slabs, lower, part, other, near, far, own, mate, out, store):
+    s = lax.axis_index("slab")
+    active = s % 2 == 1
+    linked = (s + 1 < slabs) | lower
+    first, last = (6, 8) if lower else (8, 10)
+
+    @pl.when(active & linked)
+    def _():
+        load_vector(store, near[...], far[...])
+        out[...] = part[...] - complex_product(own[first:last], mate[first:last], store)
+
+    @pl.when(active & jnp.logical_not(linked))
+    def _():
+        out[...] = part[...]
+
+    @pl.when(jnp.logical_not(active))
+    def _():
+        out[...] = other[...]
 
 
 def both_kernel(slabs, spacing, count, part, other, *refs):
@@ -456,6 +476,14 @@
                 early += both(solved, ways, ways)
         if level == levels - 1 and levels > 1:
             solved = call(kernel(settle_kernel, d), pivot, *vectors, *back, scratch=[store])
+        elif d == 1:
+            args = dict(scratch=[store], flops=1)
+            part = call(
+                kernel(side_term_kernel, slabs, False), pivot, solved, *vectors[2:], *back, **args
+            )
+            solved = call(
+                kernel(side_term_kernel, slabs, True), part, solved, *vectors[:2], *back, **args
+            )
         else:
             solved = call(
                 kernel(both_kernel, slabs, d, len(vectors)),

time: 72.1 us -> 71.5 us (level)
    pallas_call x22 -> x23, Pallas kernels: 6.16 us -> 6.19 us  [call(): pl.pallas_call(kernel, out_shape=shape if outs == 1 else (shape,) * outs,...]
  transfers between devices with their start and end apart: 32 -> 32, of which waited for: 18 -> 17; matrix products, arithmetic and copies ran while one was open for 0% -> 0% of each run, Pallas kernels for 4% -> 5%
where the time goes in v16:
time: 71.5 us; the launch traced here: 71.1 us
  starting transfers between devices  46.8 us (65%)
  waiting for transfers between devices  17.8 us (25%)
  Pallas kernels  6.19 us (9%)
    ppermute x32, starting transfers between devices, send(): lax.ppermute(values, ('slab', 'col'), completed(route, slabs * cols, cols))  46.8 us
    ppermute x32, waiting for transfers between devices, send(): lax.ppermute(values, ('slab', 'col'), completed(route, slabs * cols, cols))  17.8 us
    pallas_call x23, Pallas kernels, call(): pl.pallas_call(kernel, out_shape=shape if outs == 1 else (shape,) * outs,...  6.19 us
  transfers between devices with their start and end apart: 32, of which 17 were waited for; matrix products, arithmetic and copies ran while one was open for 0% of the time, Pallas kernels for 5%

profile of v16, /device:TPU:13, one launch (start us, length us, event | category | flops | bytes accessed | tf_op | source)
XLA Modules:
  0.0 71.1 jit_solution(5216371646773035)
XLA Ops:
  1.2 1.3 %collective-permute-done.other = f32[1,128,128]{2,1,0:T(8,128)S(1)} collective-permute-done((f32[1,128,128]{2,1,0:T(8,128)}, f32[1,128,128]{2,1,0:T(8,128)S(1)}, u32[]{:S(2)}, u32[]{:S(2)}) %collective-permute-start) | collective-permute-done | bytes 65568 | tf_op jit(solution)/shard_map/ppermute | solution.py:346
  3.3 1.3 %collective-permute-start.6 = (f32[128,128]{1,0:T(8,128)S(1)}, f32[128,128]{1,0:T(8,128)S(1)}, u32[]{:S(2)}, u32[]{:S(2)}) collective-permute-start(f32[128,128]{1,0:T(8,128)S(1)} %get-tuple-element.16), channel_id=1, source_target_pairs={{0,2},{1,3},{2,0},{3,1},{4,6},{5,7},{6,4},{7,5},{8,10},{9,11},{10,... | collective-permute-start | bytes 196616 | tf_op jit(solution)/shard_map/ppermute | solution.py:346
  4.5 1.2 %collective-permute-start.4 = (f32[128,128]{1,0:T(8,128)S(1)}, f32[128,128]{1,0:T(8,128)S(1)}, u32[]{:S(2)}, u32[]{:S(2)}) collective-permute-start(f32[128,128]{1,0:T(8,128)S(1)} %get-tuple-element.14.packed.near), channel_id=1, source_target_pairs={{0,1},{1,0},{2,3},{3,2},{4,10},{5,11},{6,8},{7,9},{8,6},{9,7},{10,... | collective-permute-start | bytes 196616 | tf_op jit(solution)/shard_map/ppermute | solution.py:346
  5.8 1.1 %collective-permute-start.3 = (f32[128,128]{1,0:T(8,128)S(1)}, f32[128,128]{1,0:T(8,128)S(1)}, u32[]{:S(2)}, u32[]{:S(2)}) collective-permute-start(f32[128,128]{1,0:T(8,128)S(1)} %get-tuple-element.14.packed.near), channel_id=1, source_target_pairs={{0,1},{1,0},{2,3},{3,2},{4,8},{5,9},{6,10},{7,11},{8,4},{9,5},{10,... | collective-permute-start | bytes 196616 | tf_op jit(solution)/shard_map/ppermute | solution.py:346
  6.9 1.2 %collective-permute-start.2 = (f32[128,128]{1,0:T(8,128)S(1)}, f32[128,128]{1,0:T(8,128)S(1)}, u32[]{:S(2)}, u32[]{:S(2)}) collective-permute-start(f32[128,128]{1,0:T(8,128)S(1)} %get-tuple-element.14.packed.near), channel_id=1, source_target_pairs={{0,2},{1,3},{2,0},{3,1},{4,6},{5,7},{6,4},{7,5},{8,10},{9,11},{10,... | collective-permute-start | bytes 196616 | tf_op jit(solution)/shard_map/ppermute | solution.py:346
  8.4 1.2 %collective-permute-done.4.next_far = f32[128,128]{1,0:T(8,128)S(1)} collective-permute-done((f32[128,128]{1,0:T(8,128)S(1)}, f32[128,128]{1,0:T(8,128)S(1)}, u32[]{:S(2)}, u32[]{:S(2)}) %collective-permute-start.4) | collective-permute-done | bytes 65568 | tf_op jit(solution)/shard_map/ppermute | solution.py:346
  10.8 1.1 %shard_map.85.rest = f32[128,128]{1,0:T(8,128)S(1)} custom-call(f32[128,128]{1,0:T(8,128)S(1)} %get-tuple-element.14.packed.near, f32[128,128]{1,0:T(8,128)S(1)} %collective-permute-done.2.far, f32[128,128]{1,0:T(8,128)S(1)} %collective-permute-done.3.next_near, f32[128,128]{1,0:T(8,128)S(1)} %collective-permute-done.4.next_far, ...), custom_call_target="tpu_custom_call" | custom-call | flops 1000000000 | bytes 1 | tf_op jit(solution)/shard_map/pallas_call | solution.py:302
  12.5 1.7 %collective-permute-start.9 = (f32[10,128,512]{2,1,0:T(8,128)S(1)}, f32[10,128,512]{2,1,0:T(8,128)S(1)}, u32[]{:S(2)}, u32[]{:S(2)}) collective-permute-start(f32[10,128,512]{2,1,0:T(8,128)S(1)} %shard_map.88.own.refs_4_.refs_6_), channel_id=1, source_target_pairs={{0,1},{1,0},{2,3},{3,2},{4,5},{5,4},{6,7},{7,6},{8,9},{9,8},{10,11... | collective-permute-start | bytes 7864328 | tf_op jit(solution)/shard_map/ppermute | solution.py:346
  15.0 2.9 %collective-permute-done.8.next_far.far = f32[128,128]{1,0:T(8,128)S(1)} collective-permute-done((f32[128,128]{1,0:T(8,128)S(1)}, f32[128,128]{1,0:T(8,128)S(1)}, u32[]{:S(2)}, u32[]{:S(2)}) %collective-permute-start.8) | collective-permute-done | bytes 65568 | tf_op jit(solution)/shard_map/ppermute | solution.py:346
  20.2 1.8 %collective-permute-start.10 = (f32[128,128]{1,0:T(8,128)S(1)}, f32[128,128]{1,0:T(8,128)S(1)}, u32[]{:S(2)}, u32[]{:S(2)}) collective-permute-start(f32[128,128]{1,0:T(8,128)S(1)} %shard_map.90.refs_0_), channel_id=1, source_target_pairs={{0,1},{1,0},{2,3},{3,2},{4,8},{5,9},{6,10},{7,11},{8,4},{9,5},{10,... | collective-permute-start | bytes 196616 | tf_op jit(solution)/shard_map/ppermute | solution.py:346
  22.0 2.3 %collective-permute-done.10.more = f32[128,128]{1,0:T(8,128)S(1)} collective-permute-done((f32[128,128]{1,0:T(8,128)S(1)}, f32[128,128]{1,0:T(8,128)S(1)}, u32[]{:S(2)}, u32[]{:S(2)}) %collective-permute-start.10) | collective-permute-done | bytes 65568 | tf_op jit(solution)/shard_map/ppermute | solution.py:346
  24.4 1.6 %collective-permute-start.12 = (f32[128,128]{1,0:T(8,128)S(1)}, f32[128,128]{1,0:T(8,128)S(1)}, u32[]{:S(2)}, u32[]{:S(2)}) collective-permute-start(f32[128,128]{1,0:T(8,128)S(1)} %shard_map.91.near.base), channel_id=1, source_target_pairs={{0,2},{1,3},{2,0},{3,1},{4,5},{5,4},{6,7},{7,6},{8,10},{9,11},{10,... | collective-permute-start | bytes 196616 | tf_op jit(solution)/shard_map/ppermute | solution.py:346
  27.2 2.8 %collective-permute-start.13 = (f32[128,128]{1,0:T(8,128)S(1)}, f32[128,128]{1,0:T(8,128)S(1)}, u32[]{:S(2)}, u32[]{:S(2)}) collective-permute-start(f32[128,128]{1,0:T(8,128)S(1)} %get-tuple-element.21), channel_id=1, source_target_pairs={{0,1},{1,0},{2,3},{3,2},{4,5},{5,4},{6,7},{7,6},{8,16},{9,17},{10,... | collective-permute-start | bytes 196616 | tf_op jit(solution)/shard_map/ppermute | solution.py:346
  30.0 3.5 %collective-permute-start.14 = (f32[128,128]{1,0:T(8,128)S(1)}, f32[128,128]{1,0:T(8,128)S(1)}, u32[]{:S(2)}, u32[]{:S(2)}) collective-permute-start(f32[128,128]{1,0:T(8,128)S(1)} %get-tuple-element.22), channel_id=1, source_target_pairs={{0,4},{1,5},{2,6},{3,7},{4,8},{5,9},{6,10},{7,11},{8,0},{9,1},{10,... | collective-permute-start | bytes 196616 | tf_op jit(solution)/shard_map/ppermute | solution.py:346
  33.5 1.9 %collective-permute-done.16.less = f32[128,128]{1,0:T(8,128)S(1)} collective-permute-done((f32[128,128]{1,0:T(8,128)S(1)}, f32[128,128]{1,0:T(8,128)S(1)}, u32[]{:S(2)}, u32[]{:S(2)}) %collective-permute-start.16) | collective-permute-done | bytes 65568 | tf_op jit(solution)/shard_map/ppermute | solution.py:346
  35.5 3.9 %collective-permute-start.18 = (f32[128,128]{1,0:T(8,128)S(1)}, f32[128,128]{1,0:T(8,128)S(1)}, u32[]{:S(2)}, u32[]{:S(2)}) collective-permute-start(f32[128,128]{1,0:T(8,128)S(1)} %shard_map.95), channel_id=1, source_target_pairs={{0,6},{1,7},{2,4},{3,5},{4,12},{5,13},{6,14},{7,15},{8,9},{9,8},{1... | collective-permute-start | bytes 196616 | tf_op jit(solution)/shard_map/ppermute | solution.py:346
  39.4 1.8 %collective-permute-start.17 = (f32[128,128]{1,0:T(8,128)S(1)}, f32[128,128]{1,0:T(8,128)S(1)}, u32[]{:S(2)}, u32[]{:S(2)}) collective-permute-start(f32[128,128]{1,0:T(8,128)S(1)} %shard_map.95), channel_id=1, source_target_pairs={{0,4},{1,5},{2,6},{3,7},{4,20},{5,21},{6,22},{7,23},{8,9},{9,8},{1... | collective-permute-start | bytes 196616 | tf_op jit(solution)/shard_map/ppermute | solution.py:346
  42.2 1.9 %collective-permute-start.20 = (f32[128,128]{1,0:T(8,128)S(1)}, f32[128,128]{1,0:T(8,128)S(1)}, u32[]{:S(2)}, u32[]{:S(2)}) collective-permute-start(f32[128,128]{1,0:T(8,128)S(1)} %shard_map.99.part), channel_id=1, source_target_pairs={{0,18},{1,19},{2,16},{3,17},{4,0},{5,1},{6,2},{7,3},{8,9},{9,8},{1... | collective-permute-start | bytes 196616 | tf_op jit(solution)/shard_map/ppermute | solution.py:346
  44.1 2.3 %collective-permute-start.26 = (f32[128,128]{1,0:T(8,128)S(1)}, f32[128,128]{1,0:T(8,128)S(1)}, u32[]{:S(2)}, u32[]{:S(2)}) collective-permute-start(f32[128,128]{1,0:T(8,128)S(1)} %shard_map.99.part), channel_id=1, source_target_pairs={{0,10},{1,11},{2,8},{3,9},{4,0},{5,1},{6,2},{7,3},{8,14},{9,15},{1... | collective-permute-start | bytes 196616 | tf_op jit(solution)/shard_map/ppermute | solution.py:346
  46.5 3.6 %collective-permute-start.24 = (f32[128,128]{1,0:T(8,128)S(1)}, f32[128,128]{1,0:T(8,128)S(1)}, u32[]{:S(2)}, u32[]{:S(2)}) collective-permute-start(f32[128,128]{1,0:T(8,128)S(1)} %shard_map.100.other), channel_id=1, source_target_pairs={{0,1},{1,0},{2,3},{3,2},{4,5},{5,4},{6,7},{7,6},{8,14},{9,15},{10,... | collective-permute-start | bytes 196616 | tf_op jit(solution)/shard_map/ppermute | solution.py:346
  50.7 4.6 %collective-permute-start.22 = (f32[128,128]{1,0:T(8,128)S(1)}, f32[128,128]{1,0:T(8,128)S(1)}, u32[]{:S(2)}, u32[]{:S(2)}) collective-permute-start(f32[128,128]{1,0:T(8,128)S(1)} %shard_map.100.other), channel_id=1, source_target_pairs={{0,1},{1,0},{2,3},{3,2},{4,5},{5,4},{6,7},{7,6},{8,9},{9,8},{10,11... | collective-permute-start | bytes 196616 | tf_op jit(solution)/shard_map/ppermute | solution.py:346
  56.7 2.8 %collective-permute-start.27 = (f32[128,128]{1,0:T(8,128)S(1)}, f32[128,128]{1,0:T(8,128)S(1)}, u32[]{:S(2)}, u32[]{:S(2)}) collective-permute-start(f32[128,128]{1,0:T(8,128)S(1)} %shard_map.101.other), channel_id=1, source_target_pairs={{0,1},{1,0},{2,3},{3,2},{4,8},{5,9},{6,10},{7,11},{8,4},{9,5},{10,... | collective-permute-start | bytes 196616 | tf_op jit(solution)/shard_map/ppermute | solution.py:346
  60.2 1.9 %collective-permute-done.28.far = f32[128,128]{1,0:T(8,128)S(1)} collective-permute-done((f32[128,128]{1,0:T(8,128)S(1)}, f32[128,128]{1,0:T(8,128)S(1)}, u32[]{:S(2)}, u32[]{:S(2)}) %collective-permute-start.28) | collective-permute-done | bytes 65568 | tf_op jit(solution)/shard_map/ppermute | solution.py:346
  63.8 5.7 %collective-permute-start.31 = (f32[128,128]{1,0:T(8,128)S(1)}, f32[128,128]{1,0:T(8,128)S(1)}, u32[]{:S(2)}, u32[]{:S(2)}) collective-permute-start(f32[128,128]{1,0:T(8,128)S(1)} %shard_map.103.mine), channel_id=1, source_target_pairs={{0,1},{1,0},{2,3},{3,2},{4,5},{5,4},{6,7},{7,6},{8,9},{9,8},{10,11... | collective-permute-start | bytes 196616 | tf_op jit(solution)/shard_map/ppermute | solution.py:346
  (79 shorter events, 15.3 us)
Async XLA Ops:
  0.7 7.7 %collective-permute-start.5 = (f32[1,128,512]{2,1,0:T(8,128)}, f32[1,128,512]{2,1,0:T(8,128)S(1)}, u32[]{:S(2)}, u32[]{:S(2)}) collective-permute-start(f32[1,128,512]{2,1,0:T(8,128)} %own_e.1), channel_id=1, source_target_pairs={{0,1},{1,0},{2,3},{3,2},{4,5},{5,4},{6,7},{7,6},{8,9},{9,8},{10,11... | collective-permute-start | bytes 786440 | tf_op jit(solution)/shard_map/ppermute | solution.py:346
  3.3 4.8 %collective-permute-start.6 = (f32[128,128]{1,0:T(8,128)S(1)}, f32[128,128]{1,0:T(8,128)S(1)}, u32[]{:S(2)}, u32[]{:S(2)}) collective-permute-start(f32[128,128]{1,0:T(8,128)S(1)} %get-tuple-element.16), channel_id=1, source_target_pairs={{0,2},{1,3},{2,0},{3,1},{4,6},{5,7},{6,4},{7,5},{8,10},{9,11},{10,... | collective-permute-start | bytes 196616 | tf_op jit(solution)/shard_map/ppermute | solution.py:346
  4.5 5.1 %collective-permute-start.4 = (f32[128,128]{1,0:T(8,128)S(1)}, f32[128,128]{1,0:T(8,128)S(1)}, u32[]{:S(2)}, u32[]{:S(2)}) collective-permute-start(f32[128,128]{1,0:T(8,128)S(1)} %get-tuple-element.14.packed.near), channel_id=1, source_target_pairs={{0,1},{1,0},{2,3},{3,2},{4,10},{5,11},{6,8},{7,9},{8,6},{9,7},{10,... | collective-permute-start | bytes 196616 | tf_op jit(solution)/shard_map/ppermute | solution.py:346
  5.8 4.9 %collective-permute-start.3 = (f32[128,128]{1,0:T(8,128)S(1)}, f32[128,128]{1,0:T(8,128)S(1)}, u32[]{:S(2)}, u32[]{:S(2)}) collective-permute-start(f32[128,128]{1,0:T(8,128)S(1)} %get-tuple-element.14.packed.near), channel_id=1, source_target_pairs={{0,1},{1,0},{2,3},{3,2},{4,8},{5,9},{6,10},{7,11},{8,4},{9,5},{10,... | collective-permute-start | bytes 196616 | tf_op jit(solution)/shard_map/ppermute | solution.py:346
  6.9 3.9 %collective-permute-start.2 = (f32[128,128]{1,0:T(8,128)S(1)}, f32[128,128]{1,0:T(8,128)S(1)}, u32[]{:S(2)}, u32[]{:S(2)}) collective-permute-start(f32[128,128]{1,0:T(8,128)S(1)} %get-tuple-element.14.packed.near), channel_id=1, source_target_pairs={{0,2},{1,3},{2,0},{3,1},{4,6},{5,7},{6,4},{7,5},{8,10},{9,11},{10,... | collective-permute-start | bytes 196616 | tf_op jit(solution)/shard_map/ppermute | solution.py:346
  8.1 4.2 %collective-permute-start.7 = (f32[128,128]{1,0:T(8,128)S(1)}, f32[128,128]{1,0:T(8,128)S(1)}, u32[]{:S(2)}, u32[]{:S(2)}) collective-permute-start(f32[128,128]{1,0:T(8,128)S(1)} %get-tuple-element.18), channel_id=1, source_target_pairs={{0,4},{1,5},{2,6},{3,7},{4,0},{5,1},{6,2},{7,3},{8,12},{9,13},{10,... | collective-permute-start | bytes 196616 | tf_op jit(solution)/shard_map/ppermute | solution.py:346
  12.5 6.3 %collective-permute-start.9 = (f32[10,128,512]{2,1,0:T(8,128)S(1)}, f32[10,128,512]{2,1,0:T(8,128)S(1)}, u32[]{:S(2)}, u32[]{:S(2)}) collective-permute-start(f32[10,128,512]{2,1,0:T(8,128)S(1)} %shard_map.88.own.refs_4_.refs_6_), channel_id=1, source_target_pairs={{0,1},{1,0},{2,3},{3,2},{4,5},{5,4},{6,7},{7,6},{8,9},{9,8},{10,11... | collective-permute-start | bytes 7864328 | tf_op jit(solution)/shard_map/ppermute | solution.py:346
  14.3 3.7 %collective-permute-start.8 = (f32[128,128]{1,0:T(8,128)S(1)}, f32[128,128]{1,0:T(8,128)S(1)}, u32[]{:S(2)}, u32[]{:S(2)}) collective-permute-start(f32[128,128]{1,0:T(8,128)S(1)} %get-tuple-element.19), channel_id=1, source_target_pairs={{0,2},{1,3},{2,0},{3,1},{4,6},{5,7},{6,4},{7,5},{8,10},{9,11},{10,... | collective-permute-start | bytes 196616 | tf_op jit(solution)/shard_map/ppermute | solution.py:346
  19.5 4.9 %collective-permute-start.11 = (f32[128,128]{1,0:T(8,128)S(1)}, f32[128,128]{1,0:T(8,128)S(1)}, u32[]{:S(2)}, u32[]{:S(2)}) collective-permute-start(f32[128,128]{1,0:T(8,128)S(1)} %shard_map.89.refs_1_), channel_id=1, source_target_pairs={{0,4},{1,5},{2,6},{3,7},{4,0},{5,1},{6,2},{7,3},{8,12},{9,13},{10,... | collective-permute-start | bytes 196616 | tf_op jit(solution)/shard_map/ppermute | solution.py:346
  20.2 4.1 %collective-permute-start.10 = (f32[128,128]{1,0:T(8,128)S(1)}, f32[128,128]{1,0:T(8,128)S(1)}, u32[]{:S(2)}, u32[]{:S(2)}) collective-permute-start(f32[128,128]{1,0:T(8,128)S(1)} %shard_map.90.refs_0_), channel_id=1, source_target_pairs={{0,1},{1,0},{2,3},{3,2},{4,8},{5,9},{6,10},{7,11},{8,4},{9,5},{10,... | collective-permute-start | bytes 196616 | tf_op jit(solution)/shard_map/ppermute | solution.py:346
  26.8 6.7 %collective-permute-start.15 = (f32[128,128]{1,0:T(8,128)S(1)}, f32[128,128]{1,0:T(8,128)S(1)}, u32[]{:S(2)}, u32[]{:S(2)}) collective-permute-start(f32[128,128]{1,0:T(8,128)S(1)} %get-tuple-element.21), channel_id=1, source_target_pairs={{0,1},{1,0},{2,3},{3,2},{4,8},{5,9},{6,10},{7,11},{8,18},{9,19},{1... | collective-permute-start | bytes 196616 | tf_op jit(solution)/shard_map/ppermute | solution.py:346
  27.2 8.3 %collective-permute-start.13 = (f32[128,128]{1,0:T(8,128)S(1)}, f32[128,128]{1,0:T(8,128)S(1)}, u32[]{:S(2)}, u32[]{:S(2)}) collective-permute-start(f32[128,128]{1,0:T(8,128)S(1)} %get-tuple-element.21), channel_id=1, source_target_pairs={{0,1},{1,0},{2,3},{3,2},{4,5},{5,4},{6,7},{7,6},{8,16},{9,17},{10,... | collective-permute-start | bytes 196616 | tf_op jit(solution)/shard_map/ppermute | solution.py:346
  30.0 5.5 %collective-permute-start.16 = (f32[128,128]{1,0:T(8,128)S(1)}, f32[128,128]{1,0:T(8,128)S(1)}, u32[]{:S(2)}, u32[]{:S(2)}) collective-permute-start(f32[128,128]{1,0:T(8,128)S(1)} %get-tuple-element.22), channel_id=1, source_target_pairs={{0,14},{1,15},{2,12},{3,13},{4,5},{5,4},{6,7},{7,6},{8,2},{9,3},{1... | collective-permute-start | bytes 196616 | tf_op jit(solution)/shard_map/ppermute | solution.py:346
  30.0 5.5 %collective-permute-start.14 = (f32[128,128]{1,0:T(8,128)S(1)}, f32[128,128]{1,0:T(8,128)S(1)}, u32[]{:S(2)}, u32[]{:S(2)}) collective-permute-start(f32[128,128]{1,0:T(8,128)S(1)} %get-tuple-element.22), channel_id=1, source_target_pairs={{0,4},{1,5},{2,6},{3,7},{4,8},{5,9},{6,10},{7,11},{8,0},{9,1},{10,... | collective-permute-start | bytes 196616 | tf_op jit(solution)/shard_map/ppermute | solution.py:346
  35.5 5.7 %collective-permute-start.18 = (f32[128,128]{1,0:T(8,128)S(1)}, f32[128,128]{1,0:T(8,128)S(1)}, u32[]{:S(2)}, u32[]{:S(2)}) collective-permute-start(f32[128,128]{1,0:T(8,128)S(1)} %shard_map.95), channel_id=1, source_target_pairs={{0,6},{1,7},{2,4},{3,5},{4,12},{5,13},{6,14},{7,15},{8,9},{9,8},{1... | collective-permute-start | bytes 196616 | tf_op jit(solution)/shard_map/ppermute | solution.py:346
  42.2 4.3 %collective-permute-start.20 = (f32[128,128]{1,0:T(8,128)S(1)}, f32[128,128]{1,0:T(8,128)S(1)}, u32[]{:S(2)}, u32[]{:S(2)}) collective-permute-start(f32[128,128]{1,0:T(8,128)S(1)} %shard_map.99.part), channel_id=1, source_target_pairs={{0,18},{1,19},{2,16},{3,17},{4,0},{5,1},{6,2},{7,3},{8,9},{9,8},{1... | collective-permute-start | bytes 196616 | tf_op jit(solution)/shard_map/ppermute | solution.py:346
  44.1 11.2 %collective-permute-start.26 = (f32[128,128]{1,0:T(8,128)S(1)}, f32[128,128]{1,0:T(8,128)S(1)}, u32[]{:S(2)}, u32[]{:S(2)}) collective-permute-start(f32[128,128]{1,0:T(8,128)S(1)} %shard_map.99.part), channel_id=1, source_target_pairs={{0,10},{1,11},{2,8},{3,9},{4,0},{5,1},{6,2},{7,3},{8,14},{9,15},{1... | collective-permute-start | bytes 196616 | tf_op jit(solution)/shard_map/ppermute | solution.py:346
  46.4 8.9 %collective-permute-start.25 = (f32[128,128]{1,0:T(8,128)S(1)}, f32[128,128]{1,0:T(8,128)S(1)}, u32[]{:S(2)}, u32[]{:S(2)}) collective-permute-start(f32[128,128]{1,0:T(8,128)S(1)} %shard_map.99.part), channel_id=1, source_target_pairs={{0,8},{1,9},{2,10},{3,11},{4,0},{5,1},{6,2},{7,3},{8,12},{9,13},{1... | collective-permute-start | bytes 196616 | tf_op jit(solution)/shard_map/ppermute | solution.py:346
  46.5 8.9 %collective-permute-start.24 = (f32[128,128]{1,0:T(8,128)S(1)}, f32[128,128]{1,0:T(8,128)S(1)}, u32[]{:S(2)}, u32[]{:S(2)}) collective-permute-start(f32[128,128]{1,0:T(8,128)S(1)} %shard_map.100.other), channel_id=1, source_target_pairs={{0,1},{1,0},{2,3},{3,2},{4,5},{5,4},{6,7},{7,6},{8,14},{9,15},{10,... | collective-permute-start | bytes 196616 | tf_op jit(solution)/shard_map/ppermute | solution.py:346
  50.1 5.2 %collective-permute-start.23 = (f32[128,128]{1,0:T(8,128)S(1)}, f32[128,128]{1,0:T(8,128)S(1)}, u32[]{:S(2)}, u32[]{:S(2)}) collective-permute-start(f32[128,128]{1,0:T(8,128)S(1)} %shard_map.100.other), channel_id=1, source_target_pairs={{0,1},{1,0},{2,3},{3,2},{4,5},{5,4},{6,7},{7,6},{8,12},{9,13},{10,... | collective-permute-start | bytes 196616 | tf_op jit(solution)/shard_map/ppermute | solution.py:346
  50.7 5.6 %collective-permute-start.22 = (f32[128,128]{1,0:T(8,128)S(1)}, f32[128,128]{1,0:T(8,128)S(1)}, u32[]{:S(2)}, u32[]{:S(2)}) collective-permute-start(f32[128,128]{1,0:T(8,128)S(1)} %shard_map.100.other), channel_id=1, source_target_pairs={{0,1},{1,0},{2,3},{3,2},{4,5},{5,4},{6,7},{7,6},{8,9},{9,8},{10,11... | collective-permute-start | bytes 196616 | tf_op jit(solution)/shard_map/ppermute | solution.py:346
  56.7 5.5 %collective-permute-start.28 = (f32[128,128]{1,0:T(8,128)S(1)}, f32[128,128]{1,0:T(8,128)S(1)}, u32[]{:S(2)}, u32[]{:S(2)}) collective-permute-start(f32[128,128]{1,0:T(8,128)S(1)} %shard_map.101.other), channel_id=1, source_target_pairs={{0,1},{1,0},{2,3},{3,2},{4,10},{5,11},{6,8},{7,9},{8,6},{9,7},{10,... | collective-permute-start | bytes 196616 | tf_op jit(solution)/shard_map/ppermute | solution.py:346
  56.7 5.7 %collective-permute-start.27 = (f32[128,128]{1,0:T(8,128)S(1)}, f32[128,128]{1,0:T(8,128)S(1)}, u32[]{:S(2)}, u32[]{:S(2)}) collective-permute-start(f32[128,128]{1,0:T(8,128)S(1)} %shard_map.101.other), channel_id=1, source_target_pairs={{0,1},{1,0},{2,3},{3,2},{4,8},{5,9},{6,10},{7,11},{8,4},{9,5},{10,... | collective-permute-start | bytes 196616 | tf_op jit(solution)/shard_map/ppermute | solution.py:346
  63.8 6.6 %collective-permute-start.31 = (f32[128,128]{1,0:T(8,128)S(1)}, f32[128,128]{1,0:T(8,128)S(1)}, u32[]{:S(2)}, u32[]{:S(2)}) collective-permute-start(f32[128,128]{1,0:T(8,128)S(1)} %shard_map.103.mine), channel_id=1, source_target_pairs={{0,1},{1,0},{2,3},{3,2},{4,5},{5,4},{6,7},{7,6},{8,9},{9,8},{10,11... | collective-permute-start | bytes 196616 | tf_op jit(solution)/shard_map/ppermute | solution.py:346
  (16 other events, 79.8 us)
